TPU v7x, 32 devices: a whole 2x2x4 slice. The times are simulated.
32 devices in a mesh: seq: 8 (over y, x, core), heads: 4 (over z).
Axes of the slice: x: 2, y: 2, z: 4, core: 2. Of those that a mesh axis runs over, the one named last changes fastest.
Arguments:
- queries: bfloat16 [16384, 2048], P('seq', 'heads'), may hold values from -120 to 120
- keys: bfloat16 [512, 2048], P(None, 'heads'), may hold values from -4.2 to 4.2
- values: bfloat16 [512, 2048], P(None, 'heads'), may hold values from -6 to 6
- out_grad: bfloat16 [16384, 2048], P('seq', 'heads'), may hold values from -6 to 6
- key_proj: bfloat16 [2048, 2048], P(None, 'heads'), may hold values from -0.125 to 0.125
- value_proj: bfloat16 [2048, 2048], P(None, 'heads'), may hold values from -0.125 to 0.125
- global_in: bfloat16 [512, 2048], P('seq', 'heads'), may hold values from -6 to 6
- up_proj: bfloat16 [2048, 8192], P('heads', 'seq'), may hold values from -0.125 to 0.125
- down_proj: bfloat16 [8192, 2048], P('seq', 'heads'), may hold values from -0.0625 to 0.0625
Outputs:
- query_grad: bfloat16 [16384, 2048], P('seq', 'heads')
- global_grad: float32 [512, 2048], P('seq', 'heads')
All inputs are finite; a program needn't handle non-finite values.
Results may differ from a plain program's by a relative error of at most 0.014.
Values may be sent and summed in bfloat16 or wider, within the bound.
No kernel may reach another device: no remote copies, remote signals or barrier semaphores. Data moves between devices by JAX's collectives and lax.ppermute only.
A program may use at most 128 MiB of HBM per device.

v0:
```python
import jax
import jax.numpy as jnp
from jax import lax
from jax.sharding import PartitionSpec as P

HD = 128


def slope_of(pre):
    return (
        0.5 * (1.0 + lax.erf(pre * 0.7071067811865476))
        + pre * jnp.exp(-0.5 * pre * pre) * 0.3989422804014327
    )


def project(key_sum, value_sum, key_proj, value_proj):
    first = jnp.einsum(
        "gc,dc->gd", key_sum.astype(jnp.bfloat16), key_proj, preferred_element_type=jnp.float32
    )
    second = jnp.einsum(
        "gc,dc->gd", value_sum.astype(jnp.bfloat16), value_proj, preferred_element_type=jnp.float32
    )
    return first + second


def local(queries, keys, values, out_grad, key_proj, value_proj, global_in, up_proj, down_proj):
    tok_rows, width = queries.shape
    glob_rows = keys.shape[0]
    local_heads = width // HD
    scale = HD ** (-0.5)
    block = min(512, tok_rows)
    blocks = tok_rows // block
    pre_part = jnp.dot(
        lax.all_gather(global_in, "seq", axis=0, tiled=True),
        up_proj,
        preferred_element_type=jnp.float32,
    )
    key_heads = keys.reshape(glob_rows, local_heads, HD)
    value_heads = values.reshape(glob_rows, local_heads, HD)
    query_blocks = queries.reshape(blocks, block, local_heads, HD)
    grad_blocks = out_grad.reshape(blocks, block, local_heads, HD)

    def attend(carry, pair):
        key_total, value_total = carry
        query_block, grad_block = pair
        scores = scale * jnp.einsum(
            "rhd,ghd->hrg", query_block, key_heads, preferred_element_type=jnp.float32
        )
        weights = jax.nn.softmax(scores, axis=-1)
        weight_grad = jnp.einsum(
            "rhd,ghd->hrg", grad_block, value_heads, preferred_element_type=jnp.float32
        )
        centre = jnp.sum(weights * weight_grad, axis=-1, keepdims=True)
        score_grad = (weights * (weight_grad - centre)).astype(jnp.bfloat16)
        weights_low = weights.astype(jnp.bfloat16)
        block_grad = (
            scale
            * jnp.einsum("hrg,ghd->rhd", score_grad, key_heads, preferred_element_type=jnp.float32)
        ).astype(jnp.bfloat16)
        key_total = key_total + jnp.einsum(
            "hrg,rhd->ghd", score_grad, query_block, preferred_element_type=jnp.float32
        )
        value_total = value_total + jnp.einsum(
            "hrg,rhd->ghd", weights_low, grad_block, preferred_element_type=jnp.float32
        )
        return ((key_total, value_total), block_grad)

    empty = jnp.zeros((glob_rows, local_heads, HD), jnp.float32)
    (key_total, value_total), block_grads = lax.scan(
        attend, (empty, empty), (query_blocks, grad_blocks)
    )
    query_grad = block_grads.reshape(tok_rows, width)
    key_total = scale * key_total.reshape(glob_rows, width)
    value_total = value_total.reshape(glob_rows, width)
    key_sum, value_sum = lax.psum((key_total, value_total), "seq")
    state_share = lax.psum_scatter(
        project(key_sum, value_sum, key_proj, value_proj).astype(jnp.bfloat16),
        "heads",
        scatter_dimension=1,
        tiled=True,
    ).astype(jnp.float32)
    state_low = state_share.astype(jnp.bfloat16)
    share_rows = glob_rows // lax.axis_size("seq")
    own_state = lax.dynamic_slice_in_dim(
        state_share, lax.axis_index("seq") * share_rows, share_rows, 0
    )
    back_part = jnp.einsum("gc,fc->gf", state_low, down_proj, preferred_element_type=jnp.float32)
    pre_total, back_total = (
        lax.psum(pre_part.astype(jnp.bfloat16), "heads").astype(jnp.float32),
        lax.psum(back_part.astype(jnp.bfloat16), "heads").astype(jnp.float32),
    )
    gated = (slope_of(pre_total) * back_total).astype(jnp.bfloat16)
    input_part = jnp.einsum("gf,cf->gc", gated, up_proj, preferred_element_type=jnp.float32)
    global_grad = own_state + lax.psum_scatter(input_part, "seq", scatter_dimension=0, tiled=True)
    return (query_grad, global_grad)


def solution(mesh):
    placed = (
        P("seq", "heads"),
        P(None, "heads"),
        P(None, "heads"),
        P("seq", "heads"),
        P(None, "heads"),
        P(None, "heads"),
        P("seq", "heads"),
        P("heads", "seq"),
        P("seq", "heads"),
    )
    return jax.shard_map(
        local,
        mesh=mesh,
        in_specs=placed,
        out_specs=(P("seq", "heads"), P("seq", "heads")),
        check_vma=False,
    )
```

profile of v0, /device:TPU:0, one launch (start us, length us, event | category | flops | bytes accessed | tf_op | source)
XLA Modules:
  0.0 349.4 jit_solution(8394042608013113043)
XLA Ops:
  7.3 1.4 copy.22
  11.2 4.0 %reshape.28 = bf16[4,512,4,128]{3,2,1,0:T(4,128)(2,1)} reshape(bf16[2048,512]{1,0:T(8,128)(2,1)} %param.11) | data formatting | bytes 4194304 | tf_op jit(solution)/shard_map/reshape | solution.py:40
  15.2 4.0 %reshape.30 = bf16[4,512,4,128]{3,2,1,0:T(4,128)(2,1)} reshape(bf16[2048,512]{1,0:T(8,128)(2,1)} %param.14) | data formatting | bytes 4194304 | tf_op jit(solution)/shard_map/reshape | solution.py:41
  19.2 83.3 %while.15 = (s32[]{:T(128)}, f32[512,4,128]{0,2,1:T(8,128)}, f32[512,4,128]{0,2,1:T(8,128)}, bf16[4,512,4,128]{3,2,1,0:T(4,128)(2,1)}, bf16[4,512,4,128]{3,2,1,0...) while((s32[]{:T(128)}, f32[512,4,128]{0,2,1:T(8,128)}, ...), condition=%wide.region_4.5_spmd.clone, body=%wide.region_0.4_spmd.clone.sunk | while | flops 1360528384 | bytes 93372648 | solution.py:69
  19.2 2.4 constant_dynamic-slice_fusion.3
  22.3 3.2 fusion.77
  25.4 6.4 %fusion.79 = f32[512,4,128]{0,2,1:T(8,128)} fusion(f32[512,4,128]{0,2,1:T(8,128)} %get-tuple-element.183, pred[]{:T(512)S(6)} %compare.3, bf16[1,512,4,128]{3,2,1,0:T(4,128)(2,1)} %get-tuple-element.168, f32[4,512]{1,0:T(4,128)S(1)} %get-tuple-element.167, f32[4,512,512]{1,2,0:T(8,128)} %copy-done.2), kind=kOutput, calls=%fused_computation.12.clone.1 | convolution fusion | flops 274205184 | bytes 6823937 | tf_op jit(solution)/shard_map/while/body/eval_jaxpr/hrg,rhd->ghd/dot_general | solution.py:63
  31.8 3.4 multiply_reduce_fusion.3
  39.9 2.4 constant_dynamic-slice_fusion.3
  42.9 3.2 fusion.77
  46.1 6.6 %fusion.79 = f32[512,4,128]{0,2,1:T(8,128)} fusion(f32[512,4,128]{0,2,1:T(8,128)} %get-tuple-element.183, pred[]{:T(512)S(6)} %compare.3, bf16[1,512,4,128]{3,2,1,0:T(4,128)(2,1)} %get-tuple-element.168, f32[4,512]{1,0:T(4,128)S(1)} %get-tuple-element.167, f32[4,512,512]{1,2,0:T(8,128)} %copy-done.2), kind=kOutput, calls=%fused_computation.12.clone.1 | convolution fusion | flops 274205184 | bytes 6823937 | tf_op jit(solution)/shard_map/while/body/eval_jaxpr/hrg,rhd->ghd/dot_general | solution.py:63
  52.7 3.4 multiply_reduce_fusion.3
  60.7 2.4 constant_dynamic-slice_fusion.3
  63.8 3.2 fusion.77
  67.0 6.6 %fusion.79 = f32[512,4,128]{0,2,1:T(8,128)} fusion(f32[512,4,128]{0,2,1:T(8,128)} %get-tuple-element.183, pred[]{:T(512)S(6)} %compare.3, bf16[1,512,4,128]{3,2,1,0:T(4,128)(2,1)} %get-tuple-element.168, f32[4,512]{1,0:T(4,128)S(1)} %get-tuple-element.167, f32[4,512,512]{1,2,0:T(8,128)} %copy-done.2), kind=kOutput, calls=%fused_computation.12.clone.1 | convolution fusion | flops 274205184 | bytes 6823937 | tf_op jit(solution)/shard_map/while/body/eval_jaxpr/hrg,rhd->ghd/dot_general | solution.py:63
  73.6 3.4 multiply_reduce_fusion.3
  81.6 2.4 constant_dynamic-slice_fusion.3
  84.7 3.2 fusion.77
  87.9 6.6 %fusion.79 = f32[512,4,128]{0,2,1:T(8,128)} fusion(f32[512,4,128]{0,2,1:T(8,128)} %get-tuple-element.183, pred[]{:T(512)S(6)} %compare.3, bf16[1,512,4,128]{3,2,1,0:T(4,128)(2,1)} %get-tuple-element.168, f32[4,512]{1,0:T(4,128)S(1)} %get-tuple-element.167, f32[4,512,512]{1,2,0:T(8,128)} %copy-done.2), kind=kOutput, calls=%fused_computation.12.clone.1 | convolution fusion | flops 274205184 | bytes 6823937 | tf_op jit(solution)/shard_map/while/body/eval_jaxpr/hrg,rhd->ghd/dot_general | solution.py:63
  94.5 3.4 multiply_reduce_fusion.3
  102.5 2.3 broadcast_multiply_fusion
  104.8 58.9 %all-reduce.6 = (bf16[512,512]{0,1:T(8,128)(2,1)S(1)}, bf16[512,512]{0,1:T(8,128)(2,1)S(1)}) all-reduce(f32[512,512]{0,1:T(8,128)} %bitcast.69, f32[512,512]{0,1:T(8,128)} %bitcast.74), channel_id=1, replica_groups=mesh['seq'=8,'heads'=4] {'seq'}, use_global_device_ids=true, to_apply=%region_5.6 | all-reduce | flops 524288 | bytes 3145728 | tf_op jit(solution)/shard_map/psum | solution.py:75
  165.3 2.6 add_convert_fusion
  168.8 9.3 %all_gather.3 = bf16[512,512]{1,0:T(8,128)(2,1)S(1)} all-gather(bf16[64,512]{1,0:T(8,128)(2,1)S(1)} %copy-done.6), channel_id=1, replica_groups=mesh['seq'=8,'heads'=4] {'seq'}, dimensions={0}, use_global_device_ids=true | all-gather | bytes 589824 | tf_op jit(solution)/shard_map/all_gather | solution.py:34
  178.1 2.9 convolution_convert_fusion.1
  181.0 31.4 %reduce-scatter.3.cloned.1.call-done = bf16[512,512]{1,0:T(8,128)(2,1)} async-done(((bf16[512,2048]{1,0:T(8,128)(2,1)}), bf16[512,512]{1,0:T(8,128)(2,1)}) %reduce-scatter.3.cloned.1.call-update) | async-done | bytes 524304 | tf_op jit(solution)/shard_map/reduce_scatter | solution.py:76
  212.4 3.1 convolution_convert_fusion
  215.6 86.5 %all-reduce.5.cloned.1.call-done = (bf16[512,1024]{1,0:T(8,128)(2,1)}, bf16[512,1024]{1,0:T(8,128)(2,1)}) async-done(((bf16[512,1024]{1,0:T(8,128)(2,1)}, bf16[512,1024]{1,0:T(8,128)(2,1)}), (bf16[512,1024]{1,0:T(8,128)(2,1)}, bf16[512,1024]{1,0:T(8,128)(2,1)})) %all-reduce.5.cloned.1.call-update) | async-done | bytes 2097168 | tf_op jit(solution)/shard_map/psum | solution.py:90
  302.1 4.0 %fusion.31 = f32[512,512]{1,0:T(8,128)} fusion(bf16[512,1024]{1,0:T(8,128)(2,1)} %param.18, bf16[512,1024]{1,0:T(8,128)(2,1)} %get-tuple-element.102, bf16[512,1024]{1,0:T(8,128)(2,1)} %get-tuple-element.103), kind=kOutput, calls=%fused_computation.41 | convolution fusion | flops 543162368 | bytes 4194304 | tf_op jit(solution)/shard_map/gf,cf->gc/dot_general | solution.py:93
  306.1 3.3 copy.49
  309.4 31.9 %reduce-scatter.5.cloned.1.call-done = f32[64,512]{1,0:T(8,128)} async-done(((f32[512,512]{1,0:T(8,128)}), f32[64,512]{1,0:T(8,128)}) %reduce-scatter.5.cloned.1.call-update) | async-done | bytes 131088 | tf_op jit(solution)/shard_map/reduce_scatter | solution.py:94
  341.3 1.6 convert_add_fusion
  (71 shorter events, 26.4 us)
Async XLA Ops:
  7.2 156.6 %copy-start = (bf16[2048,512]{1,0:T(8,128)(2,1)S(1)}, bf16[2048,512]{1,0:T(8,128)(2,1)}, u32[]{:S(2)}) copy-start(bf16[2048,512]{1,0:T(8,128)(2,1)} %param.15) | copy-start | bytes 6291460
  7.2 205.2 %reduce-scatter.3.cloned.1.call-start = ((), (), s32[]{:S(2)}) async-start(), calls=%async_computation.2 | async-start | bytes 2621440 | tf_op jit(solution)/shard_map/reduce_scatter | solution.py:76
  22.2 3.2 copy-start.2
  31.8 3.7 %copy-start.1 = (f32[4,512,512]{1,2,0:T(8,128)S(1)}, f32[4,512,512]{1,2,0:T(8,128)}, u32[]{:S(2)}) copy-start(f32[4,512,512]{1,2,0:T(8,128)} %get-tuple-element.166) | copy-start | bytes 12582916 | tf_op jit(solution)/shard_map/while
  35.6 1.2 copy-start.3
  37.7 2.2 copy-start.4
  42.9 3.2 copy-start.2
  52.7 3.7 %copy-start.1 = (f32[4,512,512]{1,2,0:T(8,128)S(1)}, f32[4,512,512]{1,2,0:T(8,128)}, u32[]{:S(2)}) copy-start(f32[4,512,512]{1,2,0:T(8,128)} %get-tuple-element.166) | copy-start | bytes 12582916 | tf_op jit(solution)/shard_map/while
  56.5 1.2 copy-start.3
  58.6 2.2 copy-start.4
  63.8 3.2 copy-start.2
  73.6 3.7 %copy-start.1 = (f32[4,512,512]{1,2,0:T(8,128)S(1)}, f32[4,512,512]{1,2,0:T(8,128)}, u32[]{:S(2)}) copy-start(f32[4,512,512]{1,2,0:T(8,128)} %get-tuple-element.166) | copy-start | bytes 12582916 | tf_op jit(solution)/shard_map/while
  77.3 1.2 copy-start.3
  79.5 2.1 copy-start.4
  84.7 3.2 copy-start.2
  94.5 3.7 %copy-start.1 = (f32[4,512,512]{1,2,0:T(8,128)S(1)}, f32[4,512,512]{1,2,0:T(8,128)}, u32[]{:S(2)}) copy-start(f32[4,512,512]{1,2,0:T(8,128)} %get-tuple-element.166) | copy-start | bytes 12582916 | tf_op jit(solution)/shard_map/while
  98.2 1.2 copy-start.3
  100.3 2.2 copy-start.4
  163.7 1.6 copy-start.5
  168.0 0.8 copy-start.6
  168.0 134.1 %all-reduce.5.cloned.1.call-start = ((), (), s32[]{:S(2)}) async-start(), calls=%async_computation.4 | async-start | bytes 4194304 | tf_op jit(solution)/shard_map/psum | solution.py:90
  215.5 125.7 %reduce-scatter.5.cloned.1.call-start = ((), (), s32[]{:S(2)}) async-start(), calls=%async_computation.3 | async-start | bytes 1179648 | tf_op jit(solution)/shard_map/reduce_scatter | solution.py:94
Sparse Core Ops, SparseCore 0:
  168.1 44.2 reduce-scatter.2
  215.7 86.3 all-reduce.4
  306.3 34.9 reduce-scatter.4
where the time goes:
time: 350 us; the launch traced here: 349 us
  waiting for transfers between devices  150 us (43%)
  blocking collectives  68.2 us (19%)
  matrix products  63.7 us (18%)
  local copies, waits for them, and re-layouts  32.2 us (9%)
  other arithmetic  21.3 us (6%)
  between operations  13.8 us (4%)
    psum x1, waiting for transfers between devices, local(): lax.psum(back_part.astype(jnp.bfloat16), 'heads').astype(jnp.float32)  86.5 us
    psum x1, blocking collectives, local(): key_sum, value_sum = lax.psum((key_total, value_total), 'seq')  58.9 us
    reduce_scatter x1, waiting for transfers between devices, local(): lax.psum_scatter(input_part, 'seq', scatter_dimension=0, tiled=True)  31.9 us
    reduce_scatter x1, waiting for transfers between devices, local(): lax.psum_scatter(project(key_sum, value_sum, key_proj, value_proj).astype...  31.4 us
    dot_general x4, matrix products, attend(): jnp.einsum('hrg,rhd->ghd', weights_low, grad_block, preferred_element_typ...  26.1 us
    dot_general x4, matrix products, attend(): jnp.einsum('rhd,ghd->hrg', grad_block, value_heads, preferred_element_typ...  13.5 us
    sub x4, other arithmetic, attend(): weights = jax.nn.softmax(scores, axis=-1)  12.7 us
    dynamic_slice x4, local copies, waits for them, and re-layouts, local(): lax.scan(attend, (empty, empty), (query_blocks, grad_blocks))  9.49 us
  transfers between devices with their start and end apart: 3, of which 3 were waited for; matrix products, arithmetic and copies ran while one was open for 2% of the time, Pallas kernels for 0%

commit v1 on v0

v1 whole, which is shorter than its diff:
```python
import functools
import math

import jax
import jax.numpy as jnp
from jax import lax
from jax.experimental import pallas as pl
from jax.experimental.pallas import tpu as pltpu
from jax.sharding import PartitionSpec as P

HD = 128
SCALE = HD**-0.5
SCALE_LOG2 = SCALE * math.log2(math.e)
BF16, F32 = jnp.bfloat16, jnp.float32
NT = (((1,), (1,)), ((), ()))
NN = (((1,), (0,)), ((), ()))
TN = (((0,), (0,)), ((), ()))
VMEM_BYTES = 48 * 2**20


def dot(a, b, dims):
    return lax.dot_general(a, b, dims, preferred_element_type=F32)


def slope_of(pre):
    return (
        0.5 * (1.0 + lax.erf(pre * 0.7071067811865476))
        + pre * jnp.exp(-0.5 * pre * pre) * 0.3989422804014327
    )


def swap(x, axis, distance):
    size = lax.axis_size(axis)
    return lax.ppermute(x, axis, [(i, i ^ distance) for i in range(size)])


def levels_of(first, count):
    levels = []
    while count > 1:
        radix = min(4, count)
        levels.append((first, radix))
        first, count = first * radix, count // radix
    return levels


def gather_blocks(x, axis, first, count):
    blocks = [x]
    for step, radix in levels_of(first, count):
        whole = blocks[0] if len(blocks) == 1 else jnp.stack(blocks)
        got = [swap(whole, axis, step * k) for k in range(1, radix)]
        for other in got:
            blocks = blocks + ([other] if whole is x else list(other))
    return blocks


def scatter_terms(blocks, axis, first, low=BF16):
    levels = levels_of(first, len(blocks))
    for step, radix in reversed(levels[1:]):
        span = step // first
        terms = [blocks[k * span : (k + 1) * span] for k in range(radix)]
        got = [swap(jnp.stack(terms[k]), axis, step * k) for k in range(1, radix)]
        blocks = [
            (terms[0][i].astype(F32) + sum(g[i].astype(F32) for g in got)).astype(low)
            for i in range(span)
        ]
    return [blocks[0]] + [swap(blocks[k], axis, first * k) for k in range(1, len(blocks))]


def attend_kernel(sub, place_ref, q_ref, g_ref, k_ref, v_ref, *rest):
    dq_ref, even_ref, odd_ref, acc_ref, turned_ref = rest[-5:]
    block = pl.program_id(1)

    @pl.when(block == 0)
    def _():
        acc_ref[...] = jnp.zeros_like(acc_ref)

    keys, values = k_ref[...], v_ref[...]
    key_part = value_part = None
    for i in range(q_ref.shape[0] // sub):
        rows = pl.ds(i * sub, sub)
        q, g = q_ref[rows, :], g_ref[rows, :]
        scores = dot(q, keys, NT)
        weight_grad = dot(g, values, NT)
        top = jnp.max(scores, axis=1, keepdims=True)
        grown = jnp.exp2((scores - top) * SCALE_LOG2)
        over = 1.0 / jnp.sum(grown, axis=1, keepdims=True)
        centre = jnp.sum(grown * weight_grad, axis=1, keepdims=True) * over
        weights = grown * over
        score_grad = (weights * (weight_grad - centre)).astype(BF16)
        dq_ref[rows, :] = (SCALE * dot(score_grad, keys, NN)).astype(BF16)
        key_term = dot(q, score_grad, TN)
        value_term = dot(g, weights.astype(BF16), TN)
        key_part = key_term if key_part is None else key_part + key_term
        value_part = value_term if value_part is None else value_part + value_term
    acc_ref[:HD, :] += key_part
    acc_ref[HD:, :] += value_part

    @pl.when(block == pl.num_programs(1) - 1)
    def _():
        turned_ref[:, :HD] = SCALE * acc_ref[:HD, :].T
        turned_ref[:, HD:] = acc_ref[HD:, :].T
        half, height = even_ref.shape[:2]
        for j in range(2 * half):
            at = pl.ds(pl.multiple_of(place_ref[j] * height, height), height)
            (odd_ref if j % 2 else even_ref)[j // 2] = turned_ref[at, :].astype(BF16)


def attend(place, queries, out_grad, keys, values, query_grad, first, count):
    tokens, width = queries.shape
    glob = keys.shape[0]
    size = place.shape[0]
    block = min(512, tokens)
    sub = min(256, block)
    token_spec = pl.BlockSpec((block, HD), lambda h, b, place: (b, h + first))
    global_spec = pl.BlockSpec((glob, HD), lambda h, b, place: (0, h + first))
    part_spec = pl.BlockSpec((size // 2, glob // size, 2 * HD), lambda h, b, place: (0, 0, h))
    part = jax.ShapeDtypeStruct((size // 2, glob // size, 2 * HD * count), BF16)
    operands = [place, queries, out_grad, keys, values]
    specs = [token_spec, token_spec, global_spec, global_spec]
    aliases = {}
    if query_grad is not None:
        operands.append(query_grad)
        specs.append(pl.BlockSpec(memory_space=pl.ANY))
        aliases = {5: 0}
    return pl.pallas_call(
        functools.partial(attend_kernel, sub),
        grid_spec=pltpu.PrefetchScalarGridSpec(
            num_scalar_prefetch=1,
            grid=(count, tokens // block),
            in_specs=specs,
            out_specs=[token_spec, part_spec, part_spec],
            scratch_shapes=[pltpu.VMEM((2 * HD, glob), F32), pltpu.VMEM((glob, 2 * HD), F32)],
        ),
        out_shape=[jax.ShapeDtypeStruct((tokens, width), BF16), part, part],
        input_output_aliases=aliases,
        compiler_params=pltpu.CompilerParams(vmem_limit_bytes=VMEM_BYTES),
        cost_estimate=pl.CostEstimate(
            flops=20 * tokens * glob * HD * count,
            bytes_accessed=6 * tokens * HD * count,
            transcendentals=tokens * glob * count,
        ),
        name="attend",
    )(*operands)


def scatter_rows(even, odd):
    got = swap(odd, "seq", 1)
    mine = (even.astype(F32) + got.astype(F32)).astype(BF16)
    return scatter_terms(list(mine), "seq", 2)


def project_kernel(count, chunk_ref, *refs):
    terms, rest = refs[:count], refs[count:]
    key_proj_ref, value_proj_ref, part_ref = rest[0], rest[1], rest[-1]
    total = sum(t[...].astype(F32) for t in terms).astype(BF16)
    heads = total.shape[1] // (2 * HD)
    pick = lambda at: [total[:, (2 * h + at) * HD : (2 * h + at + 1) * HD] for h in range(heads)]
    key_low, value_low = jnp.concatenate(pick(0), 1), jnp.concatenate(pick(1), 1)
    part = dot(key_low, key_proj_ref[...], NT) + dot(value_low, value_proj_ref[...], NT)
    if len(rest) == 4:
        part = part + rest[2][...]
    part_ref[...] = part


def project(chunk, terms, key_proj, value_proj, first, before):
    rows, width = terms[0].shape
    count = width // (2 * HD)
    size = chunk.shape[0]
    block = key_proj.shape[0] // size
    wide = count * HD
    term_spec = pl.BlockSpec((rows, width), lambda k, chunk: (0, 0))
    weight_spec = pl.BlockSpec((block, wide), lambda k, chunk: (chunk[k], first // count))
    part_spec = pl.BlockSpec((None, rows, block), lambda k, chunk: (k, 0, 0))
    operands = [chunk, *terms, key_proj, value_proj]
    specs = [term_spec] * len(terms) + [weight_spec] * 2
    if before is not None:
        operands.append(before)
        specs.append(part_spec)
    return pl.pallas_call(
        functools.partial(project_kernel, len(terms)),
        grid_spec=pltpu.PrefetchScalarGridSpec(
            num_scalar_prefetch=1, grid=(size,), in_specs=specs, out_specs=part_spec
        ),
        out_shape=jax.ShapeDtypeStruct((size, rows, block), F32),
        compiler_params=pltpu.CompilerParams(vmem_limit_bytes=VMEM_BYTES),
        name="project",
    )(*operands)


def feed_kernel(state_ref, down_ref, up_ref, slope_ref, out_ref, acc_ref):
    step = pl.program_id(0)
    back = dot(state_ref[...], down_ref[...], NT)
    gated = (slope_ref[...] * back).astype(BF16)
    part = dot(gated, up_ref[...], NT)

    @pl.when(step == 0)
    def _():
        acc_ref[...] = part

    @pl.when(step > 0)
    def _():
        acc_ref[...] += part

    @pl.when(step == pl.num_programs(0) - 1)
    def _():
        out_ref[...] = acc_ref[...].astype(BF16)


def feed(state, down, up, slope):
    rows, width = state.shape
    hidden = up.shape[1]
    chunk = hidden if hidden % 128 else 128
    return pl.pallas_call(
        feed_kernel,
        grid=(hidden // chunk,),
        in_specs=[
            pl.BlockSpec((rows, width), lambda f: (0, 0)),
            pl.BlockSpec((chunk, width), lambda f: (f, 0)),
            pl.BlockSpec((width, chunk), lambda f: (0, f)),
            pl.BlockSpec((rows, chunk), lambda f: (0, f)),
        ],
        out_specs=pl.BlockSpec((rows, width), lambda f: (0, 0)),
        out_shape=jax.ShapeDtypeStruct((rows, width), BF16),
        scratch_shapes=[pltpu.VMEM((rows, width), F32)],
        compiler_params=pltpu.CompilerParams(vmem_limit_bytes=VMEM_BYTES),
        name="feed",
    )(state, down, up, slope)


def local(queries, keys, values, out_grad, key_proj, value_proj, global_in, up_proj, down_proj):
    size, planes = lax.axis_size("seq"), lax.axis_size("heads")
    place = lax.axis_index("seq") ^ jnp.arange(size, dtype=jnp.int32)
    chunk = lax.axis_index("heads") ^ jnp.arange(planes, dtype=jnp.int32)
    local_heads = queries.shape[1] // HD
    far = size // 2

    part = up_proj.shape[1] // planes
    up_parts = [
        lax.dynamic_slice_in_dim(up_proj, chunk[k] * part, part, 1) for k in range(planes)
    ]
    up_own = jnp.concatenate(
        [up_parts[0]] + [swap(up_parts[k], "heads", k) for k in range(1, planes)], 0
    )
    up = jnp.concatenate([up_own, swap(up_own, "seq", 1)], 1)
    down_parts = [
        lax.dynamic_slice_in_dim(down_proj, chunk[k] * part, part, 0) for k in range(planes)
    ]
    down_own = jnp.concatenate(
        [down_parts[0]] + [swap(down_parts[k], "heads", k) for k in range(1, planes)], 1
    )
    down = jnp.concatenate([down_own, swap(down_own, "seq", 1)], 0)
    wide_in = jnp.concatenate(gather_blocks(global_in, "heads", 1, planes), 1)
    all_in = jnp.concatenate(gather_blocks(wide_in, "seq", 2, far), 0)
    slope = slope_of(jnp.dot(all_in, up, preferred_element_type=F32))

    split = local_heads - 1
    query_grad, even, odd = attend(place, queries, out_grad, keys, values, None, 0, split)
    terms = scatter_rows(even, odd)
    query_grad, even, odd = attend(
        place, queries, out_grad, keys, values, query_grad, split, local_heads - split
    )
    first_share = project(chunk, terms, key_proj, value_proj, 0, None)
    share = project(chunk, scatter_rows(even, odd), key_proj, value_proj, split, first_share)
    state = share[0] + sum(
        swap(share[k].astype(BF16), "heads", k).astype(F32) for k in range(1, planes)
    )
    wide_state = jnp.concatenate(gather_blocks(state.astype(BF16), "heads", 1, planes), 1)
    all_state = jnp.concatenate(gather_blocks(wide_state, "seq", 2, far), 0)

    rows = state.shape[0]
    width = state.shape[1]
    grown = feed(all_state, down, up, slope)
    own_terms = scatter_terms(list(grown.reshape(far, rows, planes * width)), "seq", 2)
    own = sum(t.astype(F32) for t in own_terms)
    blocks = [own[:, k * width : (k + 1) * width] for k in range(planes)]
    global_grad = state + blocks[0] + sum(
        swap(blocks[k].astype(BF16), "heads", k).astype(F32) for k in range(1, planes)
    )
    return (query_grad, global_grad)


def solution(mesh):
    placed = (
        P("seq", "heads"),
        P(None, "heads"),
        P(None, "heads"),
        P("seq", "heads"),
        P(None, "heads"),
        P(None, "heads"),
        P("seq", "heads"),
        P("heads", "seq"),
        P("seq", "heads"),
    )
    return jax.shard_map(
        local,
        mesh=mesh,
        in_specs=placed,
        out_specs=(P("seq", "heads"), P("seq", "heads")),
        check_vma=False,
    )
```

time: 350 us -> 171 us (0.49)
  waiting for transfers between devices: 150 us -> 50.4 us
  starting transfers between devices: 0.12 us -> 72.9 us
  blocking collectives: 68.2 us -> 0 us
  matrix products: 63.7 us -> 0.87 us
  Pallas kernels: 0 us -> 34.7 us
  local copies, waits for them, and re-layouts: 32.2 us -> 6.33 us
  other arithmetic: 21.3 us -> 1.76 us
  between operations: 13.8 us -> 3.48 us
    psum x1 -> x0, waiting for transfers between devices: 86.5 us -> none  [local(): lax.psum(back_part.astype(jnp.bfloat16), 'heads').astype(jnp.float32)]
    ppermute x0 -> x37, starting transfers between devices: none -> 72.9 us  [swap(): return lax.ppermute(x, axis, [(i, i ^ distance) for i in range(size)])]
    reduce_scatter x2 -> x0, waiting for transfers between devices: 63.2 us -> none  [the longest x1 31.9 us: local(): lax.psum_scatter(input_part, 'seq', scatter_dimension=0, tiled=True)]
    dot_general x25 -> x1, matrix products: 63.7 us -> 0.87 us  [local(): slope = slope_of(jnp.dot(all_in, up, preferred_element_type=F32))]
    psum x1 -> x0, blocking collectives: 58.9 us -> none  [local(): key_sum, value_sum = lax.psum((key_total, value_total), 'seq')]
    ppermute x0 -> x37, waiting for transfers between devices: none -> 50.4 us  [swap(): return lax.ppermute(x, axis, [(i, i ^ distance) for i in range(size)])]
    pallas_call x0 -> x5, Pallas kernels: none -> 34.7 us  [the longest x2 23.5 us: attend(): pl.pallas_call(functools.partial(attend_kernel, sub), grid_spec=pltpu.Pre...]
    sub x4 -> x0, other arithmetic: 12.7 us -> none  [attend(): weights = jax.nn.softmax(scores, axis=-1)]
  transfers between devices with their start and end apart: 3 -> 37, of which waited for: 3 -> 16; matrix products, arithmetic and copies ran while one was open for 2% -> 1% of each run, Pallas kernels for 0% -> 6%
where the time goes in v1:
time: 171 us; the launch traced here: 170 us
  starting transfers between devices  72.9 us (43%)
  waiting for transfers between devices  50.4 us (29%)
  Pallas kernels  34.7 us (20%)
  local copies, waits for them, and re-layouts  6.33 us (4%)
  between operations  3.48 us (2%)
  other arithmetic  1.76 us (1%)
    ppermute x37, starting transfers between devices, swap(): return lax.ppermute(x, axis, [(i, i ^ distance) for i in range(size)])  72.9 us
    ppermute x37, waiting for transfers between devices, swap(): return lax.ppermute(x, axis, [(i, i ^ distance) for i in range(size)])  50.4 us
    pallas_call x2, Pallas kernels, attend(): pl.pallas_call(functools.partial(attend_kernel, sub), grid_spec=pltpu.Pre...  23.5 us
    pallas_call x1, Pallas kernels, feed(): pl.pallas_call(feed_kernel, grid=(hidden // chunk,), in_specs=[pl.BlockSp...  7.1 us
    unnamed x23, local copies, waits for them, and re-layouts  5.31 us
    pallas_call x2, Pallas kernels, project(): pl.pallas_call(functools.partial(project_kernel, len(terms)), grid_spec=p...  4.16 us
  transfers between devices with their start and end apart: 37, of which 16 were waited for; matrix products, arithmetic and copies ran while one was open for 1% of the time, Pallas kernels for 6%

profile of v1, /device:TPU:0, one launch (start us, length us, event | category | flops | bytes accessed | tf_op | source)
XLA Modules:
  0.0 170.5 jit_solution(12995408523321127467)
XLA Ops:
  0.7 1.6 copy-done.2
  2.2 1.6 copy-done.3
  5.9 17.1 %attend.2 = (bf16[2048,512]{1,0:T(8,128)(2,1)}, bf16[4,64,768]{2,1,0:T(8,128)(2,1)S(1)}, bf16[4,64,768]{2,1,0:T(8,128)(2,1)S(1)}) custom-call(s32[8]{0:T(128)S(1)} %iota_xor_fusion.1.place_ref, bf16[2048,512]{1,0:T(8,128)(2,1)S(1)} %copy-done.2, bf16[2048,512]{1,0:T(8,128)(2,1)S(1)} %copy-done.3, bf16[512,512]{1,0:T(8,128)(2,1)S(1)} %copy-done.4, ...), custom_call_target="tpu_custom_call" | custom-call | flops 8053063680 | bytes 4718592 | tf_op jit(solution)/shard_map/attend/pallas_call | solution.py:125
  23.4 6.4 %attend.3 = (bf16[2048,512]{1,0:T(8,128)(2,1)}, bf16[4,64,256]{2,1,0:T(8,128)(2,1)S(1)}, bf16[4,64,256]{2,1,0:T(8,128)(2,1)S(1)}) custom-call(s32[8]{0:T(128)S(1)} %iota_xor_fusion.1.place_ref, bf16[2048,512]{1,0:T(8,128)(2,1)S(1)} %copy-done.2, bf16[2048,512]{1,0:T(8,128)(2,1)S(1)} %copy-done.3, ...), custom_call_target="tpu_custom_call", output_to_operand_aliasing={{0}: (5, {})} | custom-call | flops 2684354560 | bytes 1572864 | tf_op jit(solution)/shard_map/attend/pallas_call | solution.py:125
  33.5 3.0 %collective-permute-start.5 = (bf16[64,768]{1,0:T(8,128)(2,1)S(1)}, bf16[64,768]{1,0:T(8,128)(2,1)S(1)}, u32[]{:S(2)}, u32[]{:S(2)}) collective-permute-start(bf16[64,768]{1,0:T(8,128)(2,1)S(1)} %get-tuple-element.29), channel_id=1, source_target_pairs={{0,8},{4,12},{8,0},{12,4},{16,24},{20,28},{24,16},{28,20},{1,9},{5... | collective-permute-start | bytes 294920 | tf_op jit(solution)/shard_map/ppermute | solution.py:34
  36.6 2.0 %collective-permute-start.2 = (bf16[64,256]{1,0:T(8,128)(2,1)S(1)}, bf16[64,256]{1,0:T(8,128)(2,1)S(1)}, u32[]{:S(2)}, u32[]{:S(2)}) collective-permute-start(bf16[64,256]{1,0:T(8,128)(2,1)S(1)} %get-tuple-element.38), channel_id=1, source_target_pairs={{0,16},{4,20},{8,24},{12,28},{16,0},{20,4},{24,8},{28,12},{1,17},{... | collective-permute-start | bytes 98312 | tf_op jit(solution)/shard_map/ppermute | solution.py:34
  42.6 3.2 %collective-permute-done.6.refs_2_ = bf16[64,768]{1,0:T(8,128)(2,1)S(1)} collective-permute-done((bf16[64,768]{1,0:T(8,128)(2,1)S(1)}, bf16[64,768]{1,0:T(8,128)(2,1)S(1)}, u32[]{:S(2)}, u32[]{:S(2)}) %collective-permute-start.6) | collective-permute-done | bytes 98336 | tf_op jit(solution)/shard_map/ppermute | solution.py:34
  47.3 2.6 %collective-permute-start.22 = (bf16[512,256]{1,0:T(8,128)(2,1)S(1)}, bf16[512,256]{1,0:T(8,128)(2,1)S(1)}, u32[]{:S(2)}, u32[]{:S(2)}) collective-permute-start(bf16[512,256]{1,0:T(8,128)(2,1)S(1)} %get-tuple-element.22), channel_id=1, source_target_pairs={{0,2},{1,3},{2,0},{3,1},{4,6},{5,7},{6,4},{7,5},{8,10},{9,11},{10,... | collective-permute-start | bytes 786440 | tf_op jit(solution)/shard_map/ppermute | solution.py:34
  49.9 2.5 %project.2.refs_6_ = f32[4,64,512]{2,1,0:T(8,128)S(1)} custom-call(s32[4]{0:T(128)S(1)} %iota_xor_fusion.chunk_ref, bf16[64,768]{1,0:T(8,128)(2,1)S(1)} %get-tuple-element.30.refs_0_, bf16[64,768]{1,0:T(8,128)(2,1)S(1)} %collective-permute-done.5.refs_1_, bf16[64,768]{1,0:T(8,128)(2,1)S(1)} %collective-permute-done.6.refs_2_, ...), custom_call_target="tpu_custom_call" | custom-call | tf_op jit(solution)/shard_map/project/pallas_call | solution.py:179
  53.9 1.7 project.3
  55.7 2.9 %collective-permute-start.10 = (bf16[64,512]{1,0:T(8,128)(2,1)S(1)}, bf16[64,512]{1,0:T(8,128)(2,1)S(1)}, u32[]{:S(2)}, u32[]{:S(2)}) collective-permute-start(bf16[64,512]{1,0:T(8,128)(2,1)S(1)} %get-tuple-element.35), channel_id=1, source_target_pairs={{0,3},{1,2},{2,1},{3,0},{4,7},{5,6},{6,5},{7,4},{8,11},{9,10},{10,... | collective-permute-start | bytes 196616 | tf_op jit(solution)/shard_map/ppermute | solution.py:34
  58.6 1.6 collective-permute-start.18
  60.3 6.1 %collective-permute-done.22 = bf16[512,256]{1,0:T(8,128)(2,1)S(1)} collective-permute-done((bf16[512,256]{1,0:T(8,128)(2,1)S(1)}, bf16[512,256]{1,0:T(8,128)(2,1)S(1)}, u32[]{:S(2)}, u32[]{:S(2)}) %collective-permute-start.22) | collective-permute-done | bytes 262176 | tf_op jit(solution)/shard_map/ppermute | solution.py:34
  66.4 5.8 %collective-permute-start.19 = (bf16[256,512]{1,0:T(8,128)(2,1)S(1)}, bf16[256,512]{1,0:T(8,128)(2,1)S(1)}, u32[]{:S(2)}, u32[]{:S(2)}) collective-permute-start(bf16[256,512]{1,0:T(8,128)(2,1)S(1)} %get-tuple-element.25), channel_id=1, source_target_pairs={{0,3},{1,2},{2,1},{3,0},{4,7},{5,6},{6,5},{7,4},{8,11},{9,10},{10,... | collective-permute-start | bytes 786440 | tf_op jit(solution)/shard_map/ppermute | solution.py:34
  72.2 13.9 %collective-permute-start.8 = (bf16[64,512]{1,0:T(8,128)(2,1)S(1)}, bf16[64,512]{1,0:T(8,128)(2,1)S(1)}, u32[]{:S(2)}, u32[]{:S(2)}) collective-permute-start(bf16[64,512]{1,0:T(8,128)(2,1)S(1)} %get-tuple-element.34), channel_id=1, source_target_pairs={{0,1},{1,0},{2,3},{3,2},{4,5},{5,4},{6,7},{7,6},{8,9},{9,8},{10,11... | collective-permute-start | bytes 196616 | tf_op jit(solution)/shard_map/ppermute | solution.py:34
  86.1 2.7 %collective-permute-start.9 = (bf16[64,512]{1,0:T(8,128)(2,1)S(1)}, bf16[64,512]{1,0:T(8,128)(2,1)S(1)}, u32[]{:S(2)}, u32[]{:S(2)}) collective-permute-start(bf16[64,512]{1,0:T(8,128)(2,1)S(1)} %get-tuple-element.36), channel_id=1, source_target_pairs={{0,2},{1,3},{2,0},{3,1},{4,6},{5,7},{6,4},{7,5},{8,10},{9,11},{10,... | collective-permute-start | bytes 196616 | tf_op jit(solution)/shard_map/ppermute | solution.py:34
  89.1 1.7 %collective-permute-start.25 = (bf16[64,512]{1,0:T(8,128)(2,1)S(1)}, bf16[64,512]{1,0:T(8,128)(2,1)S(1)}, u32[]{:S(2)}, u32[]{:S(2)}) collective-permute-start(bf16[64,512]{1,0:T(8,128)(2,1)S(1)} %copy-done.9), channel_id=1, source_target_pairs={{0,1},{1,0},{2,3},{3,2},{4,5},{5,4},{6,7},{7,6},{8,9},{9,8},{10,11... | collective-permute-start | bytes 196616 | tf_op jit(solution)/shard_map/ppermute | solution.py:34
  90.8 7.9 %collective-permute-done.9 = bf16[64,512]{1,0:T(8,128)(2,1)S(1)} collective-permute-done((bf16[64,512]{1,0:T(8,128)(2,1)S(1)}, bf16[64,512]{1,0:T(8,128)(2,1)S(1)}, u32[]{:S(2)}, u32[]{:S(2)}) %collective-permute-start.9) | collective-permute-done | bytes 65568 | tf_op jit(solution)/shard_map/ppermute | solution.py:34
  99.7 3.4 %collective-permute-start.12 = (bf16[64,512]{1,0:T(8,128)(2,1)S(1)}, bf16[64,512]{1,0:T(8,128)(2,1)S(1)}, u32[]{:S(2)}, u32[]{:S(2)}) collective-permute-start(bf16[64,512]{1,0:T(8,128)(2,1)S(1)} %fusion.16), channel_id=1, source_target_pairs={{0,2},{1,3},{2,0},{3,1},{4,6},{5,7},{6,4},{7,5},{8,10},{9,11},{10,... | collective-permute-start | bytes 196616 | tf_op jit(solution)/shard_map/ppermute | solution.py:34
  103.4 2.8 %collective-permute-start.26 = (bf16[64,512]{1,0:T(8,128)(2,1)S(1)}, bf16[64,512]{1,0:T(8,128)(2,1)S(1)}, u32[]{:S(2)}, u32[]{:S(2)}) collective-permute-start(bf16[64,512]{1,0:T(8,128)(2,1)S(1)} %copy-done.9), channel_id=1, source_target_pairs={{0,2},{1,3},{2,0},{3,1},{4,6},{5,7},{6,4},{7,5},{8,10},{9,11},{10,... | collective-permute-start | bytes 196616 | tf_op jit(solution)/shard_map/ppermute | solution.py:34
  107.3 6.1 %collective-permute-start.27 = (bf16[64,512]{1,0:T(8,128)(2,1)S(1)}, bf16[64,512]{1,0:T(8,128)(2,1)S(1)}, u32[]{:S(2)}, u32[]{:S(2)}) collective-permute-start(bf16[64,512]{1,0:T(8,128)(2,1)S(1)} %copy-done.9), channel_id=1, source_target_pairs={{0,3},{1,2},{2,1},{3,0},{4,7},{5,6},{6,5},{7,4},{8,11},{9,10},{10,... | collective-permute-start | bytes 196616 | tf_op jit(solution)/shard_map/ppermute | solution.py:34
  117.0 5.6 %collective-permute-done.14 = bf16[64,2048]{1,0:T(8,128)(2,1)S(1)} collective-permute-done((bf16[64,2048]{1,0:T(8,128)(2,1)S(1)}, bf16[64,2048]{1,0:T(8,128)(2,1)S(1)}, u32[]{:S(2)}, u32[]{:S(2)}) %collective-permute-start.14) | collective-permute-done | bytes 262176 | tf_op jit(solution)/shard_map/ppermute | solution.py:34
  124.3 4.6 %collective-permute-done.16 = bf16[64,2048]{1,0:T(8,128)(2,1)S(1)} collective-permute-done((bf16[64,2048]{1,0:T(8,128)(2,1)S(1)}, bf16[64,2048]{1,0:T(8,128)(2,1)S(1)}, u32[]{:S(2)}, u32[]{:S(2)}) %collective-permute-start.16) | collective-permute-done | bytes 262176 | tf_op jit(solution)/shard_map/ppermute | solution.py:34
  128.9 2.5 %collective-permute-start.30 = (bf16[64,2048]{1,0:T(8,128)(2,1)S(1)}, bf16[64,2048]{1,0:T(8,128)(2,1)S(1)}, u32[]{:S(2)}, u32[]{:S(2)}) collective-permute-start(bf16[64,2048]{1,0:T(8,128)(2,1)S(1)} %constant_dynamic-update-slice_fusion), channel_id=1, source_target_pairs={{0,24},{4,28},{8,16},{12,20},{16,8},{20,12},{24,0},{28,4},{1,25},{... | collective-permute-start | bytes 786440 | tf_op jit(solution)/shard_map/ppermute | solution.py:34
  132.0 1.9 %collective-permute-done.28 = bf16[64,2048]{1,0:T(8,128)(2,1)S(1)} collective-permute-done((bf16[64,2048]{1,0:T(8,128)(2,1)S(1)}, bf16[64,2048]{1,0:T(8,128)(2,1)S(1)}, u32[]{:S(2)}, u32[]{:S(2)}) %collective-permute-start.28) | collective-permute-done | bytes 262176 | tf_op jit(solution)/shard_map/ppermute | solution.py:34
  134.5 5.3 %collective-permute-done.30 = bf16[64,2048]{1,0:T(8,128)(2,1)S(1)} collective-permute-done((bf16[64,2048]{1,0:T(8,128)(2,1)S(1)}, bf16[64,2048]{1,0:T(8,128)(2,1)S(1)}, u32[]{:S(2)}, u32[]{:S(2)}) %collective-permute-start.30) | collective-permute-done | bytes 262176 | tf_op jit(solution)/shard_map/ppermute | solution.py:34
  140.7 7.1 %feed.1 = bf16[256,2048]{1,0:T(8,128)(2,1)S(1)} custom-call(bf16[256,2048]{1,0:T(8,128)(2,1)S(1)} %pad_maximum_fusion.2.state_ref, bf16[512,2048]{1,0:T(8,128)(2,1)S(1)} %pad_maximum_fusion.down_ref, bf16[2048,512]{1,0:T(8,128)(2,1)} %copy-done.6, f32[256,512]{1,0:T(8,128)S(1)} %fusion.11.slope_ref), custom_call_target="tpu_custom_call" | custom-call | tf_op jit(solution)/shard_map/feed/pallas_call | solution.py:213
  147.9 2.2 %collective-permute-start.31 = (bf16[64,2048]{1,0:T(8,128)(2,1)S(1)}, bf16[64,2048]{1,0:T(8,128)(2,1)S(1)}, u32[]{:S(2)}, u32[]{:S(2)}) collective-permute-start(bf16[64,2048]{1,0:T(8,128)(2,1)S(1)} %get-tuple-element.16), channel_id=1, source_target_pairs={{0,8},{4,12},{8,0},{12,4},{16,24},{20,28},{24,16},{28,20},{1,9},{5... | collective-permute-start | bytes 786440 | tf_op jit(solution)/shard_map/ppermute | solution.py:34
  151.6 5.7 %collective-permute-done.31 = bf16[64,2048]{1,0:T(8,128)(2,1)S(1)} collective-permute-done((bf16[64,2048]{1,0:T(8,128)(2,1)S(1)}, bf16[64,2048]{1,0:T(8,128)(2,1)S(1)}, u32[]{:S(2)}, u32[]{:S(2)}) %collective-permute-start.31) | collective-permute-done | bytes 262176 | tf_op jit(solution)/shard_map/ppermute | solution.py:34
  157.3 4.8 %collective-permute-done.32 = bf16[64,2048]{1,0:T(8,128)(2,1)S(1)} collective-permute-done((bf16[64,2048]{1,0:T(8,128)(2,1)S(1)}, bf16[64,2048]{1,0:T(8,128)(2,1)S(1)}, u32[]{:S(2)}, u32[]{:S(2)}) %collective-permute-start.32) | collective-permute-done | bytes 262176 | tf_op jit(solution)/shard_map/ppermute | solution.py:34
  162.9 3.8 %collective-permute-start.36 = (bf16[64,512]{1,0:T(8,128)(2,1)S(1)}, bf16[64,512]{1,0:T(8,128)(2,1)S(1)}, u32[]{:S(2)}, u32[]{:S(2)}) collective-permute-start(bf16[64,512]{1,0:T(8,128)(2,1)S(1)} %get-tuple-element.32), channel_id=1, source_target_pairs={{0,3},{1,2},{2,1},{3,0},{4,7},{5,6},{6,5},{7,4},{8,11},{9,10},{10,... | collective-permute-start | bytes 196616 | tf_op jit(solution)/shard_map/ppermute | solution.py:34
  167.6 2.2 %collective-permute-done.36 = bf16[64,512]{1,0:T(8,128)(2,1)S(1)} collective-permute-done((bf16[64,512]{1,0:T(8,128)(2,1)S(1)}, bf16[64,512]{1,0:T(8,128)(2,1)S(1)}, u32[]{:S(2)}, u32[]{:S(2)}) %collective-permute-start.36) | collective-permute-done | bytes 65568 | tf_op jit(solution)/shard_map/ppermute | solution.py:34
  (94 shorter events, 24.6 us)
Async XLA Ops:
  23.0 10.3 %collective-permute-start.4 = (bf16[4,64,768]{2,1,0:T(8,128)(2,1)S(1)}, bf16[4,64,768]{2,1,0:T(8,128)(2,1)S(1)}, u32[]{:S(2)}, u32[]{:S(2)}) collective-permute-start(bf16[4,64,768]{2,1,0:T(8,128)(2,1)S(1)} %get-tuple-element.13), channel_id=1, source_target_pairs={{0,4},{4,0},{8,12},{12,8},{16,20},{20,16},{24,28},{28,24},{1,5},{5... | collective-permute-start | bytes 1179656 | tf_op jit(solution)/shard_map/ppermute | solution.py:34
  33.5 8.1 %collective-permute-start.5 = (bf16[64,768]{1,0:T(8,128)(2,1)S(1)}, bf16[64,768]{1,0:T(8,128)(2,1)S(1)}, u32[]{:S(2)}, u32[]{:S(2)}) collective-permute-start(bf16[64,768]{1,0:T(8,128)(2,1)S(1)} %get-tuple-element.29), channel_id=1, source_target_pairs={{0,8},{4,12},{8,0},{12,4},{16,24},{20,28},{24,16},{28,20},{1,9},{5... | collective-permute-start | bytes 294920 | tf_op jit(solution)/shard_map/ppermute | solution.py:34
  36.5 15.9 %collective-permute-start.1 = (bf16[64,256]{1,0:T(8,128)(2,1)S(1)}, bf16[64,256]{1,0:T(8,128)(2,1)S(1)}, u32[]{:S(2)}, u32[]{:S(2)}) collective-permute-start(bf16[64,256]{1,0:T(8,128)(2,1)S(1)} %get-tuple-element.39), channel_id=1, source_target_pairs={{0,8},{4,12},{8,0},{12,4},{16,24},{20,28},{24,16},{28,20},{1,9},{5... | collective-permute-start | bytes 98312 | tf_op jit(solution)/shard_map/ppermute | solution.py:34
  36.6 17.0 %collective-permute-start.2 = (bf16[64,256]{1,0:T(8,128)(2,1)S(1)}, bf16[64,256]{1,0:T(8,128)(2,1)S(1)}, u32[]{:S(2)}, u32[]{:S(2)}) collective-permute-start(bf16[64,256]{1,0:T(8,128)(2,1)S(1)} %get-tuple-element.38), channel_id=1, source_target_pairs={{0,16},{4,20},{8,24},{12,28},{16,0},{20,4},{24,8},{28,12},{1,17},{... | collective-permute-start | bytes 98312 | tf_op jit(solution)/shard_map/ppermute | solution.py:34
  38.6 15.3 %collective-permute-start.3 = (bf16[64,256]{1,0:T(8,128)(2,1)S(1)}, bf16[64,256]{1,0:T(8,128)(2,1)S(1)}, u32[]{:S(2)}, u32[]{:S(2)}) collective-permute-start(bf16[64,256]{1,0:T(8,128)(2,1)S(1)} %get-tuple-element.37), channel_id=1, source_target_pairs={{0,24},{4,28},{8,16},{12,20},{16,8},{20,12},{24,0},{28,4},{1,25},{... | collective-permute-start | bytes 98312 | tf_op jit(solution)/shard_map/ppermute | solution.py:34
  41.6 5.7 %collective-permute-start.7 = (bf16[64,768]{1,0:T(8,128)(2,1)S(1)}, bf16[64,768]{1,0:T(8,128)(2,1)S(1)}, u32[]{:S(2)}, u32[]{:S(2)}) collective-permute-start(bf16[64,768]{1,0:T(8,128)(2,1)S(1)} %get-tuple-element.27), channel_id=1, source_target_pairs={{0,24},{4,28},{8,16},{12,20},{16,8},{20,12},{24,0},{28,4},{1,25},{... | collective-permute-start | bytes 294920 | tf_op jit(solution)/shard_map/ppermute | solution.py:34
  45.7 12.9 %collective-permute-start.21 = (bf16[512,256]{1,0:T(8,128)(2,1)S(1)}, bf16[512,256]{1,0:T(8,128)(2,1)S(1)}, u32[]{:S(2)}, u32[]{:S(2)}) collective-permute-start(bf16[512,256]{1,0:T(8,128)(2,1)S(1)} %get-tuple-element.20), channel_id=1, source_target_pairs={{0,1},{1,0},{2,3},{3,2},{4,5},{5,4},{6,7},{7,6},{8,9},{9,8},{10,11... | collective-permute-start | bytes 786440 | tf_op jit(solution)/shard_map/ppermute | solution.py:34
  47.3 19.1 %collective-permute-start.22 = (bf16[512,256]{1,0:T(8,128)(2,1)S(1)}, bf16[512,256]{1,0:T(8,128)(2,1)S(1)}, u32[]{:S(2)}, u32[]{:S(2)}) collective-permute-start(bf16[512,256]{1,0:T(8,128)(2,1)S(1)} %get-tuple-element.22), channel_id=1, source_target_pairs={{0,2},{1,3},{2,0},{3,1},{4,6},{5,7},{6,4},{7,5},{8,10},{9,11},{10,... | collective-permute-start | bytes 786440 | tf_op jit(solution)/shard_map/ppermute | solution.py:34
  52.4 19.8 %collective-permute-start.23 = (bf16[512,256]{1,0:T(8,128)(2,1)S(1)}, bf16[512,256]{1,0:T(8,128)(2,1)S(1)}, u32[]{:S(2)}, u32[]{:S(2)}) collective-permute-start(bf16[512,256]{1,0:T(8,128)(2,1)S(1)} %get-tuple-element.21), channel_id=1, source_target_pairs={{0,3},{1,2},{2,1},{3,0},{4,7},{5,6},{6,5},{7,4},{8,11},{9,10},{10,... | collective-permute-start | bytes 786440 | tf_op jit(solution)/shard_map/ppermute | solution.py:34
  53.6 45.2 %collective-permute-start.17 = (bf16[256,512]{1,0:T(8,128)(2,1)S(1)}, bf16[256,512]{1,0:T(8,128)(2,1)S(1)}, u32[]{:S(2)}, u32[]{:S(2)}) collective-permute-start(bf16[256,512]{1,0:T(8,128)(2,1)S(1)} %get-tuple-element.24), channel_id=1, source_target_pairs={{0,1},{1,0},{2,3},{3,2},{4,5},{5,4},{6,7},{7,6},{8,9},{9,8},{10,11... | collective-permute-start | bytes 786440 | tf_op jit(solution)/shard_map/ppermute | solution.py:34
  55.7 30.4 %collective-permute-start.10 = (bf16[64,512]{1,0:T(8,128)(2,1)S(1)}, bf16[64,512]{1,0:T(8,128)(2,1)S(1)}, u32[]{:S(2)}, u32[]{:S(2)}) collective-permute-start(bf16[64,512]{1,0:T(8,128)(2,1)S(1)} %get-tuple-element.35), channel_id=1, source_target_pairs={{0,3},{1,2},{2,1},{3,0},{4,7},{5,6},{6,5},{7,4},{8,11},{9,10},{10,... | collective-permute-start | bytes 196616 | tf_op jit(solution)/shard_map/ppermute | solution.py:34
  58.6 41.1 %collective-permute-start.18 = (bf16[256,512]{1,0:T(8,128)(2,1)S(1)}, bf16[256,512]{1,0:T(8,128)(2,1)S(1)}, u32[]{:S(2)}, u32[]{:S(2)}) collective-permute-start(bf16[256,512]{1,0:T(8,128)(2,1)S(1)} %get-tuple-element.26), channel_id=1, source_target_pairs={{0,2},{1,3},{2,0},{3,1},{4,6},{5,7},{6,4},{7,5},{8,10},{9,11},{10,... | collective-permute-start | bytes 786440 | tf_op jit(solution)/shard_map/ppermute | solution.py:34
  66.4 36.7 %collective-permute-start.19 = (bf16[256,512]{1,0:T(8,128)(2,1)S(1)}, bf16[256,512]{1,0:T(8,128)(2,1)S(1)}, u32[]{:S(2)}, u32[]{:S(2)}) collective-permute-start(bf16[256,512]{1,0:T(8,128)(2,1)S(1)} %get-tuple-element.25), channel_id=1, source_target_pairs={{0,3},{1,2},{2,1},{3,0},{4,7},{5,6},{6,5},{7,4},{8,11},{9,10},{10,... | collective-permute-start | bytes 786440 | tf_op jit(solution)/shard_map/ppermute | solution.py:34
  72.2 16.9 %collective-permute-start.8 = (bf16[64,512]{1,0:T(8,128)(2,1)S(1)}, bf16[64,512]{1,0:T(8,128)(2,1)S(1)}, u32[]{:S(2)}, u32[]{:S(2)}) collective-permute-start(bf16[64,512]{1,0:T(8,128)(2,1)S(1)} %get-tuple-element.34), channel_id=1, source_target_pairs={{0,1},{1,0},{2,3},{3,2},{4,5},{5,4},{6,7},{7,6},{8,9},{9,8},{10,11... | collective-permute-start | bytes 196616 | tf_op jit(solution)/shard_map/ppermute | solution.py:34
  86.1 12.6 %collective-permute-start.9 = (bf16[64,512]{1,0:T(8,128)(2,1)S(1)}, bf16[64,512]{1,0:T(8,128)(2,1)S(1)}, u32[]{:S(2)}, u32[]{:S(2)}) collective-permute-start(bf16[64,512]{1,0:T(8,128)(2,1)S(1)} %get-tuple-element.36), channel_id=1, source_target_pairs={{0,2},{1,3},{2,0},{3,1},{4,6},{5,7},{6,4},{7,5},{8,10},{9,11},{10,... | collective-permute-start | bytes 196616 | tf_op jit(solution)/shard_map/ppermute | solution.py:34
  89.1 24.3 %collective-permute-start.25 = (bf16[64,512]{1,0:T(8,128)(2,1)S(1)}, bf16[64,512]{1,0:T(8,128)(2,1)S(1)}, u32[]{:S(2)}, u32[]{:S(2)}) collective-permute-start(bf16[64,512]{1,0:T(8,128)(2,1)S(1)} %copy-done.9), channel_id=1, source_target_pairs={{0,1},{1,0},{2,3},{3,2},{4,5},{5,4},{6,7},{7,6},{8,9},{9,8},{10,11... | collective-permute-start | bytes 196616 | tf_op jit(solution)/shard_map/ppermute | solution.py:34
  98.8 32.8 %collective-permute-start.24 = (bf16[2048,256]{1,0:T(8,128)(2,1)S(1)}, bf16[2048,256]{1,0:T(8,128)(2,1)S(1)}, u32[]{:S(2)}, u32[]{:S(2)}) collective-permute-start(bf16[2048,256]{1,0:T(8,128)(2,1)S(1)} %pad_maximum_fusion.4), channel_id=1, source_target_pairs={{0,4},{4,0},{8,12},{12,8},{16,20},{20,16},{24,28},{28,24},{1,5},{5... | collective-permute-start | bytes 3145736 | tf_op jit(solution)/shard_map/ppermute | solution.py:34
  99.7 7.6 %collective-permute-start.12 = (bf16[64,512]{1,0:T(8,128)(2,1)S(1)}, bf16[64,512]{1,0:T(8,128)(2,1)S(1)}, u32[]{:S(2)}, u32[]{:S(2)}) collective-permute-start(bf16[64,512]{1,0:T(8,128)(2,1)S(1)} %fusion.16), channel_id=1, source_target_pairs={{0,2},{1,3},{2,0},{3,1},{4,6},{5,7},{6,4},{7,5},{8,10},{9,11},{10,... | collective-permute-start | bytes 196616 | tf_op jit(solution)/shard_map/ppermute | solution.py:34
  103.1 10.3 %collective-permute-start.13 = (bf16[64,512]{1,0:T(8,128)(2,1)S(1)}, bf16[64,512]{1,0:T(8,128)(2,1)S(1)}, u32[]{:S(2)}, u32[]{:S(2)}) collective-permute-start(bf16[64,512]{1,0:T(8,128)(2,1)S(1)} %fusion.16), channel_id=1, source_target_pairs={{0,3},{1,2},{2,1},{3,0},{4,7},{5,6},{6,5},{7,4},{8,11},{9,10},{10,... | collective-permute-start | bytes 196616 | tf_op jit(solution)/shard_map/ppermute | solution.py:34
  103.4 10.8 %collective-permute-start.26 = (bf16[64,512]{1,0:T(8,128)(2,1)S(1)}, bf16[64,512]{1,0:T(8,128)(2,1)S(1)}, u32[]{:S(2)}, u32[]{:S(2)}) collective-permute-start(bf16[64,512]{1,0:T(8,128)(2,1)S(1)} %copy-done.9), channel_id=1, source_target_pairs={{0,2},{1,3},{2,0},{3,1},{4,6},{5,7},{6,4},{7,5},{8,10},{9,11},{10,... | collective-permute-start | bytes 196616 | tf_op jit(solution)/shard_map/ppermute | solution.py:34
  107.3 8.3 %collective-permute-start.27 = (bf16[64,512]{1,0:T(8,128)(2,1)S(1)}, bf16[64,512]{1,0:T(8,128)(2,1)S(1)}, u32[]{:S(2)}, u32[]{:S(2)}) collective-permute-start(bf16[64,512]{1,0:T(8,128)(2,1)S(1)} %copy-done.9), channel_id=1, source_target_pairs={{0,3},{1,2},{2,1},{3,0},{4,7},{5,6},{6,5},{7,4},{8,11},{9,10},{10,... | collective-permute-start | bytes 196616 | tf_op jit(solution)/shard_map/ppermute | solution.py:34
  113.4 18.4 %collective-permute-start.20 = (bf16[256,2048]{1,0:T(8,128)(2,1)S(1)}, bf16[256,2048]{1,0:T(8,128)(2,1)S(1)}, u32[]{:S(2)}, u32[]{:S(2)}) collective-permute-start(bf16[256,2048]{1,0:T(8,128)(2,1)S(1)} %pad_maximum_fusion.3), channel_id=1, source_target_pairs={{0,4},{4,0},{8,12},{12,8},{16,20},{20,16},{24,28},{28,24},{1,5},{5... | collective-permute-start | bytes 3145736 | tf_op jit(solution)/shard_map/ppermute | solution.py:34
  113.4 9.2 %collective-permute-start.14 = (bf16[64,2048]{1,0:T(8,128)(2,1)S(1)}, bf16[64,2048]{1,0:T(8,128)(2,1)S(1)}, u32[]{:S(2)}, u32[]{:S(2)}) collective-permute-start(bf16[64,2048]{1,0:T(8,128)(2,1)S(1)} %pad_maximum_fusion.5), channel_id=1, source_target_pairs={{0,8},{4,12},{8,0},{12,4},{16,24},{20,28},{24,16},{28,20},{1,9},{5... | collective-permute-start | bytes 786440 | tf_op jit(solution)/shard_map/ppermute | solution.py:34
  114.2 9.1 %collective-permute-start.15 = (bf16[64,2048]{1,0:T(8,128)(2,1)S(1)}, bf16[64,2048]{1,0:T(8,128)(2,1)S(1)}, u32[]{:S(2)}, u32[]{:S(2)}) collective-permute-start(bf16[64,2048]{1,0:T(8,128)(2,1)S(1)} %pad_maximum_fusion.5), channel_id=1, source_target_pairs={{0,16},{4,20},{8,24},{12,28},{16,0},{20,4},{24,8},{28,12},{1,17},{... | collective-permute-start | bytes 786440 | tf_op jit(solution)/shard_map/ppermute | solution.py:34
  115.6 13.3 %collective-permute-start.16 = (bf16[64,2048]{1,0:T(8,128)(2,1)S(1)}, bf16[64,2048]{1,0:T(8,128)(2,1)S(1)}, u32[]{:S(2)}, u32[]{:S(2)}) collective-permute-start(bf16[64,2048]{1,0:T(8,128)(2,1)S(1)} %pad_maximum_fusion.5), channel_id=1, source_target_pairs={{0,24},{4,28},{8,16},{12,20},{16,8},{20,12},{24,0},{28,4},{1,25},{... | collective-permute-start | bytes 786440 | tf_op jit(solution)/shard_map/ppermute | solution.py:34
  122.6 11.3 %collective-permute-start.28 = (bf16[64,2048]{1,0:T(8,128)(2,1)S(1)}, bf16[64,2048]{1,0:T(8,128)(2,1)S(1)}, u32[]{:S(2)}, u32[]{:S(2)}) collective-permute-start(bf16[64,2048]{1,0:T(8,128)(2,1)S(1)} %constant_dynamic-update-slice_fusion), channel_id=1, source_target_pairs={{0,8},{4,12},{8,0},{12,4},{16,24},{20,28},{24,16},{28,20},{1,9},{5... | collective-permute-start | bytes 786440 | tf_op jit(solution)/shard_map/ppermute | solution.py:34
  123.3 11.1 %collective-permute-start.29 = (bf16[64,2048]{1,0:T(8,128)(2,1)S(1)}, bf16[64,2048]{1,0:T(8,128)(2,1)S(1)}, u32[]{:S(2)}, u32[]{:S(2)}) collective-permute-start(bf16[64,2048]{1,0:T(8,128)(2,1)S(1)} %constant_dynamic-update-slice_fusion), channel_id=1, source_target_pairs={{0,16},{4,20},{8,24},{12,28},{16,0},{20,4},{24,8},{28,12},{1,17},{... | collective-permute-start | bytes 786440 | tf_op jit(solution)/shard_map/ppermute | solution.py:34
  128.9 10.8 %collective-permute-start.30 = (bf16[64,2048]{1,0:T(8,128)(2,1)S(1)}, bf16[64,2048]{1,0:T(8,128)(2,1)S(1)}, u32[]{:S(2)}, u32[]{:S(2)}) collective-permute-start(bf16[64,2048]{1,0:T(8,128)(2,1)S(1)} %constant_dynamic-update-slice_fusion), channel_id=1, source_target_pairs={{0,24},{4,28},{8,16},{12,20},{16,8},{20,12},{24,0},{28,4},{1,25},{... | collective-permute-start | bytes 786440 | tf_op jit(solution)/shard_map/ppermute | solution.py:34
  147.9 9.5 %collective-permute-start.31 = (bf16[64,2048]{1,0:T(8,128)(2,1)S(1)}, bf16[64,2048]{1,0:T(8,128)(2,1)S(1)}, u32[]{:S(2)}, u32[]{:S(2)}) collective-permute-start(bf16[64,2048]{1,0:T(8,128)(2,1)S(1)} %get-tuple-element.16), channel_id=1, source_target_pairs={{0,8},{4,12},{8,0},{12,4},{16,24},{20,28},{24,16},{28,20},{1,9},{5... | collective-permute-start | bytes 786440 | tf_op jit(solution)/shard_map/ppermute | solution.py:34
  150.1 12.0 %collective-permute-start.32 = (bf16[64,2048]{1,0:T(8,128)(2,1)S(1)}, bf16[64,2048]{1,0:T(8,128)(2,1)S(1)}, u32[]{:S(2)}, u32[]{:S(2)}) collective-permute-start(bf16[64,2048]{1,0:T(8,128)(2,1)S(1)} %get-tuple-element.18), channel_id=1, source_target_pairs={{0,16},{4,20},{8,24},{12,28},{16,0},{20,4},{24,8},{28,12},{1,17},{... | collective-permute-start | bytes 786440 | tf_op jit(solution)/shard_map/ppermute | solution.py:34
  151.6 10.5 %collective-permute-start.33 = (bf16[64,2048]{1,0:T(8,128)(2,1)S(1)}, bf16[64,2048]{1,0:T(8,128)(2,1)S(1)}, u32[]{:S(2)}, u32[]{:S(2)}) collective-permute-start(bf16[64,2048]{1,0:T(8,128)(2,1)S(1)} %get-tuple-element.17), channel_id=1, source_target_pairs={{0,24},{4,28},{8,16},{12,20},{16,8},{20,12},{24,0},{28,4},{1,25},{... | collective-permute-start | bytes 786440 | tf_op jit(solution)/shard_map/ppermute | solution.py:34
  162.9 6.8 %collective-permute-start.36 = (bf16[64,512]{1,0:T(8,128)(2,1)S(1)}, bf16[64,512]{1,0:T(8,128)(2,1)S(1)}, u32[]{:S(2)}, u32[]{:S(2)}) collective-permute-start(bf16[64,512]{1,0:T(8,128)(2,1)S(1)} %get-tuple-element.32), channel_id=1, source_target_pairs={{0,3},{1,2},{2,1},{3,0},{4,7},{5,6},{6,5},{7,4},{8,11},{9,10},{10,... | collective-permute-start | bytes 196616 | tf_op jit(solution)/shard_map/ppermute | solution.py:34
  (15 other events, 93.6 us)

commit v2 on v1

v2 whole, which is shorter than its diff:
```python
import functools
import math

import jax
import jax.numpy as jnp
from jax import lax
from jax.experimental import pallas as pl
from jax.experimental.pallas import tpu as pltpu
from jax.sharding import PartitionSpec as P

HD = 128
SCALE = HD**-0.5
SCALE_LOG2 = SCALE * math.log2(math.e)
BF16, F32 = jnp.bfloat16, jnp.float32
NT = (((1,), (1,)), ((), ()))
NN = (((1,), (0,)), ((), ()))
TN = (((0,), (0,)), ((), ()))
VMEM_BYTES = 48 * 2**20


def dot(a, b, dims):
    return lax.dot_general(a, b, dims, preferred_element_type=F32)


def slope_of(pre):
    return (
        0.5 * (1.0 + lax.erf(pre * 0.7071067811865476))
        + pre * jnp.exp(-0.5 * pre * pre) * 0.3989422804014327
    )


def swap(x, axis, distance):
    size = lax.axis_size(axis)
    return lax.ppermute(x, axis, [(i, i ^ distance) for i in range(size)])


def levels_of(first, count):
    levels = []
    while count > 1:
        radix = min(4, count)
        levels.append((first, radix))
        first, count = first * radix, count // radix
    return levels


def gather_blocks(x, axis, first, count):
    blocks = [x]
    for step, radix in levels_of(first, count):
        whole = blocks[0] if len(blocks) == 1 else jnp.stack(blocks)
        got = [swap(whole, axis, step * k) for k in range(1, radix)]
        for other in got:
            blocks = blocks + ([other] if whole is x else list(other))
    return blocks


def scatter_terms(blocks, axis, first, low=BF16):
    levels = levels_of(first, len(blocks))
    for step, radix in reversed(levels[1:]):
        span = step // first
        terms = [blocks[k * span : (k + 1) * span] for k in range(radix)]
        got = [swap(jnp.stack(terms[k]), axis, step * k) for k in range(1, radix)]
        blocks = [
            (terms[0][i].astype(F32) + sum(g[i].astype(F32) for g in got)).astype(low)
            for i in range(span)
        ]
    return [blocks[0]] + [swap(blocks[k], axis, first * k) for k in range(1, len(blocks))]


def attend_kernel(sub, place_ref, q_ref, g_ref, k_ref, v_ref, dq_ref, even_ref, odd_ref, acc_ref):
    block = pl.program_id(1)
    keys, values = k_ref[...], v_ref[...]

    @pl.when(block == 0)
    def _():
        acc_ref[...] = jnp.zeros_like(acc_ref)

    def products(at):
        return dot(keys, q_ref[at, :], NT), dot(values, g_ref[at, :], NT)

    def soften(scores, weight_grad):
        top = jnp.max(scores, axis=0, keepdims=True)
        grown = jnp.exp2((scores - top) * SCALE_LOG2)
        weights = grown * (1.0 / jnp.sum(grown, axis=0, keepdims=True))
        centre = jnp.sum(weights * weight_grad, axis=0, keepdims=True)
        return (weights * (weight_grad - centre)).astype(BF16), weights.astype(BF16)

    def collect(at, score_grad, weights_low):
        dq_ref[at, :] = (SCALE * dot(keys, score_grad, TN)).T.astype(BF16)
        acc_ref[:, :HD] += dot(score_grad, q_ref[at, :], NN)
        acc_ref[:, HD:] += dot(weights_low, g_ref[at, :], NN)

    pieces = [pl.ds(i * sub, sub) for i in range(q_ref.shape[0] // sub)]
    ahead, behind = products(pieces[0]), None
    for i, at in enumerate(pieces):
        now, ahead = ahead, products(pieces[i + 1]) if i + 1 < len(pieces) else None
        done = soften(*now)
        if behind is not None:
            collect(pieces[i - 1], *behind)
        behind = done
    collect(pieces[-1], *behind)

    @pl.when(block == pl.num_programs(1) - 1)
    def _():
        acc_ref[:, :HD] = SCALE * acc_ref[:, :HD]
        half, height = even_ref.shape[:2]
        for j in range(2 * half):
            at = pl.ds(pl.multiple_of(place_ref[j] * height, height), height)
            (odd_ref if j % 2 else even_ref)[j // 2] = acc_ref[at, :].astype(BF16)


def attend(place, queries, out_grad, keys, values):
    tokens, width = queries.shape
    glob, size, count = keys.shape[0], place.shape[0], width // HD
    block = min(2048, tokens)
    token_spec = pl.BlockSpec((block, HD), lambda h, b, place: (b, h))
    global_spec = pl.BlockSpec((glob, HD), lambda h, b, place: (0, h))
    part_spec = pl.BlockSpec((size // 2, glob // size, 2 * HD), lambda h, b, place: (0, 0, h))
    part = jax.ShapeDtypeStruct((size // 2, glob // size, 2 * width), BF16)
    return pl.pallas_call(
        functools.partial(attend_kernel, min(256, block)),
        grid_spec=pltpu.PrefetchScalarGridSpec(
            num_scalar_prefetch=1,
            grid=(count, tokens // block),
            in_specs=[token_spec, token_spec, global_spec, global_spec],
            out_specs=[token_spec, part_spec, part_spec],
            scratch_shapes=[pltpu.VMEM((glob, 2 * HD), F32)],
        ),
        out_shape=[jax.ShapeDtypeStruct((tokens, width), BF16), part, part],
        compiler_params=pltpu.CompilerParams(vmem_limit_bytes=60 * 2**20),
        cost_estimate=pl.CostEstimate(
            flops=20 * tokens * glob * width,
            bytes_accessed=6 * tokens * width,
            transcendentals=tokens * glob * count,
        ),
        name="attend",
    )(place, queries, out_grad, keys, values)


def merge_kernel(even_ref, got_ref, *out_refs):
    for j, out_ref in enumerate(out_refs):
        out_ref[...] = (even_ref[j].astype(F32) + got_ref[j].astype(F32)).astype(BF16)


def scatter_rows(even, odd):
    part = jax.ShapeDtypeStruct(even.shape[1:], BF16)
    mine = pl.pallas_call(
        merge_kernel,
        out_shape=[part] * even.shape[0],
        compiler_params=pltpu.CompilerParams(vmem_limit_bytes=VMEM_BYTES),
        cost_estimate=pl.CostEstimate(flops=even.size, bytes_accessed=6 * even.size, transcendentals=0),
        name="merge",
    )(even, swap(odd, "seq", 1))
    return scatter_terms(mine, "seq", 2)


def project_kernel(count, chunk_ref, *refs):
    terms = refs[:count]
    key_proj_ref, value_proj_ref, mixed_ref, part_ref, last_ref = refs[count:]
    total = sum(t[...].astype(F32) for t in terms).astype(BF16)
    heads = total.shape[1] // (2 * HD)
    pick = lambda at: [total[:, (2 * h + at) * HD : (2 * h + at + 1) * HD] for h in range(heads)]
    key_low, value_low = jnp.concatenate(pick(0), 1), jnp.concatenate(pick(1), 1)
    part = dot(key_low, key_proj_ref[...], NT) + dot(value_low, value_proj_ref[...], NT)
    part_ref[...] = part.astype(BF16)

    @pl.when(pl.program_id(0) == 0)
    def _():
        last_ref[...] = mixed_ref[...]


def project(chunk, terms, key_proj, value_proj, mixed):
    rows, width = terms[0].shape
    size = chunk.shape[0]
    block = key_proj.shape[0] // size
    last = mixed.shape[1] // rows - 1
    weight_spec = pl.BlockSpec((block, width // 2), lambda k, chunk: (chunk[k], 0))
    return pl.pallas_call(
        functools.partial(project_kernel, len(terms)),
        grid_spec=pltpu.PrefetchScalarGridSpec(
            num_scalar_prefetch=1,
            grid=(size,),
            in_specs=[pl.BlockSpec((rows, width), lambda k, chunk: (0, 0))] * len(terms)
            + [weight_spec] * 2
            + [pl.BlockSpec((size, rows, block), lambda k, chunk: (0, last, 0))],
            out_specs=[
                pl.BlockSpec((None, rows, block), lambda k, chunk: (k, 0, 0)),
                pl.BlockSpec((size, rows, block), lambda k, chunk: (0, 0, 0)),
            ],
        ),
        out_shape=[jax.ShapeDtypeStruct((size, rows, block), BF16)] * 2,
        compiler_params=pltpu.CompilerParams(vmem_limit_bytes=60 * 2**20),
        cost_estimate=pl.CostEstimate(
            flops=2 * rows * width * block * size,
            bytes_accessed=2 * width * block * size,
            transcendentals=0,
        ),
        name="project",
    )(chunk, *terms, key_proj, value_proj, mixed)


def back_kernel(count, chunk_ref, *refs):
    states, downs, out_ref = refs[:count], refs[count : count + 2], refs[-1]
    halves, size, rows, hidden = out_ref.shape
    height, hidden = states[0].shape[0] // halves, hidden // 2
    state = jnp.concatenate(
        [ref[c * height : (c + 1) * height, :] for c in range(halves) for ref in states], 0
    )
    for k in range(size):
        at = pl.ds(pl.multiple_of(chunk_ref[k] * hidden, hidden), hidden)
        for i in range(2):
            part = dot(state, downs[i][at, :], NT).astype(BF16)
            for c in range(halves):
                out_ref[c, k, :, i * hidden : (i + 1) * hidden] = part[c * rows : (c + 1) * rows]


def back_parts(chunk, states, downs, halves):
    size, (height, width) = chunk.shape[0], states[0].shape
    rows = len(states) * height
    if height % 16:
        states = [jnp.concatenate(states, 0)]
    hidden = downs[0].shape[0] // size
    return pl.pallas_call(
        functools.partial(back_kernel, len(states)),
        in_specs=[pl.BlockSpec(memory_space=pltpu.SMEM)]
        + [pl.BlockSpec(memory_space=pltpu.VMEM)] * (len(states) + 2),
        out_specs=pl.BlockSpec(memory_space=pltpu.VMEM),
        out_shape=jax.ShapeDtypeStruct((halves, size, rows // halves, 2 * hidden), BF16),
        compiler_params=pltpu.CompilerParams(vmem_limit_bytes=VMEM_BYTES),
        cost_estimate=pl.CostEstimate(
            flops=4 * rows * width * hidden * size,
            bytes_accessed=4 * width * hidden * size,
            transcendentals=0,
        ),
        name="back",
    )(chunk, *states, *downs)


def pre_kernel(count, *refs):
    inputs, ups, out_ref = refs[:count], refs[count : count + 2], refs[-1]
    halves, rows, hidden = out_ref.shape
    height, hidden = inputs[0].shape[1] // halves, hidden // 2
    size = ups[0].shape[0]
    whole = [
        jnp.concatenate(
            [ref[k, c * height : (c + 1) * height, :] for c in range(halves) for ref in inputs], 0
        )
        for k in range(size)
    ]
    for i in range(2):
        part = sum(dot(whole[k], ups[i][k, :hidden, :], NT) for k in range(size))
        for c in range(halves):
            out_ref[c, :, i * hidden : (i + 1) * hidden] = part[c * rows : (c + 1) * rows]


def pre_parts(inputs, ups, hidden, halves):
    height = inputs[0].shape[1]
    rows = len(inputs) * height // halves
    if height % 16:
        inputs = [jnp.concatenate(inputs, 1)]
    return pl.pallas_call(
        functools.partial(pre_kernel, len(inputs)),
        out_shape=jax.ShapeDtypeStruct((halves, rows, 2 * hidden), F32),
        compiler_params=pltpu.CompilerParams(vmem_limit_bytes=VMEM_BYTES),
        cost_estimate=pl.CostEstimate(
            flops=4 * halves * rows * hidden * ups[0].shape[0] * ups[0].shape[2],
            bytes_accessed=4 * ups[0].size,
            transcendentals=0,
        ),
        name="pre",
    )(*inputs, *ups)


def feed_kernel(count, chunk_ref, *refs):
    terms, slope_ref, ups, out_ref = refs[:count], refs[count], refs[count + 1 : count + 3], refs[-1]
    back = sum(ref[...].astype(F32) for ref in terms)
    gated = (slope_ref[...] * back).astype(BF16)
    hidden = gated.shape[1] // 2
    size, _, width = ups[0].shape
    for k in range(size):
        part = sum(
            dot(gated[:, i * hidden : (i + 1) * hidden], ups[i][chunk_ref[k], :hidden, :], NN)
            for i in range(2)
        )
        out_ref[:, :, k * width : (k + 1) * width] = part.astype(BF16).reshape(
            out_ref.shape[0], out_ref.shape[1], width
        )


def feed(chunk, terms, slope, ups, blocks):
    rows = terms[0].shape[0]
    size, _, width = ups[0].shape
    hidden = terms[0].shape[1] // 2
    return pl.pallas_call(
        functools.partial(feed_kernel, len(terms)),
        in_specs=[pl.BlockSpec(memory_space=pltpu.SMEM)]
        + [pl.BlockSpec(memory_space=pltpu.VMEM)] * (len(terms) + 3),
        out_specs=pl.BlockSpec(memory_space=pltpu.VMEM),
        out_shape=jax.ShapeDtypeStruct((blocks, rows // blocks, size * width), BF16),
        compiler_params=pltpu.CompilerParams(vmem_limit_bytes=VMEM_BYTES),
        cost_estimate=pl.CostEstimate(
            flops=4 * rows * hidden * width * size,
            bytes_accessed=4 * hidden * width * size,
            transcendentals=0,
        ),
        name="feed",
    )(chunk, *terms, slope, *ups)


def local(queries, keys, values, out_grad, key_proj, value_proj, global_in, up_proj, down_proj):
    size, planes = lax.axis_size("seq"), lax.axis_size("heads")
    place = lax.axis_index("seq") ^ jnp.arange(size, dtype=jnp.int32)
    chunk = lax.axis_index("heads") ^ jnp.arange(planes, dtype=jnp.int32)
    far = size // 2
    rows, width = global_in.shape
    halves = 2 if rows % 32 == 0 else 1

    own_up = up_proj.T.reshape(planes, -1, width)
    hidden = own_up.shape[1]
    sent = jnp.broadcast_to(global_in[None], (planes, rows, width))
    own_up = lax.all_to_all(jnp.concatenate([own_up, sent], 1), "heads", 0, 0)
    downs = [down_proj, swap(down_proj, "seq", 1)]

    query_grad, even, odd = attend(place, queries, out_grad, keys, values)
    share, input_part = project(chunk, scatter_rows(even, odd), key_proj, value_proj, own_up)
    late_up, share = lax.optimization_barrier((own_up, share))
    ups = [own_up, swap(late_up, "seq", 1)]
    state = sum(
        t.astype(F32) for t in [share[0]] + [swap(share[k], "heads", k) for k in range(1, planes)]
    )
    inputs = gather_blocks(input_part, "seq", 2, far)
    states = gather_blocks(state.astype(BF16), "seq", 2, far)
    parts = back_parts(chunk, states, downs, halves)
    slope = slope_of(pre_parts(inputs, ups, hidden, halves))

    terms = [
        [parts[c, 0]] + [swap(parts[c, k], "heads", k) for k in range(1, planes)]
        for c in range(halves)
    ]
    grown = [feed(chunk, terms[c], slope[c], ups, far) for c in range(halves)]
    own_terms = [scatter_terms([g[j] for j in range(far)], "seq", 2) for g in grown]
    grads = []
    for c in range(halves):
        own = sum(t.astype(F32) for t in own_terms[c])
        blocks = [own[:, k * width : (k + 1) * width] for k in range(planes)]
        grads.append(
            blocks[0]
            + sum(swap(blocks[k].astype(BF16), "heads", k).astype(F32) for k in range(1, planes))
        )
    global_grad = state + jnp.concatenate(grads, 0)
    return (query_grad, global_grad)


def solution(mesh):
    placed = (
        P("seq", "heads"),
        P(None, "heads"),
        P(None, "heads"),
        P("seq", "heads"),
        P(None, "heads"),
        P(None, "heads"),
        P("seq", "heads"),
        P("heads", "seq"),
        P("seq", "heads"),
    )
    return jax.shard_map(
        local,
        mesh=mesh,
        in_specs=placed,
        out_specs=(P("seq", "heads"), P("seq", "heads")),
        check_vma=False,
    )
```

time: 171 us -> 119 us (0.70)
  waiting for transfers between devices: 50.4 us -> 26.4 us
  starting transfers between devices: 72.9 us -> 53 us
  Pallas kernels: 34.7 us -> 27.4 us
  other arithmetic: 1.76 us -> 5.01 us
  between operations: 3.48 us -> 0.84 us
    ppermute x37 -> x33, starting transfers between devices: 72.9 us -> 46.7 us  [swap(): return lax.ppermute(x, axis, [(i, i ^ distance) for i in range(size)])]
    ppermute x37 -> x33, waiting for transfers between devices: 50.4 us -> 26.4 us  [swap(): return lax.ppermute(x, axis, [(i, i ^ distance) for i in range(size)])]
    pallas_call x3 -> x6, Pallas kernels: 30.6 us -> 21.7 us  [the longest x1 16.8 us: attend(): pl.pallas_call(functools.partial(attend_kernel, min(256, block)), grid_sp...]
    all_to_all x0 -> x1, starting transfers between devices: none -> 6.32 us  [local(): own_up = lax.all_to_all(jnp.concatenate([own_up, sent], 1), 'heads', 0, 0)]
    unnamed x23 -> x16, local copies, waits for them, and re-layouts: 5.31 us -> 2.84 us
    pallas_call x2 -> x1, Pallas kernels: 4.16 us -> 5.77 us  [project(): pl.pallas_call(functools.partial(project_kernel, len(terms)), grid_spec=p...]
  transfers between devices with their start and end apart: 37 -> 34, of which waited for: 16 -> 17; matrix products, arithmetic and copies ran while one was open for 1% -> 3% of each run, Pallas kernels for 6% -> 23%
where the time goes in v2:
time: 119 us; the launch traced here: 118 us
  starting transfers between devices  53 us (45%)
  Pallas kernels  27.4 us (23%)
  waiting for transfers between devices  26.4 us (22%)
  local copies, waits for them, and re-layouts  5.49 us (5%)
  other arithmetic  5.01 us (4%)
    ppermute x33, starting transfers between devices, swap(): return lax.ppermute(x, axis, [(i, i ^ distance) for i in range(size)])  46.7 us
    ppermute x33, waiting for transfers between devices, swap(): return lax.ppermute(x, axis, [(i, i ^ distance) for i in range(size)])  26.4 us
    pallas_call x1, Pallas kernels, attend(): pl.pallas_call(functools.partial(attend_kernel, min(256, block)), grid_sp...  16.8 us
    all_to_all x1, starting transfers between devices, local(): own_up = lax.all_to_all(jnp.concatenate([own_up, sent], 1), 'heads', 0, 0)  6.32 us
    pallas_call x1, Pallas kernels, project(): pl.pallas_call(functools.partial(project_kernel, len(terms)), grid_spec=p...  5.77 us
    unnamed x16, local copies, waits for them, and re-layouts  2.84 us
  transfers between devices with their start and end apart: 34, of which 17 were waited for; matrix products, arithmetic and copies ran while one was open for 3% of the time, Pallas kernels for 23%

profile of v2, /device:TPU:0, one launch (start us, length us, event | category | flops | bytes accessed | tf_op | source)
XLA Modules:
  0.0 118.1 jit_solution(11582350568493134716)
XLA Ops:
  0.6 1.5 %copy.11 = bf16[1024,512]{1,0:T(8,128)(2,1)S(1)} copy(bf16[1024,512]{0,1:T(8,128)(2,1)} %bitcast.60) | data formatting | bytes 2097152 | tf_op jit(solution)/shard_map/transpose | solution.py:317
  3.4 6.3 %all-to-all-start = ((bf16[4,320,512]{2,1,0:T(8,128)(2,1)}), bf16[4,320,512]{2,1,0:T(8,128)(2,1)S(1)}, u32[]{:S(2)}, u32[]{:S(2)}) async-start(bf16[4,320,512]{2,1,0:T(8,128)(2,1)} %pad_maximum_fusion), calls=%async_computation | async-start | bytes 2621440 | tf_op jit(solution)/shard_map/all_to_all | solution.py:320
  10.3 16.8 %attend.1 = (bf16[2048,512]{1,0:T(8,128)(2,1)}, bf16[4,64,1024]{2,1,0:T(8,128)(2,1)}, bf16[4,64,1024]{2,1,0:T(8,128)(2,1)}) custom-call(s32[8]{0:T(128)} %iota_xor_fusion.1.place_ref, bf16[2048,512]{1,0:T(8,128)(2,1)} %q_ref.1, bf16[2048,512]{1,0:T(8,128)(2,1)} %g_ref.1, bf16[512,512]{1,0:T(8,128)(2,1)} %k_ref.1, bf16[512,512]{1,0:T(8,128)(2,1)} %v_ref.1), custom_call_target="tpu_custom_call" | custom-call | flops 10737418240 | bytes 6291456 | tf_op jit(solution)/shard_map/attend/pallas_call | solution.py:119
  27.1 2.1 %collective-permute-done.got_ref = bf16[4,64,1024]{2,1,0:T(8,128)(2,1)S(1)} collective-permute-done((bf16[4,64,1024]{2,1,0:T(8,128)(2,1)}, bf16[4,64,1024]{2,1,0:T(8,128)(2,1)S(1)}, u32[]{:S(2)}, u32[]{:S(2)}) %collective-permute-start) | collective-permute-done | bytes 524320 | tf_op jit(solution)/shard_map/ppermute | solution.py:34
  31.7 1.5 %collective-permute-start.1 = (bf16[64,1024]{1,0:T(8,128)(2,1)}, bf16[64,1024]{1,0:T(8,128)(2,1)}, u32[]{:S(2)}, u32[]{:S(2)}) collective-permute-start(bf16[64,1024]{1,0:T(8,128)(2,1)} %get-tuple-element.17), channel_id=1, source_target_pairs={{0,8},{4,12},{8,0},{12,4},{16,24},{20,28},{24,16},{28,20},{1,9},{5... | collective-permute-start | bytes 393224 | tf_op jit(solution)/shard_map/ppermute | solution.py:34
  33.2 1.5 %collective-permute-start.2 = (bf16[64,1024]{1,0:T(8,128)(2,1)}, bf16[64,1024]{1,0:T(8,128)(2,1)}, u32[]{:S(2)}, u32[]{:S(2)}) collective-permute-start(bf16[64,1024]{1,0:T(8,128)(2,1)} %get-tuple-element.18), channel_id=1, source_target_pairs={{0,16},{4,20},{8,24},{12,28},{16,0},{20,4},{24,8},{28,12},{1,17},{... | collective-permute-start | bytes 393224 | tf_op jit(solution)/shard_map/ppermute | solution.py:34
  35.7 2.4 %collective-permute-done.1.refs_1_ = bf16[64,1024]{1,0:T(8,128)(2,1)} collective-permute-done((bf16[64,1024]{1,0:T(8,128)(2,1)}, bf16[64,1024]{1,0:T(8,128)(2,1)}, u32[]{:S(2)}, u32[]{:S(2)}) %collective-permute-start.1) | collective-permute-done | bytes 131104 | tf_op jit(solution)/shard_map/ppermute | solution.py:34
  38.1 3.4 %collective-permute-done.2.refs_2_ = bf16[64,1024]{1,0:T(8,128)(2,1)} collective-permute-done((bf16[64,1024]{1,0:T(8,128)(2,1)}, bf16[64,1024]{1,0:T(8,128)(2,1)}, u32[]{:S(2)}, u32[]{:S(2)}) %collective-permute-start.2) | collective-permute-done | bytes 131104 | tf_op jit(solution)/shard_map/ppermute | solution.py:34
  42.7 5.8 %project.1 = (bf16[4,64,512]{2,1,0:T(8,128)(2,1)}, bf16[4,64,512]{2,1,0:T(8,128)(2,1)}) custom-call(s32[4]{0:T(128)} %iota_xor_fusion.chunk_ref, bf16[64,1024]{1,0:T(8,128)(2,1)} %copy-done.5, bf16[64,1024]{1,0:T(8,128)(2,1)} %collective-permute-done.1.refs_1_, bf16[64,1024]{1,0:T(8,128)(2,1)} %collective-permute-done.2.refs_2_, ...), custom_call_target="tpu_custom_call" | custom-call | flops 268435456 | bytes 4194304 | tf_op jit(solution)/shard_map/project/pallas_call | solution.py:177
  49.4 2.1 %collective-permute-start.4 = (bf16[64,512]{1,0:T(8,128)(2,1)S(1)}, bf16[64,512]{1,0:T(8,128)(2,1)S(1)}, u32[]{:S(2)}, u32[]{:S(2)}) collective-permute-start(bf16[64,512]{1,0:T(8,128)(2,1)S(1)} %get-tuple-element.44), channel_id=1, source_target_pairs={{0,1},{1,0},{2,3},{3,2},{4,5},{5,4},{6,7},{7,6},{8,9},{9,8},{10,11... | collective-permute-start | bytes 196616 | tf_op jit(solution)/shard_map/ppermute | solution.py:34
  51.5 2.4 %collective-permute-start.6 = (bf16[64,512]{1,0:T(8,128)(2,1)S(1)}, bf16[64,512]{1,0:T(8,128)(2,1)S(1)}, u32[]{:S(2)}, u32[]{:S(2)}) collective-permute-start(bf16[64,512]{1,0:T(8,128)(2,1)S(1)} %get-tuple-element.45), channel_id=1, source_target_pairs={{0,3},{1,2},{2,1},{3,0},{4,7},{5,6},{6,5},{7,4},{8,11},{9,10},{10,... | collective-permute-start | bytes 196616 | tf_op jit(solution)/shard_map/ppermute | solution.py:34
  54.2 4.0 %collective-permute-done.6 = bf16[64,512]{1,0:T(8,128)(2,1)S(1)} collective-permute-done((bf16[64,512]{1,0:T(8,128)(2,1)S(1)}, bf16[64,512]{1,0:T(8,128)(2,1)S(1)}, u32[]{:S(2)}, u32[]{:S(2)}) %collective-permute-start.6) | collective-permute-done | bytes 65568 | tf_op jit(solution)/shard_map/ppermute | solution.py:34
  58.2 2.3 %collective-permute-done.5 = bf16[64,512]{1,0:T(8,128)(2,1)S(1)} collective-permute-done((bf16[64,512]{1,0:T(8,128)(2,1)S(1)}, bf16[64,512]{1,0:T(8,128)(2,1)S(1)}, u32[]{:S(2)}, u32[]{:S(2)}) %collective-permute-start.5) | collective-permute-done | bytes 65568 | tf_op jit(solution)/shard_map/ppermute | solution.py:34
  61.4 1.6 %collective-permute-start.9 = (bf16[64,512]{1,0:T(8,128)(2,1)S(1)}, bf16[64,512]{1,0:T(8,128)(2,1)S(1)}, u32[]{:S(2)}, u32[]{:S(2)}) collective-permute-start(bf16[64,512]{1,0:T(8,128)(2,1)S(1)} %fusion.10.refs_0_), channel_id=1, source_target_pairs={{0,24},{4,28},{8,16},{12,20},{16,8},{20,12},{24,0},{28,4},{1,25},{... | collective-permute-start | bytes 196616 | tf_op jit(solution)/shard_map/ppermute | solution.py:34
  65.0 1.5 %collective-permute-start.16 = (bf16[4,64,512]{2,1,0:T(8,128)(2,1)}, bf16[4,64,512]{2,1,0:T(8,128)(2,1)S(1)}, u32[]{:S(2)}, u32[]{:S(2)}) collective-permute-start(bf16[4,64,512]{2,1,0:T(8,128)(2,1)} %get-tuple-element.22.refs_0_), channel_id=1, source_target_pairs={{0,24},{4,28},{8,16},{12,20},{16,8},{20,12},{24,0},{28,4},{1,25},{... | collective-permute-start | bytes 786440 | tf_op jit(solution)/shard_map/ppermute | solution.py:34
  66.8 1.8 %collective-permute-start.15 = (bf16[4,64,512]{2,1,0:T(8,128)(2,1)}, bf16[4,64,512]{2,1,0:T(8,128)(2,1)S(1)}, u32[]{:S(2)}, u32[]{:S(2)}) collective-permute-start(bf16[4,64,512]{2,1,0:T(8,128)(2,1)} %get-tuple-element.22.refs_0_), channel_id=1, source_target_pairs={{0,16},{4,20},{8,24},{12,28},{16,0},{20,4},{24,8},{28,12},{1,17},{... | collective-permute-start | bytes 786440 | tf_op jit(solution)/shard_map/ppermute | solution.py:34
  69.1 1.3 %back.1 = bf16[2,4,128,512]{3,2,1,0:T(8,128)(2,1)S(1)} custom-call(s32[4]{0:T(128)S(1)} %copy-done.6, bf16[64,512]{1,0:T(8,128)(2,1)S(1)} %fusion.10.refs_0_, bf16[64,512]{1,0:T(8,128)(2,1)S(1)} %collective-permute-done.7.refs_1_, bf16[64,512]{1,0:T(8,128)(2,1)S(1)} %collective-permute-done.8.refs_2_, bf16[64,512]{1,0:T(8,128)(2,1)S(1)} %collective-permute-done.9.refs_3_, ...), custom_call_target="tpu_custom_call" | custom-call | flops 536870912 | bytes 2097152 | tf_op jit(solution)/shard_map/back/pallas_call | solution.py:222
  70.5 2.8 %collective-permute-start.13 = (bf16[128,512]{1,0:T(8,128)(2,1)S(1)}, bf16[128,512]{1,0:T(8,128)(2,1)S(1)}, u32[]{:S(2)}, u32[]{:S(2)}) collective-permute-start(bf16[128,512]{1,0:T(8,128)(2,1)S(1)} %get-tuple-element.28), channel_id=1, source_target_pairs={{0,3},{1,2},{2,1},{3,0},{4,7},{5,6},{6,5},{7,4},{8,11},{9,10},{10,... | collective-permute-start | bytes 393224 | tf_op jit(solution)/shard_map/ppermute | solution.py:34
  73.4 2.0 %collective-permute-done.16.refs_3_ = bf16[4,64,512]{2,1,0:T(8,128)(2,1)S(1)} collective-permute-done((bf16[4,64,512]{2,1,0:T(8,128)(2,1)}, bf16[4,64,512]{2,1,0:T(8,128)(2,1)S(1)}, u32[]{:S(2)}, u32[]{:S(2)}) %collective-permute-start.16) | collective-permute-done | bytes 262176 | tf_op jit(solution)/shard_map/ppermute | solution.py:34
  75.4 2.6 %collective-permute-start.26 = (bf16[128,512]{1,0:T(8,128)(2,1)S(1)}, bf16[128,512]{1,0:T(8,128)(2,1)S(1)}, u32[]{:S(2)}, u32[]{:S(2)}) collective-permute-start(bf16[128,512]{1,0:T(8,128)(2,1)S(1)} %get-tuple-element.29), channel_id=1, source_target_pairs={{0,3},{1,2},{2,1},{3,0},{4,7},{5,6},{6,5},{7,4},{8,11},{9,10},{10,... | collective-permute-start | bytes 393224 | tf_op jit(solution)/shard_map/ppermute | solution.py:34
  78.0 1.4 %collective-permute-done.15.refs_2_ = bf16[4,64,512]{2,1,0:T(8,128)(2,1)S(1)} collective-permute-done((bf16[4,64,512]{2,1,0:T(8,128)(2,1)}, bf16[4,64,512]{2,1,0:T(8,128)(2,1)S(1)}, u32[]{:S(2)}, u32[]{:S(2)}) %collective-permute-start.15) | collective-permute-done | bytes 262176 | tf_op jit(solution)/shard_map/ppermute | solution.py:34
  79.7 2.3 %collective-permute-start.24 = (bf16[128,512]{1,0:T(8,128)(2,1)S(1)}, bf16[128,512]{1,0:T(8,128)(2,1)S(1)}, u32[]{:S(2)}, u32[]{:S(2)}) collective-permute-start(bf16[128,512]{1,0:T(8,128)(2,1)S(1)} %get-tuple-element.31), channel_id=1, source_target_pairs={{0,1},{1,0},{2,3},{3,2},{4,5},{5,4},{6,7},{7,6},{8,9},{9,8},{10,11... | collective-permute-start | bytes 393224 | tf_op jit(solution)/shard_map/ppermute | solution.py:34
  83.8 8.5 %collective-permute-start.11 = (bf16[128,512]{1,0:T(8,128)(2,1)S(1)}, bf16[128,512]{1,0:T(8,128)(2,1)S(1)}, u32[]{:S(2)}, u32[]{:S(2)}) collective-permute-start(bf16[128,512]{1,0:T(8,128)(2,1)S(1)} %get-tuple-element.34), channel_id=1, source_target_pairs={{0,1},{1,0},{2,3},{3,2},{4,5},{5,4},{6,7},{7,6},{8,9},{9,8},{10,11... | collective-permute-start | bytes 393224 | tf_op jit(solution)/shard_map/ppermute | solution.py:34
  92.2 1.8 %collective-permute-done.25.refs_2_ = bf16[128,512]{1,0:T(8,128)(2,1)S(1)} collective-permute-done((bf16[128,512]{1,0:T(8,128)(2,1)S(1)}, bf16[128,512]{1,0:T(8,128)(2,1)S(1)}, u32[]{:S(2)}, u32[]{:S(2)}) %collective-permute-start.25) | collective-permute-done | bytes 131104 | tf_op jit(solution)/shard_map/ppermute | solution.py:34
  96.3 1.5 %collective-permute-start.29 = (bf16[32,2048]{1,0:T(8,128)(2,1)S(1)}, bf16[32,2048]{1,0:T(8,128)(2,1)S(1)}, u32[]{:S(2)}, u32[]{:S(2)}) collective-permute-start(bf16[32,2048]{1,0:T(8,128)(2,1)S(1)} %get-tuple-element.42), channel_id=1, source_target_pairs={{0,24},{4,28},{8,16},{12,20},{16,8},{20,12},{24,0},{28,4},{1,25},{... | collective-permute-start | bytes 393224 | tf_op jit(solution)/shard_map/ppermute | solution.py:34
  100.9 1.5 %collective-permute-start.20 = (bf16[32,2048]{1,0:T(8,128)(2,1)S(1)}, bf16[32,2048]{1,0:T(8,128)(2,1)S(1)}, u32[]{:S(2)}, u32[]{:S(2)}) collective-permute-start(bf16[32,2048]{1,0:T(8,128)(2,1)S(1)} %get-tuple-element.37), channel_id=1, source_target_pairs={{0,24},{4,28},{8,16},{12,20},{16,8},{20,12},{24,0},{28,4},{1,25},{... | collective-permute-start | bytes 393224 | tf_op jit(solution)/shard_map/ppermute | solution.py:34
  104.0 1.4 %collective-permute-done.28 = bf16[32,2048]{1,0:T(8,128)(2,1)S(1)} collective-permute-done((bf16[32,2048]{1,0:T(8,128)(2,1)S(1)}, bf16[32,2048]{1,0:T(8,128)(2,1)S(1)}, u32[]{:S(2)}, u32[]{:S(2)}) %collective-permute-start.28) | collective-permute-done | bytes 131104 | tf_op jit(solution)/shard_map/ppermute | solution.py:34
  105.5 1.4 %collective-permute-start.32 = (bf16[32,512]{1,0:T(8,128)(2,1)S(1)}, bf16[32,512]{1,0:T(8,128)(2,1)S(1)}, u32[]{:S(2)}, u32[]{:S(2)}) collective-permute-start(bf16[32,512]{1,0:T(8,128)(2,1)S(1)} %get-tuple-element.51), channel_id=1, source_target_pairs={{0,3},{1,2},{2,1},{3,0},{4,7},{5,6},{6,5},{7,4},{8,11},{9,10},{10,... | collective-permute-start | bytes 98312 | tf_op jit(solution)/shard_map/ppermute | solution.py:34
  107.0 2.1 %collective-permute-start.31 = (bf16[32,512]{1,0:T(8,128)(2,1)S(1)}, bf16[32,512]{1,0:T(8,128)(2,1)S(1)}, u32[]{:S(2)}, u32[]{:S(2)}) collective-permute-start(bf16[32,512]{1,0:T(8,128)(2,1)S(1)} %get-tuple-element.52), channel_id=1, source_target_pairs={{0,2},{1,3},{2,0},{3,1},{4,6},{5,7},{6,4},{7,5},{8,10},{9,11},{10,... | collective-permute-start | bytes 98312 | tf_op jit(solution)/shard_map/ppermute | solution.py:34
  110.2 1.4 %collective-permute-start.23 = (bf16[32,512]{1,0:T(8,128)(2,1)S(1)}, bf16[32,512]{1,0:T(8,128)(2,1)S(1)}, u32[]{:S(2)}, u32[]{:S(2)}) collective-permute-start(bf16[32,512]{1,0:T(8,128)(2,1)S(1)} %get-tuple-element.48), channel_id=1, source_target_pairs={{0,3},{1,2},{2,1},{3,0},{4,7},{5,6},{6,5},{7,4},{8,11},{9,10},{10,... | collective-permute-start | bytes 98312 | tf_op jit(solution)/shard_map/ppermute | solution.py:34
  113.2 2.7 %collective-permute-done.23 = bf16[32,512]{1,0:T(8,128)(2,1)S(1)} collective-permute-done((bf16[32,512]{1,0:T(8,128)(2,1)S(1)}, bf16[32,512]{1,0:T(8,128)(2,1)S(1)}, u32[]{:S(2)}, u32[]{:S(2)}) %collective-permute-start.23) | collective-permute-done | bytes 32800 | tf_op jit(solution)/shard_map/ppermute | solution.py:34
  116.6 1.5 %maximum_add_fusion = f32[64,512]{1,0:T(8,128)} fusion(f32[32,512]{1,0:T(8,128)S(1)} %slice_add_fusion, f32[32,512]{1,0:T(8,128)S(1)} %slice_add_fusion.1, bf16[64,512]{1,0:T(8,128)(2,1)S(1)} %collective-permute-done.6, bf16[64,512]{1,0:T(8,128)(2,1)S(1)} %collective-permute-done.5, bf16[64,512]{1,0:T(8,128)(2,1)S(1)} %collective-permute-done.4, ...), kind=kLoop, calls=%fused_computation.30 | loop fusion | flops 294912 | bytes 524288 | tf_op jit(solution)/shard_map/add | solution.py:349
  (78 shorter events, 23.9 us)
Async XLA Ops:
  3.4 38.1 %all-to-all-start = ((bf16[4,320,512]{2,1,0:T(8,128)(2,1)}), bf16[4,320,512]{2,1,0:T(8,128)(2,1)S(1)}, u32[]{:S(2)}, u32[]{:S(2)}) async-start(bf16[4,320,512]{2,1,0:T(8,128)(2,1)} %pad_maximum_fusion), calls=%async_computation | async-start | bytes 2621440 | tf_op jit(solution)/shard_map/all_to_all | solution.py:320
  31.7 6.4 %collective-permute-start.1 = (bf16[64,1024]{1,0:T(8,128)(2,1)}, bf16[64,1024]{1,0:T(8,128)(2,1)}, u32[]{:S(2)}, u32[]{:S(2)}) collective-permute-start(bf16[64,1024]{1,0:T(8,128)(2,1)} %get-tuple-element.17), channel_id=1, source_target_pairs={{0,8},{4,12},{8,0},{12,4},{16,24},{20,28},{24,16},{28,20},{1,9},{5... | collective-permute-start | bytes 393224 | tf_op jit(solution)/shard_map/ppermute | solution.py:34
  33.2 8.4 %collective-permute-start.2 = (bf16[64,1024]{1,0:T(8,128)(2,1)}, bf16[64,1024]{1,0:T(8,128)(2,1)}, u32[]{:S(2)}, u32[]{:S(2)}) collective-permute-start(bf16[64,1024]{1,0:T(8,128)(2,1)} %get-tuple-element.18), channel_id=1, source_target_pairs={{0,16},{4,20},{8,24},{12,28},{16,0},{20,4},{24,8},{28,12},{1,17},{... | collective-permute-start | bytes 393224 | tf_op jit(solution)/shard_map/ppermute | solution.py:34
  34.7 6.9 %collective-permute-start.3 = (bf16[64,1024]{1,0:T(8,128)(2,1)S(1)}, bf16[64,1024]{1,0:T(8,128)(2,1)}, u32[]{:S(2)}, u32[]{:S(2)}) collective-permute-start(bf16[64,1024]{1,0:T(8,128)(2,1)S(1)} %get-tuple-element.19), channel_id=1, source_target_pairs={{0,24},{4,28},{8,16},{12,20},{16,8},{20,12},{24,0},{28,4},{1,25},{... | collective-permute-start | bytes 393224 | tf_op jit(solution)/shard_map/ppermute | solution.py:34
  35.2 29.8 %collective-permute-start.10 = (bf16[1024,512]{1,0:T(8,128)(2,1)S(1)}, bf16[1024,512]{1,0:T(8,128)(2,1)S(1)}, u32[]{:S(2)}, u32[]{:S(2)}) collective-permute-start(bf16[1024,512]{1,0:T(8,128)(2,1)S(1)} %copy-done.2), channel_id=1, source_target_pairs={{0,4},{4,0},{8,12},{12,8},{16,20},{20,16},{24,28},{28,24},{1,5},{5... | collective-permute-start | bytes 3145736 | tf_op jit(solution)/shard_map/ppermute | solution.py:34
  48.4 33.6 %collective-permute-start.17 = (bf16[4,320,512]{2,1,0:T(8,128)(2,1)}, bf16[4,320,512]{2,1,0:T(8,128)(2,1)S(1)}, u32[]{:S(2)}, u32[]{:S(2)}) collective-permute-start(bf16[4,320,512]{2,1,0:T(8,128)(2,1)} %copy-done), channel_id=1, source_target_pairs={{0,4},{4,0},{8,12},{12,8},{16,20},{20,16},{24,28},{28,24},{1,5},{5... | collective-permute-start | bytes 3932168 | tf_op jit(solution)/shard_map/ppermute | solution.py:34
  49.4 4.8 %collective-permute-start.4 = (bf16[64,512]{1,0:T(8,128)(2,1)S(1)}, bf16[64,512]{1,0:T(8,128)(2,1)S(1)}, u32[]{:S(2)}, u32[]{:S(2)}) collective-permute-start(bf16[64,512]{1,0:T(8,128)(2,1)S(1)} %get-tuple-element.44), channel_id=1, source_target_pairs={{0,1},{1,0},{2,3},{3,2},{4,5},{5,4},{6,7},{7,6},{8,9},{9,8},{10,11... | collective-permute-start | bytes 196616 | tf_op jit(solution)/shard_map/ppermute | solution.py:34
  51.5 6.7 %collective-permute-start.6 = (bf16[64,512]{1,0:T(8,128)(2,1)S(1)}, bf16[64,512]{1,0:T(8,128)(2,1)S(1)}, u32[]{:S(2)}, u32[]{:S(2)}) collective-permute-start(bf16[64,512]{1,0:T(8,128)(2,1)S(1)} %get-tuple-element.45), channel_id=1, source_target_pairs={{0,3},{1,2},{2,1},{3,0},{4,7},{5,6},{6,5},{7,4},{8,11},{9,10},{10,... | collective-permute-start | bytes 196616 | tf_op jit(solution)/shard_map/ppermute | solution.py:34
  53.9 6.7 %collective-permute-start.5 = (bf16[64,512]{1,0:T(8,128)(2,1)S(1)}, bf16[64,512]{1,0:T(8,128)(2,1)S(1)}, u32[]{:S(2)}, u32[]{:S(2)}) collective-permute-start(bf16[64,512]{1,0:T(8,128)(2,1)S(1)} %get-tuple-element.46), channel_id=1, source_target_pairs={{0,2},{1,3},{2,0},{3,1},{4,6},{5,7},{6,4},{7,5},{8,10},{9,11},{10,... | collective-permute-start | bytes 196616 | tf_op jit(solution)/shard_map/ppermute | solution.py:34
  61.4 5.3 %collective-permute-start.9 = (bf16[64,512]{1,0:T(8,128)(2,1)S(1)}, bf16[64,512]{1,0:T(8,128)(2,1)S(1)}, u32[]{:S(2)}, u32[]{:S(2)}) collective-permute-start(bf16[64,512]{1,0:T(8,128)(2,1)S(1)} %fusion.10.refs_0_), channel_id=1, source_target_pairs={{0,24},{4,28},{8,16},{12,20},{16,8},{20,12},{24,0},{28,4},{1,25},{... | collective-permute-start | bytes 196616 | tf_op jit(solution)/shard_map/ppermute | solution.py:34
  63.0 5.6 %collective-permute-start.8 = (bf16[64,512]{1,0:T(8,128)(2,1)S(1)}, bf16[64,512]{1,0:T(8,128)(2,1)S(1)}, u32[]{:S(2)}, u32[]{:S(2)}) collective-permute-start(bf16[64,512]{1,0:T(8,128)(2,1)S(1)} %fusion.10.refs_0_), channel_id=1, source_target_pairs={{0,16},{4,20},{8,24},{12,28},{16,0},{20,4},{24,8},{28,12},{1,17},{... | collective-permute-start | bytes 196616 | tf_op jit(solution)/shard_map/ppermute | solution.py:34
  64.2 5.0 %collective-permute-start.7 = (bf16[64,512]{1,0:T(8,128)(2,1)S(1)}, bf16[64,512]{1,0:T(8,128)(2,1)S(1)}, u32[]{:S(2)}, u32[]{:S(2)}) collective-permute-start(bf16[64,512]{1,0:T(8,128)(2,1)S(1)} %fusion.10.refs_0_), channel_id=1, source_target_pairs={{0,8},{4,12},{8,0},{12,4},{16,24},{20,28},{24,16},{28,20},{1,9},{5... | collective-permute-start | bytes 196616 | tf_op jit(solution)/shard_map/ppermute | solution.py:34
  65.0 10.4 %collective-permute-start.16 = (bf16[4,64,512]{2,1,0:T(8,128)(2,1)}, bf16[4,64,512]{2,1,0:T(8,128)(2,1)S(1)}, u32[]{:S(2)}, u32[]{:S(2)}) collective-permute-start(bf16[4,64,512]{2,1,0:T(8,128)(2,1)} %get-tuple-element.22.refs_0_), channel_id=1, source_target_pairs={{0,24},{4,28},{8,16},{12,20},{16,8},{20,12},{24,0},{28,4},{1,25},{... | collective-permute-start | bytes 786440 | tf_op jit(solution)/shard_map/ppermute | solution.py:34
  66.8 12.7 %collective-permute-start.15 = (bf16[4,64,512]{2,1,0:T(8,128)(2,1)}, bf16[4,64,512]{2,1,0:T(8,128)(2,1)S(1)}, u32[]{:S(2)}, u32[]{:S(2)}) collective-permute-start(bf16[4,64,512]{2,1,0:T(8,128)(2,1)} %get-tuple-element.22.refs_0_), channel_id=1, source_target_pairs={{0,16},{4,20},{8,24},{12,28},{16,0},{20,4},{24,8},{28,12},{1,17},{... | collective-permute-start | bytes 786440 | tf_op jit(solution)/shard_map/ppermute | solution.py:34
  68.5 11.2 %collective-permute-start.14 = (bf16[4,64,512]{2,1,0:T(8,128)(2,1)}, bf16[4,64,512]{2,1,0:T(8,128)(2,1)S(1)}, u32[]{:S(2)}, u32[]{:S(2)}) collective-permute-start(bf16[4,64,512]{2,1,0:T(8,128)(2,1)} %get-tuple-element.22.refs_0_), channel_id=1, source_target_pairs={{0,8},{4,12},{8,0},{12,4},{16,24},{20,28},{24,16},{28,20},{1,9},{5... | collective-permute-start | bytes 786440 | tf_op jit(solution)/shard_map/ppermute | solution.py:34
  70.5 27.3 %collective-permute-start.13 = (bf16[128,512]{1,0:T(8,128)(2,1)S(1)}, bf16[128,512]{1,0:T(8,128)(2,1)S(1)}, u32[]{:S(2)}, u32[]{:S(2)}) collective-permute-start(bf16[128,512]{1,0:T(8,128)(2,1)S(1)} %get-tuple-element.28), channel_id=1, source_target_pairs={{0,3},{1,2},{2,1},{3,0},{4,7},{5,6},{6,5},{7,4},{8,11},{9,10},{10,... | collective-permute-start | bytes 393224 | tf_op jit(solution)/shard_map/ppermute | solution.py:34
  75.4 8.4 %collective-permute-start.26 = (bf16[128,512]{1,0:T(8,128)(2,1)S(1)}, bf16[128,512]{1,0:T(8,128)(2,1)S(1)}, u32[]{:S(2)}, u32[]{:S(2)}) collective-permute-start(bf16[128,512]{1,0:T(8,128)(2,1)S(1)} %get-tuple-element.29), channel_id=1, source_target_pairs={{0,3},{1,2},{2,1},{3,0},{4,7},{5,6},{6,5},{7,4},{8,11},{9,10},{10,... | collective-permute-start | bytes 393224 | tf_op jit(solution)/shard_map/ppermute | solution.py:34
  79.4 14.6 %collective-permute-start.25 = (bf16[128,512]{1,0:T(8,128)(2,1)S(1)}, bf16[128,512]{1,0:T(8,128)(2,1)S(1)}, u32[]{:S(2)}, u32[]{:S(2)}) collective-permute-start(bf16[128,512]{1,0:T(8,128)(2,1)S(1)} %get-tuple-element.30), channel_id=1, source_target_pairs={{0,2},{1,3},{2,0},{3,1},{4,6},{5,7},{6,4},{7,5},{8,10},{9,11},{10,... | collective-permute-start | bytes 393224 | tf_op jit(solution)/shard_map/ppermute | solution.py:34
  79.7 14.3 %collective-permute-start.24 = (bf16[128,512]{1,0:T(8,128)(2,1)S(1)}, bf16[128,512]{1,0:T(8,128)(2,1)S(1)}, u32[]{:S(2)}, u32[]{:S(2)}) collective-permute-start(bf16[128,512]{1,0:T(8,128)(2,1)S(1)} %get-tuple-element.31), channel_id=1, source_target_pairs={{0,1},{1,0},{2,3},{3,2},{4,5},{5,4},{6,7},{7,6},{8,9},{9,8},{10,11... | collective-permute-start | bytes 393224 | tf_op jit(solution)/shard_map/ppermute | solution.py:34
  82.0 16.6 %collective-permute-start.12 = (bf16[128,512]{1,0:T(8,128)(2,1)S(1)}, bf16[128,512]{1,0:T(8,128)(2,1)S(1)}, u32[]{:S(2)}, u32[]{:S(2)}) collective-permute-start(bf16[128,512]{1,0:T(8,128)(2,1)S(1)} %get-tuple-element.33), channel_id=1, source_target_pairs={{0,2},{1,3},{2,0},{3,1},{4,6},{5,7},{6,4},{7,5},{8,10},{9,11},{10,... | collective-permute-start | bytes 393224 | tf_op jit(solution)/shard_map/ppermute | solution.py:34
  83.8 14.9 %collective-permute-start.11 = (bf16[128,512]{1,0:T(8,128)(2,1)S(1)}, bf16[128,512]{1,0:T(8,128)(2,1)S(1)}, u32[]{:S(2)}, u32[]{:S(2)}) collective-permute-start(bf16[128,512]{1,0:T(8,128)(2,1)S(1)} %get-tuple-element.34), channel_id=1, source_target_pairs={{0,1},{1,0},{2,3},{3,2},{4,5},{5,4},{6,7},{7,6},{8,9},{9,8},{10,11... | collective-permute-start | bytes 393224 | tf_op jit(solution)/shard_map/ppermute | solution.py:34
  95.1 7.3 %collective-permute-start.27 = (bf16[32,2048]{1,0:T(8,128)(2,1)S(1)}, bf16[32,2048]{1,0:T(8,128)(2,1)S(1)}, u32[]{:S(2)}, u32[]{:S(2)}) collective-permute-start(bf16[32,2048]{1,0:T(8,128)(2,1)S(1)} %get-tuple-element.41), channel_id=1, source_target_pairs={{0,8},{4,12},{8,0},{12,4},{16,24},{20,28},{24,16},{28,20},{1,9},{5... | collective-permute-start | bytes 393224 | tf_op jit(solution)/shard_map/ppermute | solution.py:34
  96.3 7.7 %collective-permute-start.29 = (bf16[32,2048]{1,0:T(8,128)(2,1)S(1)}, bf16[32,2048]{1,0:T(8,128)(2,1)S(1)}, u32[]{:S(2)}, u32[]{:S(2)}) collective-permute-start(bf16[32,2048]{1,0:T(8,128)(2,1)S(1)} %get-tuple-element.42), channel_id=1, source_target_pairs={{0,24},{4,28},{8,16},{12,20},{16,8},{20,12},{24,0},{28,4},{1,25},{... | collective-permute-start | bytes 393224 | tf_op jit(solution)/shard_map/ppermute | solution.py:34
  97.8 7.6 %collective-permute-start.28 = (bf16[32,2048]{1,0:T(8,128)(2,1)S(1)}, bf16[32,2048]{1,0:T(8,128)(2,1)S(1)}, u32[]{:S(2)}, u32[]{:S(2)}) collective-permute-start(bf16[32,2048]{1,0:T(8,128)(2,1)S(1)} %get-tuple-element.43), channel_id=1, source_target_pairs={{0,16},{4,20},{8,24},{12,28},{16,0},{20,4},{24,8},{28,12},{1,17},{... | collective-permute-start | bytes 393224 | tf_op jit(solution)/shard_map/ppermute | solution.py:34
  99.7 7.3 %collective-permute-start.18 = (bf16[32,2048]{1,0:T(8,128)(2,1)S(1)}, bf16[32,2048]{1,0:T(8,128)(2,1)S(1)}, u32[]{:S(2)}, u32[]{:S(2)}) collective-permute-start(bf16[32,2048]{1,0:T(8,128)(2,1)S(1)} %get-tuple-element.36), channel_id=1, source_target_pairs={{0,8},{4,12},{8,0},{12,4},{16,24},{20,28},{24,16},{28,20},{1,9},{5... | collective-permute-start | bytes 393224 | tf_op jit(solution)/shard_map/ppermute | solution.py:34
  100.9 8.2 %collective-permute-start.20 = (bf16[32,2048]{1,0:T(8,128)(2,1)S(1)}, bf16[32,2048]{1,0:T(8,128)(2,1)S(1)}, u32[]{:S(2)}, u32[]{:S(2)}) collective-permute-start(bf16[32,2048]{1,0:T(8,128)(2,1)S(1)} %get-tuple-element.37), channel_id=1, source_target_pairs={{0,24},{4,28},{8,16},{12,20},{16,8},{20,12},{24,0},{28,4},{1,25},{... | collective-permute-start | bytes 393224 | tf_op jit(solution)/shard_map/ppermute | solution.py:34
  102.4 6.6 %collective-permute-start.19 = (bf16[32,2048]{1,0:T(8,128)(2,1)S(1)}, bf16[32,2048]{1,0:T(8,128)(2,1)S(1)}, u32[]{:S(2)}, u32[]{:S(2)}) collective-permute-start(bf16[32,2048]{1,0:T(8,128)(2,1)S(1)} %get-tuple-element.38), channel_id=1, source_target_pairs={{0,16},{4,20},{8,24},{12,28},{16,0},{20,4},{24,8},{28,12},{1,17},{... | collective-permute-start | bytes 393224 | tf_op jit(solution)/shard_map/ppermute | solution.py:34
  105.5 6.1 %collective-permute-start.30 = (bf16[32,512]{1,0:T(8,128)(2,1)S(1)}, bf16[32,512]{1,0:T(8,128)(2,1)S(1)}, u32[]{:S(2)}, u32[]{:S(2)}) collective-permute-start(bf16[32,512]{1,0:T(8,128)(2,1)S(1)} %get-tuple-element.50), channel_id=1, source_target_pairs={{0,1},{1,0},{2,3},{3,2},{4,5},{5,4},{6,7},{7,6},{8,9},{9,8},{10,11... | collective-permute-start | bytes 98312 | tf_op jit(solution)/shard_map/ppermute | solution.py:34
  105.5 7.1 %collective-permute-start.32 = (bf16[32,512]{1,0:T(8,128)(2,1)S(1)}, bf16[32,512]{1,0:T(8,128)(2,1)S(1)}, u32[]{:S(2)}, u32[]{:S(2)}) collective-permute-start(bf16[32,512]{1,0:T(8,128)(2,1)S(1)} %get-tuple-element.51), channel_id=1, source_target_pairs={{0,3},{1,2},{2,1},{3,0},{4,7},{5,6},{6,5},{7,4},{8,11},{9,10},{10,... | collective-permute-start | bytes 98312 | tf_op jit(solution)/shard_map/ppermute | solution.py:34
  107.0 5.9 %collective-permute-start.31 = (bf16[32,512]{1,0:T(8,128)(2,1)S(1)}, bf16[32,512]{1,0:T(8,128)(2,1)S(1)}, u32[]{:S(2)}, u32[]{:S(2)}) collective-permute-start(bf16[32,512]{1,0:T(8,128)(2,1)S(1)} %get-tuple-element.52), channel_id=1, source_target_pairs={{0,2},{1,3},{2,0},{3,1},{4,6},{5,7},{6,4},{7,5},{8,10},{9,11},{10,... | collective-permute-start | bytes 98312 | tf_op jit(solution)/shard_map/ppermute | solution.py:34
  110.2 5.7 %collective-permute-start.23 = (bf16[32,512]{1,0:T(8,128)(2,1)S(1)}, bf16[32,512]{1,0:T(8,128)(2,1)S(1)}, u32[]{:S(2)}, u32[]{:S(2)}) collective-permute-start(bf16[32,512]{1,0:T(8,128)(2,1)S(1)} %get-tuple-element.48), channel_id=1, source_target_pairs={{0,3},{1,2},{2,1},{3,0},{4,7},{5,6},{6,5},{7,4},{8,11},{9,10},{10,... | collective-permute-start | bytes 98312 | tf_op jit(solution)/shard_map/ppermute | solution.py:34
  111.5 5.1 %collective-permute-start.22 = (bf16[32,512]{1,0:T(8,128)(2,1)S(1)}, bf16[32,512]{1,0:T(8,128)(2,1)S(1)}, u32[]{:S(2)}, u32[]{:S(2)}) collective-permute-start(bf16[32,512]{1,0:T(8,128)(2,1)S(1)} %get-tuple-element.49), channel_id=1, source_target_pairs={{0,2},{1,3},{2,0},{3,1},{4,6},{5,7},{6,4},{7,5},{8,10},{9,11},{10,... | collective-permute-start | bytes 98312 | tf_op jit(solution)/shard_map/ppermute | solution.py:34
  (10 other events, 97.5 us)

commit v3 on v2

v3 whole, which is shorter than its diff:
```python
import functools
import math

import jax
import jax.numpy as jnp
from jax import lax
from jax.experimental import pallas as pl
from jax.experimental.pallas import tpu as pltpu
from jax.sharding import PartitionSpec as P

HD = 128
SCALE = HD**-0.5
SCALE_LOG2 = SCALE * math.log2(math.e)
BF16, F32 = jnp.bfloat16, jnp.float32
NT = (((1,), (1,)), ((), ()))
NN = (((1,), (0,)), ((), ()))
TN = (((0,), (0,)), ((), ()))
VMEM_BYTES = 24 * 2**20


def dot(a, b, dims):
    return lax.dot_general(a, b, dims, preferred_element_type=F32)


def slope_of(pre):
    return (
        0.5 * (1.0 + lax.erf(pre * 0.7071067811865476))
        + pre * jnp.exp(-0.5 * pre * pre) * 0.3989422804014327
    )


def swap(x, axis, distance):
    size = lax.axis_size(axis)
    return lax.ppermute(x, axis, [(i, i ^ distance) for i in range(size)])


def levels_of(first, count):
    levels = []
    while count > 1:
        radix = min(4, count)
        levels.append((first, radix))
        first, count = first * radix, count // radix
    return levels


def gather_blocks(x, axis, first, count):
    blocks = [x]
    for step, radix in levels_of(first, count):
        whole = blocks[0] if len(blocks) == 1 else jnp.stack(blocks)
        got = [swap(whole, axis, step * k) for k in range(1, radix)]
        for other in got:
            blocks = blocks + ([other] if whole is x else list(other))
    return blocks


def scatter_terms(blocks, axis, first, low=BF16):
    levels = levels_of(first, len(blocks))
    for step, radix in reversed(levels[1:]):
        span = step // first
        terms = [blocks[k * span : (k + 1) * span] for k in range(radix)]
        got = [swap(jnp.stack(terms[k]), axis, step * k) for k in range(1, radix)]
        blocks = [
            (terms[0][i].astype(F32) + sum(g[i].astype(F32) for g in got)).astype(low)
            for i in range(span)
        ]
    return [blocks[0]] + [swap(blocks[k], axis, first * k) for k in range(1, len(blocks))]


def attend_kernel(sub, place_ref, q_ref, g_ref, k_ref, v_ref, *rest):
    dq_ref, even_ref, odd_ref, acc_ref = rest[-4:]
    block = pl.program_id(1)
    keys, values = k_ref[...], v_ref[...]

    @pl.when(block == 0)
    def _():
        acc_ref[...] = jnp.zeros_like(acc_ref)

    def products(at):
        return dot(keys, q_ref[at, :], NT), dot(values, g_ref[at, :], NT)

    def soften(scores, weight_grad):
        top = jnp.max(scores, axis=0, keepdims=True)
        grown = jnp.exp2((scores - top) * SCALE_LOG2)
        weights = grown * (1.0 / jnp.sum(grown, axis=0, keepdims=True))
        centre = jnp.sum(weights * weight_grad, axis=0, keepdims=True)
        return (weights * (weight_grad - centre)).astype(BF16), weights.astype(BF16)

    def collect(at, score_grad, weights_low):
        dq_ref[at, :] = (SCALE * dot(keys, score_grad, TN)).T.astype(BF16)
        acc_ref[:, :HD] += dot(score_grad, q_ref[at, :], NN)
        acc_ref[:, HD:] += dot(weights_low, g_ref[at, :], NN)

    pieces = [pl.ds(i * sub, sub) for i in range(q_ref.shape[0] // sub)]
    ahead, behind = products(pieces[0]), None
    for i, at in enumerate(pieces):
        now, ahead = ahead, products(pieces[i + 1]) if i + 1 < len(pieces) else None
        done = soften(*now)
        if behind is not None:
            collect(pieces[i - 1], *behind)
        behind = done
    collect(pieces[-1], *behind)

    @pl.when(block == pl.num_programs(1) - 1)
    def _():
        acc_ref[:, :HD] = SCALE * acc_ref[:, :HD]
        half, height = even_ref.shape[:2]
        for j in range(2 * half):
            at = pl.ds(pl.multiple_of(place_ref[j] * height, height), height)
            (odd_ref if j % 2 else even_ref)[j // 2] = acc_ref[at, :].astype(BF16)


def attend(place, queries, out_grad, keys, values, first, count, query_grad=None, after=()):
    tokens, width = queries.shape
    glob, size = keys.shape[0], place.shape[0]
    block = min(2048, tokens)
    token_spec = pl.BlockSpec((block, HD), lambda h, b, place: (b, h + first))
    global_spec = pl.BlockSpec((glob, HD), lambda h, b, place: (0, h + first))
    part_spec = pl.BlockSpec((size // 2, glob // size, 2 * HD), lambda h, b, place: (0, 0, h))
    part = pltpu.HBM((size // 2, glob // size, 2 * HD * count), BF16)
    extra = [x for x in (query_grad, *after) if x is not None]
    return pl.pallas_call(
        functools.partial(attend_kernel, min(256, block)),
        grid_spec=pltpu.PrefetchScalarGridSpec(
            num_scalar_prefetch=1,
            grid=(count, tokens // block),
            in_specs=[token_spec, token_spec, global_spec, global_spec]
            + [pl.BlockSpec(memory_space=pl.ANY)] * len(extra),
            out_specs=[token_spec, part_spec, part_spec],
            scratch_shapes=[pltpu.VMEM((glob, 2 * HD), F32)],
        ),
        out_shape=[pltpu.HBM((tokens, width), BF16), part, part],
        input_output_aliases={} if query_grad is None else {5: 0},
        compiler_params=pltpu.CompilerParams(vmem_limit_bytes=VMEM_BYTES),
        cost_estimate=pl.CostEstimate(
            flops=20 * tokens * glob * HD * count,
            bytes_accessed=6 * tokens * HD * count,
            transcendentals=tokens * glob * count,
        ),
        name="attend",
    )(place, *map(hold, (queries, out_grad, keys, values)), *extra)


def hold(x):
    return pltpu.with_memory_space_constraint(x, pltpu.HBM)


def bundle_kernel(up_ref, in_ref, out_ref):
    size, depth, _ = out_ref.shape
    rows = in_ref.shape[0]
    hidden = depth - rows
    for k in range(size):
        out_ref[k, :hidden, :] = up_ref[:, k * hidden : (k + 1) * hidden].T
        out_ref[k, hidden:, :] = in_ref[...]


def bundle(up_proj, global_in, size):
    (width, hidden), rows = up_proj.shape, global_in.shape[0]
    if (hidden // size) % 128 or rows % 16:
        return jnp.concatenate(
            [
                up_proj.T.reshape(size, hidden // size, width),
                jnp.broadcast_to(global_in[None], (size, rows, width)),
            ],
            1,
        )
    return pl.pallas_call(
        bundle_kernel,
        out_shape=jax.ShapeDtypeStruct((size, hidden // size + rows, width), BF16),
        compiler_params=pltpu.CompilerParams(vmem_limit_bytes=VMEM_BYTES),
        cost_estimate=pl.CostEstimate(
            flops=0, bytes_accessed=4 * up_proj.size, transcendentals=0
        ),
        name="bundle",
    )(hold(up_proj), hold(global_in))


def merge_kernel(count, *refs):
    evens, gots = refs[:count], refs[count : 2 * count]
    out_refs = refs[len(refs) - evens[0].shape[0] :]
    at = 0
    for even_ref, got_ref in zip(evens, gots):
        cols = pl.ds(at, even_ref.shape[2])
        at += even_ref.shape[2]
        for j, out_ref in enumerate(out_refs):
            out_ref[:, cols] = (even_ref[j].astype(F32) + got_ref[j].astype(F32)).astype(BF16)


def scatter_rows(evens, odds, near):
    gots = [swap(odd, "seq", 1) for odd in odds]
    blocks, rows, _ = evens[0].shape
    width = sum(even.shape[2] for even in evens)
    spec = lambda x: pl.BlockSpec(x.shape, lambda: (0, 0, 0))
    mine = pl.pallas_call(
        functools.partial(merge_kernel, len(evens)),
        in_specs=[spec(x) for x in (*evens, *gots)]
        + [pl.BlockSpec(memory_space=pltpu.VMEM)] * len(near),
        out_shape=[jax.ShapeDtypeStruct((rows, width), BF16)] * blocks,
        compiler_params=pltpu.CompilerParams(vmem_limit_bytes=VMEM_BYTES),
        cost_estimate=pl.CostEstimate(
            flops=blocks * rows * width, bytes_accessed=6 * blocks * rows * width, transcendentals=0
        ),
        name="merge",
    )(*map(hold, evens), *gots, *near)
    return scatter_terms(mine, "seq", 2)


def project_kernel(count, chunk_ref, *refs):
    terms, sources = refs[:count], refs[count : count + 2]
    part_refs, (term_ref, held_ref, term_sems, sems) = refs[count + 2 : -4], refs[-4:]
    size, block = len(part_refs), part_refs[0].shape[1]

    def fetch(k, i):
        at = pl.ds(pl.multiple_of(chunk_ref[k] * block, block), block)
        return pltpu.make_async_copy(sources[i].at[at, :], held_ref.at[k, i], sems.at[k, i])

    given = [pltpu.make_async_copy(t, term_ref.at[j], term_sems.at[j]) for j, t in enumerate(terms)]
    for copy in given:
        copy.start()
    for k in range(size):
        for i in range(2):
            fetch(k, i).start()
    for copy in given:
        copy.wait()
    total = sum(term_ref[j].astype(F32) for j in range(count)).astype(BF16)
    heads = total.shape[1] // (2 * HD)
    low = [
        jnp.concatenate([total[:, (2 * h + i) * HD : (2 * h + i + 1) * HD] for h in range(heads)], 1)
        for i in range(2)
    ]
    for k, part_ref in enumerate(part_refs):
        part = None
        for i in range(2):
            fetch(k, i).wait()
            term = dot(low[i], held_ref[k, i], NT)
            part = term if part is None else part + term
        part_ref[...] = part.astype(BF16)


def project(chunk, terms, key_proj, value_proj):
    rows, width = terms[0].shape
    size = chunk.shape[0]
    block = key_proj.shape[0] // size
    count = len(terms)
    part = pltpu.HBM((rows, block), BF16)
    return pl.pallas_call(
        functools.partial(project_kernel, count),
        in_specs=[pl.BlockSpec(memory_space=pltpu.SMEM)]
        + [pl.BlockSpec(memory_space=pl.ANY)] * (count + 2),
        out_specs=[pl.BlockSpec((rows, block), lambda: (0, 0))] * size,
        out_shape=[part] * size,
        scratch_shapes=[
            pltpu.VMEM((count, rows, width), BF16),
            pltpu.VMEM((size, 2, block, width // 2), BF16),
            pltpu.SemaphoreType.DMA((count,)),
            pltpu.SemaphoreType.DMA((size, 2)),
        ],
        compiler_params=pltpu.CompilerParams(vmem_limit_bytes=VMEM_BYTES),
        cost_estimate=pl.CostEstimate(
            flops=2 * rows * width * block * size,
            bytes_accessed=2 * width * block * size,
            transcendentals=0,
        ),
        name="project",
    )(chunk, *terms, hold(key_proj), hold(value_proj))


def pieces_of(blocks, cuts):
    height = sum(cuts)
    starts = [sum(cuts[:c]) for c in range(len(cuts))]
    whole = blocks[0].shape[0] // height
    rows = [
        block[i * height + start : i * height + start + cut]
        for start, cut in zip(starts, cuts)
        for block in blocks
        for i in range(whole)
    ]
    count = len(blocks) * whole
    return jnp.concatenate(rows, 0), [(count * start, count * cut) for start, cut in zip(starts, cuts)]


def back_kernel(count, cuts, chunk_ref, *refs):
    states, downs, out_refs = refs[:count], refs[count : count + 2], refs[count + 2 :]
    size, _, hidden = out_refs[0].shape
    hidden = hidden // 2
    state, places = pieces_of([ref[...] for ref in states], cuts)
    for k in range(size):
        at = pl.ds(pl.multiple_of(chunk_ref[k] * hidden, hidden), hidden)
        for i in range(2):
            part = dot(state, downs[i][at, :], NT).astype(BF16)
            for (start, rows), out_ref in zip(places, out_refs):
                out_ref[k, :, i * hidden : (i + 1) * hidden] = part[start : start + rows]


def back_parts(chunk, states, downs, cuts):
    size, (height, width) = chunk.shape[0], states[0].shape
    count = len(states)
    if height % 16:
        states = [jnp.concatenate(states, 0)]
    hidden = downs[0].shape[0] // size
    return pl.pallas_call(
        functools.partial(back_kernel, len(states), cuts),
        in_specs=[pl.BlockSpec(memory_space=pltpu.SMEM)]
        + [pl.BlockSpec(memory_space=pltpu.VMEM)] * (len(states) + 2),
        out_shape=[jax.ShapeDtypeStruct((size, count * cut, 2 * hidden), BF16) for cut in cuts],
        compiler_params=pltpu.CompilerParams(vmem_limit_bytes=VMEM_BYTES),
        cost_estimate=pl.CostEstimate(
            flops=4 * count * height * width * hidden * size,
            bytes_accessed=4 * width * hidden * size,
            transcendentals=0,
        ),
        name="back",
    )(chunk, *states, *downs)


def pre_kernel(count, cuts, *refs):
    inputs, ups, out_refs = refs[:count], refs[count : count + 2], refs[len(refs) - len(cuts) :]
    hidden = out_refs[0].shape[1] // 2
    size = ups[0].shape[0]
    whole = [pieces_of([ref[k] for ref in inputs], cuts) for k in range(size)]
    for i in range(2):
        part = sum(dot(whole[k][0], ups[i][k, :hidden, :], NT) for k in range(size))
        for (start, rows), out_ref in zip(whole[0][1], out_refs):
            out_ref[:, i * hidden : (i + 1) * hidden] = part[start : start + rows]


def pre_parts(inputs, ups, hidden, cuts, after):
    count, height = len(inputs), inputs[0].shape[1]
    if height % 16:
        inputs = [jnp.concatenate(inputs, 1)]
    return pl.pallas_call(
        functools.partial(pre_kernel, len(inputs), cuts),
        in_specs=[pl.BlockSpec(x.shape, lambda: (0, 0, 0)) for x in (*inputs, *ups)]
        + [pl.BlockSpec(memory_space=pl.ANY)] * len(after),
        out_shape=[jax.ShapeDtypeStruct((count * cut, 2 * hidden), F32) for cut in cuts],
        compiler_params=pltpu.CompilerParams(vmem_limit_bytes=VMEM_BYTES),
        cost_estimate=pl.CostEstimate(
            flops=4 * count * height * hidden * ups[0].shape[0] * ups[0].shape[2],
            bytes_accessed=4 * ups[0].size,
            transcendentals=0,
        ),
        name="pre",
    )(*inputs, *ups, *after)


def feed_kernel(count, chunk_ref, *refs):
    terms, slope_ref, ups, out_ref = refs[:count], refs[count], refs[count + 1 : count + 3], refs[-1]
    back = sum(ref[...].astype(F32) for ref in terms)
    gated = (slope_ref[...] * back).astype(BF16)
    hidden = gated.shape[1] // 2
    size, _, width = ups[0].shape
    for k in range(size):
        part = sum(
            dot(gated[:, i * hidden : (i + 1) * hidden], ups[i][chunk_ref[k], :hidden, :], NN)
            for i in range(2)
        )
        out_ref[:, :, k * width : (k + 1) * width] = part.astype(BF16).reshape(
            out_ref.shape[0], out_ref.shape[1], width
        )


def feed(chunk, terms, slope, ups, blocks):
    rows = terms[0].shape[0]
    size, _, width = ups[0].shape
    hidden = terms[0].shape[1] // 2
    return pl.pallas_call(
        functools.partial(feed_kernel, len(terms)),
        in_specs=[pl.BlockSpec(memory_space=pltpu.SMEM)]
        + [pl.BlockSpec(memory_space=pltpu.VMEM)] * (len(terms) + 3),
        out_specs=pl.BlockSpec(memory_space=pltpu.VMEM),
        out_shape=jax.ShapeDtypeStruct((blocks, rows // blocks, size * width), BF16),
        compiler_params=pltpu.CompilerParams(vmem_limit_bytes=VMEM_BYTES),
        cost_estimate=pl.CostEstimate(
            flops=4 * rows * hidden * width * size,
            bytes_accessed=4 * hidden * width * size,
            transcendentals=0,
        ),
        name="feed",
    )(chunk, *terms, slope, *ups)


def local(queries, keys, values, out_grad, key_proj, value_proj, global_in, up_proj, down_proj):
    size, planes = lax.axis_size("seq"), lax.axis_size("heads")
    place = lax.axis_index("seq") ^ jnp.arange(size, dtype=jnp.int32)
    chunk = lax.axis_index("heads") ^ jnp.arange(planes, dtype=jnp.int32)
    far = size // 2
    rows, width = global_in.shape
    cuts = (rows // 2, rows // 2) if rows % 32 == 0 else (rows,)

    downs = [down_proj, swap(down_proj, "seq", 1)]
    hidden = up_proj.shape[1] // planes
    own_up = lax.all_to_all(bundle(up_proj, global_in, planes), "heads", 0, 0)

    arrays = (queries, out_grad, keys, values)
    heads = queries.shape[1] // HD
    query_grad, even, odd = attend(place, *arrays, 0, heads)
    terms = scatter_rows([even], [odd], [])
    terms[0], downs[1] = lax.optimization_barrier((terms[0], downs[1]))
    share = list(project(chunk, terms, key_proj, value_proj))
    own_up, share[0] = lax.optimization_barrier((own_up, share[0]))
    ups = [own_up, swap(own_up, "seq", 1)]
    shares = [share[0]] + [swap(share[k], "heads", k) for k in range(1, planes)]
    shares, ups[1] = lax.optimization_barrier((shares, ups[1]))
    state = sum(t.astype(F32) for t in shares)
    state_low = state.astype(BF16)
    inputs = gather_blocks(own_up[:, hidden:], "seq", 2, far)
    states = gather_blocks(state_low, "seq", 2, far)
    parts = back_parts(chunk, states, downs, cuts)
    slopes = [slope_of(pre) for pre in pre_parts(inputs, ups, hidden, cuts, parts[:1])]

    grads = []
    for part, slope in zip(parts, slopes):
        terms = [part[0]] + [swap(part[k], "heads", k) for k in range(1, planes)]
        grown = feed(chunk, terms, slope, ups, far)
        own = sum(t.astype(F32) for t in scatter_terms([grown[j] for j in range(far)], "seq", 2))
        blocks = [own[:, k * width : (k + 1) * width] for k in range(planes)]
        grads.append(
            blocks[0]
            + sum(swap(blocks[k].astype(BF16), "heads", k).astype(F32) for k in range(1, planes))
        )
    global_grad = state + jnp.concatenate(grads, 0)
    return (query_grad, global_grad)


def solution(mesh):
    placed = (
        P("seq", "heads"),
        P(None, "heads"),
        P(None, "heads"),
        P("seq", "heads"),
        P(None, "heads"),
        P(None, "heads"),
        P("seq", "heads"),
        P("heads", "seq"),
        P("seq", "heads"),
    )
    return jax.shard_map(
        local,
        mesh=mesh,
        in_specs=placed,
        out_specs=(P("seq", "heads"), P("seq", "heads")),
        check_vma=False,
    )
```

time: 119 us -> 109 us (0.916)
  local copies, waits for them, and re-layouts: 5.49 us -> 0.17 us
  Pallas kernels: 27.4 us -> 30.6 us
  other arithmetic: 5.01 us -> 1.95 us
  starting transfers between devices: 53 us -> 50 us
  waiting for transfers between devices: 26.4 us -> 25 us
    pallas_call x4 -> x5, Pallas kernels: 8.57 us -> 12 us  [the longest x1 5.35 us: project(): pl.pallas_call(functools.partial(project_kernel, count), in_specs=[pl.Blo...]
    ppermute x33, starting transfers between devices: 46.7 us -> 43.7 us  [swap(): return lax.ppermute(x, axis, [(i, i ^ distance) for i in range(size)])]
    unnamed x16 -> x4, local copies, waits for them, and re-layouts: 2.84 us -> 0.01 us
    transpose x1 -> x0, local copies, waits for them, and re-layouts: 1.53 us -> none  [local(): own_up = up_proj.T.reshape(planes, -1, width)]
    ppermute x33, waiting for transfers between devices: 26.4 us -> 25 us  [swap(): return lax.ppermute(x, axis, [(i, i ^ distance) for i in range(size)])]
    concatenate x1 -> x0, other arithmetic: 1.21 us -> none  [local(): own_up = lax.all_to_all(jnp.concatenate([own_up, sent], 1), 'heads', 0, 0)]
  transfers between devices with their start and end apart: 34 -> 34, of which waited for: 17 -> 13; matrix products, arithmetic and copies ran while one was open for 3% -> 0% of each run, Pallas kernels for 23% -> 26%
where the time goes in v3:
time: 109 us
  starting transfers between devices  50 us (46%)
  Pallas kernels  30.6 us (28%)
  waiting for transfers between devices  25 us (23%)
  other arithmetic  1.95 us (2%)
    ppermute x33, starting transfers between devices, swap(): return lax.ppermute(x, axis, [(i, i ^ distance) for i in range(size)])  43.7 us
    ppermute x33, waiting for transfers between devices, swap(): return lax.ppermute(x, axis, [(i, i ^ distance) for i in range(size)])  25 us
    pallas_call x1, Pallas kernels, attend(): pl.pallas_call(functools.partial(attend_kernel, min(256, block)), grid_sp...  16.6 us
    all_to_all x1, starting transfers between devices, local(): own_up = lax.all_to_all(bundle(up_proj, global_in, planes), 'heads', 0, 0)  6.32 us
    pallas_call x1, Pallas kernels, project(): pl.pallas_call(functools.partial(project_kernel, count), in_specs=[pl.Blo...  5.35 us
    pallas_call x1, Pallas kernels, bundle(): pl.pallas_call(bundle_kernel, out_shape=jax.ShapeDtypeStruct((size, hidde...  2.75 us
  transfers between devices with their start and end apart: 34, of which 13 were waited for; matrix products, arithmetic and copies ran while one was open for 0% of the time, Pallas kernels for 26%

profile of v3, /device:TPU:0, one launch (start us, length us, event | category | flops | bytes accessed | tf_op | source)
XLA Modules:
  0.0 108.6 jit_solution(8934530801675580539)
XLA Ops:
  0.6 2.7 %bundle.1 = bf16[4,320,512]{2,1,0:T(8,128)(2,1)} custom-call(bf16[512,1024]{1,0:T(8,128)(2,1)} %up_ref.1, bf16[64,512]{1,0:T(8,128)(2,1)} %in_ref.1), custom_call_target="tpu_custom_call" | custom-call | bytes 2097152 | tf_op jit(solution)/shard_map/bundle/pallas_call | solution.py:166
  3.4 6.3 %all-to-all-start = ((bf16[4,320,512]{2,1,0:T(8,128)(2,1)}), bf16[4,320,512]{2,1,0:T(8,128)(2,1)S(1)}, u32[]{:S(2)}, u32[]{:S(2)}) async-start(bf16[4,320,512]{2,1,0:T(8,128)(2,1)} %bundle.1), calls=%async_computation | async-start | bytes 2621440 | tf_op jit(solution)/shard_map/all_to_all | solution.py:391
  9.7 16.6 %attend.1 = (bf16[2048,512]{1,0:T(8,128)(2,1)}, bf16[4,64,1024]{2,1,0:T(8,128)(2,1)}, bf16[4,64,1024]{2,1,0:T(8,128)(2,1)}) custom-call(s32[8]{0:T(128)S(1)} %iota_xor_fusion.1.place_ref, bf16[2048,512]{1,0:T(8,128)(2,1)} %q_ref.1, bf16[2048,512]{1,0:T(8,128)(2,1)} %g_ref.1, bf16[512,512]{1,0:T(8,128)(2,1)} %k_ref.1, bf16[512,512]{1,0:T(8,128)(2,1)} %v_ref.1), custom_call_target="tpu_custom_call" | custom-call | flops 10737418240 | bytes 6291456 | tf_op jit(solution)/shard_map/attend/pallas_call | solution.py:121
  26.8 1.7 %collective-permute-done.refs_1_ = bf16[4,64,1024]{2,1,0:T(8,128)(2,1)S(1)} collective-permute-done((bf16[4,64,1024]{2,1,0:T(8,128)(2,1)}, bf16[4,64,1024]{2,1,0:T(8,128)(2,1)S(1)}, u32[]{:S(2)}, u32[]{:S(2)}) %collective-permute-start) | collective-permute-done | bytes 524320 | tf_op jit(solution)/shard_map/ppermute | solution.py:34
  28.6 1.8 %merge.1 = (bf16[64,1024]{1,0:T(8,128)(2,1)S(1)}, bf16[64,1024]{1,0:T(8,128)(2,1)}, bf16[64,1024]{1,0:T(8,128)(2,1)}, bf16[64,1024]{1,0:T(8,128)(2,1)}) custom-call(bf16[4,64,1024]{2,1,0:T(8,128)(2,1)} %get-tuple-element.27.refs_0_, bf16[4,64,1024]{2,1,0:T(8,128)(2,1)S(1)} %collective-permute-done.refs_1_), custom_call_target="tpu_custom_call" | custom-call | flops 262144 | bytes 1572864 | tf_op jit(solution)/shard_map/merge/pallas_call | solution.py:193
  30.4 1.5 %collective-permute-start.2 = (bf16[64,1024]{1,0:T(8,128)(2,1)}, bf16[64,1024]{1,0:T(8,128)(2,1)}, u32[]{:S(2)}, u32[]{:S(2)}) collective-permute-start(bf16[64,1024]{1,0:T(8,128)(2,1)} %get-tuple-element.31), channel_id=1, source_target_pairs={{0,8},{4,12},{8,0},{12,4},{16,24},{20,28},{24,16},{28,20},{1,9},{5... | collective-permute-start | bytes 393224 | tf_op jit(solution)/shard_map/ppermute | solution.py:34
  31.9 1.5 %collective-permute-start.3 = (bf16[64,1024]{1,0:T(8,128)(2,1)}, bf16[64,1024]{1,0:T(8,128)(2,1)}, u32[]{:S(2)}, u32[]{:S(2)}) collective-permute-start(bf16[64,1024]{1,0:T(8,128)(2,1)} %get-tuple-element.32), channel_id=1, source_target_pairs={{0,16},{4,20},{8,24},{12,28},{16,0},{20,4},{24,8},{28,12},{1,17},{... | collective-permute-start | bytes 393224 | tf_op jit(solution)/shard_map/ppermute | solution.py:34
  33.9 2.9 %collective-permute-done.2.refs_1_ = bf16[64,1024]{1,0:T(8,128)(2,1)} collective-permute-done((bf16[64,1024]{1,0:T(8,128)(2,1)}, bf16[64,1024]{1,0:T(8,128)(2,1)}, u32[]{:S(2)}, u32[]{:S(2)}) %collective-permute-start.2) | collective-permute-done | bytes 131104 | tf_op jit(solution)/shard_map/ppermute | solution.py:34
  36.8 3.7 %collective-permute-done.3.refs_2_ = bf16[64,1024]{1,0:T(8,128)(2,1)} collective-permute-done((bf16[64,1024]{1,0:T(8,128)(2,1)}, bf16[64,1024]{1,0:T(8,128)(2,1)}, u32[]{:S(2)}, u32[]{:S(2)}) %collective-permute-start.3) | collective-permute-done | bytes 131104 | tf_op jit(solution)/shard_map/ppermute | solution.py:34
  40.5 5.4 %project.1 = (bf16[64,512]{1,0:T(8,128)(2,1)}, bf16[64,512]{1,0:T(8,128)(2,1)}, bf16[64,512]{1,0:T(8,128)(2,1)}, bf16[64,512]{1,0:T(8,128)(2,1)}) custom-call(s32[4]{0:T(128)S(1)} %iota_xor_fusion.chunk_ref, bf16[64,1024]{1,0:T(8,128)(2,1)S(1)} %get-tuple-element.30.refs_0_, bf16[64,1024]{1,0:T(8,128)(2,1)} %collective-permute-done.2.refs_1_, ...), custom_call_target="tpu_custom_call" | custom-call | flops 268435456 | bytes 4194304 | tf_op jit(solution)/shard_map/project/pallas_call | solution.py:245
  45.9 2.1 %collective-permute-start.5 = (bf16[64,512]{1,0:T(8,128)(2,1)}, bf16[64,512]{1,0:T(8,128)(2,1)S(1)}, u32[]{:S(2)}, u32[]{:S(2)}) collective-permute-start(bf16[64,512]{1,0:T(8,128)(2,1)} %get-tuple-element.36), channel_id=1, source_target_pairs={{0,1},{1,0},{2,3},{3,2},{4,5},{5,4},{6,7},{7,6},{8,9},{9,8},{10,11... | collective-permute-start | bytes 196616 | tf_op jit(solution)/shard_map/ppermute | solution.py:34
  48.0 2.4 %collective-permute-start.6 = (bf16[64,512]{1,0:T(8,128)(2,1)}, bf16[64,512]{1,0:T(8,128)(2,1)S(1)}, u32[]{:S(2)}, u32[]{:S(2)}) collective-permute-start(bf16[64,512]{1,0:T(8,128)(2,1)} %get-tuple-element.37), channel_id=1, source_target_pairs={{0,2},{1,3},{2,0},{3,1},{4,6},{5,7},{6,4},{7,5},{8,10},{9,11},{10,... | collective-permute-start | bytes 196616 | tf_op jit(solution)/shard_map/ppermute | solution.py:34
  50.9 5.0 %collective-permute-done.6 = bf16[64,512]{1,0:T(8,128)(2,1)S(1)} collective-permute-done((bf16[64,512]{1,0:T(8,128)(2,1)}, bf16[64,512]{1,0:T(8,128)(2,1)S(1)}, u32[]{:S(2)}, u32[]{:S(2)}) %collective-permute-start.6) | collective-permute-done | bytes 65568 | tf_op jit(solution)/shard_map/ppermute | solution.py:34
  59.8 1.4 %collective-permute-start.11 = (bf16[64,512]{1,0:T(8,128)(2,1)S(1)}, bf16[64,512]{1,0:T(8,128)(2,1)S(1)}, u32[]{:S(2)}, u32[]{:S(2)}) collective-permute-start(bf16[64,512]{1,0:T(8,128)(2,1)S(1)} %fusion.12.refs_0_), channel_id=1, source_target_pairs={{0,24},{4,28},{8,16},{12,20},{16,8},{20,12},{24,0},{28,4},{1,25},{... | collective-permute-start | bytes 196616 | tf_op jit(solution)/shard_map/ppermute | solution.py:34
  61.2 1.3 %collective-permute-start.15 = (bf16[4,64,512]{2,1,0:T(8,128)(2,1)S(1)}, bf16[4,64,512]{2,1,0:T(8,128)(2,1)S(1)}, u32[]{:S(2)}, u32[]{:S(2)}) collective-permute-start(bf16[4,64,512]{2,1,0:T(8,128)(2,1)S(1)} %slice.85.refs_0_), channel_id=1, source_target_pairs={{0,8},{4,12},{8,0},{12,4},{16,24},{20,28},{24,16},{28,20},{1,9},{5... | collective-permute-start | bytes 786440 | tf_op jit(solution)/shard_map/ppermute | solution.py:34
  63.3 1.4 %collective-permute-start.17 = (bf16[4,64,512]{2,1,0:T(8,128)(2,1)S(1)}, bf16[4,64,512]{2,1,0:T(8,128)(2,1)S(1)}, u32[]{:S(2)}, u32[]{:S(2)}) collective-permute-start(bf16[4,64,512]{2,1,0:T(8,128)(2,1)S(1)} %slice.85.refs_0_), channel_id=1, source_target_pairs={{0,24},{4,28},{8,16},{12,20},{16,8},{20,12},{24,0},{28,4},{1,25},{... | collective-permute-start | bytes 786440 | tf_op jit(solution)/shard_map/ppermute | solution.py:34
  65.7 1.3 %back.1 = (bf16[4,128,512]{2,1,0:T(8,128)(2,1)S(1)}, bf16[4,128,512]{2,1,0:T(8,128)(2,1)S(1)}) custom-call(s32[4]{0:T(128)S(1)} %iota_xor_fusion.chunk_ref, bf16[64,512]{1,0:T(8,128)(2,1)S(1)} %fusion.12.refs_0_, bf16[64,512]{1,0:T(8,128)(2,1)S(1)} %collective-permute-done.9.refs_1_, bf16[64,512]{1,0:T(8,128)(2,1)S(1)} %collective-permute-done.10.refs_2_, ...), custom_call_target="tpu_custom_call" | custom-call | flops 536870912 | bytes 2097152 | tf_op jit(solution)/shard_map/back/pallas_call | solution.py:300
  67.1 1.4 %collective-permute-start.24 = (bf16[128,512]{1,0:T(8,128)(2,1)S(1)}, bf16[128,512]{1,0:T(8,128)(2,1)S(1)}, u32[]{:S(2)}, u32[]{:S(2)}) collective-permute-start(bf16[128,512]{1,0:T(8,128)(2,1)S(1)} %get-tuple-element.66), channel_id=1, source_target_pairs={{0,1},{1,0},{2,3},{3,2},{4,5},{5,4},{6,7},{7,6},{8,9},{9,8},{10,11... | collective-permute-start | bytes 393224 | tf_op jit(solution)/shard_map/ppermute | solution.py:34
  68.5 1.6 %collective-permute-start.25 = (bf16[128,512]{1,0:T(8,128)(2,1)S(1)}, bf16[128,512]{1,0:T(8,128)(2,1)S(1)}, u32[]{:S(2)}, u32[]{:S(2)}) collective-permute-start(bf16[128,512]{1,0:T(8,128)(2,1)S(1)} %get-tuple-element.65), channel_id=1, source_target_pairs={{0,2},{1,3},{2,0},{3,1},{4,6},{5,7},{6,4},{7,5},{8,10},{9,11},{10,... | collective-permute-start | bytes 393224 | tf_op jit(solution)/shard_map/ppermute | solution.py:34
  71.0 2.3 %collective-permute-start.26 = (bf16[128,512]{1,0:T(8,128)(2,1)S(1)}, bf16[128,512]{1,0:T(8,128)(2,1)S(1)}, u32[]{:S(2)}, u32[]{:S(2)}) collective-permute-start(bf16[128,512]{1,0:T(8,128)(2,1)S(1)} %get-tuple-element.64), channel_id=1, source_target_pairs={{0,3},{1,2},{2,1},{3,0},{4,7},{5,6},{6,5},{7,4},{8,11},{9,10},{10,... | collective-permute-start | bytes 393224 | tf_op jit(solution)/shard_map/ppermute | solution.py:34
  73.3 1.8 %collective-permute-done.16.refs_2_ = bf16[4,64,512]{2,1,0:T(8,128)(2,1)S(1)} collective-permute-done((bf16[4,64,512]{2,1,0:T(8,128)(2,1)S(1)}, bf16[4,64,512]{2,1,0:T(8,128)(2,1)S(1)}, u32[]{:S(2)}, u32[]{:S(2)}) %collective-permute-start.16) | collective-permute-done | bytes 262176 | tf_op jit(solution)/shard_map/ppermute | solution.py:34
  76.0 2.1 %collective-permute-start.12 = (bf16[128,512]{1,0:T(8,128)(2,1)S(1)}, bf16[128,512]{1,0:T(8,128)(2,1)S(1)}, u32[]{:S(2)}, u32[]{:S(2)}) collective-permute-start(bf16[128,512]{1,0:T(8,128)(2,1)S(1)} %get-tuple-element.59), channel_id=1, source_target_pairs={{0,1},{1,0},{2,3},{3,2},{4,5},{5,4},{6,7},{7,6},{8,9},{9,8},{10,11... | collective-permute-start | bytes 393224 | tf_op jit(solution)/shard_map/ppermute | solution.py:34
  78.6 2.1 %collective-permute-start.14 = (bf16[128,512]{1,0:T(8,128)(2,1)S(1)}, bf16[128,512]{1,0:T(8,128)(2,1)S(1)}, u32[]{:S(2)}, u32[]{:S(2)}) collective-permute-start(bf16[128,512]{1,0:T(8,128)(2,1)S(1)} %get-tuple-element.57), channel_id=1, source_target_pairs={{0,3},{1,2},{2,1},{3,0},{4,7},{5,6},{6,5},{7,4},{8,11},{9,10},{10,... | collective-permute-start | bytes 393224 | tf_op jit(solution)/shard_map/ppermute | solution.py:34
  81.7 1.8 %collective-permute-start.29 = (bf16[32,2048]{1,0:T(8,128)(2,1)S(1)}, bf16[32,2048]{1,0:T(8,128)(2,1)S(1)}, u32[]{:S(2)}, u32[]{:S(2)}) collective-permute-start(bf16[32,2048]{1,0:T(8,128)(2,1)S(1)} %get-tuple-element.62), channel_id=1, source_target_pairs={{0,24},{4,28},{8,16},{12,20},{16,8},{20,12},{24,0},{28,4},{1,25},{... | collective-permute-start | bytes 393224 | tf_op jit(solution)/shard_map/ppermute | solution.py:34
  85.3 4.6 %collective-permute-done.13.refs_2_ = bf16[128,512]{1,0:T(8,128)(2,1)S(1)} collective-permute-done((bf16[128,512]{1,0:T(8,128)(2,1)S(1)}, bf16[128,512]{1,0:T(8,128)(2,1)S(1)}, u32[]{:S(2)}, u32[]{:S(2)}) %collective-permute-start.13) | collective-permute-done | bytes 131104 | tf_op jit(solution)/shard_map/ppermute | solution.py:34
  90.9 1.5 %collective-permute-start.20 = (bf16[32,2048]{1,0:T(8,128)(2,1)S(1)}, bf16[32,2048]{1,0:T(8,128)(2,1)S(1)}, u32[]{:S(2)}, u32[]{:S(2)}) collective-permute-start(bf16[32,2048]{1,0:T(8,128)(2,1)S(1)} %get-tuple-element.55), channel_id=1, source_target_pairs={{0,24},{4,28},{8,16},{12,20},{16,8},{20,12},{24,0},{28,4},{1,25},{... | collective-permute-start | bytes 393224 | tf_op jit(solution)/shard_map/ppermute | solution.py:34
  92.4 1.6 %collective-permute-start.19 = (bf16[32,2048]{1,0:T(8,128)(2,1)S(1)}, bf16[32,2048]{1,0:T(8,128)(2,1)S(1)}, u32[]{:S(2)}, u32[]{:S(2)}) collective-permute-start(bf16[32,2048]{1,0:T(8,128)(2,1)S(1)} %get-tuple-element.56), channel_id=1, source_target_pairs={{0,16},{4,20},{8,24},{12,28},{16,0},{20,4},{24,8},{28,12},{1,17},{... | collective-permute-start | bytes 393224 | tf_op jit(solution)/shard_map/ppermute | solution.py:34
  94.6 1.8 %collective-permute-start.32 = (bf16[32,512]{1,0:T(8,128)(2,1)S(1)}, bf16[32,512]{1,0:T(8,128)(2,1)S(1)}, u32[]{:S(2)}, u32[]{:S(2)}) collective-permute-start(bf16[32,512]{1,0:T(8,128)(2,1)S(1)} %get-tuple-element.72), channel_id=1, source_target_pairs={{0,3},{1,2},{2,1},{3,0},{4,7},{5,6},{6,5},{7,4},{8,11},{9,10},{10,... | collective-permute-start | bytes 98312 | tf_op jit(solution)/shard_map/ppermute | solution.py:34
  96.4 3.2 %collective-permute-start.31 = (bf16[32,512]{1,0:T(8,128)(2,1)S(1)}, bf16[32,512]{1,0:T(8,128)(2,1)S(1)}, u32[]{:S(2)}, u32[]{:S(2)}) collective-permute-start(bf16[32,512]{1,0:T(8,128)(2,1)S(1)} %get-tuple-element.73), channel_id=1, source_target_pairs={{0,2},{1,3},{2,0},{3,1},{4,6},{5,7},{6,4},{7,5},{8,10},{9,11},{10,... | collective-permute-start | bytes 98312 | tf_op jit(solution)/shard_map/ppermute | solution.py:34
  99.7 1.4 %collective-permute-start.30 = (bf16[32,512]{1,0:T(8,128)(2,1)S(1)}, bf16[32,512]{1,0:T(8,128)(2,1)S(1)}, u32[]{:S(2)}, u32[]{:S(2)}) collective-permute-start(bf16[32,512]{1,0:T(8,128)(2,1)S(1)} %get-tuple-element.71), channel_id=1, source_target_pairs={{0,1},{1,0},{2,3},{3,2},{4,5},{5,4},{6,7},{7,6},{8,9},{9,8},{10,11... | collective-permute-start | bytes 98312 | tf_op jit(solution)/shard_map/ppermute | solution.py:34
  101.2 1.5 %collective-permute-start.23 = (bf16[32,512]{1,0:T(8,128)(2,1)S(1)}, bf16[32,512]{1,0:T(8,128)(2,1)S(1)}, u32[]{:S(2)}, u32[]{:S(2)}) collective-permute-start(bf16[32,512]{1,0:T(8,128)(2,1)S(1)} %get-tuple-element.69), channel_id=1, source_target_pairs={{0,3},{1,2},{2,1},{3,0},{4,7},{5,6},{6,5},{7,4},{8,11},{9,10},{10,... | collective-permute-start | bytes 98312 | tf_op jit(solution)/shard_map/ppermute | solution.py:34
  103.9 1.7 %collective-permute-start.21 = (bf16[32,512]{1,0:T(8,128)(2,1)S(1)}, bf16[32,512]{1,0:T(8,128)(2,1)S(1)}, u32[]{:S(2)}, u32[]{:S(2)}) collective-permute-start(bf16[32,512]{1,0:T(8,128)(2,1)S(1)} %get-tuple-element.68), channel_id=1, source_target_pairs={{0,1},{1,0},{2,3},{3,2},{4,5},{5,4},{6,7},{7,6},{8,9},{9,8},{10,11... | collective-permute-start | bytes 98312 | tf_op jit(solution)/shard_map/ppermute | solution.py:34
  (65 shorter events, 18.2 us)
Async XLA Ops:
  3.4 42.5 %all-to-all-start = ((bf16[4,320,512]{2,1,0:T(8,128)(2,1)}), bf16[4,320,512]{2,1,0:T(8,128)(2,1)S(1)}, u32[]{:S(2)}, u32[]{:S(2)}) async-start(bf16[4,320,512]{2,1,0:T(8,128)(2,1)} %bundle.1), calls=%async_computation | async-start | bytes 2621440 | tf_op jit(solution)/shard_map/all_to_all | solution.py:391
  9.7 24.2 %collective-permute-start.1 = (bf16[1024,512]{1,0:T(8,128)(2,1)S(1)}, bf16[1024,512]{1,0:T(8,128)(2,1)S(1)}, u32[]{:S(2)}, u32[]{:S(2)}) collective-permute-start(bf16[1024,512]{1,0:T(8,128)(2,1)S(1)} %copy-done), channel_id=1, source_target_pairs={{0,4},{4,0},{8,12},{12,8},{16,20},{20,16},{24,28},{28,24},{1,5},{5... | collective-permute-start | bytes 3145736 | tf_op jit(solution)/shard_map/ppermute | solution.py:34
  30.4 6.4 %collective-permute-start.2 = (bf16[64,1024]{1,0:T(8,128)(2,1)}, bf16[64,1024]{1,0:T(8,128)(2,1)}, u32[]{:S(2)}, u32[]{:S(2)}) collective-permute-start(bf16[64,1024]{1,0:T(8,128)(2,1)} %get-tuple-element.31), channel_id=1, source_target_pairs={{0,8},{4,12},{8,0},{12,4},{16,24},{20,28},{24,16},{28,20},{1,9},{5... | collective-permute-start | bytes 393224 | tf_op jit(solution)/shard_map/ppermute | solution.py:34
  31.9 8.6 %collective-permute-start.3 = (bf16[64,1024]{1,0:T(8,128)(2,1)}, bf16[64,1024]{1,0:T(8,128)(2,1)}, u32[]{:S(2)}, u32[]{:S(2)}) collective-permute-start(bf16[64,1024]{1,0:T(8,128)(2,1)} %get-tuple-element.32), channel_id=1, source_target_pairs={{0,16},{4,20},{8,24},{12,28},{16,0},{20,4},{24,8},{28,12},{1,17},{... | collective-permute-start | bytes 393224 | tf_op jit(solution)/shard_map/ppermute | solution.py:34
  33.4 7.1 %collective-permute-start.4 = (bf16[64,1024]{1,0:T(8,128)(2,1)}, bf16[64,1024]{1,0:T(8,128)(2,1)}, u32[]{:S(2)}, u32[]{:S(2)}) collective-permute-start(bf16[64,1024]{1,0:T(8,128)(2,1)} %get-tuple-element.33), channel_id=1, source_target_pairs={{0,24},{4,28},{8,16},{12,20},{16,8},{20,12},{24,0},{28,4},{1,25},{... | collective-permute-start | bytes 393224 | tf_op jit(solution)/shard_map/ppermute | solution.py:34
  45.9 10.9 %collective-permute-start.8 = (bf16[4,320,512]{2,1,0:T(8,128)(2,1)S(1)}, bf16[4,320,512]{2,1,0:T(8,128)(2,1)S(1)}, u32[]{:S(2)}, u32[]{:S(2)}) collective-permute-start(bf16[4,320,512]{2,1,0:T(8,128)(2,1)S(1)} %all-to-all-done.refs_4_.refs_5_), channel_id=1, source_target_pairs={{0,4},{4,0},{8,12},{12,8},{16,20},{20,16},{24,28},{28,24},{1,5},{5... | collective-permute-start | bytes 3932168 | tf_op jit(solution)/shard_map/ppermute | solution.py:34
  45.9 5.0 %collective-permute-start.5 = (bf16[64,512]{1,0:T(8,128)(2,1)}, bf16[64,512]{1,0:T(8,128)(2,1)S(1)}, u32[]{:S(2)}, u32[]{:S(2)}) collective-permute-start(bf16[64,512]{1,0:T(8,128)(2,1)} %get-tuple-element.36), channel_id=1, source_target_pairs={{0,1},{1,0},{2,3},{3,2},{4,5},{5,4},{6,7},{7,6},{8,9},{9,8},{10,11... | collective-permute-start | bytes 196616 | tf_op jit(solution)/shard_map/ppermute | solution.py:34
  48.0 7.9 %collective-permute-start.6 = (bf16[64,512]{1,0:T(8,128)(2,1)}, bf16[64,512]{1,0:T(8,128)(2,1)S(1)}, u32[]{:S(2)}, u32[]{:S(2)}) collective-permute-start(bf16[64,512]{1,0:T(8,128)(2,1)} %get-tuple-element.37), channel_id=1, source_target_pairs={{0,2},{1,3},{2,0},{3,1},{4,6},{5,7},{6,4},{7,5},{8,10},{9,11},{10,... | collective-permute-start | bytes 196616 | tf_op jit(solution)/shard_map/ppermute | solution.py:34
  50.4 6.3 %collective-permute-start.7 = (bf16[64,512]{1,0:T(8,128)(2,1)}, bf16[64,512]{1,0:T(8,128)(2,1)S(1)}, u32[]{:S(2)}, u32[]{:S(2)}) collective-permute-start(bf16[64,512]{1,0:T(8,128)(2,1)} %get-tuple-element.38), channel_id=1, source_target_pairs={{0,3},{1,2},{2,1},{3,0},{4,7},{5,6},{6,5},{7,4},{8,11},{9,10},{10,... | collective-permute-start | bytes 196616 | tf_op jit(solution)/shard_map/ppermute | solution.py:34
  57.6 5.7 %collective-permute-start.9 = (bf16[64,512]{1,0:T(8,128)(2,1)S(1)}, bf16[64,512]{1,0:T(8,128)(2,1)S(1)}, u32[]{:S(2)}, u32[]{:S(2)}) collective-permute-start(bf16[64,512]{1,0:T(8,128)(2,1)S(1)} %fusion.12.refs_0_), channel_id=1, source_target_pairs={{0,8},{4,12},{8,0},{12,4},{16,24},{20,28},{24,16},{28,20},{1,9},{5... | collective-permute-start | bytes 196616 | tf_op jit(solution)/shard_map/ppermute | solution.py:34
  58.9 5.8 %collective-permute-start.10 = (bf16[64,512]{1,0:T(8,128)(2,1)S(1)}, bf16[64,512]{1,0:T(8,128)(2,1)S(1)}, u32[]{:S(2)}, u32[]{:S(2)}) collective-permute-start(bf16[64,512]{1,0:T(8,128)(2,1)S(1)} %fusion.12.refs_0_), channel_id=1, source_target_pairs={{0,16},{4,20},{8,24},{12,28},{16,0},{20,4},{24,8},{28,12},{1,17},{... | collective-permute-start | bytes 196616 | tf_op jit(solution)/shard_map/ppermute | solution.py:34
  59.8 5.9 %collective-permute-start.11 = (bf16[64,512]{1,0:T(8,128)(2,1)S(1)}, bf16[64,512]{1,0:T(8,128)(2,1)S(1)}, u32[]{:S(2)}, u32[]{:S(2)}) collective-permute-start(bf16[64,512]{1,0:T(8,128)(2,1)S(1)} %fusion.12.refs_0_), channel_id=1, source_target_pairs={{0,24},{4,28},{8,16},{12,20},{16,8},{20,12},{24,0},{28,4},{1,25},{... | collective-permute-start | bytes 196616 | tf_op jit(solution)/shard_map/ppermute | solution.py:34
  61.2 9.8 %collective-permute-start.15 = (bf16[4,64,512]{2,1,0:T(8,128)(2,1)S(1)}, bf16[4,64,512]{2,1,0:T(8,128)(2,1)S(1)}, u32[]{:S(2)}, u32[]{:S(2)}) collective-permute-start(bf16[4,64,512]{2,1,0:T(8,128)(2,1)S(1)} %slice.85.refs_0_), channel_id=1, source_target_pairs={{0,8},{4,12},{8,0},{12,4},{16,24},{20,28},{24,16},{28,20},{1,9},{5... | collective-permute-start | bytes 786440 | tf_op jit(solution)/shard_map/ppermute | solution.py:34
  62.5 12.6 %collective-permute-start.16 = (bf16[4,64,512]{2,1,0:T(8,128)(2,1)S(1)}, bf16[4,64,512]{2,1,0:T(8,128)(2,1)S(1)}, u32[]{:S(2)}, u32[]{:S(2)}) collective-permute-start(bf16[4,64,512]{2,1,0:T(8,128)(2,1)S(1)} %slice.85.refs_0_), channel_id=1, source_target_pairs={{0,16},{4,20},{8,24},{12,28},{16,0},{20,4},{24,8},{28,12},{1,17},{... | collective-permute-start | bytes 786440 | tf_op jit(solution)/shard_map/ppermute | solution.py:34
  63.3 11.8 %collective-permute-start.17 = (bf16[4,64,512]{2,1,0:T(8,128)(2,1)S(1)}, bf16[4,64,512]{2,1,0:T(8,128)(2,1)S(1)}, u32[]{:S(2)}, u32[]{:S(2)}) collective-permute-start(bf16[4,64,512]{2,1,0:T(8,128)(2,1)S(1)} %slice.85.refs_0_), channel_id=1, source_target_pairs={{0,24},{4,28},{8,16},{12,20},{16,8},{20,12},{24,0},{28,4},{1,25},{... | collective-permute-start | bytes 786440 | tf_op jit(solution)/shard_map/ppermute | solution.py:34
  67.1 11.5 %collective-permute-start.24 = (bf16[128,512]{1,0:T(8,128)(2,1)S(1)}, bf16[128,512]{1,0:T(8,128)(2,1)S(1)}, u32[]{:S(2)}, u32[]{:S(2)}) collective-permute-start(bf16[128,512]{1,0:T(8,128)(2,1)S(1)} %get-tuple-element.66), channel_id=1, source_target_pairs={{0,1},{1,0},{2,3},{3,2},{4,5},{5,4},{6,7},{7,6},{8,9},{9,8},{10,11... | collective-permute-start | bytes 393224 | tf_op jit(solution)/shard_map/ppermute | solution.py:34
  68.5 12.1 %collective-permute-start.25 = (bf16[128,512]{1,0:T(8,128)(2,1)S(1)}, bf16[128,512]{1,0:T(8,128)(2,1)S(1)}, u32[]{:S(2)}, u32[]{:S(2)}) collective-permute-start(bf16[128,512]{1,0:T(8,128)(2,1)S(1)} %get-tuple-element.65), channel_id=1, source_target_pairs={{0,2},{1,3},{2,0},{3,1},{4,6},{5,7},{6,4},{7,5},{8,10},{9,11},{10,... | collective-permute-start | bytes 393224 | tf_op jit(solution)/shard_map/ppermute | solution.py:34
  71.0 9.6 %collective-permute-start.26 = (bf16[128,512]{1,0:T(8,128)(2,1)S(1)}, bf16[128,512]{1,0:T(8,128)(2,1)S(1)}, u32[]{:S(2)}, u32[]{:S(2)}) collective-permute-start(bf16[128,512]{1,0:T(8,128)(2,1)S(1)} %get-tuple-element.64), channel_id=1, source_target_pairs={{0,3},{1,2},{2,1},{3,0},{4,7},{5,6},{6,5},{7,4},{8,11},{9,10},{10,... | collective-permute-start | bytes 393224 | tf_op jit(solution)/shard_map/ppermute | solution.py:34
  76.0 8.5 %collective-permute-start.12 = (bf16[128,512]{1,0:T(8,128)(2,1)S(1)}, bf16[128,512]{1,0:T(8,128)(2,1)S(1)}, u32[]{:S(2)}, u32[]{:S(2)}) collective-permute-start(bf16[128,512]{1,0:T(8,128)(2,1)S(1)} %get-tuple-element.59), channel_id=1, source_target_pairs={{0,1},{1,0},{2,3},{3,2},{4,5},{5,4},{6,7},{7,6},{8,9},{9,8},{10,11... | collective-permute-start | bytes 393224 | tf_op jit(solution)/shard_map/ppermute | solution.py:34
  78.0 11.8 %collective-permute-start.13 = (bf16[128,512]{1,0:T(8,128)(2,1)S(1)}, bf16[128,512]{1,0:T(8,128)(2,1)S(1)}, u32[]{:S(2)}, u32[]{:S(2)}) collective-permute-start(bf16[128,512]{1,0:T(8,128)(2,1)S(1)} %get-tuple-element.58), channel_id=1, source_target_pairs={{0,2},{1,3},{2,0},{3,1},{4,6},{5,7},{6,4},{7,5},{8,10},{9,11},{10,... | collective-permute-start | bytes 393224 | tf_op jit(solution)/shard_map/ppermute | solution.py:34
  78.6 11.3 %collective-permute-start.14 = (bf16[128,512]{1,0:T(8,128)(2,1)S(1)}, bf16[128,512]{1,0:T(8,128)(2,1)S(1)}, u32[]{:S(2)}, u32[]{:S(2)}) collective-permute-start(bf16[128,512]{1,0:T(8,128)(2,1)S(1)} %get-tuple-element.57), channel_id=1, source_target_pairs={{0,3},{1,2},{2,1},{3,0},{4,7},{5,6},{6,5},{7,4},{8,11},{9,10},{10,... | collective-permute-start | bytes 393224 | tf_op jit(solution)/shard_map/ppermute | solution.py:34
  81.7 12.3 %collective-permute-start.29 = (bf16[32,2048]{1,0:T(8,128)(2,1)S(1)}, bf16[32,2048]{1,0:T(8,128)(2,1)S(1)}, u32[]{:S(2)}, u32[]{:S(2)}) collective-permute-start(bf16[32,2048]{1,0:T(8,128)(2,1)S(1)} %get-tuple-element.62), channel_id=1, source_target_pairs={{0,24},{4,28},{8,16},{12,20},{16,8},{20,12},{24,0},{28,4},{1,25},{... | collective-permute-start | bytes 393224 | tf_op jit(solution)/shard_map/ppermute | solution.py:34
  83.5 11.0 %collective-permute-start.28 = (bf16[32,2048]{1,0:T(8,128)(2,1)S(1)}, bf16[32,2048]{1,0:T(8,128)(2,1)S(1)}, u32[]{:S(2)}, u32[]{:S(2)}) collective-permute-start(bf16[32,2048]{1,0:T(8,128)(2,1)S(1)} %get-tuple-element.63), channel_id=1, source_target_pairs={{0,16},{4,20},{8,24},{12,28},{16,0},{20,4},{24,8},{28,12},{1,17},{... | collective-permute-start | bytes 393224 | tf_op jit(solution)/shard_map/ppermute | solution.py:34
  84.5 10.0 %collective-permute-start.27 = (bf16[32,2048]{1,0:T(8,128)(2,1)S(1)}, bf16[32,2048]{1,0:T(8,128)(2,1)S(1)}, u32[]{:S(2)}, u32[]{:S(2)}) collective-permute-start(bf16[32,2048]{1,0:T(8,128)(2,1)S(1)} %get-tuple-element.61), channel_id=1, source_target_pairs={{0,8},{4,12},{8,0},{12,4},{16,24},{20,28},{24,16},{28,20},{1,9},{5... | collective-permute-start | bytes 393224 | tf_op jit(solution)/shard_map/ppermute | solution.py:34
  90.9 8.7 %collective-permute-start.20 = (bf16[32,2048]{1,0:T(8,128)(2,1)S(1)}, bf16[32,2048]{1,0:T(8,128)(2,1)S(1)}, u32[]{:S(2)}, u32[]{:S(2)}) collective-permute-start(bf16[32,2048]{1,0:T(8,128)(2,1)S(1)} %get-tuple-element.55), channel_id=1, source_target_pairs={{0,24},{4,28},{8,16},{12,20},{16,8},{20,12},{24,0},{28,4},{1,25},{... | collective-permute-start | bytes 393224 | tf_op jit(solution)/shard_map/ppermute | solution.py:34
  92.4 8.6 %collective-permute-start.19 = (bf16[32,2048]{1,0:T(8,128)(2,1)S(1)}, bf16[32,2048]{1,0:T(8,128)(2,1)S(1)}, u32[]{:S(2)}, u32[]{:S(2)}) collective-permute-start(bf16[32,2048]{1,0:T(8,128)(2,1)S(1)} %get-tuple-element.56), channel_id=1, source_target_pairs={{0,16},{4,20},{8,24},{12,28},{16,0},{20,4},{24,8},{28,12},{1,17},{... | collective-permute-start | bytes 393224 | tf_op jit(solution)/shard_map/ppermute | solution.py:34
  94.0 7.1 %collective-permute-start.18 = (bf16[32,2048]{1,0:T(8,128)(2,1)S(1)}, bf16[32,2048]{1,0:T(8,128)(2,1)S(1)}, u32[]{:S(2)}, u32[]{:S(2)}) collective-permute-start(bf16[32,2048]{1,0:T(8,128)(2,1)S(1)} %get-tuple-element.54), channel_id=1, source_target_pairs={{0,8},{4,12},{8,0},{12,4},{16,24},{20,28},{24,16},{28,20},{1,9},{5... | collective-permute-start | bytes 393224 | tf_op jit(solution)/shard_map/ppermute | solution.py:34
  94.6 9.4 %collective-permute-start.32 = (bf16[32,512]{1,0:T(8,128)(2,1)S(1)}, bf16[32,512]{1,0:T(8,128)(2,1)S(1)}, u32[]{:S(2)}, u32[]{:S(2)}) collective-permute-start(bf16[32,512]{1,0:T(8,128)(2,1)S(1)} %get-tuple-element.72), channel_id=1, source_target_pairs={{0,3},{1,2},{2,1},{3,0},{4,7},{5,6},{6,5},{7,4},{8,11},{9,10},{10,... | collective-permute-start | bytes 98312 | tf_op jit(solution)/shard_map/ppermute | solution.py:34
  96.4 9.2 %collective-permute-start.31 = (bf16[32,512]{1,0:T(8,128)(2,1)S(1)}, bf16[32,512]{1,0:T(8,128)(2,1)S(1)}, u32[]{:S(2)}, u32[]{:S(2)}) collective-permute-start(bf16[32,512]{1,0:T(8,128)(2,1)S(1)} %get-tuple-element.73), channel_id=1, source_target_pairs={{0,2},{1,3},{2,0},{3,1},{4,6},{5,7},{6,4},{7,5},{8,10},{9,11},{10,... | collective-permute-start | bytes 98312 | tf_op jit(solution)/shard_map/ppermute | solution.py:34
  99.7 6.0 %collective-permute-start.30 = (bf16[32,512]{1,0:T(8,128)(2,1)S(1)}, bf16[32,512]{1,0:T(8,128)(2,1)S(1)}, u32[]{:S(2)}, u32[]{:S(2)}) collective-permute-start(bf16[32,512]{1,0:T(8,128)(2,1)S(1)} %get-tuple-element.71), channel_id=1, source_target_pairs={{0,1},{1,0},{2,3},{3,2},{4,5},{5,4},{6,7},{7,6},{8,9},{9,8},{10,11... | collective-permute-start | bytes 98312 | tf_op jit(solution)/shard_map/ppermute | solution.py:34
  101.2 5.8 %collective-permute-start.23 = (bf16[32,512]{1,0:T(8,128)(2,1)S(1)}, bf16[32,512]{1,0:T(8,128)(2,1)S(1)}, u32[]{:S(2)}, u32[]{:S(2)}) collective-permute-start(bf16[32,512]{1,0:T(8,128)(2,1)S(1)} %get-tuple-element.69), channel_id=1, source_target_pairs={{0,3},{1,2},{2,1},{3,0},{4,7},{5,6},{6,5},{7,4},{8,11},{9,10},{10,... | collective-permute-start | bytes 98312 | tf_op jit(solution)/shard_map/ppermute | solution.py:34
  102.7 4.8 %collective-permute-start.22 = (bf16[32,512]{1,0:T(8,128)(2,1)S(1)}, bf16[32,512]{1,0:T(8,128)(2,1)S(1)}, u32[]{:S(2)}, u32[]{:S(2)}) collective-permute-start(bf16[32,512]{1,0:T(8,128)(2,1)S(1)} %get-tuple-element.70), channel_id=1, source_target_pairs={{0,2},{1,3},{2,0},{3,1},{4,6},{5,7},{6,4},{7,5},{8,10},{9,11},{10,... | collective-permute-start | bytes 98312 | tf_op jit(solution)/shard_map/ppermute | solution.py:34
  (4 other events, 32.2 us)

commit v4 on v3

--- a/solution.py
+++ b/solution.py
@@ -116,7 +116,7 @@
     token_spec = pl.BlockSpec((block, HD), lambda h, b, place: (b, h + first))
     global_spec = pl.BlockSpec((glob, HD), lambda h, b, place: (0, h + first))
     part_spec = pl.BlockSpec((size // 2, glob // size, 2 * HD), lambda h, b, place: (0, 0, h))
-    part = pltpu.HBM((size // 2, glob // size, 2 * HD * count), BF16)
+    part = pltpu.VMEM((size // 2, glob // size, 2 * HD * count), BF16)
     extra = [x for x in (query_grad, *after) if x is not None]
     return pl.pallas_call(
         functools.partial(attend_kernel, min(256, block)),
@@ -194,66 +194,64 @@
         functools.partial(merge_kernel, len(evens)),
         in_specs=[spec(x) for x in (*evens, *gots)]
         + [pl.BlockSpec(memory_space=pltpu.VMEM)] * len(near),
-        out_shape=[jax.ShapeDtypeStruct((rows, width), BF16)] * blocks,
+        out_shape=[pltpu.VMEM((rows, width), BF16)] * blocks,
         compiler_params=pltpu.CompilerParams(vmem_limit_bytes=VMEM_BYTES),
         cost_estimate=pl.CostEstimate(
             flops=blocks * rows * width, bytes_accessed=6 * blocks * rows * width, transcendentals=0
         ),
         name="merge",
-    )(*map(hold, evens), *gots, *near)
+    )(*evens, *gots, *near)
     return scatter_terms(mine, "seq", 2)
 
 
+def prepare_kernel(*refs):
+    half = len(refs) // 2
+    for from_ref, to_ref in zip(refs[:half], refs[half:]):
+        to_ref[...] = from_ref[...]
+
+
+def prepare(arrays, after):
+    count = len(arrays)
+    return pl.pallas_call(
+        lambda *refs: prepare_kernel(*refs[:count], *refs[count + len(after) :]),
+        grid=(4,),
+        in_specs=[pl.BlockSpec((x.shape[0] // 4, x.shape[1]), lambda i: (i, 0)) for x in arrays]
+        + [pl.BlockSpec(memory_space=pl.ANY)] * len(after),
+        out_specs=[pl.BlockSpec((x.shape[0] // 4, x.shape[1]), lambda i: (i, 0)) for x in arrays],
+        out_shape=[pltpu.VMEM(x.shape, x.dtype) for x in arrays],
+        compiler_params=pltpu.CompilerParams(vmem_limit_bytes=VMEM_BYTES),
+        cost_estimate=pl.CostEstimate(
+            flops=0, bytes_accessed=4 * sum(x.size for x in arrays), transcendentals=0
+        ),
+        name="prepare",
+    )(*map(hold, arrays), *after)
+
+
 def project_kernel(count, chunk_ref, *refs):
-    terms, sources = refs[:count], refs[count : count + 2]
-    part_refs, (term_ref, held_ref, term_sems, sems) = refs[count + 2 : -4], refs[-4:]
-    size, block = len(part_refs), part_refs[0].shape[1]
-
-    def fetch(k, i):
+    terms, (key_proj_ref, value_proj_ref) = refs[:count], refs[count : count + 2]
+    part_refs = refs[count + 2 :]
+    total = sum(t[...].astype(F32) for t in terms).astype(BF16)
+    heads = total.shape[1] // (2 * HD)
+    pick = lambda at: [total[:, (2 * h + at) * HD : (2 * h + at + 1) * HD] for h in range(heads)]
+    key_low, value_low = jnp.concatenate(pick(0), 1), jnp.concatenate(pick(1), 1)
+    block = part_refs[0].shape[1]
+    for k, part_ref in enumerate(part_refs):
         at = pl.ds(pl.multiple_of(chunk_ref[k] * block, block), block)
-        return pltpu.make_async_copy(sources[i].at[at, :], held_ref.at[k, i], sems.at[k, i])
-
-    given = [pltpu.make_async_copy(t, term_ref.at[j], term_sems.at[j]) for j, t in enumerate(terms)]
-    for copy in given:
-        copy.start()
-    for k in range(size):
-        for i in range(2):
-            fetch(k, i).start()
-    for copy in given:
-        copy.wait()
-    total = sum(term_ref[j].astype(F32) for j in range(count)).astype(BF16)
-    heads = total.shape[1] // (2 * HD)
-    low = [
-        jnp.concatenate([total[:, (2 * h + i) * HD : (2 * h + i + 1) * HD] for h in range(heads)], 1)
-        for i in range(2)
-    ]
-    for k, part_ref in enumerate(part_refs):
-        part = None
-        for i in range(2):
-            fetch(k, i).wait()
-            term = dot(low[i], held_ref[k, i], NT)
-            part = term if part is None else part + term
-        part_ref[...] = part.astype(BF16)
+        part = dot(key_proj_ref[at, :], key_low, NT) + dot(value_proj_ref[at, :], value_low, NT)
+        part_ref[...] = part.T.astype(BF16)
 
 
 def project(chunk, terms, key_proj, value_proj):
     rows, width = terms[0].shape
     size = chunk.shape[0]
     block = key_proj.shape[0] // size
-    count = len(terms)
     part = pltpu.HBM((rows, block), BF16)
     return pl.pallas_call(
-        functools.partial(project_kernel, count),
+        functools.partial(project_kernel, len(terms)),
         in_specs=[pl.BlockSpec(memory_space=pltpu.SMEM)]
-        + [pl.BlockSpec(memory_space=pl.ANY)] * (count + 2),
+        + [pl.BlockSpec(memory_space=pltpu.VMEM)] * (len(terms) + 2),
         out_specs=[pl.BlockSpec((rows, block), lambda: (0, 0))] * size,
         out_shape=[part] * size,
-        scratch_shapes=[
-            pltpu.VMEM((count, rows, width), BF16),
-            pltpu.VMEM((size, 2, block, width // 2), BF16),
-            pltpu.SemaphoreType.DMA((count,)),
-            pltpu.SemaphoreType.DMA((size, 2)),
-        ],
         compiler_params=pltpu.CompilerParams(vmem_limit_bytes=VMEM_BYTES),
         cost_estimate=pl.CostEstimate(
             flops=2 * rows * width * block * size,
@@ -261,7 +259,7 @@
             transcendentals=0,
         ),
         name="project",
-    )(chunk, *terms, hold(key_proj), hold(value_proj))
+    )(chunk, *terms, key_proj, value_proj)
 
 
 def pieces_of(blocks, cuts):
@@ -395,7 +393,8 @@
     query_grad, even, odd = attend(place, *arrays, 0, heads)
     terms = scatter_rows([even], [odd], [])
     terms[0], downs[1] = lax.optimization_barrier((terms[0], downs[1]))
-    share = list(project(chunk, terms, key_proj, value_proj))
+    near = prepare([value_proj], terms[:1])
+    share = list(project(chunk, terms, key_proj, *near))
     own_up, share[0] = lax.optimization_barrier((own_up, share[0]))
     ups = [own_up, swap(own_up, "seq", 1)]
     shares = [share[0]] + [swap(share[k], "heads", k) for k in range(1, planes)]

time: 109 us -> 105 us (0.963)
  waiting for transfers between devices: 25 us -> 22.3 us
    ppermute x33, waiting for transfers between devices: 25 us -> 22.3 us  [swap(): return lax.ppermute(x, axis, [(i, i ^ distance) for i in range(size)])]
    pallas_call x1 -> x2, Pallas kernels: 5.35 us -> 5.52 us  [the longest x1 3 us: project(): pl.pallas_call(functools.partial(project_kernel, len(terms)), in_specs=[p...]
  transfers between devices with their start and end apart: 34 -> 34, of which waited for: 13 -> 13; matrix products, arithmetic and copies ran while one was open for 0% -> 1% of each run, Pallas kernels for 26% -> 26%
where the time goes in v4:
time: 105 us
  starting transfers between devices  49.9 us (48%)
  Pallas kernels  29.7 us (28%)
  waiting for transfers between devices  22.3 us (21%)
  other arithmetic  1.95 us (2%)
    ppermute x33, starting transfers between devices, swap(): return lax.ppermute(x, axis, [(i, i ^ distance) for i in range(size)])  43.6 us
    ppermute x33, waiting for transfers between devices, swap(): return lax.ppermute(x, axis, [(i, i ^ distance) for i in range(size)])  22.3 us
    pallas_call x1, Pallas kernels, attend(): pl.pallas_call(functools.partial(attend_kernel, min(256, block)), grid_sp...  16.7 us
    all_to_all x1, starting transfers between devices, local(): own_up = lax.all_to_all(bundle(up_proj, global_in, planes), 'heads', 0, 0)  6.32 us
    pallas_call x1, Pallas kernels, project(): pl.pallas_call(functools.partial(project_kernel, len(terms)), in_specs=[p...  3 us
    pallas_call x1, Pallas kernels, bundle(): pl.pallas_call(bundle_kernel, out_shape=jax.ShapeDtypeStruct((size, hidde...  2.74 us
    pallas_call x1, Pallas kernels, prepare(): pl.pallas_call(lambda *refs: prepare_kernel(*refs[:count], *refs[count +...  2.53 us
  transfers between devices with their start and end apart: 34, of which 13 were waited for; matrix products, arithmetic and copies ran while one was open for 1% of the time, Pallas kernels for 26%

profile of v4, /device:TPU:0, one launch (start us, length us, event | category | flops | bytes accessed | tf_op | source)
XLA Modules:
  0.0 104.9 jit_solution(2240335910504726353)
XLA Ops:
  0.6 2.7 %bundle.1 = bf16[4,320,512]{2,1,0:T(8,128)(2,1)} custom-call(bf16[512,1024]{1,0:T(8,128)(2,1)} %up_ref.1, bf16[64,512]{1,0:T(8,128)(2,1)} %in_ref.1), custom_call_target="tpu_custom_call" | custom-call | bytes 2097152 | tf_op jit(solution)/shard_map/bundle/pallas_call | solution.py:166
  3.4 6.3 %all-to-all-start = ((bf16[4,320,512]{2,1,0:T(8,128)(2,1)}), bf16[4,320,512]{2,1,0:T(8,128)(2,1)S(1)}, u32[]{:S(2)}, u32[]{:S(2)}) async-start(bf16[4,320,512]{2,1,0:T(8,128)(2,1)} %bundle.1), calls=%async_computation | async-start | bytes 2621440 | tf_op jit(solution)/shard_map/all_to_all | solution.py:389
  9.7 16.7 %attend.1 = (bf16[2048,512]{1,0:T(8,128)(2,1)}, bf16[4,64,1024]{2,1,0:T(8,128)(2,1)S(1)}, bf16[4,64,1024]{2,1,0:T(8,128)(2,1)S(1)}) custom-call(s32[8]{0:T(128)S(1)} %iota_xor_fusion.1.place_ref, bf16[2048,512]{1,0:T(8,128)(2,1)} %q_ref.1, bf16[2048,512]{1,0:T(8,128)(2,1)} %g_ref.1, bf16[512,512]{1,0:T(8,128)(2,1)} %k_ref.1, bf16[512,512]{1,0:T(8,128)(2,1)} %v_ref.1), custom_call_target="tpu_custom_call" | custom-call | flops 10737418240 | bytes 6291456 | tf_op jit(solution)/shard_map/attend/pallas_call | solution.py:121
  26.9 1.5 %collective-permute-done.refs_1_ = bf16[4,64,1024]{2,1,0:T(8,128)(2,1)S(1)} collective-permute-done((bf16[4,64,1024]{2,1,0:T(8,128)(2,1)S(1)}, bf16[4,64,1024]{2,1,0:T(8,128)(2,1)S(1)}, u32[]{:S(2)}, u32[]{:S(2)}) %collective-permute-start) | collective-permute-done | bytes 524320 | tf_op jit(solution)/shard_map/ppermute | solution.py:34
  29.2 1.5 %collective-permute-start.2 = (bf16[64,1024]{1,0:T(8,128)(2,1)}, bf16[64,1024]{1,0:T(8,128)(2,1)}, u32[]{:S(2)}, u32[]{:S(2)}) collective-permute-start(bf16[64,1024]{1,0:T(8,128)(2,1)} %get-tuple-element.31), channel_id=1, source_target_pairs={{0,8},{4,12},{8,0},{12,4},{16,24},{20,28},{24,16},{28,20},{1,9},{5... | collective-permute-start | bytes 393224 | tf_op jit(solution)/shard_map/ppermute | solution.py:34
  30.7 1.5 %collective-permute-start.3 = (bf16[64,1024]{1,0:T(8,128)(2,1)}, bf16[64,1024]{1,0:T(8,128)(2,1)}, u32[]{:S(2)}, u32[]{:S(2)}) collective-permute-start(bf16[64,1024]{1,0:T(8,128)(2,1)} %get-tuple-element.32), channel_id=1, source_target_pairs={{0,16},{4,20},{8,24},{12,28},{16,0},{20,4},{24,8},{28,12},{1,17},{... | collective-permute-start | bytes 393224 | tf_op jit(solution)/shard_map/ppermute | solution.py:34
  32.7 2.5 %prepare.1.refs_5_ = bf16[2048,512]{1,0:T(8,128)(2,1)S(1)} custom-call(bf16[2048,512]{1,0:T(8,128)(2,1)} %refs_0_.1, bf16[64,1024]{1,0:T(8,128)(2,1)S(1)} %get-tuple-element.30.refs_1_.refs_0_), custom_call_target="tpu_custom_call" | custom-call | bytes 4194304 | tf_op jit(solution)/shard_map/prepare/pallas_call | solution.py:215
  35.6 3.7 %collective-permute-done.3.refs_2_ = bf16[64,1024]{1,0:T(8,128)(2,1)} collective-permute-done((bf16[64,1024]{1,0:T(8,128)(2,1)}, bf16[64,1024]{1,0:T(8,128)(2,1)}, u32[]{:S(2)}, u32[]{:S(2)}) %collective-permute-start.3) | collective-permute-done | bytes 131104 | tf_op jit(solution)/shard_map/ppermute | solution.py:34
  39.3 3.0 %project.1 = (bf16[64,512]{1,0:T(8,128)(2,1)}, bf16[64,512]{1,0:T(8,128)(2,1)}, bf16[64,512]{1,0:T(8,128)(2,1)}, bf16[64,512]{1,0:T(8,128)(2,1)}) custom-call(s32[4]{0:T(128)S(1)} %iota_xor_fusion.chunk_ref, bf16[64,1024]{1,0:T(8,128)(2,1)S(1)} %get-tuple-element.30.refs_1_.refs_0_, bf16[64,1024]{1,0:T(8,128)(2,1)} %collective-permute-done.2.refs_1_, ...), custom_call_target="tpu_custom_call" | custom-call | flops 268435456 | bytes 4194304 | tf_op jit(solution)/shard_map/project/pallas_call | solution.py:249
  42.3 2.1 %collective-permute-start.5 = (bf16[64,512]{1,0:T(8,128)(2,1)}, bf16[64,512]{1,0:T(8,128)(2,1)S(1)}, u32[]{:S(2)}, u32[]{:S(2)}) collective-permute-start(bf16[64,512]{1,0:T(8,128)(2,1)} %get-tuple-element.36), channel_id=1, source_target_pairs={{0,1},{1,0},{2,3},{3,2},{4,5},{5,4},{6,7},{7,6},{8,9},{9,8},{10,11... | collective-permute-start | bytes 196616 | tf_op jit(solution)/shard_map/ppermute | solution.py:34
  44.4 2.4 %collective-permute-start.6 = (bf16[64,512]{1,0:T(8,128)(2,1)}, bf16[64,512]{1,0:T(8,128)(2,1)S(1)}, u32[]{:S(2)}, u32[]{:S(2)}) collective-permute-start(bf16[64,512]{1,0:T(8,128)(2,1)} %get-tuple-element.37), channel_id=1, source_target_pairs={{0,2},{1,3},{2,0},{3,1},{4,6},{5,7},{6,4},{7,5},{8,10},{9,11},{10,... | collective-permute-start | bytes 196616 | tf_op jit(solution)/shard_map/ppermute | solution.py:34
  47.3 5.0 %collective-permute-done.6 = bf16[64,512]{1,0:T(8,128)(2,1)S(1)} collective-permute-done((bf16[64,512]{1,0:T(8,128)(2,1)}, bf16[64,512]{1,0:T(8,128)(2,1)S(1)}, u32[]{:S(2)}, u32[]{:S(2)}) %collective-permute-start.6) | collective-permute-done | bytes 65568 | tf_op jit(solution)/shard_map/ppermute | solution.py:34
  56.1 1.4 %collective-permute-start.11 = (bf16[64,512]{1,0:T(8,128)(2,1)S(1)}, bf16[64,512]{1,0:T(8,128)(2,1)S(1)}, u32[]{:S(2)}, u32[]{:S(2)}) collective-permute-start(bf16[64,512]{1,0:T(8,128)(2,1)S(1)} %fusion.12.refs_0_), channel_id=1, source_target_pairs={{0,24},{4,28},{8,16},{12,20},{16,8},{20,12},{24,0},{28,4},{1,25},{... | collective-permute-start | bytes 196616 | tf_op jit(solution)/shard_map/ppermute | solution.py:34
  57.5 1.3 %collective-permute-start.15 = (bf16[4,64,512]{2,1,0:T(8,128)(2,1)S(1)}, bf16[4,64,512]{2,1,0:T(8,128)(2,1)S(1)}, u32[]{:S(2)}, u32[]{:S(2)}) collective-permute-start(bf16[4,64,512]{2,1,0:T(8,128)(2,1)S(1)} %slice.85.refs_0_), channel_id=1, source_target_pairs={{0,8},{4,12},{8,0},{12,4},{16,24},{20,28},{24,16},{28,20},{1,9},{5... | collective-permute-start | bytes 786440 | tf_op jit(solution)/shard_map/ppermute | solution.py:34
  59.7 1.4 %collective-permute-start.17 = (bf16[4,64,512]{2,1,0:T(8,128)(2,1)S(1)}, bf16[4,64,512]{2,1,0:T(8,128)(2,1)S(1)}, u32[]{:S(2)}, u32[]{:S(2)}) collective-permute-start(bf16[4,64,512]{2,1,0:T(8,128)(2,1)S(1)} %slice.85.refs_0_), channel_id=1, source_target_pairs={{0,24},{4,28},{8,16},{12,20},{16,8},{20,12},{24,0},{28,4},{1,25},{... | collective-permute-start | bytes 786440 | tf_op jit(solution)/shard_map/ppermute | solution.py:34
  62.0 1.3 %back.1 = (bf16[4,128,512]{2,1,0:T(8,128)(2,1)S(1)}, bf16[4,128,512]{2,1,0:T(8,128)(2,1)S(1)}) custom-call(s32[4]{0:T(128)S(1)} %iota_xor_fusion.chunk_ref, bf16[64,512]{1,0:T(8,128)(2,1)S(1)} %fusion.12.refs_0_, bf16[64,512]{1,0:T(8,128)(2,1)S(1)} %collective-permute-done.9.refs_1_, bf16[64,512]{1,0:T(8,128)(2,1)S(1)} %collective-permute-done.10.refs_2_, ...), custom_call_target="tpu_custom_call" | custom-call | flops 536870912 | bytes 2097152 | tf_op jit(solution)/shard_map/back/pallas_call | solution.py:298
  63.4 1.4 %collective-permute-start.24 = (bf16[128,512]{1,0:T(8,128)(2,1)S(1)}, bf16[128,512]{1,0:T(8,128)(2,1)S(1)}, u32[]{:S(2)}, u32[]{:S(2)}) collective-permute-start(bf16[128,512]{1,0:T(8,128)(2,1)S(1)} %get-tuple-element.66), channel_id=1, source_target_pairs={{0,1},{1,0},{2,3},{3,2},{4,5},{5,4},{6,7},{7,6},{8,9},{9,8},{10,11... | collective-permute-start | bytes 393224 | tf_op jit(solution)/shard_map/ppermute | solution.py:34
  64.8 1.6 %collective-permute-start.25 = (bf16[128,512]{1,0:T(8,128)(2,1)S(1)}, bf16[128,512]{1,0:T(8,128)(2,1)S(1)}, u32[]{:S(2)}, u32[]{:S(2)}) collective-permute-start(bf16[128,512]{1,0:T(8,128)(2,1)S(1)} %get-tuple-element.65), channel_id=1, source_target_pairs={{0,2},{1,3},{2,0},{3,1},{4,6},{5,7},{6,4},{7,5},{8,10},{9,11},{10,... | collective-permute-start | bytes 393224 | tf_op jit(solution)/shard_map/ppermute | solution.py:34
  67.4 2.3 %collective-permute-start.26 = (bf16[128,512]{1,0:T(8,128)(2,1)S(1)}, bf16[128,512]{1,0:T(8,128)(2,1)S(1)}, u32[]{:S(2)}, u32[]{:S(2)}) collective-permute-start(bf16[128,512]{1,0:T(8,128)(2,1)S(1)} %get-tuple-element.64), channel_id=1, source_target_pairs={{0,3},{1,2},{2,1},{3,0},{4,7},{5,6},{6,5},{7,4},{8,11},{9,10},{10,... | collective-permute-start | bytes 393224 | tf_op jit(solution)/shard_map/ppermute | solution.py:34
  69.7 1.8 %collective-permute-done.16.refs_2_ = bf16[4,64,512]{2,1,0:T(8,128)(2,1)S(1)} collective-permute-done((bf16[4,64,512]{2,1,0:T(8,128)(2,1)S(1)}, bf16[4,64,512]{2,1,0:T(8,128)(2,1)S(1)}, u32[]{:S(2)}, u32[]{:S(2)}) %collective-permute-start.16) | collective-permute-done | bytes 262176 | tf_op jit(solution)/shard_map/ppermute | solution.py:34
  72.3 2.0 %collective-permute-start.12 = (bf16[128,512]{1,0:T(8,128)(2,1)S(1)}, bf16[128,512]{1,0:T(8,128)(2,1)S(1)}, u32[]{:S(2)}, u32[]{:S(2)}) collective-permute-start(bf16[128,512]{1,0:T(8,128)(2,1)S(1)} %get-tuple-element.59), channel_id=1, source_target_pairs={{0,1},{1,0},{2,3},{3,2},{4,5},{5,4},{6,7},{7,6},{8,9},{9,8},{10,11... | collective-permute-start | bytes 393224 | tf_op jit(solution)/shard_map/ppermute | solution.py:34
  74.9 2.1 %collective-permute-start.14 = (bf16[128,512]{1,0:T(8,128)(2,1)S(1)}, bf16[128,512]{1,0:T(8,128)(2,1)S(1)}, u32[]{:S(2)}, u32[]{:S(2)}) collective-permute-start(bf16[128,512]{1,0:T(8,128)(2,1)S(1)} %get-tuple-element.57), channel_id=1, source_target_pairs={{0,3},{1,2},{2,1},{3,0},{4,7},{5,6},{6,5},{7,4},{8,11},{9,10},{10,... | collective-permute-start | bytes 393224 | tf_op jit(solution)/shard_map/ppermute | solution.py:34
  78.0 1.8 %collective-permute-start.29 = (bf16[32,2048]{1,0:T(8,128)(2,1)S(1)}, bf16[32,2048]{1,0:T(8,128)(2,1)S(1)}, u32[]{:S(2)}, u32[]{:S(2)}) collective-permute-start(bf16[32,2048]{1,0:T(8,128)(2,1)S(1)} %get-tuple-element.62), channel_id=1, source_target_pairs={{0,24},{4,28},{8,16},{12,20},{16,8},{20,12},{24,0},{28,4},{1,25},{... | collective-permute-start | bytes 393224 | tf_op jit(solution)/shard_map/ppermute | solution.py:34
  81.6 4.6 %collective-permute-done.13.refs_2_ = bf16[128,512]{1,0:T(8,128)(2,1)S(1)} collective-permute-done((bf16[128,512]{1,0:T(8,128)(2,1)S(1)}, bf16[128,512]{1,0:T(8,128)(2,1)S(1)}, u32[]{:S(2)}, u32[]{:S(2)}) %collective-permute-start.13) | collective-permute-done | bytes 131104 | tf_op jit(solution)/shard_map/ppermute | solution.py:34
  87.3 1.5 %collective-permute-start.20 = (bf16[32,2048]{1,0:T(8,128)(2,1)S(1)}, bf16[32,2048]{1,0:T(8,128)(2,1)S(1)}, u32[]{:S(2)}, u32[]{:S(2)}) collective-permute-start(bf16[32,2048]{1,0:T(8,128)(2,1)S(1)} %get-tuple-element.55), channel_id=1, source_target_pairs={{0,24},{4,28},{8,16},{12,20},{16,8},{20,12},{24,0},{28,4},{1,25},{... | collective-permute-start | bytes 393224 | tf_op jit(solution)/shard_map/ppermute | solution.py:34
  88.8 1.6 %collective-permute-start.19 = (bf16[32,2048]{1,0:T(8,128)(2,1)S(1)}, bf16[32,2048]{1,0:T(8,128)(2,1)S(1)}, u32[]{:S(2)}, u32[]{:S(2)}) collective-permute-start(bf16[32,2048]{1,0:T(8,128)(2,1)S(1)} %get-tuple-element.56), channel_id=1, source_target_pairs={{0,16},{4,20},{8,24},{12,28},{16,0},{20,4},{24,8},{28,12},{1,17},{... | collective-permute-start | bytes 393224 | tf_op jit(solution)/shard_map/ppermute | solution.py:34
  90.9 1.8 %collective-permute-start.32 = (bf16[32,512]{1,0:T(8,128)(2,1)S(1)}, bf16[32,512]{1,0:T(8,128)(2,1)S(1)}, u32[]{:S(2)}, u32[]{:S(2)}) collective-permute-start(bf16[32,512]{1,0:T(8,128)(2,1)S(1)} %get-tuple-element.72), channel_id=1, source_target_pairs={{0,3},{1,2},{2,1},{3,0},{4,7},{5,6},{6,5},{7,4},{8,11},{9,10},{10,... | collective-permute-start | bytes 98312 | tf_op jit(solution)/shard_map/ppermute | solution.py:34
  92.8 3.2 %collective-permute-start.31 = (bf16[32,512]{1,0:T(8,128)(2,1)S(1)}, bf16[32,512]{1,0:T(8,128)(2,1)S(1)}, u32[]{:S(2)}, u32[]{:S(2)}) collective-permute-start(bf16[32,512]{1,0:T(8,128)(2,1)S(1)} %get-tuple-element.73), channel_id=1, source_target_pairs={{0,2},{1,3},{2,0},{3,1},{4,6},{5,7},{6,4},{7,5},{8,10},{9,11},{10,... | collective-permute-start | bytes 98312 | tf_op jit(solution)/shard_map/ppermute | solution.py:34
  96.0 1.4 %collective-permute-start.30 = (bf16[32,512]{1,0:T(8,128)(2,1)S(1)}, bf16[32,512]{1,0:T(8,128)(2,1)S(1)}, u32[]{:S(2)}, u32[]{:S(2)}) collective-permute-start(bf16[32,512]{1,0:T(8,128)(2,1)S(1)} %get-tuple-element.71), channel_id=1, source_target_pairs={{0,1},{1,0},{2,3},{3,2},{4,5},{5,4},{6,7},{7,6},{8,9},{9,8},{10,11... | collective-permute-start | bytes 98312 | tf_op jit(solution)/shard_map/ppermute | solution.py:34
  97.5 1.5 %collective-permute-start.23 = (bf16[32,512]{1,0:T(8,128)(2,1)S(1)}, bf16[32,512]{1,0:T(8,128)(2,1)S(1)}, u32[]{:S(2)}, u32[]{:S(2)}) collective-permute-start(bf16[32,512]{1,0:T(8,128)(2,1)S(1)} %get-tuple-element.69), channel_id=1, source_target_pairs={{0,3},{1,2},{2,1},{3,0},{4,7},{5,6},{6,5},{7,4},{8,11},{9,10},{10,... | collective-permute-start | bytes 98312 | tf_op jit(solution)/shard_map/ppermute | solution.py:34
  99.0 1.3 %collective-permute-start.22 = (bf16[32,512]{1,0:T(8,128)(2,1)S(1)}, bf16[32,512]{1,0:T(8,128)(2,1)S(1)}, u32[]{:S(2)}, u32[]{:S(2)}) collective-permute-start(bf16[32,512]{1,0:T(8,128)(2,1)S(1)} %get-tuple-element.70), channel_id=1, source_target_pairs={{0,2},{1,3},{2,0},{3,1},{4,6},{5,7},{6,4},{7,5},{8,10},{9,11},{10,... | collective-permute-start | bytes 98312 | tf_op jit(solution)/shard_map/ppermute | solution.py:34
  100.3 1.7 %collective-permute-start.21 = (bf16[32,512]{1,0:T(8,128)(2,1)S(1)}, bf16[32,512]{1,0:T(8,128)(2,1)S(1)}, u32[]{:S(2)}, u32[]{:S(2)}) collective-permute-start(bf16[32,512]{1,0:T(8,128)(2,1)S(1)} %get-tuple-element.68), channel_id=1, source_target_pairs={{0,1},{1,0},{2,3},{3,2},{4,5},{5,4},{6,7},{7,6},{8,9},{9,8},{10,11... | collective-permute-start | bytes 98312 | tf_op jit(solution)/shard_map/ppermute | solution.py:34
  (68 shorter events, 18.0 us)
Async XLA Ops:
  3.4 38.9 %all-to-all-start = ((bf16[4,320,512]{2,1,0:T(8,128)(2,1)}), bf16[4,320,512]{2,1,0:T(8,128)(2,1)S(1)}, u32[]{:S(2)}, u32[]{:S(2)}) async-start(bf16[4,320,512]{2,1,0:T(8,128)(2,1)} %bundle.1), calls=%async_computation | async-start | bytes 2621440 | tf_op jit(solution)/shard_map/all_to_all | solution.py:389
  9.7 23.0 %collective-permute-start.1 = (bf16[1024,512]{1,0:T(8,128)(2,1)S(1)}, bf16[1024,512]{1,0:T(8,128)(2,1)S(1)}, u32[]{:S(2)}, u32[]{:S(2)}) collective-permute-start(bf16[1024,512]{1,0:T(8,128)(2,1)S(1)} %copy-done.1), channel_id=1, source_target_pairs={{0,4},{4,0},{8,12},{12,8},{16,20},{20,16},{24,28},{28,24},{1,5},{5... | collective-permute-start | bytes 3145736 | tf_op jit(solution)/shard_map/ppermute | solution.py:34
  29.2 6.4 %collective-permute-start.2 = (bf16[64,1024]{1,0:T(8,128)(2,1)}, bf16[64,1024]{1,0:T(8,128)(2,1)}, u32[]{:S(2)}, u32[]{:S(2)}) collective-permute-start(bf16[64,1024]{1,0:T(8,128)(2,1)} %get-tuple-element.31), channel_id=1, source_target_pairs={{0,8},{4,12},{8,0},{12,4},{16,24},{20,28},{24,16},{28,20},{1,9},{5... | collective-permute-start | bytes 393224 | tf_op jit(solution)/shard_map/ppermute | solution.py:34
  30.7 8.6 %collective-permute-start.3 = (bf16[64,1024]{1,0:T(8,128)(2,1)}, bf16[64,1024]{1,0:T(8,128)(2,1)}, u32[]{:S(2)}, u32[]{:S(2)}) collective-permute-start(bf16[64,1024]{1,0:T(8,128)(2,1)} %get-tuple-element.32), channel_id=1, source_target_pairs={{0,16},{4,20},{8,24},{12,28},{16,0},{20,4},{24,8},{28,12},{1,17},{... | collective-permute-start | bytes 393224 | tf_op jit(solution)/shard_map/ppermute | solution.py:34
  32.2 7.1 %collective-permute-start.4 = (bf16[64,1024]{1,0:T(8,128)(2,1)}, bf16[64,1024]{1,0:T(8,128)(2,1)}, u32[]{:S(2)}, u32[]{:S(2)}) collective-permute-start(bf16[64,1024]{1,0:T(8,128)(2,1)} %get-tuple-element.33), channel_id=1, source_target_pairs={{0,24},{4,28},{8,16},{12,20},{16,8},{20,12},{24,0},{28,4},{1,25},{... | collective-permute-start | bytes 393224 | tf_op jit(solution)/shard_map/ppermute | solution.py:34
  42.3 10.8 %collective-permute-start.8 = (bf16[4,320,512]{2,1,0:T(8,128)(2,1)S(1)}, bf16[4,320,512]{2,1,0:T(8,128)(2,1)S(1)}, u32[]{:S(2)}, u32[]{:S(2)}) collective-permute-start(bf16[4,320,512]{2,1,0:T(8,128)(2,1)S(1)} %all-to-all-done.refs_4_.refs_5_), channel_id=1, source_target_pairs={{0,4},{4,0},{8,12},{12,8},{16,20},{20,16},{24,28},{28,24},{1,5},{5... | collective-permute-start | bytes 3932168 | tf_op jit(solution)/shard_map/ppermute | solution.py:34
  42.3 5.0 %collective-permute-start.5 = (bf16[64,512]{1,0:T(8,128)(2,1)}, bf16[64,512]{1,0:T(8,128)(2,1)S(1)}, u32[]{:S(2)}, u32[]{:S(2)}) collective-permute-start(bf16[64,512]{1,0:T(8,128)(2,1)} %get-tuple-element.36), channel_id=1, source_target_pairs={{0,1},{1,0},{2,3},{3,2},{4,5},{5,4},{6,7},{7,6},{8,9},{9,8},{10,11... | collective-permute-start | bytes 196616 | tf_op jit(solution)/shard_map/ppermute | solution.py:34
  44.4 7.9 %collective-permute-start.6 = (bf16[64,512]{1,0:T(8,128)(2,1)}, bf16[64,512]{1,0:T(8,128)(2,1)S(1)}, u32[]{:S(2)}, u32[]{:S(2)}) collective-permute-start(bf16[64,512]{1,0:T(8,128)(2,1)} %get-tuple-element.37), channel_id=1, source_target_pairs={{0,2},{1,3},{2,0},{3,1},{4,6},{5,7},{6,4},{7,5},{8,10},{9,11},{10,... | collective-permute-start | bytes 196616 | tf_op jit(solution)/shard_map/ppermute | solution.py:34
  46.8 6.3 %collective-permute-start.7 = (bf16[64,512]{1,0:T(8,128)(2,1)}, bf16[64,512]{1,0:T(8,128)(2,1)S(1)}, u32[]{:S(2)}, u32[]{:S(2)}) collective-permute-start(bf16[64,512]{1,0:T(8,128)(2,1)} %get-tuple-element.38), channel_id=1, source_target_pairs={{0,3},{1,2},{2,1},{3,0},{4,7},{5,6},{6,5},{7,4},{8,11},{9,10},{10,... | collective-permute-start | bytes 196616 | tf_op jit(solution)/shard_map/ppermute | solution.py:34
  54.0 5.7 %collective-permute-start.9 = (bf16[64,512]{1,0:T(8,128)(2,1)S(1)}, bf16[64,512]{1,0:T(8,128)(2,1)S(1)}, u32[]{:S(2)}, u32[]{:S(2)}) collective-permute-start(bf16[64,512]{1,0:T(8,128)(2,1)S(1)} %fusion.12.refs_0_), channel_id=1, source_target_pairs={{0,8},{4,12},{8,0},{12,4},{16,24},{20,28},{24,16},{28,20},{1,9},{5... | collective-permute-start | bytes 196616 | tf_op jit(solution)/shard_map/ppermute | solution.py:34
  55.3 5.8 %collective-permute-start.10 = (bf16[64,512]{1,0:T(8,128)(2,1)S(1)}, bf16[64,512]{1,0:T(8,128)(2,1)S(1)}, u32[]{:S(2)}, u32[]{:S(2)}) collective-permute-start(bf16[64,512]{1,0:T(8,128)(2,1)S(1)} %fusion.12.refs_0_), channel_id=1, source_target_pairs={{0,16},{4,20},{8,24},{12,28},{16,0},{20,4},{24,8},{28,12},{1,17},{... | collective-permute-start | bytes 196616 | tf_op jit(solution)/shard_map/ppermute | solution.py:34
  56.1 5.9 %collective-permute-start.11 = (bf16[64,512]{1,0:T(8,128)(2,1)S(1)}, bf16[64,512]{1,0:T(8,128)(2,1)S(1)}, u32[]{:S(2)}, u32[]{:S(2)}) collective-permute-start(bf16[64,512]{1,0:T(8,128)(2,1)S(1)} %fusion.12.refs_0_), channel_id=1, source_target_pairs={{0,24},{4,28},{8,16},{12,20},{16,8},{20,12},{24,0},{28,4},{1,25},{... | collective-permute-start | bytes 196616 | tf_op jit(solution)/shard_map/ppermute | solution.py:34
  57.5 9.8 %collective-permute-start.15 = (bf16[4,64,512]{2,1,0:T(8,128)(2,1)S(1)}, bf16[4,64,512]{2,1,0:T(8,128)(2,1)S(1)}, u32[]{:S(2)}, u32[]{:S(2)}) collective-permute-start(bf16[4,64,512]{2,1,0:T(8,128)(2,1)S(1)} %slice.85.refs_0_), channel_id=1, source_target_pairs={{0,8},{4,12},{8,0},{12,4},{16,24},{20,28},{24,16},{28,20},{1,9},{5... | collective-permute-start | bytes 786440 | tf_op jit(solution)/shard_map/ppermute | solution.py:34
  58.8 12.6 %collective-permute-start.16 = (bf16[4,64,512]{2,1,0:T(8,128)(2,1)S(1)}, bf16[4,64,512]{2,1,0:T(8,128)(2,1)S(1)}, u32[]{:S(2)}, u32[]{:S(2)}) collective-permute-start(bf16[4,64,512]{2,1,0:T(8,128)(2,1)S(1)} %slice.85.refs_0_), channel_id=1, source_target_pairs={{0,16},{4,20},{8,24},{12,28},{16,0},{20,4},{24,8},{28,12},{1,17},{... | collective-permute-start | bytes 786440 | tf_op jit(solution)/shard_map/ppermute | solution.py:34
  59.7 11.8 %collective-permute-start.17 = (bf16[4,64,512]{2,1,0:T(8,128)(2,1)S(1)}, bf16[4,64,512]{2,1,0:T(8,128)(2,1)S(1)}, u32[]{:S(2)}, u32[]{:S(2)}) collective-permute-start(bf16[4,64,512]{2,1,0:T(8,128)(2,1)S(1)} %slice.85.refs_0_), channel_id=1, source_target_pairs={{0,24},{4,28},{8,16},{12,20},{16,8},{20,12},{24,0},{28,4},{1,25},{... | collective-permute-start | bytes 786440 | tf_op jit(solution)/shard_map/ppermute | solution.py:34
  63.4 11.5 %collective-permute-start.24 = (bf16[128,512]{1,0:T(8,128)(2,1)S(1)}, bf16[128,512]{1,0:T(8,128)(2,1)S(1)}, u32[]{:S(2)}, u32[]{:S(2)}) collective-permute-start(bf16[128,512]{1,0:T(8,128)(2,1)S(1)} %get-tuple-element.66), channel_id=1, source_target_pairs={{0,1},{1,0},{2,3},{3,2},{4,5},{5,4},{6,7},{7,6},{8,9},{9,8},{10,11... | collective-permute-start | bytes 393224 | tf_op jit(solution)/shard_map/ppermute | solution.py:34
  64.8 12.1 %collective-permute-start.25 = (bf16[128,512]{1,0:T(8,128)(2,1)S(1)}, bf16[128,512]{1,0:T(8,128)(2,1)S(1)}, u32[]{:S(2)}, u32[]{:S(2)}) collective-permute-start(bf16[128,512]{1,0:T(8,128)(2,1)S(1)} %get-tuple-element.65), channel_id=1, source_target_pairs={{0,2},{1,3},{2,0},{3,1},{4,6},{5,7},{6,4},{7,5},{8,10},{9,11},{10,... | collective-permute-start | bytes 393224 | tf_op jit(solution)/shard_map/ppermute | solution.py:34
  67.4 9.6 %collective-permute-start.26 = (bf16[128,512]{1,0:T(8,128)(2,1)S(1)}, bf16[128,512]{1,0:T(8,128)(2,1)S(1)}, u32[]{:S(2)}, u32[]{:S(2)}) collective-permute-start(bf16[128,512]{1,0:T(8,128)(2,1)S(1)} %get-tuple-element.64), channel_id=1, source_target_pairs={{0,3},{1,2},{2,1},{3,0},{4,7},{5,6},{6,5},{7,4},{8,11},{9,10},{10,... | collective-permute-start | bytes 393224 | tf_op jit(solution)/shard_map/ppermute | solution.py:34
  72.3 8.5 %collective-permute-start.12 = (bf16[128,512]{1,0:T(8,128)(2,1)S(1)}, bf16[128,512]{1,0:T(8,128)(2,1)S(1)}, u32[]{:S(2)}, u32[]{:S(2)}) collective-permute-start(bf16[128,512]{1,0:T(8,128)(2,1)S(1)} %get-tuple-element.59), channel_id=1, source_target_pairs={{0,1},{1,0},{2,3},{3,2},{4,5},{5,4},{6,7},{7,6},{8,9},{9,8},{10,11... | collective-permute-start | bytes 393224 | tf_op jit(solution)/shard_map/ppermute | solution.py:34
  74.4 11.9 %collective-permute-start.13 = (bf16[128,512]{1,0:T(8,128)(2,1)S(1)}, bf16[128,512]{1,0:T(8,128)(2,1)S(1)}, u32[]{:S(2)}, u32[]{:S(2)}) collective-permute-start(bf16[128,512]{1,0:T(8,128)(2,1)S(1)} %get-tuple-element.58), channel_id=1, source_target_pairs={{0,2},{1,3},{2,0},{3,1},{4,6},{5,7},{6,4},{7,5},{8,10},{9,11},{10,... | collective-permute-start | bytes 393224 | tf_op jit(solution)/shard_map/ppermute | solution.py:34
  74.9 11.3 %collective-permute-start.14 = (bf16[128,512]{1,0:T(8,128)(2,1)S(1)}, bf16[128,512]{1,0:T(8,128)(2,1)S(1)}, u32[]{:S(2)}, u32[]{:S(2)}) collective-permute-start(bf16[128,512]{1,0:T(8,128)(2,1)S(1)} %get-tuple-element.57), channel_id=1, source_target_pairs={{0,3},{1,2},{2,1},{3,0},{4,7},{5,6},{6,5},{7,4},{8,11},{9,10},{10,... | collective-permute-start | bytes 393224 | tf_op jit(solution)/shard_map/ppermute | solution.py:34
  78.0 12.3 %collective-permute-start.29 = (bf16[32,2048]{1,0:T(8,128)(2,1)S(1)}, bf16[32,2048]{1,0:T(8,128)(2,1)S(1)}, u32[]{:S(2)}, u32[]{:S(2)}) collective-permute-start(bf16[32,2048]{1,0:T(8,128)(2,1)S(1)} %get-tuple-element.62), channel_id=1, source_target_pairs={{0,24},{4,28},{8,16},{12,20},{16,8},{20,12},{24,0},{28,4},{1,25},{... | collective-permute-start | bytes 393224 | tf_op jit(solution)/shard_map/ppermute | solution.py:34
  79.8 11.0 %collective-permute-start.28 = (bf16[32,2048]{1,0:T(8,128)(2,1)S(1)}, bf16[32,2048]{1,0:T(8,128)(2,1)S(1)}, u32[]{:S(2)}, u32[]{:S(2)}) collective-permute-start(bf16[32,2048]{1,0:T(8,128)(2,1)S(1)} %get-tuple-element.63), channel_id=1, source_target_pairs={{0,16},{4,20},{8,24},{12,28},{16,0},{20,4},{24,8},{28,12},{1,17},{... | collective-permute-start | bytes 393224 | tf_op jit(solution)/shard_map/ppermute | solution.py:34
  80.8 10.0 %collective-permute-start.27 = (bf16[32,2048]{1,0:T(8,128)(2,1)S(1)}, bf16[32,2048]{1,0:T(8,128)(2,1)S(1)}, u32[]{:S(2)}, u32[]{:S(2)}) collective-permute-start(bf16[32,2048]{1,0:T(8,128)(2,1)S(1)} %get-tuple-element.61), channel_id=1, source_target_pairs={{0,8},{4,12},{8,0},{12,4},{16,24},{20,28},{24,16},{28,20},{1,9},{5... | collective-permute-start | bytes 393224 | tf_op jit(solution)/shard_map/ppermute | solution.py:34
  87.3 8.7 %collective-permute-start.20 = (bf16[32,2048]{1,0:T(8,128)(2,1)S(1)}, bf16[32,2048]{1,0:T(8,128)(2,1)S(1)}, u32[]{:S(2)}, u32[]{:S(2)}) collective-permute-start(bf16[32,2048]{1,0:T(8,128)(2,1)S(1)} %get-tuple-element.55), channel_id=1, source_target_pairs={{0,24},{4,28},{8,16},{12,20},{16,8},{20,12},{24,0},{28,4},{1,25},{... | collective-permute-start | bytes 393224 | tf_op jit(solution)/shard_map/ppermute | solution.py:34
  88.8 8.6 %collective-permute-start.19 = (bf16[32,2048]{1,0:T(8,128)(2,1)S(1)}, bf16[32,2048]{1,0:T(8,128)(2,1)S(1)}, u32[]{:S(2)}, u32[]{:S(2)}) collective-permute-start(bf16[32,2048]{1,0:T(8,128)(2,1)S(1)} %get-tuple-element.56), channel_id=1, source_target_pairs={{0,16},{4,20},{8,24},{12,28},{16,0},{20,4},{24,8},{28,12},{1,17},{... | collective-permute-start | bytes 393224 | tf_op jit(solution)/shard_map/ppermute | solution.py:34
  90.3 7.1 %collective-permute-start.18 = (bf16[32,2048]{1,0:T(8,128)(2,1)S(1)}, bf16[32,2048]{1,0:T(8,128)(2,1)S(1)}, u32[]{:S(2)}, u32[]{:S(2)}) collective-permute-start(bf16[32,2048]{1,0:T(8,128)(2,1)S(1)} %get-tuple-element.54), channel_id=1, source_target_pairs={{0,8},{4,12},{8,0},{12,4},{16,24},{20,28},{24,16},{28,20},{1,9},{5... | collective-permute-start | bytes 393224 | tf_op jit(solution)/shard_map/ppermute | solution.py:34
  90.9 9.3 %collective-permute-start.32 = (bf16[32,512]{1,0:T(8,128)(2,1)S(1)}, bf16[32,512]{1,0:T(8,128)(2,1)S(1)}, u32[]{:S(2)}, u32[]{:S(2)}) collective-permute-start(bf16[32,512]{1,0:T(8,128)(2,1)S(1)} %get-tuple-element.72), channel_id=1, source_target_pairs={{0,3},{1,2},{2,1},{3,0},{4,7},{5,6},{6,5},{7,4},{8,11},{9,10},{10,... | collective-permute-start | bytes 98312 | tf_op jit(solution)/shard_map/ppermute | solution.py:34
  92.8 9.2 %collective-permute-start.31 = (bf16[32,512]{1,0:T(8,128)(2,1)S(1)}, bf16[32,512]{1,0:T(8,128)(2,1)S(1)}, u32[]{:S(2)}, u32[]{:S(2)}) collective-permute-start(bf16[32,512]{1,0:T(8,128)(2,1)S(1)} %get-tuple-element.73), channel_id=1, source_target_pairs={{0,2},{1,3},{2,0},{3,1},{4,6},{5,7},{6,4},{7,5},{8,10},{9,11},{10,... | collective-permute-start | bytes 98312 | tf_op jit(solution)/shard_map/ppermute | solution.py:34
  96.0 6.0 %collective-permute-start.30 = (bf16[32,512]{1,0:T(8,128)(2,1)S(1)}, bf16[32,512]{1,0:T(8,128)(2,1)S(1)}, u32[]{:S(2)}, u32[]{:S(2)}) collective-permute-start(bf16[32,512]{1,0:T(8,128)(2,1)S(1)} %get-tuple-element.71), channel_id=1, source_target_pairs={{0,1},{1,0},{2,3},{3,2},{4,5},{5,4},{6,7},{7,6},{8,9},{9,8},{10,11... | collective-permute-start | bytes 98312 | tf_op jit(solution)/shard_map/ppermute | solution.py:34
  97.5 5.8 %collective-permute-start.23 = (bf16[32,512]{1,0:T(8,128)(2,1)S(1)}, bf16[32,512]{1,0:T(8,128)(2,1)S(1)}, u32[]{:S(2)}, u32[]{:S(2)}) collective-permute-start(bf16[32,512]{1,0:T(8,128)(2,1)S(1)} %get-tuple-element.69), channel_id=1, source_target_pairs={{0,3},{1,2},{2,1},{3,0},{4,7},{5,6},{6,5},{7,4},{8,11},{9,10},{10,... | collective-permute-start | bytes 98312 | tf_op jit(solution)/shard_map/ppermute | solution.py:34
  99.0 4.8 %collective-permute-start.22 = (bf16[32,512]{1,0:T(8,128)(2,1)S(1)}, bf16[32,512]{1,0:T(8,128)(2,1)S(1)}, u32[]{:S(2)}, u32[]{:S(2)}) collective-permute-start(bf16[32,512]{1,0:T(8,128)(2,1)S(1)} %get-tuple-element.70), channel_id=1, source_target_pairs={{0,2},{1,3},{2,0},{3,1},{4,6},{5,7},{6,4},{7,5},{8,10},{9,11},{10,... | collective-permute-start | bytes 98312 | tf_op jit(solution)/shard_map/ppermute | solution.py:34
  (5 other events, 38.6 us)

commit v5 on v4

--- a/solution.py
+++ b/solution.py
@@ -94,10 +94,9 @@
     ahead, behind = products(pieces[0]), None
     for i, at in enumerate(pieces):
         now, ahead = ahead, products(pieces[i + 1]) if i + 1 < len(pieces) else None
-        done = soften(*now)
         if behind is not None:
             collect(pieces[i - 1], *behind)
-        behind = done
+        behind = soften(*now)
     collect(pieces[-1], *behind)
 
     @pl.when(block == pl.num_programs(1) - 1)
@@ -207,7 +206,7 @@
 def prepare_kernel(*refs):
     half = len(refs) // 2
     for from_ref, to_ref in zip(refs[:half], refs[half:]):
-        to_ref[...] = from_ref[...]
+        to_ref[...] = from_ref[...].T
 
 
 def prepare(arrays, after):
@@ -217,11 +216,11 @@
         grid=(4,),
         in_specs=[pl.BlockSpec((x.shape[0] // 4, x.shape[1]), lambda i: (i, 0)) for x in arrays]
         + [pl.BlockSpec(memory_space=pl.ANY)] * len(after),
-        out_specs=[pl.BlockSpec((x.shape[0] // 4, x.shape[1]), lambda i: (i, 0)) for x in arrays],
-        out_shape=[pltpu.VMEM(x.shape, x.dtype) for x in arrays],
-        compiler_params=pltpu.CompilerParams(vmem_limit_bytes=VMEM_BYTES),
-        cost_estimate=pl.CostEstimate(
-            flops=0, bytes_accessed=4 * sum(x.size for x in arrays), transcendentals=0
+        out_specs=[pl.BlockSpec((x.shape[1], x.shape[0] // 4), lambda i: (0, i)) for x in arrays],
+        out_shape=[pltpu.VMEM(x.shape[::-1], x.dtype) for x in arrays],
+        compiler_params=pltpu.CompilerParams(vmem_limit_bytes=VMEM_BYTES),
+        cost_estimate=pl.CostEstimate(
+            flops=0, bytes_accessed=4 * arrays[0].size, transcendentals=0
         ),
         name="prepare",
     )(*map(hold, arrays), *after)
@@ -237,8 +236,8 @@
     block = part_refs[0].shape[1]
     for k, part_ref in enumerate(part_refs):
         at = pl.ds(pl.multiple_of(chunk_ref[k] * block, block), block)
-        part = dot(key_proj_ref[at, :], key_low, NT) + dot(value_proj_ref[at, :], value_low, NT)
-        part_ref[...] = part.T.astype(BF16)
+        part = dot(key_low, key_proj_ref[at, :], NT) + dot(value_low, value_proj_ref[:, at], NN)
+        part_ref[...] = part.astype(BF16)
 
 
 def project(chunk, terms, key_proj, value_proj):

time: 105 us -> 105 us (level)
  transfers between devices with their start and end apart: 34 -> 34, of which waited for: 13 -> 12; matrix products, arithmetic and copies ran while one was open for 1% -> 1% of each run, Pallas kernels for 26% -> 26%
where the time goes in v5:
time: 105 us
  starting transfers between devices  49.9 us (48%)
  Pallas kernels  30 us (29%)
  waiting for transfers between devices  21.8 us (21%)
  other arithmetic  1.95 us (2%)
    ppermute x33, starting transfers between devices, swap(): return lax.ppermute(x, axis, [(i, i ^ distance) for i in range(size)])  43.6 us
    ppermute x33, waiting for transfers between devices, swap(): return lax.ppermute(x, axis, [(i, i ^ distance) for i in range(size)])  21.8 us
    pallas_call x1, Pallas kernels, attend(): pl.pallas_call(functools.partial(attend_kernel, min(256, block)), grid_sp...  16.7 us
    all_to_all x1, starting transfers between devices, local(): own_up = lax.all_to_all(bundle(up_proj, global_in, planes), 'heads', 0, 0)  6.32 us
    pallas_call x1, Pallas kernels, prepare(): pl.pallas_call(lambda *refs: prepare_kernel(*refs[:count], *refs[count +...  2.98 us
    pallas_call x1, Pallas kernels, project(): pl.pallas_call(functools.partial(project_kernel, len(terms)), in_specs=[p...  2.81 us
    pallas_call x1, Pallas kernels, bundle(): pl.pallas_call(bundle_kernel, out_shape=jax.ShapeDtypeStruct((size, hidde...  2.74 us
  transfers between devices with their start and end apart: 34, of which 12 were waited for; matrix products, arithmetic and copies ran while one was open for 1% of the time, Pallas kernels for 26%

profile of v5, /device:TPU:0, one launch (start us, length us, event | category | flops | bytes accessed | tf_op | source)
XLA Modules:
  0.0 104.7 jit_solution(13306825683937642582)
XLA Ops:
  0.6 2.7 %bundle.1 = bf16[4,320,512]{2,1,0:T(8,128)(2,1)} custom-call(bf16[512,1024]{1,0:T(8,128)(2,1)} %up_ref.1, bf16[64,512]{1,0:T(8,128)(2,1)} %in_ref.1), custom_call_target="tpu_custom_call" | custom-call | bytes 2097152 | tf_op jit(solution)/shard_map/bundle/pallas_call | solution.py:165
  3.4 6.3 %all-to-all-start = ((bf16[4,320,512]{2,1,0:T(8,128)(2,1)}), bf16[4,320,512]{2,1,0:T(8,128)(2,1)S(1)}, u32[]{:S(2)}, u32[]{:S(2)}) async-start(bf16[4,320,512]{2,1,0:T(8,128)(2,1)} %bundle.1), calls=%async_computation | async-start | bytes 2621440 | tf_op jit(solution)/shard_map/all_to_all | solution.py:388
  9.7 16.7 %attend.1 = (bf16[2048,512]{1,0:T(8,128)(2,1)}, bf16[4,64,1024]{2,1,0:T(8,128)(2,1)S(1)}, bf16[4,64,1024]{2,1,0:T(8,128)(2,1)S(1)}) custom-call(s32[8]{0:T(128)S(1)} %iota_xor_fusion.1.place_ref, bf16[2048,512]{1,0:T(8,128)(2,1)} %q_ref.1, bf16[2048,512]{1,0:T(8,128)(2,1)} %g_ref.1, bf16[512,512]{1,0:T(8,128)(2,1)} %k_ref.1, bf16[512,512]{1,0:T(8,128)(2,1)} %v_ref.1), custom_call_target="tpu_custom_call" | custom-call | flops 10737418240 | bytes 6291456 | tf_op jit(solution)/shard_map/attend/pallas_call | solution.py:120
  26.9 1.5 %collective-permute-done.refs_1_ = bf16[4,64,1024]{2,1,0:T(8,128)(2,1)S(1)} collective-permute-done((bf16[4,64,1024]{2,1,0:T(8,128)(2,1)S(1)}, bf16[4,64,1024]{2,1,0:T(8,128)(2,1)S(1)}, u32[]{:S(2)}, u32[]{:S(2)}) %collective-permute-start) | collective-permute-done | bytes 524320 | tf_op jit(solution)/shard_map/ppermute | solution.py:34
  29.2 1.5 %collective-permute-start.2 = (bf16[64,1024]{1,0:T(8,128)(2,1)}, bf16[64,1024]{1,0:T(8,128)(2,1)}, u32[]{:S(2)}, u32[]{:S(2)}) collective-permute-start(bf16[64,1024]{1,0:T(8,128)(2,1)} %get-tuple-element.31), channel_id=1, source_target_pairs={{0,8},{4,12},{8,0},{12,4},{16,24},{20,28},{24,16},{28,20},{1,9},{5... | collective-permute-start | bytes 393224 | tf_op jit(solution)/shard_map/ppermute | solution.py:34
  30.7 1.5 %collective-permute-start.3 = (bf16[64,1024]{1,0:T(8,128)(2,1)}, bf16[64,1024]{1,0:T(8,128)(2,1)}, u32[]{:S(2)}, u32[]{:S(2)}) collective-permute-start(bf16[64,1024]{1,0:T(8,128)(2,1)} %get-tuple-element.32), channel_id=1, source_target_pairs={{0,16},{4,20},{8,24},{12,28},{16,0},{20,4},{24,8},{28,12},{1,17},{... | collective-permute-start | bytes 393224 | tf_op jit(solution)/shard_map/ppermute | solution.py:34
  32.7 3.0 %prepare.1.refs_5_ = bf16[512,2048]{1,0:T(8,128)(2,1)S(1)} custom-call(bf16[2048,512]{1,0:T(8,128)(2,1)} %refs_0_.1, bf16[64,1024]{1,0:T(8,128)(2,1)S(1)} %get-tuple-element.30.refs_1_.refs_0_), custom_call_target="tpu_custom_call" | custom-call | bytes 4194304 | tf_op jit(solution)/shard_map/prepare/pallas_call | solution.py:214
  35.7 3.6 %collective-permute-done.3.refs_2_ = bf16[64,1024]{1,0:T(8,128)(2,1)} collective-permute-done((bf16[64,1024]{1,0:T(8,128)(2,1)}, bf16[64,1024]{1,0:T(8,128)(2,1)}, u32[]{:S(2)}, u32[]{:S(2)}) %collective-permute-start.3) | collective-permute-done | bytes 131104 | tf_op jit(solution)/shard_map/ppermute | solution.py:34
  39.3 2.8 %project.1 = (bf16[64,512]{1,0:T(8,128)(2,1)}, bf16[64,512]{1,0:T(8,128)(2,1)}, bf16[64,512]{1,0:T(8,128)(2,1)}, bf16[64,512]{1,0:T(8,128)(2,1)}) custom-call(s32[4]{0:T(128)S(1)} %iota_xor_fusion.chunk_ref, bf16[64,1024]{1,0:T(8,128)(2,1)S(1)} %get-tuple-element.30.refs_1_.refs_0_, bf16[64,1024]{1,0:T(8,128)(2,1)} %collective-permute-done.2.refs_1_, ...), custom_call_target="tpu_custom_call" | custom-call | flops 268435456 | bytes 4194304 | tf_op jit(solution)/shard_map/project/pallas_call | solution.py:248
  42.1 2.1 %collective-permute-start.5 = (bf16[64,512]{1,0:T(8,128)(2,1)}, bf16[64,512]{1,0:T(8,128)(2,1)S(1)}, u32[]{:S(2)}, u32[]{:S(2)}) collective-permute-start(bf16[64,512]{1,0:T(8,128)(2,1)} %get-tuple-element.36), channel_id=1, source_target_pairs={{0,1},{1,0},{2,3},{3,2},{4,5},{5,4},{6,7},{7,6},{8,9},{9,8},{10,11... | collective-permute-start | bytes 196616 | tf_op jit(solution)/shard_map/ppermute | solution.py:34
  44.2 2.4 %collective-permute-start.6 = (bf16[64,512]{1,0:T(8,128)(2,1)}, bf16[64,512]{1,0:T(8,128)(2,1)S(1)}, u32[]{:S(2)}, u32[]{:S(2)}) collective-permute-start(bf16[64,512]{1,0:T(8,128)(2,1)} %get-tuple-element.37), channel_id=1, source_target_pairs={{0,2},{1,3},{2,0},{3,1},{4,6},{5,7},{6,4},{7,5},{8,10},{9,11},{10,... | collective-permute-start | bytes 196616 | tf_op jit(solution)/shard_map/ppermute | solution.py:34
  47.1 5.0 %collective-permute-done.6 = bf16[64,512]{1,0:T(8,128)(2,1)S(1)} collective-permute-done((bf16[64,512]{1,0:T(8,128)(2,1)}, bf16[64,512]{1,0:T(8,128)(2,1)S(1)}, u32[]{:S(2)}, u32[]{:S(2)}) %collective-permute-start.6) | collective-permute-done | bytes 65568 | tf_op jit(solution)/shard_map/ppermute | solution.py:34
  55.9 1.4 %collective-permute-start.11 = (bf16[64,512]{1,0:T(8,128)(2,1)S(1)}, bf16[64,512]{1,0:T(8,128)(2,1)S(1)}, u32[]{:S(2)}, u32[]{:S(2)}) collective-permute-start(bf16[64,512]{1,0:T(8,128)(2,1)S(1)} %fusion.12.refs_0_), channel_id=1, source_target_pairs={{0,24},{4,28},{8,16},{12,20},{16,8},{20,12},{24,0},{28,4},{1,25},{... | collective-permute-start | bytes 196616 | tf_op jit(solution)/shard_map/ppermute | solution.py:34
  57.4 1.3 %collective-permute-start.15 = (bf16[4,64,512]{2,1,0:T(8,128)(2,1)S(1)}, bf16[4,64,512]{2,1,0:T(8,128)(2,1)S(1)}, u32[]{:S(2)}, u32[]{:S(2)}) collective-permute-start(bf16[4,64,512]{2,1,0:T(8,128)(2,1)S(1)} %slice.85.refs_0_), channel_id=1, source_target_pairs={{0,8},{4,12},{8,0},{12,4},{16,24},{20,28},{24,16},{28,20},{1,9},{5... | collective-permute-start | bytes 786440 | tf_op jit(solution)/shard_map/ppermute | solution.py:34
  59.5 1.4 %collective-permute-start.17 = (bf16[4,64,512]{2,1,0:T(8,128)(2,1)S(1)}, bf16[4,64,512]{2,1,0:T(8,128)(2,1)S(1)}, u32[]{:S(2)}, u32[]{:S(2)}) collective-permute-start(bf16[4,64,512]{2,1,0:T(8,128)(2,1)S(1)} %slice.85.refs_0_), channel_id=1, source_target_pairs={{0,24},{4,28},{8,16},{12,20},{16,8},{20,12},{24,0},{28,4},{1,25},{... | collective-permute-start | bytes 786440 | tf_op jit(solution)/shard_map/ppermute | solution.py:34
  61.8 1.3 %back.1 = (bf16[4,128,512]{2,1,0:T(8,128)(2,1)S(1)}, bf16[4,128,512]{2,1,0:T(8,128)(2,1)S(1)}) custom-call(s32[4]{0:T(128)S(1)} %iota_xor_fusion.chunk_ref, bf16[64,512]{1,0:T(8,128)(2,1)S(1)} %fusion.12.refs_0_, bf16[64,512]{1,0:T(8,128)(2,1)S(1)} %collective-permute-done.9.refs_1_, bf16[64,512]{1,0:T(8,128)(2,1)S(1)} %collective-permute-done.10.refs_2_, ...), custom_call_target="tpu_custom_call" | custom-call | flops 536870912 | bytes 2097152 | tf_op jit(solution)/shard_map/back/pallas_call | solution.py:297
  63.2 1.4 %collective-permute-start.24 = (bf16[128,512]{1,0:T(8,128)(2,1)S(1)}, bf16[128,512]{1,0:T(8,128)(2,1)S(1)}, u32[]{:S(2)}, u32[]{:S(2)}) collective-permute-start(bf16[128,512]{1,0:T(8,128)(2,1)S(1)} %get-tuple-element.66), channel_id=1, source_target_pairs={{0,1},{1,0},{2,3},{3,2},{4,5},{5,4},{6,7},{7,6},{8,9},{9,8},{10,11... | collective-permute-start | bytes 393224 | tf_op jit(solution)/shard_map/ppermute | solution.py:34
  64.7 1.7 %collective-permute-start.25 = (bf16[128,512]{1,0:T(8,128)(2,1)S(1)}, bf16[128,512]{1,0:T(8,128)(2,1)S(1)}, u32[]{:S(2)}, u32[]{:S(2)}) collective-permute-start(bf16[128,512]{1,0:T(8,128)(2,1)S(1)} %get-tuple-element.65), channel_id=1, source_target_pairs={{0,2},{1,3},{2,0},{3,1},{4,6},{5,7},{6,4},{7,5},{8,10},{9,11},{10,... | collective-permute-start | bytes 393224 | tf_op jit(solution)/shard_map/ppermute | solution.py:34
  67.2 2.3 %collective-permute-start.26 = (bf16[128,512]{1,0:T(8,128)(2,1)S(1)}, bf16[128,512]{1,0:T(8,128)(2,1)S(1)}, u32[]{:S(2)}, u32[]{:S(2)}) collective-permute-start(bf16[128,512]{1,0:T(8,128)(2,1)S(1)} %get-tuple-element.64), channel_id=1, source_target_pairs={{0,3},{1,2},{2,1},{3,0},{4,7},{5,6},{6,5},{7,4},{8,11},{9,10},{10,... | collective-permute-start | bytes 393224 | tf_op jit(solution)/shard_map/ppermute | solution.py:34
  69.5 1.8 %collective-permute-done.16.refs_2_ = bf16[4,64,512]{2,1,0:T(8,128)(2,1)S(1)} collective-permute-done((bf16[4,64,512]{2,1,0:T(8,128)(2,1)S(1)}, bf16[4,64,512]{2,1,0:T(8,128)(2,1)S(1)}, u32[]{:S(2)}, u32[]{:S(2)}) %collective-permute-start.16) | collective-permute-done | bytes 262176 | tf_op jit(solution)/shard_map/ppermute | solution.py:34
  72.1 2.0 %collective-permute-start.12 = (bf16[128,512]{1,0:T(8,128)(2,1)S(1)}, bf16[128,512]{1,0:T(8,128)(2,1)S(1)}, u32[]{:S(2)}, u32[]{:S(2)}) collective-permute-start(bf16[128,512]{1,0:T(8,128)(2,1)S(1)} %get-tuple-element.59), channel_id=1, source_target_pairs={{0,1},{1,0},{2,3},{3,2},{4,5},{5,4},{6,7},{7,6},{8,9},{9,8},{10,11... | collective-permute-start | bytes 393224 | tf_op jit(solution)/shard_map/ppermute | solution.py:34
  74.7 2.1 %collective-permute-start.14 = (bf16[128,512]{1,0:T(8,128)(2,1)S(1)}, bf16[128,512]{1,0:T(8,128)(2,1)S(1)}, u32[]{:S(2)}, u32[]{:S(2)}) collective-permute-start(bf16[128,512]{1,0:T(8,128)(2,1)S(1)} %get-tuple-element.57), channel_id=1, source_target_pairs={{0,3},{1,2},{2,1},{3,0},{4,7},{5,6},{6,5},{7,4},{8,11},{9,10},{10,... | collective-permute-start | bytes 393224 | tf_op jit(solution)/shard_map/ppermute | solution.py:34
  77.8 1.8 %collective-permute-start.29 = (bf16[32,2048]{1,0:T(8,128)(2,1)S(1)}, bf16[32,2048]{1,0:T(8,128)(2,1)S(1)}, u32[]{:S(2)}, u32[]{:S(2)}) collective-permute-start(bf16[32,2048]{1,0:T(8,128)(2,1)S(1)} %get-tuple-element.62), channel_id=1, source_target_pairs={{0,24},{4,28},{8,16},{12,20},{16,8},{20,12},{24,0},{28,4},{1,25},{... | collective-permute-start | bytes 393224 | tf_op jit(solution)/shard_map/ppermute | solution.py:34
  81.4 4.6 %collective-permute-done.13.refs_2_ = bf16[128,512]{1,0:T(8,128)(2,1)S(1)} collective-permute-done((bf16[128,512]{1,0:T(8,128)(2,1)S(1)}, bf16[128,512]{1,0:T(8,128)(2,1)S(1)}, u32[]{:S(2)}, u32[]{:S(2)}) %collective-permute-start.13) | collective-permute-done | bytes 131104 | tf_op jit(solution)/shard_map/ppermute | solution.py:34
  87.1 1.5 %collective-permute-start.20 = (bf16[32,2048]{1,0:T(8,128)(2,1)S(1)}, bf16[32,2048]{1,0:T(8,128)(2,1)S(1)}, u32[]{:S(2)}, u32[]{:S(2)}) collective-permute-start(bf16[32,2048]{1,0:T(8,128)(2,1)S(1)} %get-tuple-element.55), channel_id=1, source_target_pairs={{0,24},{4,28},{8,16},{12,20},{16,8},{20,12},{24,0},{28,4},{1,25},{... | collective-permute-start | bytes 393224 | tf_op jit(solution)/shard_map/ppermute | solution.py:34
  88.6 1.5 %collective-permute-start.19 = (bf16[32,2048]{1,0:T(8,128)(2,1)S(1)}, bf16[32,2048]{1,0:T(8,128)(2,1)S(1)}, u32[]{:S(2)}, u32[]{:S(2)}) collective-permute-start(bf16[32,2048]{1,0:T(8,128)(2,1)S(1)} %get-tuple-element.56), channel_id=1, source_target_pairs={{0,16},{4,20},{8,24},{12,28},{16,0},{20,4},{24,8},{28,12},{1,17},{... | collective-permute-start | bytes 393224 | tf_op jit(solution)/shard_map/ppermute | solution.py:34
  90.7 1.8 %collective-permute-start.32 = (bf16[32,512]{1,0:T(8,128)(2,1)S(1)}, bf16[32,512]{1,0:T(8,128)(2,1)S(1)}, u32[]{:S(2)}, u32[]{:S(2)}) collective-permute-start(bf16[32,512]{1,0:T(8,128)(2,1)S(1)} %get-tuple-element.72), channel_id=1, source_target_pairs={{0,3},{1,2},{2,1},{3,0},{4,7},{5,6},{6,5},{7,4},{8,11},{9,10},{10,... | collective-permute-start | bytes 98312 | tf_op jit(solution)/shard_map/ppermute | solution.py:34
  92.6 3.2 %collective-permute-start.31 = (bf16[32,512]{1,0:T(8,128)(2,1)S(1)}, bf16[32,512]{1,0:T(8,128)(2,1)S(1)}, u32[]{:S(2)}, u32[]{:S(2)}) collective-permute-start(bf16[32,512]{1,0:T(8,128)(2,1)S(1)} %get-tuple-element.73), channel_id=1, source_target_pairs={{0,2},{1,3},{2,0},{3,1},{4,6},{5,7},{6,4},{7,5},{8,10},{9,11},{10,... | collective-permute-start | bytes 98312 | tf_op jit(solution)/shard_map/ppermute | solution.py:34
  95.8 1.4 %collective-permute-start.30 = (bf16[32,512]{1,0:T(8,128)(2,1)S(1)}, bf16[32,512]{1,0:T(8,128)(2,1)S(1)}, u32[]{:S(2)}, u32[]{:S(2)}) collective-permute-start(bf16[32,512]{1,0:T(8,128)(2,1)S(1)} %get-tuple-element.71), channel_id=1, source_target_pairs={{0,1},{1,0},{2,3},{3,2},{4,5},{5,4},{6,7},{7,6},{8,9},{9,8},{10,11... | collective-permute-start | bytes 98312 | tf_op jit(solution)/shard_map/ppermute | solution.py:34
  97.3 1.5 %collective-permute-start.23 = (bf16[32,512]{1,0:T(8,128)(2,1)S(1)}, bf16[32,512]{1,0:T(8,128)(2,1)S(1)}, u32[]{:S(2)}, u32[]{:S(2)}) collective-permute-start(bf16[32,512]{1,0:T(8,128)(2,1)S(1)} %get-tuple-element.69), channel_id=1, source_target_pairs={{0,3},{1,2},{2,1},{3,0},{4,7},{5,6},{6,5},{7,4},{8,11},{9,10},{10,... | collective-permute-start | bytes 98312 | tf_op jit(solution)/shard_map/ppermute | solution.py:34
  100.1 1.7 %collective-permute-start.21 = (bf16[32,512]{1,0:T(8,128)(2,1)S(1)}, bf16[32,512]{1,0:T(8,128)(2,1)S(1)}, u32[]{:S(2)}, u32[]{:S(2)}) collective-permute-start(bf16[32,512]{1,0:T(8,128)(2,1)S(1)} %get-tuple-element.68), channel_id=1, source_target_pairs={{0,1},{1,0},{2,3},{3,2},{4,5},{5,4},{6,7},{7,6},{8,9},{9,8},{10,11... | collective-permute-start | bytes 98312 | tf_op jit(solution)/shard_map/ppermute | solution.py:34
  101.8 1.3 %collective-permute-done.23 = bf16[32,512]{1,0:T(8,128)(2,1)S(1)} collective-permute-done((bf16[32,512]{1,0:T(8,128)(2,1)S(1)}, bf16[32,512]{1,0:T(8,128)(2,1)S(1)}, u32[]{:S(2)}, u32[]{:S(2)}) %collective-permute-start.23) | collective-permute-done | bytes 32800 | tf_op jit(solution)/shard_map/ppermute | solution.py:34
  (68 shorter events, 17.6 us)
Async XLA Ops:
  3.4 38.7 %all-to-all-start = ((bf16[4,320,512]{2,1,0:T(8,128)(2,1)}), bf16[4,320,512]{2,1,0:T(8,128)(2,1)S(1)}, u32[]{:S(2)}, u32[]{:S(2)}) async-start(bf16[4,320,512]{2,1,0:T(8,128)(2,1)} %bundle.1), calls=%async_computation | async-start | bytes 2621440 | tf_op jit(solution)/shard_map/all_to_all | solution.py:388
  9.7 23.0 %collective-permute-start.1 = (bf16[1024,512]{1,0:T(8,128)(2,1)S(1)}, bf16[1024,512]{1,0:T(8,128)(2,1)S(1)}, u32[]{:S(2)}, u32[]{:S(2)}) collective-permute-start(bf16[1024,512]{1,0:T(8,128)(2,1)S(1)} %copy-done.1), channel_id=1, source_target_pairs={{0,4},{4,0},{8,12},{12,8},{16,20},{20,16},{24,28},{28,24},{1,5},{5... | collective-permute-start | bytes 3145736 | tf_op jit(solution)/shard_map/ppermute | solution.py:34
  29.2 6.5 %collective-permute-start.2 = (bf16[64,1024]{1,0:T(8,128)(2,1)}, bf16[64,1024]{1,0:T(8,128)(2,1)}, u32[]{:S(2)}, u32[]{:S(2)}) collective-permute-start(bf16[64,1024]{1,0:T(8,128)(2,1)} %get-tuple-element.31), channel_id=1, source_target_pairs={{0,8},{4,12},{8,0},{12,4},{16,24},{20,28},{24,16},{28,20},{1,9},{5... | collective-permute-start | bytes 393224 | tf_op jit(solution)/shard_map/ppermute | solution.py:34
  30.7 8.6 %collective-permute-start.3 = (bf16[64,1024]{1,0:T(8,128)(2,1)}, bf16[64,1024]{1,0:T(8,128)(2,1)}, u32[]{:S(2)}, u32[]{:S(2)}) collective-permute-start(bf16[64,1024]{1,0:T(8,128)(2,1)} %get-tuple-element.32), channel_id=1, source_target_pairs={{0,16},{4,20},{8,24},{12,28},{16,0},{20,4},{24,8},{28,12},{1,17},{... | collective-permute-start | bytes 393224 | tf_op jit(solution)/shard_map/ppermute | solution.py:34
  32.2 7.1 %collective-permute-start.4 = (bf16[64,1024]{1,0:T(8,128)(2,1)}, bf16[64,1024]{1,0:T(8,128)(2,1)}, u32[]{:S(2)}, u32[]{:S(2)}) collective-permute-start(bf16[64,1024]{1,0:T(8,128)(2,1)} %get-tuple-element.33), channel_id=1, source_target_pairs={{0,24},{4,28},{8,16},{12,20},{16,8},{20,12},{24,0},{28,4},{1,25},{... | collective-permute-start | bytes 393224 | tf_op jit(solution)/shard_map/ppermute | solution.py:34
  42.1 10.8 %collective-permute-start.8 = (bf16[4,320,512]{2,1,0:T(8,128)(2,1)S(1)}, bf16[4,320,512]{2,1,0:T(8,128)(2,1)S(1)}, u32[]{:S(2)}, u32[]{:S(2)}) collective-permute-start(bf16[4,320,512]{2,1,0:T(8,128)(2,1)S(1)} %all-to-all-done.refs_4_.refs_5_), channel_id=1, source_target_pairs={{0,4},{4,0},{8,12},{12,8},{16,20},{20,16},{24,28},{28,24},{1,5},{5... | collective-permute-start | bytes 3932168 | tf_op jit(solution)/shard_map/ppermute | solution.py:34
  42.1 5.0 %collective-permute-start.5 = (bf16[64,512]{1,0:T(8,128)(2,1)}, bf16[64,512]{1,0:T(8,128)(2,1)S(1)}, u32[]{:S(2)}, u32[]{:S(2)}) collective-permute-start(bf16[64,512]{1,0:T(8,128)(2,1)} %get-tuple-element.36), channel_id=1, source_target_pairs={{0,1},{1,0},{2,3},{3,2},{4,5},{5,4},{6,7},{7,6},{8,9},{9,8},{10,11... | collective-permute-start | bytes 196616 | tf_op jit(solution)/shard_map/ppermute | solution.py:34
  44.2 7.9 %collective-permute-start.6 = (bf16[64,512]{1,0:T(8,128)(2,1)}, bf16[64,512]{1,0:T(8,128)(2,1)S(1)}, u32[]{:S(2)}, u32[]{:S(2)}) collective-permute-start(bf16[64,512]{1,0:T(8,128)(2,1)} %get-tuple-element.37), channel_id=1, source_target_pairs={{0,2},{1,3},{2,0},{3,1},{4,6},{5,7},{6,4},{7,5},{8,10},{9,11},{10,... | collective-permute-start | bytes 196616 | tf_op jit(solution)/shard_map/ppermute | solution.py:34
  46.6 6.3 %collective-permute-start.7 = (bf16[64,512]{1,0:T(8,128)(2,1)}, bf16[64,512]{1,0:T(8,128)(2,1)S(1)}, u32[]{:S(2)}, u32[]{:S(2)}) collective-permute-start(bf16[64,512]{1,0:T(8,128)(2,1)} %get-tuple-element.38), channel_id=1, source_target_pairs={{0,3},{1,2},{2,1},{3,0},{4,7},{5,6},{6,5},{7,4},{8,11},{9,10},{10,... | collective-permute-start | bytes 196616 | tf_op jit(solution)/shard_map/ppermute | solution.py:34
  53.8 5.7 %collective-permute-start.9 = (bf16[64,512]{1,0:T(8,128)(2,1)S(1)}, bf16[64,512]{1,0:T(8,128)(2,1)S(1)}, u32[]{:S(2)}, u32[]{:S(2)}) collective-permute-start(bf16[64,512]{1,0:T(8,128)(2,1)S(1)} %fusion.12.refs_0_), channel_id=1, source_target_pairs={{0,8},{4,12},{8,0},{12,4},{16,24},{20,28},{24,16},{28,20},{1,9},{5... | collective-permute-start | bytes 196616 | tf_op jit(solution)/shard_map/ppermute | solution.py:34
  55.1 5.8 %collective-permute-start.10 = (bf16[64,512]{1,0:T(8,128)(2,1)S(1)}, bf16[64,512]{1,0:T(8,128)(2,1)S(1)}, u32[]{:S(2)}, u32[]{:S(2)}) collective-permute-start(bf16[64,512]{1,0:T(8,128)(2,1)S(1)} %fusion.12.refs_0_), channel_id=1, source_target_pairs={{0,16},{4,20},{8,24},{12,28},{16,0},{20,4},{24,8},{28,12},{1,17},{... | collective-permute-start | bytes 196616 | tf_op jit(solution)/shard_map/ppermute | solution.py:34
  55.9 5.9 %collective-permute-start.11 = (bf16[64,512]{1,0:T(8,128)(2,1)S(1)}, bf16[64,512]{1,0:T(8,128)(2,1)S(1)}, u32[]{:S(2)}, u32[]{:S(2)}) collective-permute-start(bf16[64,512]{1,0:T(8,128)(2,1)S(1)} %fusion.12.refs_0_), channel_id=1, source_target_pairs={{0,24},{4,28},{8,16},{12,20},{16,8},{20,12},{24,0},{28,4},{1,25},{... | collective-permute-start | bytes 196616 | tf_op jit(solution)/shard_map/ppermute | solution.py:34
  57.4 9.8 %collective-permute-start.15 = (bf16[4,64,512]{2,1,0:T(8,128)(2,1)S(1)}, bf16[4,64,512]{2,1,0:T(8,128)(2,1)S(1)}, u32[]{:S(2)}, u32[]{:S(2)}) collective-permute-start(bf16[4,64,512]{2,1,0:T(8,128)(2,1)S(1)} %slice.85.refs_0_), channel_id=1, source_target_pairs={{0,8},{4,12},{8,0},{12,4},{16,24},{20,28},{24,16},{28,20},{1,9},{5... | collective-permute-start | bytes 786440 | tf_op jit(solution)/shard_map/ppermute | solution.py:34
  58.6 12.6 %collective-permute-start.16 = (bf16[4,64,512]{2,1,0:T(8,128)(2,1)S(1)}, bf16[4,64,512]{2,1,0:T(8,128)(2,1)S(1)}, u32[]{:S(2)}, u32[]{:S(2)}) collective-permute-start(bf16[4,64,512]{2,1,0:T(8,128)(2,1)S(1)} %slice.85.refs_0_), channel_id=1, source_target_pairs={{0,16},{4,20},{8,24},{12,28},{16,0},{20,4},{24,8},{28,12},{1,17},{... | collective-permute-start | bytes 786440 | tf_op jit(solution)/shard_map/ppermute | solution.py:34
  59.5 11.8 %collective-permute-start.17 = (bf16[4,64,512]{2,1,0:T(8,128)(2,1)S(1)}, bf16[4,64,512]{2,1,0:T(8,128)(2,1)S(1)}, u32[]{:S(2)}, u32[]{:S(2)}) collective-permute-start(bf16[4,64,512]{2,1,0:T(8,128)(2,1)S(1)} %slice.85.refs_0_), channel_id=1, source_target_pairs={{0,24},{4,28},{8,16},{12,20},{16,8},{20,12},{24,0},{28,4},{1,25},{... | collective-permute-start | bytes 786440 | tf_op jit(solution)/shard_map/ppermute | solution.py:34
  63.2 11.5 %collective-permute-start.24 = (bf16[128,512]{1,0:T(8,128)(2,1)S(1)}, bf16[128,512]{1,0:T(8,128)(2,1)S(1)}, u32[]{:S(2)}, u32[]{:S(2)}) collective-permute-start(bf16[128,512]{1,0:T(8,128)(2,1)S(1)} %get-tuple-element.66), channel_id=1, source_target_pairs={{0,1},{1,0},{2,3},{3,2},{4,5},{5,4},{6,7},{7,6},{8,9},{9,8},{10,11... | collective-permute-start | bytes 393224 | tf_op jit(solution)/shard_map/ppermute | solution.py:34
  64.7 12.1 %collective-permute-start.25 = (bf16[128,512]{1,0:T(8,128)(2,1)S(1)}, bf16[128,512]{1,0:T(8,128)(2,1)S(1)}, u32[]{:S(2)}, u32[]{:S(2)}) collective-permute-start(bf16[128,512]{1,0:T(8,128)(2,1)S(1)} %get-tuple-element.65), channel_id=1, source_target_pairs={{0,2},{1,3},{2,0},{3,1},{4,6},{5,7},{6,4},{7,5},{8,10},{9,11},{10,... | collective-permute-start | bytes 393224 | tf_op jit(solution)/shard_map/ppermute | solution.py:34
  67.2 9.6 %collective-permute-start.26 = (bf16[128,512]{1,0:T(8,128)(2,1)S(1)}, bf16[128,512]{1,0:T(8,128)(2,1)S(1)}, u32[]{:S(2)}, u32[]{:S(2)}) collective-permute-start(bf16[128,512]{1,0:T(8,128)(2,1)S(1)} %get-tuple-element.64), channel_id=1, source_target_pairs={{0,3},{1,2},{2,1},{3,0},{4,7},{5,6},{6,5},{7,4},{8,11},{9,10},{10,... | collective-permute-start | bytes 393224 | tf_op jit(solution)/shard_map/ppermute | solution.py:34
  72.1 8.5 %collective-permute-start.12 = (bf16[128,512]{1,0:T(8,128)(2,1)S(1)}, bf16[128,512]{1,0:T(8,128)(2,1)S(1)}, u32[]{:S(2)}, u32[]{:S(2)}) collective-permute-start(bf16[128,512]{1,0:T(8,128)(2,1)S(1)} %get-tuple-element.59), channel_id=1, source_target_pairs={{0,1},{1,0},{2,3},{3,2},{4,5},{5,4},{6,7},{7,6},{8,9},{9,8},{10,11... | collective-permute-start | bytes 393224 | tf_op jit(solution)/shard_map/ppermute | solution.py:34
  74.2 11.9 %collective-permute-start.13 = (bf16[128,512]{1,0:T(8,128)(2,1)S(1)}, bf16[128,512]{1,0:T(8,128)(2,1)S(1)}, u32[]{:S(2)}, u32[]{:S(2)}) collective-permute-start(bf16[128,512]{1,0:T(8,128)(2,1)S(1)} %get-tuple-element.58), channel_id=1, source_target_pairs={{0,2},{1,3},{2,0},{3,1},{4,6},{5,7},{6,4},{7,5},{8,10},{9,11},{10,... | collective-permute-start | bytes 393224 | tf_op jit(solution)/shard_map/ppermute | solution.py:34
  74.7 11.3 %collective-permute-start.14 = (bf16[128,512]{1,0:T(8,128)(2,1)S(1)}, bf16[128,512]{1,0:T(8,128)(2,1)S(1)}, u32[]{:S(2)}, u32[]{:S(2)}) collective-permute-start(bf16[128,512]{1,0:T(8,128)(2,1)S(1)} %get-tuple-element.57), channel_id=1, source_target_pairs={{0,3},{1,2},{2,1},{3,0},{4,7},{5,6},{6,5},{7,4},{8,11},{9,10},{10,... | collective-permute-start | bytes 393224 | tf_op jit(solution)/shard_map/ppermute | solution.py:34
  77.8 12.3 %collective-permute-start.29 = (bf16[32,2048]{1,0:T(8,128)(2,1)S(1)}, bf16[32,2048]{1,0:T(8,128)(2,1)S(1)}, u32[]{:S(2)}, u32[]{:S(2)}) collective-permute-start(bf16[32,2048]{1,0:T(8,128)(2,1)S(1)} %get-tuple-element.62), channel_id=1, source_target_pairs={{0,24},{4,28},{8,16},{12,20},{16,8},{20,12},{24,0},{28,4},{1,25},{... | collective-permute-start | bytes 393224 | tf_op jit(solution)/shard_map/ppermute | solution.py:34
  79.6 11.0 %collective-permute-start.28 = (bf16[32,2048]{1,0:T(8,128)(2,1)S(1)}, bf16[32,2048]{1,0:T(8,128)(2,1)S(1)}, u32[]{:S(2)}, u32[]{:S(2)}) collective-permute-start(bf16[32,2048]{1,0:T(8,128)(2,1)S(1)} %get-tuple-element.63), channel_id=1, source_target_pairs={{0,16},{4,20},{8,24},{12,28},{16,0},{20,4},{24,8},{28,12},{1,17},{... | collective-permute-start | bytes 393224 | tf_op jit(solution)/shard_map/ppermute | solution.py:34
  80.6 10.0 %collective-permute-start.27 = (bf16[32,2048]{1,0:T(8,128)(2,1)S(1)}, bf16[32,2048]{1,0:T(8,128)(2,1)S(1)}, u32[]{:S(2)}, u32[]{:S(2)}) collective-permute-start(bf16[32,2048]{1,0:T(8,128)(2,1)S(1)} %get-tuple-element.61), channel_id=1, source_target_pairs={{0,8},{4,12},{8,0},{12,4},{16,24},{20,28},{24,16},{28,20},{1,9},{5... | collective-permute-start | bytes 393224 | tf_op jit(solution)/shard_map/ppermute | solution.py:34
  87.1 8.7 %collective-permute-start.20 = (bf16[32,2048]{1,0:T(8,128)(2,1)S(1)}, bf16[32,2048]{1,0:T(8,128)(2,1)S(1)}, u32[]{:S(2)}, u32[]{:S(2)}) collective-permute-start(bf16[32,2048]{1,0:T(8,128)(2,1)S(1)} %get-tuple-element.55), channel_id=1, source_target_pairs={{0,24},{4,28},{8,16},{12,20},{16,8},{20,12},{24,0},{28,4},{1,25},{... | collective-permute-start | bytes 393224 | tf_op jit(solution)/shard_map/ppermute | solution.py:34
  88.6 8.6 %collective-permute-start.19 = (bf16[32,2048]{1,0:T(8,128)(2,1)S(1)}, bf16[32,2048]{1,0:T(8,128)(2,1)S(1)}, u32[]{:S(2)}, u32[]{:S(2)}) collective-permute-start(bf16[32,2048]{1,0:T(8,128)(2,1)S(1)} %get-tuple-element.56), channel_id=1, source_target_pairs={{0,16},{4,20},{8,24},{12,28},{16,0},{20,4},{24,8},{28,12},{1,17},{... | collective-permute-start | bytes 393224 | tf_op jit(solution)/shard_map/ppermute | solution.py:34
  90.1 7.1 %collective-permute-start.18 = (bf16[32,2048]{1,0:T(8,128)(2,1)S(1)}, bf16[32,2048]{1,0:T(8,128)(2,1)S(1)}, u32[]{:S(2)}, u32[]{:S(2)}) collective-permute-start(bf16[32,2048]{1,0:T(8,128)(2,1)S(1)} %get-tuple-element.54), channel_id=1, source_target_pairs={{0,8},{4,12},{8,0},{12,4},{16,24},{20,28},{24,16},{28,20},{1,9},{5... | collective-permute-start | bytes 393224 | tf_op jit(solution)/shard_map/ppermute | solution.py:34
  90.7 9.3 %collective-permute-start.32 = (bf16[32,512]{1,0:T(8,128)(2,1)S(1)}, bf16[32,512]{1,0:T(8,128)(2,1)S(1)}, u32[]{:S(2)}, u32[]{:S(2)}) collective-permute-start(bf16[32,512]{1,0:T(8,128)(2,1)S(1)} %get-tuple-element.72), channel_id=1, source_target_pairs={{0,3},{1,2},{2,1},{3,0},{4,7},{5,6},{6,5},{7,4},{8,11},{9,10},{10,... | collective-permute-start | bytes 98312 | tf_op jit(solution)/shard_map/ppermute | solution.py:34
  92.6 9.2 %collective-permute-start.31 = (bf16[32,512]{1,0:T(8,128)(2,1)S(1)}, bf16[32,512]{1,0:T(8,128)(2,1)S(1)}, u32[]{:S(2)}, u32[]{:S(2)}) collective-permute-start(bf16[32,512]{1,0:T(8,128)(2,1)S(1)} %get-tuple-element.73), channel_id=1, source_target_pairs={{0,2},{1,3},{2,0},{3,1},{4,6},{5,7},{6,4},{7,5},{8,10},{9,11},{10,... | collective-permute-start | bytes 98312 | tf_op jit(solution)/shard_map/ppermute | solution.py:34
  95.8 6.0 %collective-permute-start.30 = (bf16[32,512]{1,0:T(8,128)(2,1)S(1)}, bf16[32,512]{1,0:T(8,128)(2,1)S(1)}, u32[]{:S(2)}, u32[]{:S(2)}) collective-permute-start(bf16[32,512]{1,0:T(8,128)(2,1)S(1)} %get-tuple-element.71), channel_id=1, source_target_pairs={{0,1},{1,0},{2,3},{3,2},{4,5},{5,4},{6,7},{7,6},{8,9},{9,8},{10,11... | collective-permute-start | bytes 98312 | tf_op jit(solution)/shard_map/ppermute | solution.py:34
  97.3 5.8 %collective-permute-start.23 = (bf16[32,512]{1,0:T(8,128)(2,1)S(1)}, bf16[32,512]{1,0:T(8,128)(2,1)S(1)}, u32[]{:S(2)}, u32[]{:S(2)}) collective-permute-start(bf16[32,512]{1,0:T(8,128)(2,1)S(1)} %get-tuple-element.69), channel_id=1, source_target_pairs={{0,3},{1,2},{2,1},{3,0},{4,7},{5,6},{6,5},{7,4},{8,11},{9,10},{10,... | collective-permute-start | bytes 98312 | tf_op jit(solution)/shard_map/ppermute | solution.py:34
  98.8 4.8 %collective-permute-start.22 = (bf16[32,512]{1,0:T(8,128)(2,1)S(1)}, bf16[32,512]{1,0:T(8,128)(2,1)S(1)}, u32[]{:S(2)}, u32[]{:S(2)}) collective-permute-start(bf16[32,512]{1,0:T(8,128)(2,1)S(1)} %get-tuple-element.70), channel_id=1, source_target_pairs={{0,2},{1,3},{2,0},{3,1},{4,6},{5,7},{6,4},{7,5},{8,10},{9,11},{10,... | collective-permute-start | bytes 98312 | tf_op jit(solution)/shard_map/ppermute | solution.py:34
  (5 other events, 38.6 us)

commit v6 on v5

--- a/solution.py
+++ b/solution.py
@@ -381,7 +381,7 @@
     chunk = lax.axis_index("heads") ^ jnp.arange(planes, dtype=jnp.int32)
     far = size // 2
     rows, width = global_in.shape
-    cuts = (rows // 2, rows // 2) if rows % 32 == 0 else (rows,)
+    cuts = (rows,)
 
     downs = [down_proj, swap(down_proj, "seq", 1)]
     hidden = up_proj.shape[1] // planes
@@ -402,14 +402,26 @@
     state_low = state.astype(BF16)
     inputs = gather_blocks(own_up[:, hidden:], "seq", 2, far)
     states = gather_blocks(state_low, "seq", 2, far)
-    parts = back_parts(chunk, states, downs, cuts)
-    slopes = [slope_of(pre) for pre in pre_parts(inputs, ups, hidden, cuts, parts[:1])]
-
-    grads = []
-    for part, slope in zip(parts, slopes):
+    own_parts = back_parts(chunk, states[:1], downs, (rows,))
+    parts = back_parts(chunk, states[1:], downs, cuts)
+    inputs = gather_blocks(own_up[:, hidden:], "seq", 2, far)
+    own_pre = pre_parts(inputs[:1], ups, hidden, (rows,), own_parts)
+    pres = pre_parts(inputs[1:], ups, hidden, cuts, parts[:1])
+
+    def grow(part, pre, blocks):
         terms = [part[0]] + [swap(part[k], "heads", k) for k in range(1, planes)]
-        grown = feed(chunk, terms, slope, ups, far)
-        own = sum(t.astype(F32) for t in scatter_terms([grown[j] for j in range(far)], "seq", 2))
+        return feed(chunk, terms, slope_of(pre), ups, blocks)
+
+    first_terms = [parts[0][0]] + [swap(parts[0][k], "heads", k) for k in range(1, planes)]
+    own_part, first_terms[2] = lax.optimization_barrier((own_parts[0], first_terms[2]))
+    first_grown = feed(chunk, first_terms, slope_of(pres[0]), ups, far - 1)
+    own_grown = grow(own_part, own_pre[0], 1)[0]
+    grads, start = [], 0
+    for part, pre, cut in zip(parts, pres, cuts):
+        grown = first_grown if start == 0 else grow(part, pre, far - 1)
+        blocks = [own_grown[start : start + cut]] + [grown[j] for j in range(far - 1)]
+        start += cut
+        own = sum(t.astype(F32) for t in scatter_terms(blocks, "seq", 2))
         blocks = [own[:, k * width : (k + 1) * width] for k in range(planes)]
         grads.append(
             blocks[0]

time: 105 us -> 105 us (level)
  starting transfers between devices: 49.9 us -> 39.9 us
  waiting for transfers between devices: 21.8 us -> 29.6 us
  Pallas kernels: 30 us -> 32.3 us
    ppermute x33 -> x27, starting transfers between devices: 43.6 us -> 33.5 us  [swap(): return lax.ppermute(x, axis, [(i, i ^ distance) for i in range(size)])]
    ppermute x33 -> x27, waiting for transfers between devices: 21.8 us -> 29.6 us  [swap(): return lax.ppermute(x, axis, [(i, i ^ distance) for i in range(size)])]
    pallas_call x1 -> x2, Pallas kernels: 1.32 us -> 2.67 us  [back_parts(): pl.pallas_call(functools.partial(back_kernel, len(states), cuts), in_spec...]
  transfers between devices with their start and end apart: 34 -> 28, of which waited for: 12 -> 13; matrix products, arithmetic and copies ran while one was open for 1% -> 0% of each run, Pallas kernels for 26% -> 28%
where the time goes in v6:
time: 105 us
  starting transfers between devices  39.9 us (38%)
  Pallas kernels  32.3 us (31%)
  waiting for transfers between devices  29.6 us (28%)
  other arithmetic  1.95 us (2%)
    ppermute x27, starting transfers between devices, swap(): return lax.ppermute(x, axis, [(i, i ^ distance) for i in range(size)])  33.5 us
    ppermute x27, waiting for transfers between devices, swap(): return lax.ppermute(x, axis, [(i, i ^ distance) for i in range(size)])  29.6 us
    pallas_call x1, Pallas kernels, attend(): pl.pallas_call(functools.partial(attend_kernel, min(256, block)), grid_sp...  16.7 us
    all_to_all x1, starting transfers between devices, local(): own_up = lax.all_to_all(bundle(up_proj, global_in, planes), 'heads', 0, 0)  6.32 us
    pallas_call x1, Pallas kernels, prepare(): pl.pallas_call(lambda *refs: prepare_kernel(*refs[:count], *refs[count +...  2.98 us
    pallas_call x1, Pallas kernels, project(): pl.pallas_call(functools.partial(project_kernel, len(terms)), in_specs=[p...  2.81 us
    pallas_call x1, Pallas kernels, bundle(): pl.pallas_call(bundle_kernel, out_shape=jax.ShapeDtypeStruct((size, hidde...  2.72 us
    pallas_call x2, Pallas kernels, back_parts(): pl.pallas_call(functools.partial(back_kernel, len(states), cuts), in_spec...  2.67 us
  transfers between devices with their start and end apart: 28, of which 13 were waited for; matrix products, arithmetic and copies ran while one was open for 0% of the time, Pallas kernels for 28%

profile of v6, /device:TPU:0, one launch (start us, length us, event | category | flops | bytes accessed | tf_op | source)
XLA Modules:
  0.0 104.7 jit_solution(1068171255818986895)
XLA Ops:
  0.6 2.7 %bundle.1 = bf16[4,320,512]{2,1,0:T(8,128)(2,1)} custom-call(bf16[512,1024]{1,0:T(8,128)(2,1)} %up_ref.1, bf16[64,512]{1,0:T(8,128)(2,1)} %in_ref.1), custom_call_target="tpu_custom_call" | custom-call | bytes 2097152 | tf_op jit(solution)/shard_map/bundle/pallas_call | solution.py:165
  3.4 6.3 %all-to-all-start = ((bf16[4,320,512]{2,1,0:T(8,128)(2,1)}), bf16[4,320,512]{2,1,0:T(8,128)(2,1)S(1)}, u32[]{:S(2)}, u32[]{:S(2)}) async-start(bf16[4,320,512]{2,1,0:T(8,128)(2,1)} %bundle.1), calls=%async_computation | async-start | bytes 2621440 | tf_op jit(solution)/shard_map/all_to_all | solution.py:388
  9.7 16.7 %attend.1 = (bf16[2048,512]{1,0:T(8,128)(2,1)}, bf16[4,64,1024]{2,1,0:T(8,128)(2,1)S(1)}, bf16[4,64,1024]{2,1,0:T(8,128)(2,1)S(1)}) custom-call(s32[8]{0:T(128)S(1)} %iota_xor_fusion.1.place_ref, bf16[2048,512]{1,0:T(8,128)(2,1)} %q_ref.1, bf16[2048,512]{1,0:T(8,128)(2,1)} %g_ref.1, bf16[512,512]{1,0:T(8,128)(2,1)} %k_ref.1, bf16[512,512]{1,0:T(8,128)(2,1)} %v_ref.1), custom_call_target="tpu_custom_call" | custom-call | flops 10737418240 | bytes 6291456 | tf_op jit(solution)/shard_map/attend/pallas_call | solution.py:120
  26.8 1.5 %collective-permute-done.refs_1_ = bf16[4,64,1024]{2,1,0:T(8,128)(2,1)S(1)} collective-permute-done((bf16[4,64,1024]{2,1,0:T(8,128)(2,1)S(1)}, bf16[4,64,1024]{2,1,0:T(8,128)(2,1)S(1)}, u32[]{:S(2)}, u32[]{:S(2)}) %collective-permute-start) | collective-permute-done | bytes 524320 | tf_op jit(solution)/shard_map/ppermute | solution.py:34
  29.2 1.5 %collective-permute-start.2 = (bf16[64,1024]{1,0:T(8,128)(2,1)}, bf16[64,1024]{1,0:T(8,128)(2,1)}, u32[]{:S(2)}, u32[]{:S(2)}) collective-permute-start(bf16[64,1024]{1,0:T(8,128)(2,1)} %get-tuple-element.29), channel_id=1, source_target_pairs={{0,8},{4,12},{8,0},{12,4},{16,24},{20,28},{24,16},{28,20},{1,9},{5... | collective-permute-start | bytes 393224 | tf_op jit(solution)/shard_map/ppermute | solution.py:34
  30.7 1.5 %collective-permute-start.3 = (bf16[64,1024]{1,0:T(8,128)(2,1)}, bf16[64,1024]{1,0:T(8,128)(2,1)}, u32[]{:S(2)}, u32[]{:S(2)}) collective-permute-start(bf16[64,1024]{1,0:T(8,128)(2,1)} %get-tuple-element.30), channel_id=1, source_target_pairs={{0,16},{4,20},{8,24},{12,28},{16,0},{20,4},{24,8},{28,12},{1,17},{... | collective-permute-start | bytes 393224 | tf_op jit(solution)/shard_map/ppermute | solution.py:34
  32.7 3.0 %prepare.1.refs_5_ = bf16[512,2048]{1,0:T(8,128)(2,1)S(1)} custom-call(bf16[2048,512]{1,0:T(8,128)(2,1)} %refs_0_.1, bf16[64,1024]{1,0:T(8,128)(2,1)S(1)} %get-tuple-element.28.refs_1_.refs_0_), custom_call_target="tpu_custom_call" | custom-call | bytes 4194304 | tf_op jit(solution)/shard_map/prepare/pallas_call | solution.py:214
  35.7 3.6 %collective-permute-done.3.refs_2_ = bf16[64,1024]{1,0:T(8,128)(2,1)} collective-permute-done((bf16[64,1024]{1,0:T(8,128)(2,1)}, bf16[64,1024]{1,0:T(8,128)(2,1)}, u32[]{:S(2)}, u32[]{:S(2)}) %collective-permute-start.3) | collective-permute-done | bytes 131104 | tf_op jit(solution)/shard_map/ppermute | solution.py:34
  39.3 2.8 %project.1 = (bf16[64,512]{1,0:T(8,128)(2,1)}, bf16[64,512]{1,0:T(8,128)(2,1)}, bf16[64,512]{1,0:T(8,128)(2,1)}, bf16[64,512]{1,0:T(8,128)(2,1)}) custom-call(s32[4]{0:T(128)S(1)} %iota_xor_fusion.chunk_ref, bf16[64,1024]{1,0:T(8,128)(2,1)S(1)} %get-tuple-element.28.refs_1_.refs_0_, bf16[64,1024]{1,0:T(8,128)(2,1)} %collective-permute-done.2.refs_1_, ...), custom_call_target="tpu_custom_call" | custom-call | flops 268435456 | bytes 4194304 | tf_op jit(solution)/shard_map/project/pallas_call | solution.py:248
  42.1 2.1 %collective-permute-start.5 = (bf16[64,512]{1,0:T(8,128)(2,1)}, bf16[64,512]{1,0:T(8,128)(2,1)S(1)}, u32[]{:S(2)}, u32[]{:S(2)}) collective-permute-start(bf16[64,512]{1,0:T(8,128)(2,1)} %get-tuple-element.34), channel_id=1, source_target_pairs={{0,1},{1,0},{2,3},{3,2},{4,5},{5,4},{6,7},{7,6},{8,9},{9,8},{10,11... | collective-permute-start | bytes 196616 | tf_op jit(solution)/shard_map/ppermute | solution.py:34
  44.2 2.4 %collective-permute-start.6 = (bf16[64,512]{1,0:T(8,128)(2,1)}, bf16[64,512]{1,0:T(8,128)(2,1)S(1)}, u32[]{:S(2)}, u32[]{:S(2)}) collective-permute-start(bf16[64,512]{1,0:T(8,128)(2,1)} %get-tuple-element.35), channel_id=1, source_target_pairs={{0,2},{1,3},{2,0},{3,1},{4,6},{5,7},{6,4},{7,5},{8,10},{9,11},{10,... | collective-permute-start | bytes 196616 | tf_op jit(solution)/shard_map/ppermute | solution.py:34
  47.1 5.0 %collective-permute-done.6 = bf16[64,512]{1,0:T(8,128)(2,1)S(1)} collective-permute-done((bf16[64,512]{1,0:T(8,128)(2,1)}, bf16[64,512]{1,0:T(8,128)(2,1)S(1)}, u32[]{:S(2)}, u32[]{:S(2)}) %collective-permute-start.6) | collective-permute-done | bytes 65568 | tf_op jit(solution)/shard_map/ppermute | solution.py:34
  53.8 1.6 %collective-permute-start.10 = (bf16[64,512]{1,0:T(8,128)(2,1)S(1)}, bf16[64,512]{1,0:T(8,128)(2,1)S(1)}, u32[]{:S(2)}, u32[]{:S(2)}) collective-permute-start(bf16[64,512]{1,0:T(8,128)(2,1)S(1)} %fusion.11.refs_0_), channel_id=1, source_target_pairs={{0,16},{4,20},{8,24},{12,28},{16,0},{20,4},{24,8},{28,12},{1,17},{... | collective-permute-start | bytes 196616 | tf_op jit(solution)/shard_map/ppermute | solution.py:34
  55.4 1.2 %collective-permute-start.11 = (bf16[64,512]{1,0:T(8,128)(2,1)S(1)}, bf16[64,512]{1,0:T(8,128)(2,1)S(1)}, u32[]{:S(2)}, u32[]{:S(2)}) collective-permute-start(bf16[64,512]{1,0:T(8,128)(2,1)S(1)} %fusion.11.refs_0_), channel_id=1, source_target_pairs={{0,24},{4,28},{8,16},{12,20},{16,8},{20,12},{24,0},{28,4},{1,25},{... | collective-permute-start | bytes 196616 | tf_op jit(solution)/shard_map/ppermute | solution.py:34
  57.3 1.3 %collective-permute-start.18 = (bf16[4,64,512]{2,1,0:T(8,128)(2,1)S(1)}, bf16[4,64,512]{2,1,0:T(8,128)(2,1)S(1)}, u32[]{:S(2)}, u32[]{:S(2)}) collective-permute-start(bf16[4,64,512]{2,1,0:T(8,128)(2,1)S(1)} %slice.56.refs_0_), channel_id=1, source_target_pairs={{0,8},{4,12},{8,0},{12,4},{16,24},{20,28},{24,16},{28,20},{1,9},{5... | collective-permute-start | bytes 786440 | tf_op jit(solution)/shard_map/ppermute | solution.py:34
  59.5 1.3 %back.2.refs_3_ = bf16[4,64,512]{2,1,0:T(8,128)(2,1)S(1)} custom-call(s32[4]{0:T(128)S(1)} %iota_xor_fusion.chunk_ref, bf16[64,512]{1,0:T(8,128)(2,1)S(1)} %fusion.11.refs_0_, bf16[1024,512]{1,0:T(8,128)(2,1)S(1)} %copy-done, bf16[1024,512]{1,0:T(8,128)(2,1)S(1)} %collective-permute-done.1.refs_2_.refs_4_), custom_call_target="tpu_custom_call" | custom-call | flops 134217728 | bytes 2097152 | tf_op jit(solution)/shard_map/back/pallas_call | solution.py:297
  60.8 1.5 %collective-permute-start.20 = (bf16[4,64,512]{2,1,0:T(8,128)(2,1)S(1)}, bf16[4,64,512]{2,1,0:T(8,128)(2,1)S(1)}, u32[]{:S(2)}, u32[]{:S(2)}) collective-permute-start(bf16[4,64,512]{2,1,0:T(8,128)(2,1)S(1)} %slice.56.refs_0_), channel_id=1, source_target_pairs={{0,24},{4,28},{8,16},{12,20},{16,8},{20,12},{24,0},{28,4},{1,25},{... | collective-permute-start | bytes 786440 | tf_op jit(solution)/shard_map/ppermute | solution.py:34
  62.3 1.4 %back.3.refs_5_ = bf16[4,192,512]{2,1,0:T(8,128)(2,1)S(1)} custom-call(s32[4]{0:T(128)S(1)} %iota_xor_fusion.chunk_ref, bf16[64,512]{1,0:T(8,128)(2,1)S(1)} %collective-permute-done.9.refs_0_, bf16[64,512]{1,0:T(8,128)(2,1)S(1)} %collective-permute-done.10.refs_1_, bf16[64,512]{1,0:T(8,128)(2,1)S(1)} %collective-permute-done.11.refs_2_, ...), custom_call_target="tpu_custom_call" | custom-call | flops 402653184 | bytes 2097152 | tf_op jit(solution)/shard_map/back/pallas_call | solution.py:297
  63.7 2.3 %collective-permute-start.12 = (bf16[192,512]{1,0:T(8,128)(2,1)S(1)}, bf16[192,512]{1,0:T(8,128)(2,1)S(1)}, u32[]{:S(2)}, u32[]{:S(2)}) collective-permute-start(bf16[192,512]{1,0:T(8,128)(2,1)S(1)} %get-tuple-element.54), channel_id=1, source_target_pairs={{0,2},{1,3},{2,0},{3,1},{4,6},{5,7},{6,4},{7,5},{8,10},{9,11},{10,... | collective-permute-start | bytes 589832 | tf_op jit(solution)/shard_map/ppermute | solution.py:34
  67.3 2.1 %collective-permute-start.17 = (bf16[192,512]{1,0:T(8,128)(2,1)S(1)}, bf16[192,512]{1,0:T(8,128)(2,1)S(1)}, u32[]{:S(2)}, u32[]{:S(2)}) collective-permute-start(bf16[192,512]{1,0:T(8,128)(2,1)S(1)} %get-tuple-element.51), channel_id=1, source_target_pairs={{0,3},{1,2},{2,1},{3,0},{4,7},{5,6},{6,5},{7,4},{8,11},{9,10},{10,... | collective-permute-start | bytes 589832 | tf_op jit(solution)/shard_map/ppermute | solution.py:34
  69.5 2.0 %collective-permute-done.20.refs_2_ = bf16[4,64,512]{2,1,0:T(8,128)(2,1)S(1)} collective-permute-done((bf16[4,64,512]{2,1,0:T(8,128)(2,1)S(1)}, bf16[4,64,512]{2,1,0:T(8,128)(2,1)S(1)}, u32[]{:S(2)}, u32[]{:S(2)}) %collective-permute-start.20) | collective-permute-done | bytes 262176 | tf_op jit(solution)/shard_map/ppermute | solution.py:34
  72.4 4.3 %collective-permute-done.12.refs_2_ = bf16[192,512]{1,0:T(8,128)(2,1)S(1)} collective-permute-done((bf16[192,512]{1,0:T(8,128)(2,1)S(1)}, bf16[192,512]{1,0:T(8,128)(2,1)S(1)}, u32[]{:S(2)}, u32[]{:S(2)}) %collective-permute-start.12) | collective-permute-done | bytes 196640 | tf_op jit(solution)/shard_map/ppermute | solution.py:34
  76.8 2.7 %collective-permute-done.17.refs_3_ = bf16[192,512]{1,0:T(8,128)(2,1)S(1)} collective-permute-done((bf16[192,512]{1,0:T(8,128)(2,1)S(1)}, bf16[192,512]{1,0:T(8,128)(2,1)S(1)}, u32[]{:S(2)}, u32[]{:S(2)}) %collective-permute-start.17) | collective-permute-done | bytes 196640 | tf_op jit(solution)/shard_map/ppermute | solution.py:34
  79.5 1.1 %feed.3 = bf16[3,64,2048]{2,1,0:T(8,128)(2,1)S(1)} custom-call(s32[4]{0:T(128)S(1)} %iota_xor_fusion.chunk_ref, bf16[192,512]{1,0:T(8,128)(2,1)S(1)} %get-tuple-element.53.refs_0_, bf16[192,512]{1,0:T(8,128)(2,1)S(1)} %collective-permute-done.16.refs_1_, bf16[192,512]{1,0:T(8,128)(2,1)S(1)} %collective-permute-done.12.refs_2_, ...), custom_call_target="tpu_custom_call" | custom-call | flops 402653184 | bytes 2097152 | tf_op jit(solution)/shard_map/feed/pallas_call | solution.py:362
  80.8 1.3 %collective-permute-start.21 = (bf16[64,2048]{1,0:T(8,128)(2,1)S(1)}, bf16[64,2048]{1,0:T(8,128)(2,1)S(1)}, u32[]{:S(2)}, u32[]{:S(2)}) collective-permute-start(bf16[64,2048]{1,0:T(8,128)(2,1)S(1)} %get-tuple-element.48), channel_id=1, source_target_pairs={{0,8},{4,12},{8,0},{12,4},{16,24},{20,28},{24,16},{28,20},{1,9},{5... | collective-permute-start | bytes 786440 | tf_op jit(solution)/shard_map/ppermute | solution.py:34
  82.9 1.4 %collective-permute-start.23 = (bf16[64,2048]{1,0:T(8,128)(2,1)S(1)}, bf16[64,2048]{1,0:T(8,128)(2,1)S(1)}, u32[]{:S(2)}, u32[]{:S(2)}) collective-permute-start(bf16[64,2048]{1,0:T(8,128)(2,1)S(1)} %get-tuple-element.49), channel_id=1, source_target_pairs={{0,24},{4,28},{8,16},{12,20},{16,8},{20,12},{24,0},{28,4},{1,25},{... | collective-permute-start | bytes 786440 | tf_op jit(solution)/shard_map/ppermute | solution.py:34
  85.1 2.8 %collective-permute-start.14 = (bf16[64,512]{1,0:T(8,128)(2,1)S(1)}, bf16[64,512]{1,0:T(8,128)(2,1)S(1)}, u32[]{:S(2)}, u32[]{:S(2)}) collective-permute-start(bf16[64,512]{1,0:T(8,128)(2,1)S(1)} %get-tuple-element.59), channel_id=1, source_target_pairs={{0,2},{1,3},{2,0},{3,1},{4,6},{5,7},{6,4},{7,5},{8,10},{9,11},{10,... | collective-permute-start | bytes 196616 | tf_op jit(solution)/shard_map/ppermute | solution.py:34
  87.8 1.8 %collective-permute-start.15 = (bf16[64,512]{1,0:T(8,128)(2,1)S(1)}, bf16[64,512]{1,0:T(8,128)(2,1)S(1)}, u32[]{:S(2)}, u32[]{:S(2)}) collective-permute-start(bf16[64,512]{1,0:T(8,128)(2,1)S(1)} %get-tuple-element.58), channel_id=1, source_target_pairs={{0,3},{1,2},{2,1},{3,0},{4,7},{5,6},{6,5},{7,4},{8,11},{9,10},{10,... | collective-permute-start | bytes 196616 | tf_op jit(solution)/shard_map/ppermute | solution.py:34
  90.3 4.3 %collective-permute-done.15.refs_3_ = bf16[64,512]{1,0:T(8,128)(2,1)S(1)} collective-permute-done((bf16[64,512]{1,0:T(8,128)(2,1)S(1)}, bf16[64,512]{1,0:T(8,128)(2,1)S(1)}, u32[]{:S(2)}, u32[]{:S(2)}) %collective-permute-start.15) | collective-permute-done | bytes 65568 | tf_op jit(solution)/shard_map/ppermute | solution.py:34
  95.9 2.0 %collective-permute-start.25 = (bf16[64,512]{1,0:T(8,128)(2,1)S(1)}, bf16[64,512]{1,0:T(8,128)(2,1)S(1)}, u32[]{:S(2)}, u32[]{:S(2)}) collective-permute-start(bf16[64,512]{1,0:T(8,128)(2,1)S(1)} %get-tuple-element.57), channel_id=1, source_target_pairs={{0,2},{1,3},{2,0},{3,1},{4,6},{5,7},{6,4},{7,5},{8,10},{9,11},{10,... | collective-permute-start | bytes 196616 | tf_op jit(solution)/shard_map/ppermute | solution.py:34
  98.0 2.4 %collective-permute-start.26 = (bf16[64,512]{1,0:T(8,128)(2,1)S(1)}, bf16[64,512]{1,0:T(8,128)(2,1)S(1)}, u32[]{:S(2)}, u32[]{:S(2)}) collective-permute-start(bf16[64,512]{1,0:T(8,128)(2,1)S(1)} %get-tuple-element.56), channel_id=1, source_target_pairs={{0,3},{1,2},{2,1},{3,0},{4,7},{5,6},{6,5},{7,4},{8,11},{9,10},{10,... | collective-permute-start | bytes 196616 | tf_op jit(solution)/shard_map/ppermute | solution.py:34
  101.2 2.8 %collective-permute-done.26 = bf16[64,512]{1,0:T(8,128)(2,1)S(1)} collective-permute-done((bf16[64,512]{1,0:T(8,128)(2,1)S(1)}, bf16[64,512]{1,0:T(8,128)(2,1)S(1)}, u32[]{:S(2)}, u32[]{:S(2)}) %collective-permute-start.26) | collective-permute-done | bytes 65568 | tf_op jit(solution)/shard_map/ppermute | solution.py:34
  (53 shorter events, 13.2 us)
Async XLA Ops:
  0.6 9.1 %copy-start = (bf16[1024,512]{1,0:T(8,128)(2,1)S(1)}, bf16[1024,512]{1,0:T(8,128)(2,1)}, u32[]{:S(2)}) copy-start(bf16[1024,512]{1,0:T(8,128)(2,1)} %refs_3_.1) | copy-start | bytes 3145732
  3.4 38.7 %all-to-all-start = ((bf16[4,320,512]{2,1,0:T(8,128)(2,1)}), bf16[4,320,512]{2,1,0:T(8,128)(2,1)S(1)}, u32[]{:S(2)}, u32[]{:S(2)}) async-start(bf16[4,320,512]{2,1,0:T(8,128)(2,1)} %bundle.1), calls=%async_computation | async-start | bytes 2621440 | tf_op jit(solution)/shard_map/all_to_all | solution.py:388
  9.7 23.0 %collective-permute-start.1 = (bf16[1024,512]{1,0:T(8,128)(2,1)S(1)}, bf16[1024,512]{1,0:T(8,128)(2,1)S(1)}, u32[]{:S(2)}, u32[]{:S(2)}) collective-permute-start(bf16[1024,512]{1,0:T(8,128)(2,1)S(1)} %copy-done), channel_id=1, source_target_pairs={{0,4},{4,0},{8,12},{12,8},{16,20},{20,16},{24,28},{28,24},{1,5},{5... | collective-permute-start | bytes 3145736 | tf_op jit(solution)/shard_map/ppermute | solution.py:34
  26.4 2.0 %collective-permute-start = (bf16[4,64,1024]{2,1,0:T(8,128)(2,1)S(1)}, bf16[4,64,1024]{2,1,0:T(8,128)(2,1)S(1)}, u32[]{:S(2)}, u32[]{:S(2)}) collective-permute-start(bf16[4,64,1024]{2,1,0:T(8,128)(2,1)S(1)} %get-tuple-element.26), channel_id=1, source_target_pairs={{0,4},{4,0},{8,12},{12,8},{16,20},{20,16},{24,28},{28,24},{1,5},{5... | collective-permute-start | bytes 1572872 | tf_op jit(solution)/shard_map/ppermute | solution.py:34
  29.2 6.5 %collective-permute-start.2 = (bf16[64,1024]{1,0:T(8,128)(2,1)}, bf16[64,1024]{1,0:T(8,128)(2,1)}, u32[]{:S(2)}, u32[]{:S(2)}) collective-permute-start(bf16[64,1024]{1,0:T(8,128)(2,1)} %get-tuple-element.29), channel_id=1, source_target_pairs={{0,8},{4,12},{8,0},{12,4},{16,24},{20,28},{24,16},{28,20},{1,9},{5... | collective-permute-start | bytes 393224 | tf_op jit(solution)/shard_map/ppermute | solution.py:34
  30.7 8.6 %collective-permute-start.3 = (bf16[64,1024]{1,0:T(8,128)(2,1)}, bf16[64,1024]{1,0:T(8,128)(2,1)}, u32[]{:S(2)}, u32[]{:S(2)}) collective-permute-start(bf16[64,1024]{1,0:T(8,128)(2,1)} %get-tuple-element.30), channel_id=1, source_target_pairs={{0,16},{4,20},{8,24},{12,28},{16,0},{20,4},{24,8},{28,12},{1,17},{... | collective-permute-start | bytes 393224 | tf_op jit(solution)/shard_map/ppermute | solution.py:34
  32.2 7.1 %collective-permute-start.4 = (bf16[64,1024]{1,0:T(8,128)(2,1)}, bf16[64,1024]{1,0:T(8,128)(2,1)}, u32[]{:S(2)}, u32[]{:S(2)}) collective-permute-start(bf16[64,1024]{1,0:T(8,128)(2,1)} %get-tuple-element.31), channel_id=1, source_target_pairs={{0,24},{4,28},{8,16},{12,20},{16,8},{20,12},{24,0},{28,4},{1,25},{... | collective-permute-start | bytes 393224 | tf_op jit(solution)/shard_map/ppermute | solution.py:34
  32.7 6.6 %copy-start.1 = (bf16[2048,512]{1,0:T(8,128)(2,1)S(1)}, bf16[2048,512]{1,0:T(8,128)(2,1)}, u32[]{:S(2)}) copy-start(bf16[2048,512]{1,0:T(8,128)(2,1)} %refs_4_.1) | copy-start | bytes 6291460
  42.1 10.8 %collective-permute-start.8 = (bf16[4,320,512]{2,1,0:T(8,128)(2,1)S(1)}, bf16[4,320,512]{2,1,0:T(8,128)(2,1)S(1)}, u32[]{:S(2)}, u32[]{:S(2)}) collective-permute-start(bf16[4,320,512]{2,1,0:T(8,128)(2,1)S(1)} %all-to-all-done.refs_1_.refs_5_.refs_3_), channel_id=1, source_target_pairs={{0,4},{4,0},{8,12},{12,8},{16,20},{20,16},{24,28},{28,24},{1,5},{5... | collective-permute-start | bytes 3932168 | tf_op jit(solution)/shard_map/ppermute | solution.py:34
  42.1 5.0 %collective-permute-start.5 = (bf16[64,512]{1,0:T(8,128)(2,1)}, bf16[64,512]{1,0:T(8,128)(2,1)S(1)}, u32[]{:S(2)}, u32[]{:S(2)}) collective-permute-start(bf16[64,512]{1,0:T(8,128)(2,1)} %get-tuple-element.34), channel_id=1, source_target_pairs={{0,1},{1,0},{2,3},{3,2},{4,5},{5,4},{6,7},{7,6},{8,9},{9,8},{10,11... | collective-permute-start | bytes 196616 | tf_op jit(solution)/shard_map/ppermute | solution.py:34
  44.2 7.9 %collective-permute-start.6 = (bf16[64,512]{1,0:T(8,128)(2,1)}, bf16[64,512]{1,0:T(8,128)(2,1)S(1)}, u32[]{:S(2)}, u32[]{:S(2)}) collective-permute-start(bf16[64,512]{1,0:T(8,128)(2,1)} %get-tuple-element.35), channel_id=1, source_target_pairs={{0,2},{1,3},{2,0},{3,1},{4,6},{5,7},{6,4},{7,5},{8,10},{9,11},{10,... | collective-permute-start | bytes 196616 | tf_op jit(solution)/shard_map/ppermute | solution.py:34
  46.5 6.3 %collective-permute-start.7 = (bf16[64,512]{1,0:T(8,128)(2,1)}, bf16[64,512]{1,0:T(8,128)(2,1)S(1)}, u32[]{:S(2)}, u32[]{:S(2)}) collective-permute-start(bf16[64,512]{1,0:T(8,128)(2,1)} %get-tuple-element.36), channel_id=1, source_target_pairs={{0,3},{1,2},{2,1},{3,0},{4,7},{5,6},{6,5},{7,4},{8,11},{9,10},{10,... | collective-permute-start | bytes 196616 | tf_op jit(solution)/shard_map/ppermute | solution.py:34
  53.8 7.0 %collective-permute-start.10 = (bf16[64,512]{1,0:T(8,128)(2,1)S(1)}, bf16[64,512]{1,0:T(8,128)(2,1)S(1)}, u32[]{:S(2)}, u32[]{:S(2)}) collective-permute-start(bf16[64,512]{1,0:T(8,128)(2,1)S(1)} %fusion.11.refs_0_), channel_id=1, source_target_pairs={{0,16},{4,20},{8,24},{12,28},{16,0},{20,4},{24,8},{28,12},{1,17},{... | collective-permute-start | bytes 196616 | tf_op jit(solution)/shard_map/ppermute | solution.py:34
  55.4 6.9 %collective-permute-start.11 = (bf16[64,512]{1,0:T(8,128)(2,1)S(1)}, bf16[64,512]{1,0:T(8,128)(2,1)S(1)}, u32[]{:S(2)}, u32[]{:S(2)}) collective-permute-start(bf16[64,512]{1,0:T(8,128)(2,1)S(1)} %fusion.11.refs_0_), channel_id=1, source_target_pairs={{0,24},{4,28},{8,16},{12,20},{16,8},{20,12},{24,0},{28,4},{1,25},{... | collective-permute-start | bytes 196616 | tf_op jit(solution)/shard_map/ppermute | solution.py:34
  56.5 5.7 %collective-permute-start.9 = (bf16[64,512]{1,0:T(8,128)(2,1)S(1)}, bf16[64,512]{1,0:T(8,128)(2,1)S(1)}, u32[]{:S(2)}, u32[]{:S(2)}) collective-permute-start(bf16[64,512]{1,0:T(8,128)(2,1)S(1)} %fusion.11.refs_0_), channel_id=1, source_target_pairs={{0,8},{4,12},{8,0},{12,4},{16,24},{20,28},{24,16},{28,20},{1,9},{5... | collective-permute-start | bytes 196616 | tf_op jit(solution)/shard_map/ppermute | solution.py:34
  57.3 10.0 %collective-permute-start.18 = (bf16[4,64,512]{2,1,0:T(8,128)(2,1)S(1)}, bf16[4,64,512]{2,1,0:T(8,128)(2,1)S(1)}, u32[]{:S(2)}, u32[]{:S(2)}) collective-permute-start(bf16[4,64,512]{2,1,0:T(8,128)(2,1)S(1)} %slice.56.refs_0_), channel_id=1, source_target_pairs={{0,8},{4,12},{8,0},{12,4},{16,24},{20,28},{24,16},{28,20},{1,9},{5... | collective-permute-start | bytes 786440 | tf_op jit(solution)/shard_map/ppermute | solution.py:34
  58.6 10.8 %collective-permute-start.19 = (bf16[4,64,512]{2,1,0:T(8,128)(2,1)S(1)}, bf16[4,64,512]{2,1,0:T(8,128)(2,1)S(1)}, u32[]{:S(2)}, u32[]{:S(2)}) collective-permute-start(bf16[4,64,512]{2,1,0:T(8,128)(2,1)S(1)} %slice.56.refs_0_), channel_id=1, source_target_pairs={{0,16},{4,20},{8,24},{12,28},{16,0},{20,4},{24,8},{28,12},{1,17},{... | collective-permute-start | bytes 786440 | tf_op jit(solution)/shard_map/ppermute | solution.py:34
  60.8 10.7 %collective-permute-start.20 = (bf16[4,64,512]{2,1,0:T(8,128)(2,1)S(1)}, bf16[4,64,512]{2,1,0:T(8,128)(2,1)S(1)}, u32[]{:S(2)}, u32[]{:S(2)}) collective-permute-start(bf16[4,64,512]{2,1,0:T(8,128)(2,1)S(1)} %slice.56.refs_0_), channel_id=1, source_target_pairs={{0,24},{4,28},{8,16},{12,20},{16,8},{20,12},{24,0},{28,4},{1,25},{... | collective-permute-start | bytes 786440 | tf_op jit(solution)/shard_map/ppermute | solution.py:34
  63.7 13.0 %collective-permute-start.12 = (bf16[192,512]{1,0:T(8,128)(2,1)S(1)}, bf16[192,512]{1,0:T(8,128)(2,1)S(1)}, u32[]{:S(2)}, u32[]{:S(2)}) collective-permute-start(bf16[192,512]{1,0:T(8,128)(2,1)S(1)} %get-tuple-element.54), channel_id=1, source_target_pairs={{0,2},{1,3},{2,0},{3,1},{4,6},{5,7},{6,4},{7,5},{8,10},{9,11},{10,... | collective-permute-start | bytes 589832 | tf_op jit(solution)/shard_map/ppermute | solution.py:34
  66.0 10.8 %collective-permute-start.16 = (bf16[192,512]{1,0:T(8,128)(2,1)S(1)}, bf16[192,512]{1,0:T(8,128)(2,1)S(1)}, u32[]{:S(2)}, u32[]{:S(2)}) collective-permute-start(bf16[192,512]{1,0:T(8,128)(2,1)S(1)} %get-tuple-element.52), channel_id=1, source_target_pairs={{0,1},{1,0},{2,3},{3,2},{4,5},{5,4},{6,7},{7,6},{8,9},{9,8},{10,11... | collective-permute-start | bytes 589832 | tf_op jit(solution)/shard_map/ppermute | solution.py:34
  67.3 12.2 %collective-permute-start.17 = (bf16[192,512]{1,0:T(8,128)(2,1)S(1)}, bf16[192,512]{1,0:T(8,128)(2,1)S(1)}, u32[]{:S(2)}, u32[]{:S(2)}) collective-permute-start(bf16[192,512]{1,0:T(8,128)(2,1)S(1)} %get-tuple-element.51), channel_id=1, source_target_pairs={{0,3},{1,2},{2,1},{3,0},{4,7},{5,6},{6,5},{7,4},{8,11},{9,10},{10,... | collective-permute-start | bytes 589832 | tf_op jit(solution)/shard_map/ppermute | solution.py:34
  76.8 11.1 %collective-permute-start.13 = (bf16[64,512]{1,0:T(8,128)(2,1)S(1)}, bf16[64,512]{1,0:T(8,128)(2,1)S(1)}, u32[]{:S(2)}, u32[]{:S(2)}) collective-permute-start(bf16[64,512]{1,0:T(8,128)(2,1)S(1)} %get-tuple-element.60), channel_id=1, source_target_pairs={{0,1},{1,0},{2,3},{3,2},{4,5},{5,4},{6,7},{7,6},{8,9},{9,8},{10,11... | collective-permute-start | bytes 196616 | tf_op jit(solution)/shard_map/ppermute | solution.py:34
  80.8 14.9 %collective-permute-start.21 = (bf16[64,2048]{1,0:T(8,128)(2,1)S(1)}, bf16[64,2048]{1,0:T(8,128)(2,1)S(1)}, u32[]{:S(2)}, u32[]{:S(2)}) collective-permute-start(bf16[64,2048]{1,0:T(8,128)(2,1)S(1)} %get-tuple-element.48), channel_id=1, source_target_pairs={{0,8},{4,12},{8,0},{12,4},{16,24},{20,28},{24,16},{28,20},{1,9},{5... | collective-permute-start | bytes 786440 | tf_op jit(solution)/shard_map/ppermute | solution.py:34
  82.1 13.6 %collective-permute-start.22 = (bf16[64,2048]{1,0:T(8,128)(2,1)S(1)}, bf16[64,2048]{1,0:T(8,128)(2,1)S(1)}, u32[]{:S(2)}, u32[]{:S(2)}) collective-permute-start(bf16[64,2048]{1,0:T(8,128)(2,1)S(1)} %get-tuple-element.50), channel_id=1, source_target_pairs={{0,16},{4,20},{8,24},{12,28},{16,0},{20,4},{24,8},{28,12},{1,17},{... | collective-permute-start | bytes 786440 | tf_op jit(solution)/shard_map/ppermute | solution.py:34
  82.9 12.8 %collective-permute-start.23 = (bf16[64,2048]{1,0:T(8,128)(2,1)S(1)}, bf16[64,2048]{1,0:T(8,128)(2,1)S(1)}, u32[]{:S(2)}, u32[]{:S(2)}) collective-permute-start(bf16[64,2048]{1,0:T(8,128)(2,1)S(1)} %get-tuple-element.49), channel_id=1, source_target_pairs={{0,24},{4,28},{8,16},{12,20},{16,8},{20,12},{24,0},{28,4},{1,25},{... | collective-permute-start | bytes 786440 | tf_op jit(solution)/shard_map/ppermute | solution.py:34
  85.1 5.2 %collective-permute-start.14 = (bf16[64,512]{1,0:T(8,128)(2,1)S(1)}, bf16[64,512]{1,0:T(8,128)(2,1)S(1)}, u32[]{:S(2)}, u32[]{:S(2)}) collective-permute-start(bf16[64,512]{1,0:T(8,128)(2,1)S(1)} %get-tuple-element.59), channel_id=1, source_target_pairs={{0,2},{1,3},{2,0},{3,1},{4,6},{5,7},{6,4},{7,5},{8,10},{9,11},{10,... | collective-permute-start | bytes 196616 | tf_op jit(solution)/shard_map/ppermute | solution.py:34
  87.8 6.8 %collective-permute-start.15 = (bf16[64,512]{1,0:T(8,128)(2,1)S(1)}, bf16[64,512]{1,0:T(8,128)(2,1)S(1)}, u32[]{:S(2)}, u32[]{:S(2)}) collective-permute-start(bf16[64,512]{1,0:T(8,128)(2,1)S(1)} %get-tuple-element.58), channel_id=1, source_target_pairs={{0,3},{1,2},{2,1},{3,0},{4,7},{5,6},{6,5},{7,4},{8,11},{9,10},{10,... | collective-permute-start | bytes 196616 | tf_op jit(solution)/shard_map/ppermute | solution.py:34
  94.6 9.4 %copy-start.2 = (bf16[64,512]{1,0:T(8,128)(2,1)S(1)}, bf16[64,512]{1,0:T(8,128)(2,1)}, u32[]{:S(2)}) copy-start(bf16[64,512]{1,0:T(8,128)(2,1)} %get-tuple-element.38) | copy-start | bytes 196612
  95.9 4.5 %collective-permute-start.24 = (bf16[64,512]{1,0:T(8,128)(2,1)S(1)}, bf16[64,512]{1,0:T(8,128)(2,1)S(1)}, u32[]{:S(2)}, u32[]{:S(2)}) collective-permute-start(bf16[64,512]{1,0:T(8,128)(2,1)S(1)} %get-tuple-element.55), channel_id=1, source_target_pairs={{0,1},{1,0},{2,3},{3,2},{4,5},{5,4},{6,7},{7,6},{8,9},{9,8},{10,11... | collective-permute-start | bytes 196616 | tf_op jit(solution)/shard_map/ppermute | solution.py:34
  95.9 5.2 %collective-permute-start.25 = (bf16[64,512]{1,0:T(8,128)(2,1)S(1)}, bf16[64,512]{1,0:T(8,128)(2,1)S(1)}, u32[]{:S(2)}, u32[]{:S(2)}) collective-permute-start(bf16[64,512]{1,0:T(8,128)(2,1)S(1)} %get-tuple-element.57), channel_id=1, source_target_pairs={{0,2},{1,3},{2,0},{3,1},{4,6},{5,7},{6,4},{7,5},{8,10},{9,11},{10,... | collective-permute-start | bytes 196616 | tf_op jit(solution)/shard_map/ppermute | solution.py:34
  98.0 6.1 %collective-permute-start.26 = (bf16[64,512]{1,0:T(8,128)(2,1)S(1)}, bf16[64,512]{1,0:T(8,128)(2,1)S(1)}, u32[]{:S(2)}, u32[]{:S(2)}) collective-permute-start(bf16[64,512]{1,0:T(8,128)(2,1)S(1)} %get-tuple-element.56), channel_id=1, source_target_pairs={{0,3},{1,2},{2,1},{3,0},{4,7},{5,6},{6,5},{7,4},{8,11},{9,10},{10,... | collective-permute-start | bytes 196616 | tf_op jit(solution)/shard_map/ppermute | solution.py:34

commit v7 on v6

--- a/solution.py
+++ b/solution.py
@@ -236,14 +236,14 @@
     block = part_refs[0].shape[1]
     for k, part_ref in enumerate(part_refs):
         at = pl.ds(pl.multiple_of(chunk_ref[k] * block, block), block)
-        part = dot(key_low, key_proj_ref[at, :], NT) + dot(value_low, value_proj_ref[:, at], NN)
+        part = dot(key_low, key_proj_ref[:, at], NN) + dot(value_low, value_proj_ref[:, at], NN)
         part_ref[...] = part.astype(BF16)
 
 
 def project(chunk, terms, key_proj, value_proj):
     rows, width = terms[0].shape
     size = chunk.shape[0]
-    block = key_proj.shape[0] // size
+    block = key_proj.shape[1] // size
     part = pltpu.HBM((rows, block), BF16)
     return pl.pallas_call(
         functools.partial(project_kernel, len(terms)),
@@ -392,8 +392,8 @@
     query_grad, even, odd = attend(place, *arrays, 0, heads)
     terms = scatter_rows([even], [odd], [])
     terms[0], downs[1] = lax.optimization_barrier((terms[0], downs[1]))
-    near = prepare([value_proj], terms[:1])
-    share = list(project(chunk, terms, key_proj, *near))
+    near = prepare([key_proj, value_proj], terms[:1])
+    share = list(project(chunk, terms, *near))
     own_up, share[0] = lax.optimization_barrier((own_up, share[0]))
     ups = [own_up, swap(own_up, "seq", 1)]
     shares = [share[0]] + [swap(share[k], "heads", k) for k in range(1, planes)]

time: 105 us -> 105 us (level)
  transfers between devices with their start and end apart: 28 -> 28, of which waited for: 13 -> 13; matrix products, arithmetic and copies ran while one was open for 0% -> 0% of each run, Pallas kernels for 28% -> 29%
where the time goes in v7:
time: 105 us; the launch traced here: 104 us
  starting transfers between devices  39.9 us (38%)
  Pallas kernels  32.8 us (31%)
  waiting for transfers between devices  28.8 us (27%)
  other arithmetic  1.95 us (2%)
    ppermute x27, starting transfers between devices, swap(): return lax.ppermute(x, axis, [(i, i ^ distance) for i in range(size)])  33.5 us
    ppermute x27, waiting for transfers between devices, swap(): return lax.ppermute(x, axis, [(i, i ^ distance) for i in range(size)])  28.8 us
    pallas_call x1, Pallas kernels, attend(): pl.pallas_call(functools.partial(attend_kernel, min(256, block)), grid_sp...  16.7 us
    all_to_all x1, starting transfers between devices, local(): own_up = lax.all_to_all(bundle(up_proj, global_in, planes), 'heads', 0, 0)  6.32 us
    pallas_call x1, Pallas kernels, prepare(): pl.pallas_call(lambda *refs: prepare_kernel(*refs[:count], *refs[count +...  3.7 us
    pallas_call x1, Pallas kernels, bundle(): pl.pallas_call(bundle_kernel, out_shape=jax.ShapeDtypeStruct((size, hidde...  2.72 us
    pallas_call x2, Pallas kernels, back_parts(): pl.pallas_call(functools.partial(back_kernel, len(states), cuts), in_spec...  2.67 us
    pallas_call x1, Pallas kernels, project(): pl.pallas_call(functools.partial(project_kernel, len(terms)), in_specs=[p...  2.56 us
  transfers between devices with their start and end apart: 28, of which 13 were waited for; matrix products, arithmetic and copies ran while one was open for 0% of the time, Pallas kernels for 29%

profile of v7, /device:TPU:0, one launch (start us, length us, event | category | flops | bytes accessed | tf_op | source)
XLA Modules:
  0.0 104.5 jit_solution(13227252995834770)
XLA Ops:
  0.6 2.7 %bundle.1 = bf16[4,320,512]{2,1,0:T(8,128)(2,1)} custom-call(bf16[512,1024]{1,0:T(8,128)(2,1)} %up_ref.1, bf16[64,512]{1,0:T(8,128)(2,1)} %in_ref.1), custom_call_target="tpu_custom_call" | custom-call | bytes 2097152 | tf_op jit(solution)/shard_map/bundle/pallas_call | solution.py:165
  3.4 6.3 %all-to-all-start = ((bf16[4,320,512]{2,1,0:T(8,128)(2,1)}), bf16[4,320,512]{2,1,0:T(8,128)(2,1)S(1)}, u32[]{:S(2)}, u32[]{:S(2)}) async-start(bf16[4,320,512]{2,1,0:T(8,128)(2,1)} %bundle.1), calls=%async_computation | async-start | bytes 2621440 | tf_op jit(solution)/shard_map/all_to_all | solution.py:388
  9.7 16.7 %attend.1 = (bf16[2048,512]{1,0:T(8,128)(2,1)}, bf16[4,64,1024]{2,1,0:T(8,128)(2,1)S(1)}, bf16[4,64,1024]{2,1,0:T(8,128)(2,1)S(1)}) custom-call(s32[8]{0:T(128)S(1)} %iota_xor_fusion.1.place_ref, bf16[2048,512]{1,0:T(8,128)(2,1)} %q_ref.1, bf16[2048,512]{1,0:T(8,128)(2,1)} %g_ref.1, bf16[512,512]{1,0:T(8,128)(2,1)} %k_ref.1, bf16[512,512]{1,0:T(8,128)(2,1)} %v_ref.1), custom_call_target="tpu_custom_call" | custom-call | flops 10737418240 | bytes 6291456 | tf_op jit(solution)/shard_map/attend/pallas_call | solution.py:120
  26.8 1.5 %collective-permute-done.refs_1_ = bf16[4,64,1024]{2,1,0:T(8,128)(2,1)S(1)} collective-permute-done((bf16[4,64,1024]{2,1,0:T(8,128)(2,1)S(1)}, bf16[4,64,1024]{2,1,0:T(8,128)(2,1)S(1)}, u32[]{:S(2)}, u32[]{:S(2)}) %collective-permute-start) | collective-permute-done | bytes 524320 | tf_op jit(solution)/shard_map/ppermute | solution.py:34
  29.2 1.5 %collective-permute-start.2 = (bf16[64,1024]{1,0:T(8,128)(2,1)}, bf16[64,1024]{1,0:T(8,128)(2,1)}, u32[]{:S(2)}, u32[]{:S(2)}) collective-permute-start(bf16[64,1024]{1,0:T(8,128)(2,1)} %get-tuple-element.31), channel_id=1, source_target_pairs={{0,8},{4,12},{8,0},{12,4},{16,24},{20,28},{24,16},{28,20},{1,9},{5... | collective-permute-start | bytes 393224 | tf_op jit(solution)/shard_map/ppermute | solution.py:34
  30.7 1.5 %collective-permute-start.3 = (bf16[64,1024]{1,0:T(8,128)(2,1)}, bf16[64,1024]{1,0:T(8,128)(2,1)}, u32[]{:S(2)}, u32[]{:S(2)}) collective-permute-start(bf16[64,1024]{1,0:T(8,128)(2,1)} %get-tuple-element.32), channel_id=1, source_target_pairs={{0,16},{4,20},{8,24},{12,28},{16,0},{20,4},{24,8},{28,12},{1,17},{... | collective-permute-start | bytes 393224 | tf_op jit(solution)/shard_map/ppermute | solution.py:34
  32.7 3.7 %prepare.1 = (bf16[512,2048]{1,0:T(8,128)(2,1)S(1)}, bf16[512,2048]{1,0:T(8,128)(2,1)S(1)}) custom-call(bf16[2048,512]{1,0:T(8,128)(2,1)} %refs_0_.1, bf16[2048,512]{1,0:T(8,128)(2,1)} %refs_1_.2, bf16[64,1024]{1,0:T(8,128)(2,1)S(1)} %get-tuple-element.30.refs_2_.refs_0_), custom_call_target="tpu_custom_call" | custom-call | bytes 4194304 | tf_op jit(solution)/shard_map/prepare/pallas_call | solution.py:214
  36.4 2.9 %collective-permute-done.3.refs_2_ = bf16[64,1024]{1,0:T(8,128)(2,1)} collective-permute-done((bf16[64,1024]{1,0:T(8,128)(2,1)}, bf16[64,1024]{1,0:T(8,128)(2,1)}, u32[]{:S(2)}, u32[]{:S(2)}) %collective-permute-start.3) | collective-permute-done | bytes 131104 | tf_op jit(solution)/shard_map/ppermute | solution.py:34
  39.3 2.6 %project.1 = (bf16[64,512]{1,0:T(8,128)(2,1)}, bf16[64,512]{1,0:T(8,128)(2,1)}, bf16[64,512]{1,0:T(8,128)(2,1)}, bf16[64,512]{1,0:T(8,128)(2,1)}) custom-call(s32[4]{0:T(128)S(1)} %iota_xor_fusion.chunk_ref, bf16[64,1024]{1,0:T(8,128)(2,1)S(1)} %get-tuple-element.30.refs_2_.refs_0_, bf16[64,1024]{1,0:T(8,128)(2,1)} %collective-permute-done.2.refs_1_, ...), custom_call_target="tpu_custom_call" | custom-call | flops 268435456 | bytes 4194304 | tf_op jit(solution)/shard_map/project/pallas_call | solution.py:248
  41.8 2.1 %collective-permute-start.5 = (bf16[64,512]{1,0:T(8,128)(2,1)}, bf16[64,512]{1,0:T(8,128)(2,1)S(1)}, u32[]{:S(2)}, u32[]{:S(2)}) collective-permute-start(bf16[64,512]{1,0:T(8,128)(2,1)} %get-tuple-element.38), channel_id=1, source_target_pairs={{0,1},{1,0},{2,3},{3,2},{4,5},{5,4},{6,7},{7,6},{8,9},{9,8},{10,11... | collective-permute-start | bytes 196616 | tf_op jit(solution)/shard_map/ppermute | solution.py:34
  43.9 2.4 %collective-permute-start.6 = (bf16[64,512]{1,0:T(8,128)(2,1)}, bf16[64,512]{1,0:T(8,128)(2,1)S(1)}, u32[]{:S(2)}, u32[]{:S(2)}) collective-permute-start(bf16[64,512]{1,0:T(8,128)(2,1)} %get-tuple-element.39), channel_id=1, source_target_pairs={{0,2},{1,3},{2,0},{3,1},{4,6},{5,7},{6,4},{7,5},{8,10},{9,11},{10,... | collective-permute-start | bytes 196616 | tf_op jit(solution)/shard_map/ppermute | solution.py:34
  46.8 5.0 %collective-permute-done.6 = bf16[64,512]{1,0:T(8,128)(2,1)S(1)} collective-permute-done((bf16[64,512]{1,0:T(8,128)(2,1)}, bf16[64,512]{1,0:T(8,128)(2,1)S(1)}, u32[]{:S(2)}, u32[]{:S(2)}) %collective-permute-start.6) | collective-permute-done | bytes 65568 | tf_op jit(solution)/shard_map/ppermute | solution.py:34
  53.5 1.6 %collective-permute-start.10 = (bf16[64,512]{1,0:T(8,128)(2,1)S(1)}, bf16[64,512]{1,0:T(8,128)(2,1)S(1)}, u32[]{:S(2)}, u32[]{:S(2)}) collective-permute-start(bf16[64,512]{1,0:T(8,128)(2,1)S(1)} %fusion.11.refs_0_), channel_id=1, source_target_pairs={{0,16},{4,20},{8,24},{12,28},{16,0},{20,4},{24,8},{28,12},{1,17},{... | collective-permute-start | bytes 196616 | tf_op jit(solution)/shard_map/ppermute | solution.py:34
  55.1 1.2 %collective-permute-start.11 = (bf16[64,512]{1,0:T(8,128)(2,1)S(1)}, bf16[64,512]{1,0:T(8,128)(2,1)S(1)}, u32[]{:S(2)}, u32[]{:S(2)}) collective-permute-start(bf16[64,512]{1,0:T(8,128)(2,1)S(1)} %fusion.11.refs_0_), channel_id=1, source_target_pairs={{0,24},{4,28},{8,16},{12,20},{16,8},{20,12},{24,0},{28,4},{1,25},{... | collective-permute-start | bytes 196616 | tf_op jit(solution)/shard_map/ppermute | solution.py:34
  57.1 1.3 %collective-permute-start.18 = (bf16[4,64,512]{2,1,0:T(8,128)(2,1)S(1)}, bf16[4,64,512]{2,1,0:T(8,128)(2,1)S(1)}, u32[]{:S(2)}, u32[]{:S(2)}) collective-permute-start(bf16[4,64,512]{2,1,0:T(8,128)(2,1)S(1)} %slice.56.refs_0_), channel_id=1, source_target_pairs={{0,8},{4,12},{8,0},{12,4},{16,24},{20,28},{24,16},{28,20},{1,9},{5... | collective-permute-start | bytes 786440 | tf_op jit(solution)/shard_map/ppermute | solution.py:34
  59.2 1.3 %back.2.refs_3_ = bf16[4,64,512]{2,1,0:T(8,128)(2,1)S(1)} custom-call(s32[4]{0:T(128)S(1)} %iota_xor_fusion.chunk_ref, bf16[64,512]{1,0:T(8,128)(2,1)S(1)} %fusion.11.refs_0_, bf16[1024,512]{1,0:T(8,128)(2,1)S(1)} %copy-done, bf16[1024,512]{1,0:T(8,128)(2,1)S(1)} %collective-permute-done.1.refs_2_.refs_4_), custom_call_target="tpu_custom_call" | custom-call | flops 134217728 | bytes 2097152 | tf_op jit(solution)/shard_map/back/pallas_call | solution.py:297
  60.5 1.5 %collective-permute-start.20 = (bf16[4,64,512]{2,1,0:T(8,128)(2,1)S(1)}, bf16[4,64,512]{2,1,0:T(8,128)(2,1)S(1)}, u32[]{:S(2)}, u32[]{:S(2)}) collective-permute-start(bf16[4,64,512]{2,1,0:T(8,128)(2,1)S(1)} %slice.56.refs_0_), channel_id=1, source_target_pairs={{0,24},{4,28},{8,16},{12,20},{16,8},{20,12},{24,0},{28,4},{1,25},{... | collective-permute-start | bytes 786440 | tf_op jit(solution)/shard_map/ppermute | solution.py:34
  62.0 1.4 %back.3.refs_5_ = bf16[4,192,512]{2,1,0:T(8,128)(2,1)S(1)} custom-call(s32[4]{0:T(128)S(1)} %iota_xor_fusion.chunk_ref, bf16[64,512]{1,0:T(8,128)(2,1)S(1)} %collective-permute-done.9.refs_0_, bf16[64,512]{1,0:T(8,128)(2,1)S(1)} %collective-permute-done.10.refs_1_, bf16[64,512]{1,0:T(8,128)(2,1)S(1)} %collective-permute-done.11.refs_2_, ...), custom_call_target="tpu_custom_call" | custom-call | flops 402653184 | bytes 2097152 | tf_op jit(solution)/shard_map/back/pallas_call | solution.py:297
  63.4 2.3 %collective-permute-start.12 = (bf16[192,512]{1,0:T(8,128)(2,1)S(1)}, bf16[192,512]{1,0:T(8,128)(2,1)S(1)}, u32[]{:S(2)}, u32[]{:S(2)}) collective-permute-start(bf16[192,512]{1,0:T(8,128)(2,1)S(1)} %get-tuple-element.58), channel_id=1, source_target_pairs={{0,2},{1,3},{2,0},{3,1},{4,6},{5,7},{6,4},{7,5},{8,10},{9,11},{10,... | collective-permute-start | bytes 589832 | tf_op jit(solution)/shard_map/ppermute | solution.py:34
  67.1 2.1 %collective-permute-start.17 = (bf16[192,512]{1,0:T(8,128)(2,1)S(1)}, bf16[192,512]{1,0:T(8,128)(2,1)S(1)}, u32[]{:S(2)}, u32[]{:S(2)}) collective-permute-start(bf16[192,512]{1,0:T(8,128)(2,1)S(1)} %get-tuple-element.55), channel_id=1, source_target_pairs={{0,3},{1,2},{2,1},{3,0},{4,7},{5,6},{6,5},{7,4},{8,11},{9,10},{10,... | collective-permute-start | bytes 589832 | tf_op jit(solution)/shard_map/ppermute | solution.py:34
  69.2 2.0 %collective-permute-done.20.refs_2_ = bf16[4,64,512]{2,1,0:T(8,128)(2,1)S(1)} collective-permute-done((bf16[4,64,512]{2,1,0:T(8,128)(2,1)S(1)}, bf16[4,64,512]{2,1,0:T(8,128)(2,1)S(1)}, u32[]{:S(2)}, u32[]{:S(2)}) %collective-permute-start.20) | collective-permute-done | bytes 262176 | tf_op jit(solution)/shard_map/ppermute | solution.py:34
  72.2 4.3 %collective-permute-done.12.refs_2_ = bf16[192,512]{1,0:T(8,128)(2,1)S(1)} collective-permute-done((bf16[192,512]{1,0:T(8,128)(2,1)S(1)}, bf16[192,512]{1,0:T(8,128)(2,1)S(1)}, u32[]{:S(2)}, u32[]{:S(2)}) %collective-permute-start.12) | collective-permute-done | bytes 196640 | tf_op jit(solution)/shard_map/ppermute | solution.py:34
  76.6 2.7 %collective-permute-done.17.refs_3_ = bf16[192,512]{1,0:T(8,128)(2,1)S(1)} collective-permute-done((bf16[192,512]{1,0:T(8,128)(2,1)S(1)}, bf16[192,512]{1,0:T(8,128)(2,1)S(1)}, u32[]{:S(2)}, u32[]{:S(2)}) %collective-permute-start.17) | collective-permute-done | bytes 196640 | tf_op jit(solution)/shard_map/ppermute | solution.py:34
  79.3 1.1 %feed.3 = bf16[3,64,2048]{2,1,0:T(8,128)(2,1)S(1)} custom-call(s32[4]{0:T(128)S(1)} %iota_xor_fusion.chunk_ref, bf16[192,512]{1,0:T(8,128)(2,1)S(1)} %get-tuple-element.57.refs_0_, bf16[192,512]{1,0:T(8,128)(2,1)S(1)} %collective-permute-done.16.refs_1_, bf16[192,512]{1,0:T(8,128)(2,1)S(1)} %collective-permute-done.12.refs_2_, ...), custom_call_target="tpu_custom_call" | custom-call | flops 402653184 | bytes 2097152 | tf_op jit(solution)/shard_map/feed/pallas_call | solution.py:362
  80.5 1.3 %collective-permute-start.21 = (bf16[64,2048]{1,0:T(8,128)(2,1)S(1)}, bf16[64,2048]{1,0:T(8,128)(2,1)S(1)}, u32[]{:S(2)}, u32[]{:S(2)}) collective-permute-start(bf16[64,2048]{1,0:T(8,128)(2,1)S(1)} %get-tuple-element.52), channel_id=1, source_target_pairs={{0,8},{4,12},{8,0},{12,4},{16,24},{20,28},{24,16},{28,20},{1,9},{5... | collective-permute-start | bytes 786440 | tf_op jit(solution)/shard_map/ppermute | solution.py:34
  82.6 1.4 %collective-permute-start.23 = (bf16[64,2048]{1,0:T(8,128)(2,1)S(1)}, bf16[64,2048]{1,0:T(8,128)(2,1)S(1)}, u32[]{:S(2)}, u32[]{:S(2)}) collective-permute-start(bf16[64,2048]{1,0:T(8,128)(2,1)S(1)} %get-tuple-element.53), channel_id=1, source_target_pairs={{0,24},{4,28},{8,16},{12,20},{16,8},{20,12},{24,0},{28,4},{1,25},{... | collective-permute-start | bytes 786440 | tf_op jit(solution)/shard_map/ppermute | solution.py:34
  84.8 2.8 %collective-permute-start.14 = (bf16[64,512]{1,0:T(8,128)(2,1)S(1)}, bf16[64,512]{1,0:T(8,128)(2,1)S(1)}, u32[]{:S(2)}, u32[]{:S(2)}) collective-permute-start(bf16[64,512]{1,0:T(8,128)(2,1)S(1)} %get-tuple-element.63), channel_id=1, source_target_pairs={{0,2},{1,3},{2,0},{3,1},{4,6},{5,7},{6,4},{7,5},{8,10},{9,11},{10,... | collective-permute-start | bytes 196616 | tf_op jit(solution)/shard_map/ppermute | solution.py:34
  87.6 1.8 %collective-permute-start.15 = (bf16[64,512]{1,0:T(8,128)(2,1)S(1)}, bf16[64,512]{1,0:T(8,128)(2,1)S(1)}, u32[]{:S(2)}, u32[]{:S(2)}) collective-permute-start(bf16[64,512]{1,0:T(8,128)(2,1)S(1)} %get-tuple-element.62), channel_id=1, source_target_pairs={{0,3},{1,2},{2,1},{3,0},{4,7},{5,6},{6,5},{7,4},{8,11},{9,10},{10,... | collective-permute-start | bytes 196616 | tf_op jit(solution)/shard_map/ppermute | solution.py:34
  90.0 4.3 %collective-permute-done.15.refs_3_ = bf16[64,512]{1,0:T(8,128)(2,1)S(1)} collective-permute-done((bf16[64,512]{1,0:T(8,128)(2,1)S(1)}, bf16[64,512]{1,0:T(8,128)(2,1)S(1)}, u32[]{:S(2)}, u32[]{:S(2)}) %collective-permute-start.15) | collective-permute-done | bytes 65568 | tf_op jit(solution)/shard_map/ppermute | solution.py:34
  95.7 2.0 %collective-permute-start.25 = (bf16[64,512]{1,0:T(8,128)(2,1)S(1)}, bf16[64,512]{1,0:T(8,128)(2,1)S(1)}, u32[]{:S(2)}, u32[]{:S(2)}) collective-permute-start(bf16[64,512]{1,0:T(8,128)(2,1)S(1)} %get-tuple-element.61), channel_id=1, source_target_pairs={{0,2},{1,3},{2,0},{3,1},{4,6},{5,7},{6,4},{7,5},{8,10},{9,11},{10,... | collective-permute-start | bytes 196616 | tf_op jit(solution)/shard_map/ppermute | solution.py:34
  97.7 2.4 %collective-permute-start.26 = (bf16[64,512]{1,0:T(8,128)(2,1)S(1)}, bf16[64,512]{1,0:T(8,128)(2,1)S(1)}, u32[]{:S(2)}, u32[]{:S(2)}) collective-permute-start(bf16[64,512]{1,0:T(8,128)(2,1)S(1)} %get-tuple-element.60), channel_id=1, source_target_pairs={{0,3},{1,2},{2,1},{3,0},{4,7},{5,6},{6,5},{7,4},{8,11},{9,10},{10,... | collective-permute-start | bytes 196616 | tf_op jit(solution)/shard_map/ppermute | solution.py:34
  100.9 2.8 %collective-permute-done.26 = bf16[64,512]{1,0:T(8,128)(2,1)S(1)} collective-permute-done((bf16[64,512]{1,0:T(8,128)(2,1)S(1)}, bf16[64,512]{1,0:T(8,128)(2,1)S(1)}, u32[]{:S(2)}, u32[]{:S(2)}) %collective-permute-start.26) | collective-permute-done | bytes 65568 | tf_op jit(solution)/shard_map/ppermute | solution.py:34
  (51 shorter events, 13.2 us)
Async XLA Ops:
  0.6 9.1 %copy-start = (bf16[1024,512]{1,0:T(8,128)(2,1)S(1)}, bf16[1024,512]{1,0:T(8,128)(2,1)}, u32[]{:S(2)}) copy-start(bf16[1024,512]{1,0:T(8,128)(2,1)} %refs_3_.1) | copy-start | bytes 3145732
  3.4 38.5 %all-to-all-start = ((bf16[4,320,512]{2,1,0:T(8,128)(2,1)}), bf16[4,320,512]{2,1,0:T(8,128)(2,1)S(1)}, u32[]{:S(2)}, u32[]{:S(2)}) async-start(bf16[4,320,512]{2,1,0:T(8,128)(2,1)} %bundle.1), calls=%async_computation | async-start | bytes 2621440 | tf_op jit(solution)/shard_map/all_to_all | solution.py:388
  9.7 23.0 %collective-permute-start.1 = (bf16[1024,512]{1,0:T(8,128)(2,1)S(1)}, bf16[1024,512]{1,0:T(8,128)(2,1)S(1)}, u32[]{:S(2)}, u32[]{:S(2)}) collective-permute-start(bf16[1024,512]{1,0:T(8,128)(2,1)S(1)} %copy-done), channel_id=1, source_target_pairs={{0,4},{4,0},{8,12},{12,8},{16,20},{20,16},{24,28},{28,24},{1,5},{5... | collective-permute-start | bytes 3145736 | tf_op jit(solution)/shard_map/ppermute | solution.py:34
  26.4 2.0 %collective-permute-start = (bf16[4,64,1024]{2,1,0:T(8,128)(2,1)S(1)}, bf16[4,64,1024]{2,1,0:T(8,128)(2,1)S(1)}, u32[]{:S(2)}, u32[]{:S(2)}) collective-permute-start(bf16[4,64,1024]{2,1,0:T(8,128)(2,1)S(1)} %get-tuple-element.28), channel_id=1, source_target_pairs={{0,4},{4,0},{8,12},{12,8},{16,20},{20,16},{24,28},{28,24},{1,5},{5... | collective-permute-start | bytes 1572872 | tf_op jit(solution)/shard_map/ppermute | solution.py:34
  29.2 7.2 %collective-permute-start.2 = (bf16[64,1024]{1,0:T(8,128)(2,1)}, bf16[64,1024]{1,0:T(8,128)(2,1)}, u32[]{:S(2)}, u32[]{:S(2)}) collective-permute-start(bf16[64,1024]{1,0:T(8,128)(2,1)} %get-tuple-element.31), channel_id=1, source_target_pairs={{0,8},{4,12},{8,0},{12,4},{16,24},{20,28},{24,16},{28,20},{1,9},{5... | collective-permute-start | bytes 393224 | tf_op jit(solution)/shard_map/ppermute | solution.py:34
  30.7 8.6 %collective-permute-start.3 = (bf16[64,1024]{1,0:T(8,128)(2,1)}, bf16[64,1024]{1,0:T(8,128)(2,1)}, u32[]{:S(2)}, u32[]{:S(2)}) collective-permute-start(bf16[64,1024]{1,0:T(8,128)(2,1)} %get-tuple-element.32), channel_id=1, source_target_pairs={{0,16},{4,20},{8,24},{12,28},{16,0},{20,4},{24,8},{28,12},{1,17},{... | collective-permute-start | bytes 393224 | tf_op jit(solution)/shard_map/ppermute | solution.py:34
  32.2 7.1 %collective-permute-start.4 = (bf16[64,1024]{1,0:T(8,128)(2,1)}, bf16[64,1024]{1,0:T(8,128)(2,1)}, u32[]{:S(2)}, u32[]{:S(2)}) collective-permute-start(bf16[64,1024]{1,0:T(8,128)(2,1)} %get-tuple-element.33), channel_id=1, source_target_pairs={{0,24},{4,28},{8,16},{12,20},{16,8},{20,12},{24,0},{28,4},{1,25},{... | collective-permute-start | bytes 393224 | tf_op jit(solution)/shard_map/ppermute | solution.py:34
  41.8 10.8 %collective-permute-start.8 = (bf16[4,320,512]{2,1,0:T(8,128)(2,1)S(1)}, bf16[4,320,512]{2,1,0:T(8,128)(2,1)S(1)}, u32[]{:S(2)}, u32[]{:S(2)}) collective-permute-start(bf16[4,320,512]{2,1,0:T(8,128)(2,1)S(1)} %all-to-all-done.refs_1_.refs_5_.refs_3_), channel_id=1, source_target_pairs={{0,4},{4,0},{8,12},{12,8},{16,20},{20,16},{24,28},{28,24},{1,5},{5... | collective-permute-start | bytes 3932168 | tf_op jit(solution)/shard_map/ppermute | solution.py:34
  41.8 5.0 %collective-permute-start.5 = (bf16[64,512]{1,0:T(8,128)(2,1)}, bf16[64,512]{1,0:T(8,128)(2,1)S(1)}, u32[]{:S(2)}, u32[]{:S(2)}) collective-permute-start(bf16[64,512]{1,0:T(8,128)(2,1)} %get-tuple-element.38), channel_id=1, source_target_pairs={{0,1},{1,0},{2,3},{3,2},{4,5},{5,4},{6,7},{7,6},{8,9},{9,8},{10,11... | collective-permute-start | bytes 196616 | tf_op jit(solution)/shard_map/ppermute | solution.py:34
  43.9 7.9 %collective-permute-start.6 = (bf16[64,512]{1,0:T(8,128)(2,1)}, bf16[64,512]{1,0:T(8,128)(2,1)S(1)}, u32[]{:S(2)}, u32[]{:S(2)}) collective-permute-start(bf16[64,512]{1,0:T(8,128)(2,1)} %get-tuple-element.39), channel_id=1, source_target_pairs={{0,2},{1,3},{2,0},{3,1},{4,6},{5,7},{6,4},{7,5},{8,10},{9,11},{10,... | collective-permute-start | bytes 196616 | tf_op jit(solution)/shard_map/ppermute | solution.py:34
  46.3 6.3 %collective-permute-start.7 = (bf16[64,512]{1,0:T(8,128)(2,1)}, bf16[64,512]{1,0:T(8,128)(2,1)S(1)}, u32[]{:S(2)}, u32[]{:S(2)}) collective-permute-start(bf16[64,512]{1,0:T(8,128)(2,1)} %get-tuple-element.40), channel_id=1, source_target_pairs={{0,3},{1,2},{2,1},{3,0},{4,7},{5,6},{6,5},{7,4},{8,11},{9,10},{10,... | collective-permute-start | bytes 196616 | tf_op jit(solution)/shard_map/ppermute | solution.py:34
  53.5 7.0 %collective-permute-start.10 = (bf16[64,512]{1,0:T(8,128)(2,1)S(1)}, bf16[64,512]{1,0:T(8,128)(2,1)S(1)}, u32[]{:S(2)}, u32[]{:S(2)}) collective-permute-start(bf16[64,512]{1,0:T(8,128)(2,1)S(1)} %fusion.11.refs_0_), channel_id=1, source_target_pairs={{0,16},{4,20},{8,24},{12,28},{16,0},{20,4},{24,8},{28,12},{1,17},{... | collective-permute-start | bytes 196616 | tf_op jit(solution)/shard_map/ppermute | solution.py:34
  55.1 6.9 %collective-permute-start.11 = (bf16[64,512]{1,0:T(8,128)(2,1)S(1)}, bf16[64,512]{1,0:T(8,128)(2,1)S(1)}, u32[]{:S(2)}, u32[]{:S(2)}) collective-permute-start(bf16[64,512]{1,0:T(8,128)(2,1)S(1)} %fusion.11.refs_0_), channel_id=1, source_target_pairs={{0,24},{4,28},{8,16},{12,20},{16,8},{20,12},{24,0},{28,4},{1,25},{... | collective-permute-start | bytes 196616 | tf_op jit(solution)/shard_map/ppermute | solution.py:34
  56.3 5.7 %collective-permute-start.9 = (bf16[64,512]{1,0:T(8,128)(2,1)S(1)}, bf16[64,512]{1,0:T(8,128)(2,1)S(1)}, u32[]{:S(2)}, u32[]{:S(2)}) collective-permute-start(bf16[64,512]{1,0:T(8,128)(2,1)S(1)} %fusion.11.refs_0_), channel_id=1, source_target_pairs={{0,8},{4,12},{8,0},{12,4},{16,24},{20,28},{24,16},{28,20},{1,9},{5... | collective-permute-start | bytes 196616 | tf_op jit(solution)/shard_map/ppermute | solution.py:34
  57.1 10.0 %collective-permute-start.18 = (bf16[4,64,512]{2,1,0:T(8,128)(2,1)S(1)}, bf16[4,64,512]{2,1,0:T(8,128)(2,1)S(1)}, u32[]{:S(2)}, u32[]{:S(2)}) collective-permute-start(bf16[4,64,512]{2,1,0:T(8,128)(2,1)S(1)} %slice.56.refs_0_), channel_id=1, source_target_pairs={{0,8},{4,12},{8,0},{12,4},{16,24},{20,28},{24,16},{28,20},{1,9},{5... | collective-permute-start | bytes 786440 | tf_op jit(solution)/shard_map/ppermute | solution.py:34
  58.4 10.8 %collective-permute-start.19 = (bf16[4,64,512]{2,1,0:T(8,128)(2,1)S(1)}, bf16[4,64,512]{2,1,0:T(8,128)(2,1)S(1)}, u32[]{:S(2)}, u32[]{:S(2)}) collective-permute-start(bf16[4,64,512]{2,1,0:T(8,128)(2,1)S(1)} %slice.56.refs_0_), channel_id=1, source_target_pairs={{0,16},{4,20},{8,24},{12,28},{16,0},{20,4},{24,8},{28,12},{1,17},{... | collective-permute-start | bytes 786440 | tf_op jit(solution)/shard_map/ppermute | solution.py:34
  60.5 10.7 %collective-permute-start.20 = (bf16[4,64,512]{2,1,0:T(8,128)(2,1)S(1)}, bf16[4,64,512]{2,1,0:T(8,128)(2,1)S(1)}, u32[]{:S(2)}, u32[]{:S(2)}) collective-permute-start(bf16[4,64,512]{2,1,0:T(8,128)(2,1)S(1)} %slice.56.refs_0_), channel_id=1, source_target_pairs={{0,24},{4,28},{8,16},{12,20},{16,8},{20,12},{24,0},{28,4},{1,25},{... | collective-permute-start | bytes 786440 | tf_op jit(solution)/shard_map/ppermute | solution.py:34
  63.4 13.0 %collective-permute-start.12 = (bf16[192,512]{1,0:T(8,128)(2,1)S(1)}, bf16[192,512]{1,0:T(8,128)(2,1)S(1)}, u32[]{:S(2)}, u32[]{:S(2)}) collective-permute-start(bf16[192,512]{1,0:T(8,128)(2,1)S(1)} %get-tuple-element.58), channel_id=1, source_target_pairs={{0,2},{1,3},{2,0},{3,1},{4,6},{5,7},{6,4},{7,5},{8,10},{9,11},{10,... | collective-permute-start | bytes 589832 | tf_op jit(solution)/shard_map/ppermute | solution.py:34
  65.8 10.8 %collective-permute-start.16 = (bf16[192,512]{1,0:T(8,128)(2,1)S(1)}, bf16[192,512]{1,0:T(8,128)(2,1)S(1)}, u32[]{:S(2)}, u32[]{:S(2)}) collective-permute-start(bf16[192,512]{1,0:T(8,128)(2,1)S(1)} %get-tuple-element.56), channel_id=1, source_target_pairs={{0,1},{1,0},{2,3},{3,2},{4,5},{5,4},{6,7},{7,6},{8,9},{9,8},{10,11... | collective-permute-start | bytes 589832 | tf_op jit(solution)/shard_map/ppermute | solution.py:34
  67.1 12.2 %collective-permute-start.17 = (bf16[192,512]{1,0:T(8,128)(2,1)S(1)}, bf16[192,512]{1,0:T(8,128)(2,1)S(1)}, u32[]{:S(2)}, u32[]{:S(2)}) collective-permute-start(bf16[192,512]{1,0:T(8,128)(2,1)S(1)} %get-tuple-element.55), channel_id=1, source_target_pairs={{0,3},{1,2},{2,1},{3,0},{4,7},{5,6},{6,5},{7,4},{8,11},{9,10},{10,... | collective-permute-start | bytes 589832 | tf_op jit(solution)/shard_map/ppermute | solution.py:34
  76.5 11.1 %collective-permute-start.13 = (bf16[64,512]{1,0:T(8,128)(2,1)S(1)}, bf16[64,512]{1,0:T(8,128)(2,1)S(1)}, u32[]{:S(2)}, u32[]{:S(2)}) collective-permute-start(bf16[64,512]{1,0:T(8,128)(2,1)S(1)} %get-tuple-element.64), channel_id=1, source_target_pairs={{0,1},{1,0},{2,3},{3,2},{4,5},{5,4},{6,7},{7,6},{8,9},{9,8},{10,11... | collective-permute-start | bytes 196616 | tf_op jit(solution)/shard_map/ppermute | solution.py:34
  80.5 14.9 %collective-permute-start.21 = (bf16[64,2048]{1,0:T(8,128)(2,1)S(1)}, bf16[64,2048]{1,0:T(8,128)(2,1)S(1)}, u32[]{:S(2)}, u32[]{:S(2)}) collective-permute-start(bf16[64,2048]{1,0:T(8,128)(2,1)S(1)} %get-tuple-element.52), channel_id=1, source_target_pairs={{0,8},{4,12},{8,0},{12,4},{16,24},{20,28},{24,16},{28,20},{1,9},{5... | collective-permute-start | bytes 786440 | tf_op jit(solution)/shard_map/ppermute | solution.py:34
  81.8 13.6 %collective-permute-start.22 = (bf16[64,2048]{1,0:T(8,128)(2,1)S(1)}, bf16[64,2048]{1,0:T(8,128)(2,1)S(1)}, u32[]{:S(2)}, u32[]{:S(2)}) collective-permute-start(bf16[64,2048]{1,0:T(8,128)(2,1)S(1)} %get-tuple-element.54), channel_id=1, source_target_pairs={{0,16},{4,20},{8,24},{12,28},{16,0},{20,4},{24,8},{28,12},{1,17},{... | collective-permute-start | bytes 786440 | tf_op jit(solution)/shard_map/ppermute | solution.py:34
  82.6 12.8 %collective-permute-start.23 = (bf16[64,2048]{1,0:T(8,128)(2,1)S(1)}, bf16[64,2048]{1,0:T(8,128)(2,1)S(1)}, u32[]{:S(2)}, u32[]{:S(2)}) collective-permute-start(bf16[64,2048]{1,0:T(8,128)(2,1)S(1)} %get-tuple-element.53), channel_id=1, source_target_pairs={{0,24},{4,28},{8,16},{12,20},{16,8},{20,12},{24,0},{28,4},{1,25},{... | collective-permute-start | bytes 786440 | tf_op jit(solution)/shard_map/ppermute | solution.py:34
  84.8 5.2 %collective-permute-start.14 = (bf16[64,512]{1,0:T(8,128)(2,1)S(1)}, bf16[64,512]{1,0:T(8,128)(2,1)S(1)}, u32[]{:S(2)}, u32[]{:S(2)}) collective-permute-start(bf16[64,512]{1,0:T(8,128)(2,1)S(1)} %get-tuple-element.63), channel_id=1, source_target_pairs={{0,2},{1,3},{2,0},{3,1},{4,6},{5,7},{6,4},{7,5},{8,10},{9,11},{10,... | collective-permute-start | bytes 196616 | tf_op jit(solution)/shard_map/ppermute | solution.py:34
  87.6 6.8 %collective-permute-start.15 = (bf16[64,512]{1,0:T(8,128)(2,1)S(1)}, bf16[64,512]{1,0:T(8,128)(2,1)S(1)}, u32[]{:S(2)}, u32[]{:S(2)}) collective-permute-start(bf16[64,512]{1,0:T(8,128)(2,1)S(1)} %get-tuple-element.62), channel_id=1, source_target_pairs={{0,3},{1,2},{2,1},{3,0},{4,7},{5,6},{6,5},{7,4},{8,11},{9,10},{10,... | collective-permute-start | bytes 196616 | tf_op jit(solution)/shard_map/ppermute | solution.py:34
  94.4 9.4 %copy-start.1 = (bf16[64,512]{1,0:T(8,128)(2,1)S(1)}, bf16[64,512]{1,0:T(8,128)(2,1)}, u32[]{:S(2)}) copy-start(bf16[64,512]{1,0:T(8,128)(2,1)} %get-tuple-element.42) | copy-start | bytes 196612
  95.6 4.5 %collective-permute-start.24 = (bf16[64,512]{1,0:T(8,128)(2,1)S(1)}, bf16[64,512]{1,0:T(8,128)(2,1)S(1)}, u32[]{:S(2)}, u32[]{:S(2)}) collective-permute-start(bf16[64,512]{1,0:T(8,128)(2,1)S(1)} %get-tuple-element.59), channel_id=1, source_target_pairs={{0,1},{1,0},{2,3},{3,2},{4,5},{5,4},{6,7},{7,6},{8,9},{9,8},{10,11... | collective-permute-start | bytes 196616 | tf_op jit(solution)/shard_map/ppermute | solution.py:34
  95.7 5.2 %collective-permute-start.25 = (bf16[64,512]{1,0:T(8,128)(2,1)S(1)}, bf16[64,512]{1,0:T(8,128)(2,1)S(1)}, u32[]{:S(2)}, u32[]{:S(2)}) collective-permute-start(bf16[64,512]{1,0:T(8,128)(2,1)S(1)} %get-tuple-element.61), channel_id=1, source_target_pairs={{0,2},{1,3},{2,0},{3,1},{4,6},{5,7},{6,4},{7,5},{8,10},{9,11},{10,... | collective-permute-start | bytes 196616 | tf_op jit(solution)/shard_map/ppermute | solution.py:34
  97.7 6.1 %collective-permute-start.26 = (bf16[64,512]{1,0:T(8,128)(2,1)S(1)}, bf16[64,512]{1,0:T(8,128)(2,1)S(1)}, u32[]{:S(2)}, u32[]{:S(2)}) collective-permute-start(bf16[64,512]{1,0:T(8,128)(2,1)S(1)} %get-tuple-element.60), channel_id=1, source_target_pairs={{0,3},{1,2},{2,1},{3,0},{4,7},{5,6},{6,5},{7,4},{8,11},{9,10},{10,... | collective-permute-start | bytes 196616 | tf_op jit(solution)/shard_map/ppermute | solution.py:34

commit v8 on v7

--- a/solution.py
+++ b/solution.py
@@ -405,8 +405,8 @@
     own_parts = back_parts(chunk, states[:1], downs, (rows,))
     parts = back_parts(chunk, states[1:], downs, cuts)
     inputs = gather_blocks(own_up[:, hidden:], "seq", 2, far)
-    own_pre = pre_parts(inputs[:1], ups, hidden, (rows,), own_parts)
-    pres = pre_parts(inputs[1:], ups, hidden, cuts, parts[:1])
+    pre = pre_parts(inputs, ups, hidden, cuts, parts[:1])[0]
+    own_pre, pres = [pre[:rows]], [pre[rows:]]
 
     def grow(part, pre, blocks):
         terms = [part[0]] + [swap(part[k], "heads", k) for k in range(1, planes)]

time: 105 us -> 104 us (level)
  transfers between devices with their start and end apart: 28 -> 28, of which waited for: 13 -> 13; matrix products, arithmetic and copies ran while one was open for 0% -> 0% of each run, Pallas kernels for 29% -> 28%
where the time goes in v8:
time: 104 us
  starting transfers between devices  39.8 us (38%)
  Pallas kernels  32 us (31%)
  waiting for transfers between devices  28.9 us (28%)
  other arithmetic  1.95 us (2%)
    ppermute x27, starting transfers between devices, swap(): return lax.ppermute(x, axis, [(i, i ^ distance) for i in range(size)])  33.5 us
    ppermute x27, waiting for transfers between devices, swap(): return lax.ppermute(x, axis, [(i, i ^ distance) for i in range(size)])  28.9 us
    pallas_call x1, Pallas kernels, attend(): pl.pallas_call(functools.partial(attend_kernel, min(256, block)), grid_sp...  16.7 us
    all_to_all x1, starting transfers between devices, local(): own_up = lax.all_to_all(bundle(up_proj, global_in, planes), 'heads', 0, 0)  6.32 us
    pallas_call x1, Pallas kernels, prepare(): pl.pallas_call(lambda *refs: prepare_kernel(*refs[:count], *refs[count +...  3.7 us
    pallas_call x1, Pallas kernels, bundle(): pl.pallas_call(bundle_kernel, out_shape=jax.ShapeDtypeStruct((size, hidde...  2.72 us
    pallas_call x2, Pallas kernels, back_parts(): pl.pallas_call(functools.partial(back_kernel, len(states), cuts), in_spec...  2.67 us
    pallas_call x1, Pallas kernels, project(): pl.pallas_call(functools.partial(project_kernel, len(terms)), in_specs=[p...  2.56 us
  transfers between devices with their start and end apart: 28, of which 13 were waited for; matrix products, arithmetic and copies ran while one was open for 0% of the time, Pallas kernels for 28%

profile of v8, /device:TPU:0, one launch (start us, length us, event | category | flops | bytes accessed | tf_op | source)
XLA Modules:
  0.0 103.7 jit_solution(7888695481400978665)
XLA Ops:
  0.6 2.7 %bundle.1 = bf16[4,320,512]{2,1,0:T(8,128)(2,1)} custom-call(bf16[512,1024]{1,0:T(8,128)(2,1)} %up_ref.1, bf16[64,512]{1,0:T(8,128)(2,1)} %in_ref.1), custom_call_target="tpu_custom_call" | custom-call | bytes 2097152 | tf_op jit(solution)/shard_map/bundle/pallas_call | solution.py:165
  3.4 6.3 %all-to-all-start = ((bf16[4,320,512]{2,1,0:T(8,128)(2,1)}), bf16[4,320,512]{2,1,0:T(8,128)(2,1)S(1)}, u32[]{:S(2)}, u32[]{:S(2)}) async-start(bf16[4,320,512]{2,1,0:T(8,128)(2,1)} %bundle.1), calls=%async_computation | async-start | bytes 2621440 | tf_op jit(solution)/shard_map/all_to_all | solution.py:388
  9.7 16.7 %attend.1 = (bf16[2048,512]{1,0:T(8,128)(2,1)}, bf16[4,64,1024]{2,1,0:T(8,128)(2,1)S(1)}, bf16[4,64,1024]{2,1,0:T(8,128)(2,1)S(1)}) custom-call(s32[8]{0:T(128)S(1)} %iota_xor_fusion.1.place_ref, bf16[2048,512]{1,0:T(8,128)(2,1)} %q_ref.1, bf16[2048,512]{1,0:T(8,128)(2,1)} %g_ref.1, bf16[512,512]{1,0:T(8,128)(2,1)} %k_ref.1, bf16[512,512]{1,0:T(8,128)(2,1)} %v_ref.1), custom_call_target="tpu_custom_call" | custom-call | flops 10737418240 | bytes 6291456 | tf_op jit(solution)/shard_map/attend/pallas_call | solution.py:120
  26.8 1.5 %collective-permute-done.refs_1_ = bf16[4,64,1024]{2,1,0:T(8,128)(2,1)S(1)} collective-permute-done((bf16[4,64,1024]{2,1,0:T(8,128)(2,1)S(1)}, bf16[4,64,1024]{2,1,0:T(8,128)(2,1)S(1)}, u32[]{:S(2)}, u32[]{:S(2)}) %collective-permute-start) | collective-permute-done | bytes 524320 | tf_op jit(solution)/shard_map/ppermute | solution.py:34
  29.2 1.5 %collective-permute-start.2 = (bf16[64,1024]{1,0:T(8,128)(2,1)}, bf16[64,1024]{1,0:T(8,128)(2,1)}, u32[]{:S(2)}, u32[]{:S(2)}) collective-permute-start(bf16[64,1024]{1,0:T(8,128)(2,1)} %get-tuple-element.31), channel_id=1, source_target_pairs={{0,8},{4,12},{8,0},{12,4},{16,24},{20,28},{24,16},{28,20},{1,9},{5... | collective-permute-start | bytes 393224 | tf_op jit(solution)/shard_map/ppermute | solution.py:34
  30.7 1.5 %collective-permute-start.3 = (bf16[64,1024]{1,0:T(8,128)(2,1)}, bf16[64,1024]{1,0:T(8,128)(2,1)}, u32[]{:S(2)}, u32[]{:S(2)}) collective-permute-start(bf16[64,1024]{1,0:T(8,128)(2,1)} %get-tuple-element.32), channel_id=1, source_target_pairs={{0,16},{4,20},{8,24},{12,28},{16,0},{20,4},{24,8},{28,12},{1,17},{... | collective-permute-start | bytes 393224 | tf_op jit(solution)/shard_map/ppermute | solution.py:34
  32.7 3.7 %prepare.1 = (bf16[512,2048]{1,0:T(8,128)(2,1)S(1)}, bf16[512,2048]{1,0:T(8,128)(2,1)S(1)}) custom-call(bf16[2048,512]{1,0:T(8,128)(2,1)} %refs_0_.1, bf16[2048,512]{1,0:T(8,128)(2,1)} %refs_1_.2, bf16[64,1024]{1,0:T(8,128)(2,1)S(1)} %get-tuple-element.30.refs_2_.refs_0_), custom_call_target="tpu_custom_call" | custom-call | bytes 4194304 | tf_op jit(solution)/shard_map/prepare/pallas_call | solution.py:214
  36.4 2.9 %collective-permute-done.3.refs_2_ = bf16[64,1024]{1,0:T(8,128)(2,1)} collective-permute-done((bf16[64,1024]{1,0:T(8,128)(2,1)}, bf16[64,1024]{1,0:T(8,128)(2,1)}, u32[]{:S(2)}, u32[]{:S(2)}) %collective-permute-start.3) | collective-permute-done | bytes 131104 | tf_op jit(solution)/shard_map/ppermute | solution.py:34
  39.3 2.6 %project.1 = (bf16[64,512]{1,0:T(8,128)(2,1)}, bf16[64,512]{1,0:T(8,128)(2,1)}, bf16[64,512]{1,0:T(8,128)(2,1)}, bf16[64,512]{1,0:T(8,128)(2,1)}) custom-call(s32[4]{0:T(128)S(1)} %iota_xor_fusion.chunk_ref, bf16[64,1024]{1,0:T(8,128)(2,1)S(1)} %get-tuple-element.30.refs_2_.refs_0_, bf16[64,1024]{1,0:T(8,128)(2,1)} %collective-permute-done.2.refs_1_, ...), custom_call_target="tpu_custom_call" | custom-call | flops 268435456 | bytes 4194304 | tf_op jit(solution)/shard_map/project/pallas_call | solution.py:248
  41.8 2.1 %collective-permute-start.5 = (bf16[64,512]{1,0:T(8,128)(2,1)}, bf16[64,512]{1,0:T(8,128)(2,1)S(1)}, u32[]{:S(2)}, u32[]{:S(2)}) collective-permute-start(bf16[64,512]{1,0:T(8,128)(2,1)} %get-tuple-element.38), channel_id=1, source_target_pairs={{0,1},{1,0},{2,3},{3,2},{4,5},{5,4},{6,7},{7,6},{8,9},{9,8},{10,11... | collective-permute-start | bytes 196616 | tf_op jit(solution)/shard_map/ppermute | solution.py:34
  43.9 2.4 %collective-permute-start.6 = (bf16[64,512]{1,0:T(8,128)(2,1)}, bf16[64,512]{1,0:T(8,128)(2,1)S(1)}, u32[]{:S(2)}, u32[]{:S(2)}) collective-permute-start(bf16[64,512]{1,0:T(8,128)(2,1)} %get-tuple-element.39), channel_id=1, source_target_pairs={{0,2},{1,3},{2,0},{3,1},{4,6},{5,7},{6,4},{7,5},{8,10},{9,11},{10,... | collective-permute-start | bytes 196616 | tf_op jit(solution)/shard_map/ppermute | solution.py:34
  46.8 5.0 %collective-permute-done.6 = bf16[64,512]{1,0:T(8,128)(2,1)S(1)} collective-permute-done((bf16[64,512]{1,0:T(8,128)(2,1)}, bf16[64,512]{1,0:T(8,128)(2,1)S(1)}, u32[]{:S(2)}, u32[]{:S(2)}) %collective-permute-start.6) | collective-permute-done | bytes 65568 | tf_op jit(solution)/shard_map/ppermute | solution.py:34
  53.5 1.6 %collective-permute-start.10 = (bf16[64,512]{1,0:T(8,128)(2,1)S(1)}, bf16[64,512]{1,0:T(8,128)(2,1)S(1)}, u32[]{:S(2)}, u32[]{:S(2)}) collective-permute-start(bf16[64,512]{1,0:T(8,128)(2,1)S(1)} %fusion.11.refs_0_), channel_id=1, source_target_pairs={{0,16},{4,20},{8,24},{12,28},{16,0},{20,4},{24,8},{28,12},{1,17},{... | collective-permute-start | bytes 196616 | tf_op jit(solution)/shard_map/ppermute | solution.py:34
  55.1 1.2 %collective-permute-start.11 = (bf16[64,512]{1,0:T(8,128)(2,1)S(1)}, bf16[64,512]{1,0:T(8,128)(2,1)S(1)}, u32[]{:S(2)}, u32[]{:S(2)}) collective-permute-start(bf16[64,512]{1,0:T(8,128)(2,1)S(1)} %fusion.11.refs_0_), channel_id=1, source_target_pairs={{0,24},{4,28},{8,16},{12,20},{16,8},{20,12},{24,0},{28,4},{1,25},{... | collective-permute-start | bytes 196616 | tf_op jit(solution)/shard_map/ppermute | solution.py:34
  57.1 1.3 %collective-permute-start.16 = (bf16[4,64,512]{2,1,0:T(8,128)(2,1)S(1)}, bf16[4,64,512]{2,1,0:T(8,128)(2,1)S(1)}, u32[]{:S(2)}, u32[]{:S(2)}) collective-permute-start(bf16[4,64,512]{2,1,0:T(8,128)(2,1)S(1)} %slice.62.refs_0_), channel_id=1, source_target_pairs={{0,8},{4,12},{8,0},{12,4},{16,24},{20,28},{24,16},{28,20},{1,9},{5... | collective-permute-start | bytes 786440 | tf_op jit(solution)/shard_map/ppermute | solution.py:34
  59.2 1.3 %back.2 = bf16[4,64,512]{2,1,0:T(8,128)(2,1)S(1)} custom-call(s32[4]{0:T(128)S(1)} %iota_xor_fusion.chunk_ref, bf16[64,512]{1,0:T(8,128)(2,1)S(1)} %fusion.11.refs_0_, bf16[1024,512]{1,0:T(8,128)(2,1)S(1)} %copy-done, bf16[1024,512]{1,0:T(8,128)(2,1)S(1)} %collective-permute-done.1.refs_2_.refs_4_), custom_call_target="tpu_custom_call" | custom-call | flops 134217728 | bytes 2097152 | tf_op jit(solution)/shard_map/back/pallas_call | solution.py:297
  60.5 1.5 %collective-permute-start.18 = (bf16[4,64,512]{2,1,0:T(8,128)(2,1)S(1)}, bf16[4,64,512]{2,1,0:T(8,128)(2,1)S(1)}, u32[]{:S(2)}, u32[]{:S(2)}) collective-permute-start(bf16[4,64,512]{2,1,0:T(8,128)(2,1)S(1)} %slice.62.refs_0_), channel_id=1, source_target_pairs={{0,24},{4,28},{8,16},{12,20},{16,8},{20,12},{24,0},{28,4},{1,25},{... | collective-permute-start | bytes 786440 | tf_op jit(solution)/shard_map/ppermute | solution.py:34
  62.0 1.4 %back.3.refs_6_ = bf16[4,192,512]{2,1,0:T(8,128)(2,1)S(1)} custom-call(s32[4]{0:T(128)S(1)} %iota_xor_fusion.chunk_ref, bf16[64,512]{1,0:T(8,128)(2,1)S(1)} %collective-permute-done.9.refs_0_, bf16[64,512]{1,0:T(8,128)(2,1)S(1)} %collective-permute-done.10.refs_1_, bf16[64,512]{1,0:T(8,128)(2,1)S(1)} %collective-permute-done.11.refs_2_, ...), custom_call_target="tpu_custom_call" | custom-call | flops 402653184 | bytes 2097152 | tf_op jit(solution)/shard_map/back/pallas_call | solution.py:297
  63.4 2.3 %collective-permute-start.12 = (bf16[192,512]{1,0:T(8,128)(2,1)S(1)}, bf16[192,512]{1,0:T(8,128)(2,1)S(1)}, u32[]{:S(2)}, u32[]{:S(2)}) collective-permute-start(bf16[192,512]{1,0:T(8,128)(2,1)S(1)} %get-tuple-element.58), channel_id=1, source_target_pairs={{0,2},{1,3},{2,0},{3,1},{4,6},{5,7},{6,4},{7,5},{8,10},{9,11},{10,... | collective-permute-start | bytes 589832 | tf_op jit(solution)/shard_map/ppermute | solution.py:34
  67.1 2.1 %collective-permute-start.20 = (bf16[192,512]{1,0:T(8,128)(2,1)S(1)}, bf16[192,512]{1,0:T(8,128)(2,1)S(1)}, u32[]{:S(2)}, u32[]{:S(2)}) collective-permute-start(bf16[192,512]{1,0:T(8,128)(2,1)S(1)} %get-tuple-element.55), channel_id=1, source_target_pairs={{0,3},{1,2},{2,1},{3,0},{4,7},{5,6},{6,5},{7,4},{8,11},{9,10},{10,... | collective-permute-start | bytes 589832 | tf_op jit(solution)/shard_map/ppermute | solution.py:34
  69.2 2.0 %collective-permute-done.18.refs_3_ = bf16[4,64,512]{2,1,0:T(8,128)(2,1)S(1)} collective-permute-done((bf16[4,64,512]{2,1,0:T(8,128)(2,1)S(1)}, bf16[4,64,512]{2,1,0:T(8,128)(2,1)S(1)}, u32[]{:S(2)}, u32[]{:S(2)}) %collective-permute-start.18) | collective-permute-done | bytes 262176 | tf_op jit(solution)/shard_map/ppermute | solution.py:34
  72.1 4.4 %collective-permute-done.12.refs_2_ = bf16[192,512]{1,0:T(8,128)(2,1)S(1)} collective-permute-done((bf16[192,512]{1,0:T(8,128)(2,1)S(1)}, bf16[192,512]{1,0:T(8,128)(2,1)S(1)}, u32[]{:S(2)}, u32[]{:S(2)}) %collective-permute-start.12) | collective-permute-done | bytes 196640 | tf_op jit(solution)/shard_map/ppermute | solution.py:34
  76.6 2.7 %collective-permute-done.20.refs_3_ = bf16[192,512]{1,0:T(8,128)(2,1)S(1)} collective-permute-done((bf16[192,512]{1,0:T(8,128)(2,1)S(1)}, bf16[192,512]{1,0:T(8,128)(2,1)S(1)}, u32[]{:S(2)}, u32[]{:S(2)}) %collective-permute-start.20) | collective-permute-done | bytes 196640 | tf_op jit(solution)/shard_map/ppermute | solution.py:34
  79.3 1.1 %feed.3 = bf16[3,64,2048]{2,1,0:T(8,128)(2,1)S(1)} custom-call(s32[4]{0:T(128)S(1)} %iota_xor_fusion.chunk_ref, bf16[192,512]{1,0:T(8,128)(2,1)S(1)} %get-tuple-element.57.refs_0_, bf16[192,512]{1,0:T(8,128)(2,1)S(1)} %collective-permute-done.19.refs_1_, bf16[192,512]{1,0:T(8,128)(2,1)S(1)} %collective-permute-done.12.refs_2_, ...), custom_call_target="tpu_custom_call" | custom-call | flops 402653184 | bytes 2097152 | tf_op jit(solution)/shard_map/feed/pallas_call | solution.py:362
  80.5 1.3 %collective-permute-start.21 = (bf16[64,2048]{1,0:T(8,128)(2,1)S(1)}, bf16[64,2048]{1,0:T(8,128)(2,1)S(1)}, u32[]{:S(2)}, u32[]{:S(2)}) collective-permute-start(bf16[64,2048]{1,0:T(8,128)(2,1)S(1)} %get-tuple-element.52), channel_id=1, source_target_pairs={{0,8},{4,12},{8,0},{12,4},{16,24},{20,28},{24,16},{28,20},{1,9},{5... | collective-permute-start | bytes 786440 | tf_op jit(solution)/shard_map/ppermute | solution.py:34
  82.6 1.4 %collective-permute-start.23 = (bf16[64,2048]{1,0:T(8,128)(2,1)S(1)}, bf16[64,2048]{1,0:T(8,128)(2,1)S(1)}, u32[]{:S(2)}, u32[]{:S(2)}) collective-permute-start(bf16[64,2048]{1,0:T(8,128)(2,1)S(1)} %get-tuple-element.53), channel_id=1, source_target_pairs={{0,24},{4,28},{8,16},{12,20},{16,8},{20,12},{24,0},{28,4},{1,25},{... | collective-permute-start | bytes 786440 | tf_op jit(solution)/shard_map/ppermute | solution.py:34
  84.1 2.7 %collective-permute-start.14 = (bf16[64,512]{1,0:T(8,128)(2,1)S(1)}, bf16[64,512]{1,0:T(8,128)(2,1)S(1)}, u32[]{:S(2)}, u32[]{:S(2)}) collective-permute-start(bf16[64,512]{1,0:T(8,128)(2,1)S(1)} %get-tuple-element.63), channel_id=1, source_target_pairs={{0,2},{1,3},{2,0},{3,1},{4,6},{5,7},{6,4},{7,5},{8,10},{9,11},{10,... | collective-permute-start | bytes 196616 | tf_op jit(solution)/shard_map/ppermute | solution.py:34
  86.8 1.8 %collective-permute-start.15 = (bf16[64,512]{1,0:T(8,128)(2,1)S(1)}, bf16[64,512]{1,0:T(8,128)(2,1)S(1)}, u32[]{:S(2)}, u32[]{:S(2)}) collective-permute-start(bf16[64,512]{1,0:T(8,128)(2,1)S(1)} %get-tuple-element.62), channel_id=1, source_target_pairs={{0,3},{1,2},{2,1},{3,0},{4,7},{5,6},{6,5},{7,4},{8,11},{9,10},{10,... | collective-permute-start | bytes 196616 | tf_op jit(solution)/shard_map/ppermute | solution.py:34
  89.2 4.3 %collective-permute-done.15.refs_3_ = bf16[64,512]{1,0:T(8,128)(2,1)S(1)} collective-permute-done((bf16[64,512]{1,0:T(8,128)(2,1)S(1)}, bf16[64,512]{1,0:T(8,128)(2,1)S(1)}, u32[]{:S(2)}, u32[]{:S(2)}) %collective-permute-start.15) | collective-permute-done | bytes 65568 | tf_op jit(solution)/shard_map/ppermute | solution.py:34
  94.9 2.0 %collective-permute-start.25 = (bf16[64,512]{1,0:T(8,128)(2,1)S(1)}, bf16[64,512]{1,0:T(8,128)(2,1)S(1)}, u32[]{:S(2)}, u32[]{:S(2)}) collective-permute-start(bf16[64,512]{1,0:T(8,128)(2,1)S(1)} %get-tuple-element.61), channel_id=1, source_target_pairs={{0,2},{1,3},{2,0},{3,1},{4,6},{5,7},{6,4},{7,5},{8,10},{9,11},{10,... | collective-permute-start | bytes 196616 | tf_op jit(solution)/shard_map/ppermute | solution.py:34
  96.9 2.4 %collective-permute-start.26 = (bf16[64,512]{1,0:T(8,128)(2,1)S(1)}, bf16[64,512]{1,0:T(8,128)(2,1)S(1)}, u32[]{:S(2)}, u32[]{:S(2)}) collective-permute-start(bf16[64,512]{1,0:T(8,128)(2,1)S(1)} %get-tuple-element.60), channel_id=1, source_target_pairs={{0,3},{1,2},{2,1},{3,0},{4,7},{5,6},{6,5},{7,4},{8,11},{9,10},{10,... | collective-permute-start | bytes 196616 | tf_op jit(solution)/shard_map/ppermute | solution.py:34
  100.1 2.8 %collective-permute-done.26 = bf16[64,512]{1,0:T(8,128)(2,1)S(1)} collective-permute-done((bf16[64,512]{1,0:T(8,128)(2,1)S(1)}, bf16[64,512]{1,0:T(8,128)(2,1)S(1)}, u32[]{:S(2)}, u32[]{:S(2)}) %collective-permute-start.26) | collective-permute-done | bytes 65568 | tf_op jit(solution)/shard_map/ppermute | solution.py:34
  (50 shorter events, 12.3 us)
Async XLA Ops:
  0.6 9.1 %copy-start = (bf16[1024,512]{1,0:T(8,128)(2,1)S(1)}, bf16[1024,512]{1,0:T(8,128)(2,1)}, u32[]{:S(2)}) copy-start(bf16[1024,512]{1,0:T(8,128)(2,1)} %refs_3_.1) | copy-start | bytes 3145732
  3.4 38.5 %all-to-all-start = ((bf16[4,320,512]{2,1,0:T(8,128)(2,1)}), bf16[4,320,512]{2,1,0:T(8,128)(2,1)S(1)}, u32[]{:S(2)}, u32[]{:S(2)}) async-start(bf16[4,320,512]{2,1,0:T(8,128)(2,1)} %bundle.1), calls=%async_computation | async-start | bytes 2621440 | tf_op jit(solution)/shard_map/all_to_all | solution.py:388
  9.7 23.0 %collective-permute-start.1 = (bf16[1024,512]{1,0:T(8,128)(2,1)S(1)}, bf16[1024,512]{1,0:T(8,128)(2,1)S(1)}, u32[]{:S(2)}, u32[]{:S(2)}) collective-permute-start(bf16[1024,512]{1,0:T(8,128)(2,1)S(1)} %copy-done), channel_id=1, source_target_pairs={{0,4},{4,0},{8,12},{12,8},{16,20},{20,16},{24,28},{28,24},{1,5},{5... | collective-permute-start | bytes 3145736 | tf_op jit(solution)/shard_map/ppermute | solution.py:34
  26.4 2.0 %collective-permute-start = (bf16[4,64,1024]{2,1,0:T(8,128)(2,1)S(1)}, bf16[4,64,1024]{2,1,0:T(8,128)(2,1)S(1)}, u32[]{:S(2)}, u32[]{:S(2)}) collective-permute-start(bf16[4,64,1024]{2,1,0:T(8,128)(2,1)S(1)} %get-tuple-element.28), channel_id=1, source_target_pairs={{0,4},{4,0},{8,12},{12,8},{16,20},{20,16},{24,28},{28,24},{1,5},{5... | collective-permute-start | bytes 1572872 | tf_op jit(solution)/shard_map/ppermute | solution.py:34
  29.2 7.2 %collective-permute-start.2 = (bf16[64,1024]{1,0:T(8,128)(2,1)}, bf16[64,1024]{1,0:T(8,128)(2,1)}, u32[]{:S(2)}, u32[]{:S(2)}) collective-permute-start(bf16[64,1024]{1,0:T(8,128)(2,1)} %get-tuple-element.31), channel_id=1, source_target_pairs={{0,8},{4,12},{8,0},{12,4},{16,24},{20,28},{24,16},{28,20},{1,9},{5... | collective-permute-start | bytes 393224 | tf_op jit(solution)/shard_map/ppermute | solution.py:34
  30.7 8.6 %collective-permute-start.3 = (bf16[64,1024]{1,0:T(8,128)(2,1)}, bf16[64,1024]{1,0:T(8,128)(2,1)}, u32[]{:S(2)}, u32[]{:S(2)}) collective-permute-start(bf16[64,1024]{1,0:T(8,128)(2,1)} %get-tuple-element.32), channel_id=1, source_target_pairs={{0,16},{4,20},{8,24},{12,28},{16,0},{20,4},{24,8},{28,12},{1,17},{... | collective-permute-start | bytes 393224 | tf_op jit(solution)/shard_map/ppermute | solution.py:34
  32.2 7.1 %collective-permute-start.4 = (bf16[64,1024]{1,0:T(8,128)(2,1)}, bf16[64,1024]{1,0:T(8,128)(2,1)}, u32[]{:S(2)}, u32[]{:S(2)}) collective-permute-start(bf16[64,1024]{1,0:T(8,128)(2,1)} %get-tuple-element.33), channel_id=1, source_target_pairs={{0,24},{4,28},{8,16},{12,20},{16,8},{20,12},{24,0},{28,4},{1,25},{... | collective-permute-start | bytes 393224 | tf_op jit(solution)/shard_map/ppermute | solution.py:34
  41.8 10.8 %collective-permute-start.8 = (bf16[4,320,512]{2,1,0:T(8,128)(2,1)S(1)}, bf16[4,320,512]{2,1,0:T(8,128)(2,1)S(1)}, u32[]{:S(2)}, u32[]{:S(2)}) collective-permute-start(bf16[4,320,512]{2,1,0:T(8,128)(2,1)S(1)} %all-to-all-done.refs_4_.refs_5_), channel_id=1, source_target_pairs={{0,4},{4,0},{8,12},{12,8},{16,20},{20,16},{24,28},{28,24},{1,5},{5... | collective-permute-start | bytes 3932168 | tf_op jit(solution)/shard_map/ppermute | solution.py:34
  41.8 5.0 %collective-permute-start.5 = (bf16[64,512]{1,0:T(8,128)(2,1)}, bf16[64,512]{1,0:T(8,128)(2,1)S(1)}, u32[]{:S(2)}, u32[]{:S(2)}) collective-permute-start(bf16[64,512]{1,0:T(8,128)(2,1)} %get-tuple-element.38), channel_id=1, source_target_pairs={{0,1},{1,0},{2,3},{3,2},{4,5},{5,4},{6,7},{7,6},{8,9},{9,8},{10,11... | collective-permute-start | bytes 196616 | tf_op jit(solution)/shard_map/ppermute | solution.py:34
  43.9 7.9 %collective-permute-start.6 = (bf16[64,512]{1,0:T(8,128)(2,1)}, bf16[64,512]{1,0:T(8,128)(2,1)S(1)}, u32[]{:S(2)}, u32[]{:S(2)}) collective-permute-start(bf16[64,512]{1,0:T(8,128)(2,1)} %get-tuple-element.39), channel_id=1, source_target_pairs={{0,2},{1,3},{2,0},{3,1},{4,6},{5,7},{6,4},{7,5},{8,10},{9,11},{10,... | collective-permute-start | bytes 196616 | tf_op jit(solution)/shard_map/ppermute | solution.py:34
  46.3 6.3 %collective-permute-start.7 = (bf16[64,512]{1,0:T(8,128)(2,1)}, bf16[64,512]{1,0:T(8,128)(2,1)S(1)}, u32[]{:S(2)}, u32[]{:S(2)}) collective-permute-start(bf16[64,512]{1,0:T(8,128)(2,1)} %get-tuple-element.40), channel_id=1, source_target_pairs={{0,3},{1,2},{2,1},{3,0},{4,7},{5,6},{6,5},{7,4},{8,11},{9,10},{10,... | collective-permute-start | bytes 196616 | tf_op jit(solution)/shard_map/ppermute | solution.py:34
  53.5 7.0 %collective-permute-start.10 = (bf16[64,512]{1,0:T(8,128)(2,1)S(1)}, bf16[64,512]{1,0:T(8,128)(2,1)S(1)}, u32[]{:S(2)}, u32[]{:S(2)}) collective-permute-start(bf16[64,512]{1,0:T(8,128)(2,1)S(1)} %fusion.11.refs_0_), channel_id=1, source_target_pairs={{0,16},{4,20},{8,24},{12,28},{16,0},{20,4},{24,8},{28,12},{1,17},{... | collective-permute-start | bytes 196616 | tf_op jit(solution)/shard_map/ppermute | solution.py:34
  55.1 6.9 %collective-permute-start.11 = (bf16[64,512]{1,0:T(8,128)(2,1)S(1)}, bf16[64,512]{1,0:T(8,128)(2,1)S(1)}, u32[]{:S(2)}, u32[]{:S(2)}) collective-permute-start(bf16[64,512]{1,0:T(8,128)(2,1)S(1)} %fusion.11.refs_0_), channel_id=1, source_target_pairs={{0,24},{4,28},{8,16},{12,20},{16,8},{20,12},{24,0},{28,4},{1,25},{... | collective-permute-start | bytes 196616 | tf_op jit(solution)/shard_map/ppermute | solution.py:34
  56.3 5.7 %collective-permute-start.9 = (bf16[64,512]{1,0:T(8,128)(2,1)S(1)}, bf16[64,512]{1,0:T(8,128)(2,1)S(1)}, u32[]{:S(2)}, u32[]{:S(2)}) collective-permute-start(bf16[64,512]{1,0:T(8,128)(2,1)S(1)} %fusion.11.refs_0_), channel_id=1, source_target_pairs={{0,8},{4,12},{8,0},{12,4},{16,24},{20,28},{24,16},{28,20},{1,9},{5... | collective-permute-start | bytes 196616 | tf_op jit(solution)/shard_map/ppermute | solution.py:34
  57.1 10.0 %collective-permute-start.16 = (bf16[4,64,512]{2,1,0:T(8,128)(2,1)S(1)}, bf16[4,64,512]{2,1,0:T(8,128)(2,1)S(1)}, u32[]{:S(2)}, u32[]{:S(2)}) collective-permute-start(bf16[4,64,512]{2,1,0:T(8,128)(2,1)S(1)} %slice.62.refs_0_), channel_id=1, source_target_pairs={{0,8},{4,12},{8,0},{12,4},{16,24},{20,28},{24,16},{28,20},{1,9},{5... | collective-permute-start | bytes 786440 | tf_op jit(solution)/shard_map/ppermute | solution.py:34
  58.4 10.8 %collective-permute-start.17 = (bf16[4,64,512]{2,1,0:T(8,128)(2,1)S(1)}, bf16[4,64,512]{2,1,0:T(8,128)(2,1)S(1)}, u32[]{:S(2)}, u32[]{:S(2)}) collective-permute-start(bf16[4,64,512]{2,1,0:T(8,128)(2,1)S(1)} %slice.62.refs_0_), channel_id=1, source_target_pairs={{0,16},{4,20},{8,24},{12,28},{16,0},{20,4},{24,8},{28,12},{1,17},{... | collective-permute-start | bytes 786440 | tf_op jit(solution)/shard_map/ppermute | solution.py:34
  60.5 10.7 %collective-permute-start.18 = (bf16[4,64,512]{2,1,0:T(8,128)(2,1)S(1)}, bf16[4,64,512]{2,1,0:T(8,128)(2,1)S(1)}, u32[]{:S(2)}, u32[]{:S(2)}) collective-permute-start(bf16[4,64,512]{2,1,0:T(8,128)(2,1)S(1)} %slice.62.refs_0_), channel_id=1, source_target_pairs={{0,24},{4,28},{8,16},{12,20},{16,8},{20,12},{24,0},{28,4},{1,25},{... | collective-permute-start | bytes 786440 | tf_op jit(solution)/shard_map/ppermute | solution.py:34
  63.4 13.0 %collective-permute-start.12 = (bf16[192,512]{1,0:T(8,128)(2,1)S(1)}, bf16[192,512]{1,0:T(8,128)(2,1)S(1)}, u32[]{:S(2)}, u32[]{:S(2)}) collective-permute-start(bf16[192,512]{1,0:T(8,128)(2,1)S(1)} %get-tuple-element.58), channel_id=1, source_target_pairs={{0,2},{1,3},{2,0},{3,1},{4,6},{5,7},{6,4},{7,5},{8,10},{9,11},{10,... | collective-permute-start | bytes 589832 | tf_op jit(solution)/shard_map/ppermute | solution.py:34
  65.8 10.8 %collective-permute-start.19 = (bf16[192,512]{1,0:T(8,128)(2,1)S(1)}, bf16[192,512]{1,0:T(8,128)(2,1)S(1)}, u32[]{:S(2)}, u32[]{:S(2)}) collective-permute-start(bf16[192,512]{1,0:T(8,128)(2,1)S(1)} %get-tuple-element.56), channel_id=1, source_target_pairs={{0,1},{1,0},{2,3},{3,2},{4,5},{5,4},{6,7},{7,6},{8,9},{9,8},{10,11... | collective-permute-start | bytes 589832 | tf_op jit(solution)/shard_map/ppermute | solution.py:34
  67.1 12.2 %collective-permute-start.20 = (bf16[192,512]{1,0:T(8,128)(2,1)S(1)}, bf16[192,512]{1,0:T(8,128)(2,1)S(1)}, u32[]{:S(2)}, u32[]{:S(2)}) collective-permute-start(bf16[192,512]{1,0:T(8,128)(2,1)S(1)} %get-tuple-element.55), channel_id=1, source_target_pairs={{0,3},{1,2},{2,1},{3,0},{4,7},{5,6},{6,5},{7,4},{8,11},{9,10},{10,... | collective-permute-start | bytes 589832 | tf_op jit(solution)/shard_map/ppermute | solution.py:34
  76.5 10.3 %collective-permute-start.13 = (bf16[64,512]{1,0:T(8,128)(2,1)S(1)}, bf16[64,512]{1,0:T(8,128)(2,1)S(1)}, u32[]{:S(2)}, u32[]{:S(2)}) collective-permute-start(bf16[64,512]{1,0:T(8,128)(2,1)S(1)} %get-tuple-element.64), channel_id=1, source_target_pairs={{0,1},{1,0},{2,3},{3,2},{4,5},{5,4},{6,7},{7,6},{8,9},{9,8},{10,11... | collective-permute-start | bytes 196616 | tf_op jit(solution)/shard_map/ppermute | solution.py:34
  80.5 14.1 %collective-permute-start.21 = (bf16[64,2048]{1,0:T(8,128)(2,1)S(1)}, bf16[64,2048]{1,0:T(8,128)(2,1)S(1)}, u32[]{:S(2)}, u32[]{:S(2)}) collective-permute-start(bf16[64,2048]{1,0:T(8,128)(2,1)S(1)} %get-tuple-element.52), channel_id=1, source_target_pairs={{0,8},{4,12},{8,0},{12,4},{16,24},{20,28},{24,16},{28,20},{1,9},{5... | collective-permute-start | bytes 786440 | tf_op jit(solution)/shard_map/ppermute | solution.py:34
  81.8 12.8 %collective-permute-start.22 = (bf16[64,2048]{1,0:T(8,128)(2,1)S(1)}, bf16[64,2048]{1,0:T(8,128)(2,1)S(1)}, u32[]{:S(2)}, u32[]{:S(2)}) collective-permute-start(bf16[64,2048]{1,0:T(8,128)(2,1)S(1)} %get-tuple-element.54), channel_id=1, source_target_pairs={{0,16},{4,20},{8,24},{12,28},{16,0},{20,4},{24,8},{28,12},{1,17},{... | collective-permute-start | bytes 786440 | tf_op jit(solution)/shard_map/ppermute | solution.py:34
  82.6 12.0 %collective-permute-start.23 = (bf16[64,2048]{1,0:T(8,128)(2,1)S(1)}, bf16[64,2048]{1,0:T(8,128)(2,1)S(1)}, u32[]{:S(2)}, u32[]{:S(2)}) collective-permute-start(bf16[64,2048]{1,0:T(8,128)(2,1)S(1)} %get-tuple-element.53), channel_id=1, source_target_pairs={{0,24},{4,28},{8,16},{12,20},{16,8},{20,12},{24,0},{28,4},{1,25},{... | collective-permute-start | bytes 786440 | tf_op jit(solution)/shard_map/ppermute | solution.py:34
  84.1 5.2 %collective-permute-start.14 = (bf16[64,512]{1,0:T(8,128)(2,1)S(1)}, bf16[64,512]{1,0:T(8,128)(2,1)S(1)}, u32[]{:S(2)}, u32[]{:S(2)}) collective-permute-start(bf16[64,512]{1,0:T(8,128)(2,1)S(1)} %get-tuple-element.63), channel_id=1, source_target_pairs={{0,2},{1,3},{2,0},{3,1},{4,6},{5,7},{6,4},{7,5},{8,10},{9,11},{10,... | collective-permute-start | bytes 196616 | tf_op jit(solution)/shard_map/ppermute | solution.py:34
  86.8 6.8 %collective-permute-start.15 = (bf16[64,512]{1,0:T(8,128)(2,1)S(1)}, bf16[64,512]{1,0:T(8,128)(2,1)S(1)}, u32[]{:S(2)}, u32[]{:S(2)}) collective-permute-start(bf16[64,512]{1,0:T(8,128)(2,1)S(1)} %get-tuple-element.62), channel_id=1, source_target_pairs={{0,3},{1,2},{2,1},{3,0},{4,7},{5,6},{6,5},{7,4},{8,11},{9,10},{10,... | collective-permute-start | bytes 196616 | tf_op jit(solution)/shard_map/ppermute | solution.py:34
  93.6 9.4 %copy-start.1 = (bf16[64,512]{1,0:T(8,128)(2,1)S(1)}, bf16[64,512]{1,0:T(8,128)(2,1)}, u32[]{:S(2)}) copy-start(bf16[64,512]{1,0:T(8,128)(2,1)} %get-tuple-element.42) | copy-start | bytes 196612
  94.8 4.5 %collective-permute-start.24 = (bf16[64,512]{1,0:T(8,128)(2,1)S(1)}, bf16[64,512]{1,0:T(8,128)(2,1)S(1)}, u32[]{:S(2)}, u32[]{:S(2)}) collective-permute-start(bf16[64,512]{1,0:T(8,128)(2,1)S(1)} %get-tuple-element.59), channel_id=1, source_target_pairs={{0,1},{1,0},{2,3},{3,2},{4,5},{5,4},{6,7},{7,6},{8,9},{9,8},{10,11... | collective-permute-start | bytes 196616 | tf_op jit(solution)/shard_map/ppermute | solution.py:34
  94.9 5.2 %collective-permute-start.25 = (bf16[64,512]{1,0:T(8,128)(2,1)S(1)}, bf16[64,512]{1,0:T(8,128)(2,1)S(1)}, u32[]{:S(2)}, u32[]{:S(2)}) collective-permute-start(bf16[64,512]{1,0:T(8,128)(2,1)S(1)} %get-tuple-element.61), channel_id=1, source_target_pairs={{0,2},{1,3},{2,0},{3,1},{4,6},{5,7},{6,4},{7,5},{8,10},{9,11},{10,... | collective-permute-start | bytes 196616 | tf_op jit(solution)/shard_map/ppermute | solution.py:34
  96.9 6.1 %collective-permute-start.26 = (bf16[64,512]{1,0:T(8,128)(2,1)S(1)}, bf16[64,512]{1,0:T(8,128)(2,1)S(1)}, u32[]{:S(2)}, u32[]{:S(2)}) collective-permute-start(bf16[64,512]{1,0:T(8,128)(2,1)S(1)} %get-tuple-element.60), channel_id=1, source_target_pairs={{0,3},{1,2},{2,1},{3,0},{4,7},{5,6},{6,5},{7,4},{8,11},{9,10},{10,... | collective-permute-start | bytes 196616 | tf_op jit(solution)/shard_map/ppermute | solution.py:34
